TPU v7x, 32 devices: a whole 2x2x4 slice. The times are simulated.
32 devices in a mesh: dp: 8 (over z, core), seq: 4 (over y, x).
Axes of the slice: x: 2, y: 2, z: 4, core: 2. Of those that a mesh axis runs over, the one named last changes fastest.
Arguments:
- inputs: bfloat16 [16, 1024, 1024], P('dp', 'seq'), may hold values from -6 to 6
- cotangent: bfloat16 [16, 1024, 1024], P('dp', 'seq'), may hold values from -6 to 6
- segments: int32 [16, 1024], P('dp', 'seq'), may hold values from 0 to 4, as said below
- w_in: float32 [1024, 3072], P(('dp', 'seq')), may hold values from -0.1875 to 0.1875
- w_out: float32 [1024, 1024], P(('dp', 'seq')), may hold values from -0.1875 to 0.1875
- conv_w: float32 [3, 1024], P(None, ('dp', 'seq')), may hold values from -3.5 to 3.5
- w_gate: float32 [1024, 4608], P(('dp', 'seq')), may hold values from -0.1875 to 0.1875
- w_up: float32 [1024, 4608], P(('dp', 'seq')), may hold values from -0.1875 to 0.1875
- w_down: float32 [4608, 1024], P(('dp', 'seq')), may hold values from -0.09375 to 0.09375
- gains: float32 [2, 1024], P(None, ('dp', 'seq')), may hold values from 0.5 to 1.5
- m_in: float32 [1024, 3072], P(('dp', 'seq')), may hold values from -80 to 80
- m_out: float32 [1024, 1024], P(('dp', 'seq')), may hold values from -96 to 96
- m_conv: float32 [3, 1024], P(None, ('dp', 'seq')), may hold values from -80 to 80
- m_gate: float32 [1024, 4608], P(('dp', 'seq')), may hold values from -24 to 24
- m_up: float32 [1024, 4608], P(('dp', 'seq')), may hold values from -24 to 24
- m_down: float32 [4608, 1024], P(('dp', 'seq')), may hold values from -48 to 48
- m_gains: float32 [2, 1024], P(None, ('dp', 'seq')), may hold values from -80 to 80
- v_in: float32 [1024, 3072], P(('dp', 'seq')), may hold values from 868.352 to 3440.64
- v_out: float32 [1024, 1024], P(('dp', 'seq')), may hold values from 1245.184 to 4915.2
- v_conv: float32 [3, 1024], P(None, ('dp', 'seq')), may hold values from 868.352 to 3440.64
- v_gate: float32 [1024, 4608], P(('dp', 'seq')), may hold values from 78.6432 to 311.296
- v_up: float32 [1024, 4608], P(('dp', 'seq')), may hold values from 78.6432 to 311.296
- v_down: float32 [4608, 1024], P(('dp', 'seq')), may hold values from 311.296 to 1245.184
- v_gains: float32 [2, 1024], P(None, ('dp', 'seq')), may hold values from 868.352 to 3440.64
Outputs:
- output: bfloat16 [16, 1024, 1024], P('dp', 'seq')
- input_grad: float32 [16, 1024, 1024], P('dp', 'seq')
- new_w_in: float32 [1024, 3072], P(('dp', 'seq'))
- new_w_out: float32 [1024, 1024], P(('dp', 'seq'))
- new_conv_w: float32 [3, 1024], P(None, ('dp', 'seq'))
- new_w_gate: float32 [1024, 4608], P(('dp', 'seq'))
- new_w_up: float32 [1024, 4608], P(('dp', 'seq'))
- new_w_down: float32 [4608, 1024], P(('dp', 'seq'))
- new_gains: float32 [2, 1024], P(None, ('dp', 'seq'))
- new_m_in: float32 [1024, 3072], P(('dp', 'seq'))
- new_m_out: float32 [1024, 1024], P(('dp', 'seq'))
- new_m_conv: float32 [3, 1024], P(None, ('dp', 'seq'))
- new_m_gate: float32 [1024, 4608], P(('dp', 'seq'))
- new_m_up: float32 [1024, 4608], P(('dp', 'seq'))
- new_m_down: float32 [4608, 1024], P(('dp', 'seq'))
- new_m_gains: float32 [2, 1024], P(None, ('dp', 'seq'))
- new_v_in: float32 [1024, 3072], P(('dp', 'seq'))
- new_v_out: float32 [1024, 1024], P(('dp', 'seq'))
- new_v_conv: float32 [3, 1024], P(None, ('dp', 'seq'))
- new_v_gate: float32 [1024, 4608], P(('dp', 'seq'))
- new_v_up: float32 [1024, 4608], P(('dp', 'seq'))
- new_v_down: float32 [4608, 1024], P(('dp', 'seq'))
- new_v_gains: float32 [2, 1024], P(None, ('dp', 'seq'))
Inputs may be any that keep to these rules, and one draw needn't show every extreme that they name: `segments`: within each sequence the numbers never fall. In each group of 2 sequences on one index of dp, one sequence has a single document covering positions 255 to 768.
All inputs are finite; a program needn't handle non-finite values.
Results may differ from a plain program's by a relative error of at most 0.012.
The roundings to bfloat16 on the way count: a program that leaves them out, or rounds other values in their place, can miss the bound.
Values may be sent and summed in bfloat16 or wider, within the bound.
No kernel may reach another device: no remote copies, remote signals or barrier semaphores. Data moves between devices by JAX's collectives and lax.ppermute only.
A program may use at most 192 MiB of HBM per device.

v0:
```python
import jax
import jax.numpy as jnp
from jax import lax
from jax.sharding import PartitionSpec as P

STEP = 10


norm_eps = 1e-05
learn_rate = 0.02
small_rate = 1.0
beta_one = 0.9
beta_two = 0.95
adam_eps = 1e-08
weight_decay = 0.1


def from_behind(shard, axis, by):
    peers = lax.axis_size(axis)
    pairs = [(i, i + by) for i in range(peers) if 0 <= i + by < peers]
    return lax.ppermute(shard, axis, pairs)


def left_contract(first, second):
    return lax.dot_general(
        first, second, (((0,), (0,)), ((), ())), preferred_element_type=jnp.float32
    )


def right_contract(first, second):
    return lax.dot_general(
        first, second, (((1,), (1,)), ((), ())), preferred_element_type=jnp.float32
    )


def normed(values, gain):
    scale = lax.rsqrt(jnp.mean(values * values, -1, keepdims=True) + norm_eps)
    unit = values * scale
    return (unit, scale, (unit * gain).astype(jnp.bfloat16))


def norm_back(grad_out, unit, scale, gain):
    grad_gain = jnp.sum(grad_out * unit, 0)
    grad_unit = grad_out * gain
    grad_in = scale * (grad_unit - unit * jnp.mean(grad_unit * unit, -1, keepdims=True))
    return (grad_in, grad_gain)


def adamw(master, first, second, grad, rate, decay):
    first_new = beta_one * first + (1.0 - beta_one) * grad
    second_new = beta_two * second + (1.0 - beta_two) * grad * grad
    first_hat = first_new / (1.0 - beta_one**STEP)
    second_hat = second_new / (1.0 - beta_two**STEP)
    master_new = master - rate * (first_hat / (jnp.sqrt(second_hat) + adam_eps) + decay * master)
    return (master_new, first_new, second_new)


def local(
    inputs,
    cotangent,
    segments,
    w_in,
    w_out,
    conv_w,
    w_gate,
    w_up,
    w_down,
    gains,
    m_in,
    m_out,
    m_conv,
    m_gate,
    m_up,
    m_down,
    m_gains,
    v_in,
    v_out,
    v_conv,
    v_gate,
    v_up,
    v_down,
    v_gains,
):
    seqs_here, stretch, width = inputs.shape
    rows = seqs_here * stretch
    low_in = w_in.astype(jnp.bfloat16)
    low_out = w_out.astype(jnp.bfloat16)
    low_conv = conv_w.astype(jnp.bfloat16)
    low_gate = w_gate.astype(jnp.bfloat16)
    low_up = w_up.astype(jnp.bfloat16)
    low_down = w_down.astype(jnp.bfloat16)
    low_gains = gains.astype(jnp.bfloat16)
    full_w = (
        lax.all_gather(low_in, ("dp", "seq"), axis=0, tiled=True),
        lax.all_gather(low_out, ("dp", "seq"), axis=0, tiled=True),
        lax.all_gather(low_conv, ("dp", "seq"), axis=1, tiled=True),
        lax.all_gather(low_gate, ("dp", "seq"), axis=0, tiled=True),
        lax.all_gather(low_up, ("dp", "seq"), axis=0, tiled=True),
        lax.all_gather(low_down, ("dp", "seq"), axis=0, tiled=True),
        lax.all_gather(low_gains, ("dp", "seq"), axis=1, tiled=True),
    )
    mat_in, mat_out, conv_taps, mat_gate, mat_up, mat_down, gain_pair = full_w
    taps = conv_taps.astype(jnp.float32)
    gain_vals = gain_pair.astype(jnp.float32)
    residual = inputs.reshape(rows, width).astype(jnp.float32)
    unit_one, scale_one, norm_one = normed(residual, gain_vals[0])
    projected = jnp.dot(norm_one, mat_in, preferred_element_type=jnp.float32)
    b_gate = projected[:, :width]
    c_gate = projected[:, width : 2 * width]
    x_part = projected[:, 2 * width :]
    conv_in = (b_gate * x_part).astype(jnp.bfloat16).reshape(seqs_here, stretch, width)
    prev_rows, prev_ids = from_behind(
        (conv_in[:, -2:, :], segments[:, -2:].astype(jnp.bfloat16)), "seq", 1
    )
    extended = jnp.concatenate([prev_rows, conv_in], 1).astype(jnp.float32)
    ext_ids = jnp.concatenate([prev_ids.astype(jnp.int32), segments], 1)
    near_one = (ext_ids[:, 1:-1] == segments).astype(jnp.float32)[..., None]
    near_two = (ext_ids[:, :-2] == segments).astype(jnp.float32)[..., None]
    tap_now = extended[:, 2:]
    tap_one = extended[:, 1:-1] * near_one
    tap_two = extended[:, :-2] * near_two
    conv_out = (taps[2] * tap_now + taps[1] * tap_one + taps[0] * tap_two).reshape(rows, width)
    mixed_in = (c_gate * conv_out).astype(jnp.bfloat16)
    middle = residual + jnp.dot(mixed_in, mat_out, preferred_element_type=jnp.float32)
    unit_two, scale_two, norm_two = normed(middle, gain_vals[1])
    gate = jnp.dot(norm_two, mat_gate, preferred_element_type=jnp.float32)
    up_part = jnp.dot(norm_two, mat_up, preferred_element_type=jnp.float32)
    sigma = jax.nn.sigmoid(gate)
    silu_vals = gate * sigma
    hidden = (silu_vals * up_part).astype(jnp.bfloat16)
    output = (middle + jnp.dot(hidden, mat_down, preferred_element_type=jnp.float32)).astype(
        jnp.bfloat16
    )
    grad_top = cotangent.reshape(rows, width)
    grad_down = left_contract(hidden, grad_top)
    grad_hidden = right_contract(grad_top, mat_down)
    grad_gate_act = (grad_hidden * up_part * sigma * (1.0 + gate * (1.0 - sigma))).astype(
        jnp.bfloat16
    )
    grad_up_act = (grad_hidden * silu_vals).astype(jnp.bfloat16)
    grad_gate = left_contract(norm_two, grad_gate_act)
    grad_up = left_contract(norm_two, grad_up_act)
    grad_norm_two = right_contract(grad_gate_act, mat_gate) + right_contract(grad_up_act, mat_up)
    back_two, gain_two = norm_back(grad_norm_two, unit_two, scale_two, gain_vals[1])
    grad_middle = grad_top.astype(jnp.float32) + back_two
    grad_branch = grad_middle.astype(jnp.bfloat16)
    grad_out = left_contract(mixed_in, grad_branch)
    grad_mixed = right_contract(grad_branch, mat_out)
    grad_c = grad_mixed * conv_out
    grad_conv = (grad_mixed * c_gate).reshape(seqs_here, stretch, width)
    grad_taps = jnp.stack(
        [
            jnp.sum(tap_two * grad_conv, (0, 1)),
            jnp.sum(tap_one * grad_conv, (0, 1)),
            jnp.sum(tap_now * grad_conv, (0, 1)),
        ],
        0,
    )
    term_now = taps[2] * grad_conv
    term_one = taps[1] * grad_conv * near_one
    term_two = taps[0] * grad_conv * near_two
    grad_ext = (
        jnp.pad(term_now, ((0, 0), (2, 0), (0, 0)))
        + jnp.pad(term_one, ((0, 0), (1, 1), (0, 0)))
        + jnp.pad(term_two, ((0, 0), (0, 2), (0, 0)))
    )
    next_terms = from_behind(grad_ext[:, :2, :], "seq", -1)
    grad_conv_in = (
        grad_ext[:, 2:, :] + jnp.pad(next_terms, ((0, 0), (stretch - 2, 0), (0, 0)))
    ).reshape(rows, width)
    grad_proj = jnp.concatenate([grad_conv_in * x_part, grad_c, grad_conv_in * b_gate], -1).astype(
        jnp.bfloat16
    )
    grad_in = left_contract(norm_one, grad_proj)
    grad_norm_one = right_contract(grad_proj, mat_in)
    back_one, gain_one = norm_back(grad_norm_one, unit_one, scale_one, gain_vals[0])
    input_grad = (grad_middle + back_one).reshape(seqs_here, stretch, width)
    grad_gains = jnp.stack([gain_one, gain_two], 0)
    reduced = (
        lax.psum_scatter(grad_in, ("dp", "seq"), scatter_dimension=0, tiled=True),
        lax.psum_scatter(grad_out, ("dp", "seq"), scatter_dimension=0, tiled=True),
        lax.psum_scatter(grad_taps, ("dp", "seq"), scatter_dimension=1, tiled=True),
        lax.psum_scatter(grad_gate, ("dp", "seq"), scatter_dimension=0, tiled=True),
        lax.psum_scatter(grad_up, ("dp", "seq"), scatter_dimension=0, tiled=True),
        lax.psum_scatter(grad_down, ("dp", "seq"), scatter_dimension=0, tiled=True),
        lax.psum_scatter(grad_gains, ("dp", "seq"), scatter_dimension=1, tiled=True),
    )
    masters = (w_in, w_out, conv_w, w_gate, w_up, w_down, gains)
    firsts = (m_in, m_out, m_conv, m_gate, m_up, m_down, m_gains)
    seconds = (v_in, v_out, v_conv, v_gate, v_up, v_down, v_gains)
    rates = (learn_rate, learn_rate, small_rate, learn_rate, learn_rate, learn_rate, small_rate)
    decays = (weight_decay, weight_decay, 0.0, weight_decay, weight_decay, weight_decay, 0.0)
    updated = [
        adamw(
            masters[index],
            firsts[index],
            seconds[index],
            reduced[index],
            rates[index],
            decays[index],
        )
        for index in range(7)
    ]
    new_w = [item[0] for item in updated]
    new_m = [item[1] for item in updated]
    new_v = [item[2] for item in updated]
    return (
        output.reshape(seqs_here, stretch, width),
        input_grad,
        new_w[0],
        new_w[1],
        new_w[2],
        new_w[3],
        new_w[4],
        new_w[5],
        new_w[6],
        new_m[0],
        new_m[1],
        new_m[2],
        new_m[3],
        new_m[4],
        new_m[5],
        new_m[6],
        new_v[0],
        new_v[1],
        new_v[2],
        new_v[3],
        new_v[4],
        new_v[5],
        new_v[6],
    )


def solution(mesh):
    return jax.shard_map(
        local,
        mesh=mesh,
        in_specs=(
            P("dp", "seq", None),
            P("dp", "seq", None),
            P("dp", "seq"),
            P(("dp", "seq"), None),
            P(("dp", "seq"), None),
            P(None, ("dp", "seq")),
            P(("dp", "seq"), None),
            P(("dp", "seq"), None),
            P(("dp", "seq"), None),
            P(None, ("dp", "seq")),
            P(("dp", "seq"), None),
            P(("dp", "seq"), None),
            P(None, ("dp", "seq")),
            P(("dp", "seq"), None),
            P(("dp", "seq"), None),
            P(("dp", "seq"), None),
            P(None, ("dp", "seq")),
            P(("dp", "seq"), None),
            P(("dp", "seq"), None),
            P(None, ("dp", "seq")),
            P(("dp", "seq"), None),
            P(("dp", "seq"), None),
            P(("dp", "seq"), None),
            P(None, ("dp", "seq")),
        ),
        out_specs=(
            P("dp", "seq", None),
            P("dp", "seq", None),
            P(("dp", "seq"), None),
            P(("dp", "seq"), None),
            P(None, ("dp", "seq")),
            P(("dp", "seq"), None),
            P(("dp", "seq"), None),
            P(("dp", "seq"), None),
            P(None, ("dp", "seq")),
            P(("dp", "seq"), None),
            P(("dp", "seq"), None),
            P(None, ("dp", "seq")),
            P(("dp", "seq"), None),
            P(("dp", "seq"), None),
            P(("dp", "seq"), None),
            P(None, ("dp", "seq")),
            P(("dp", "seq"), None),
            P(("dp", "seq"), None),
            P(None, ("dp", "seq")),
            P(("dp", "seq"), None),
            P(("dp", "seq"), None),
            P(("dp", "seq"), None),
            P(None, ("dp", "seq")),
        ),
        check_vma=False,
    )
```

profile of v0, /device:TPU:8, one launch (start us, length us, event | category | flops | bytes accessed | tf_op | source)
XLA Modules:
  0.0 1655.8 jit_solution(3580765805610579751)
XLA Ops:
  14.5 3.4 collective-permute-start.1
  18.2 54.7 %all-gather = bf16[32,32,2]{1,2,0:T(2,128)(2,1)S(1)} all-gather(bf16[1,32,2]{1,2,0:T(2,128)(2,1)S(1)} %convert_bitcast_fusion.1), channel_id=1, replica_groups=mesh['dp'=8,'seq'=4] {'dp','seq'}, dimensions={0}, use_global_device_ids=true | all-gather | bytes 4224 | tf_op jit(solution)/shard_map/all_gather | solution.py:100
  73.0 63.1 %all-gather.1 = bf16[32,32,3]{1,2,0:T(4,128)(2,1)S(1)} all-gather(bf16[1,32,3]{1,2,0:T(4,128)(2,1)S(1)} %convert_bitcast_fusion), channel_id=1, replica_groups=mesh['dp'=8,'seq'=4] {'dp','seq'}, dimensions={0}, use_global_device_ids=true | all-gather | bytes 6336 | tf_op jit(solution)/shard_map/all_gather | solution.py:96
  136.6 5.9 fusion.41
  142.8 4.2 collective-permute-start
  152.3 3.3 multiply_reduce_fusion.5
  157.2 68.1 %all-gather.14.cloned.1.call-done = bf16[1024,4608]{1,0:T(8,128)(2,1)} async-done(((bf16[32,4608]{1,0:T(8,128)(2,1)}), bf16[1024,4608]{1,0:T(8,128)(2,1)}) %all-gather.14.cloned.1.call-update) | async-done | bytes 9437200 | tf_op jit(solution)/shard_map/all_gather | solution.py:98
  225.3 11.3 fusion.43
  236.6 72.7 %all-gather.12.cloned.1.call-done = bf16[1024,4608]{1,0:T(8,128)(2,1)} async-done(((bf16[32,4608]{1,0:T(8,128)(2,1)}), bf16[1024,4608]{1,0:T(8,128)(2,1)}) %all-gather.12.cloned.1.call-update) | async-done | bytes 9437200 | tf_op jit(solution)/shard_map/all_gather | solution.py:97
  309.3 11.0 fusion.42
  320.3 72.9 %all-gather.16.cloned.1.call-done = bf16[4608,1024]{1,0:T(8,128)(2,1)} async-done(((bf16[144,1024]{1,0:T(8,128)(2,1)}), bf16[4608,1024]{1,0:T(8,128)(2,1)}) %all-gather.16.cloned.1.call-update) | async-done | bytes 9437200 | tf_op jit(solution)/shard_map/all_gather | solution.py:99
  393.3 17.9 %multiply_convert_fusion = (bf16[512,4608]{1,0:T(8,128)(2,1)}, bf16[512,4608]{1,0:T(8,128)(2,1)}, bf16[512,4608]{1,0:T(8,128)(2,1)}) fusion(f32[512,4608]{1,0:T(8,128)} %fusion.42, f32[512,4608]{1,0:T(8,128)} %fusion.43, bf16[512,1024]{1,0:T(8,128)(2,1)} %bitcast.109, bf16[4608,1024]{1,0:T(8,128)(2,1)} %all-gather.16.cloned.1.call-done), kind=kOutput, calls=%fused_computation | convolution fusion | flops 4867227648 | bytes 43515904 | tf_op jit(solution)/shard_map/dot_general | solution.py:31
  411.2 9.2 fusion.44
  420.4 8.1 multiply_reduce_fusion
  430.1 5.0 multiply_reduce_fusion.3
  440.2 3.2 collective-permute-done.2
  445.4 3.5 fusion.1
  449.0 5.0 fusion.14
  455.1 4.5 fusion.21
  459.7 10.2 fusion.16
  469.9 11.8 fusion.46
  481.8 11.6 fusion.45
  494.6 11.4 fusion.47
  506.0 10.3 add_convert_fusion
  518.3 44.3 %reduce-scatter.22.cloned.1.call-done = f32[32,3]{1,0:T(8,128)} async-done(((f32[1024,3]{1,0:T(8,128)}), f32[32,3]{1,0:T(8,128)}) %reduce-scatter.22.cloned.1.call-update) | async-done | bytes 400
  564.0 131.3 %reduce-scatter.24.cloned.1.call-done = f32[32,2]{1,0:T(8,128)} async-done(((f32[1024,2]{1,0:T(8,128)}), f32[32,2]{1,0:T(8,128)}) %reduce-scatter.24.cloned.1.call-update) | async-done | bytes 272
  696.7 140.3 %reduce-scatter.14.cloned.1.call-done = f32[32,1024]{1,0:T(8,128)} async-done(((f32[1024,1024]{1,0:T(8,128)}), f32[32,1024]{1,0:T(8,128)}) %reduce-scatter.14.cloned.1.call-update) | async-done | bytes 131088 | tf_op jit(solution)/shard_map/reduce_scatter | solution.py:181
  838.8 168.0 %reduce-scatter.12.cloned.1.call-done = f32[32,3072]{1,0:T(8,128)} async-done(((f32[1024,3072]{1,0:T(8,128)}), f32[32,3072]{1,0:T(8,128)}) %reduce-scatter.12.cloned.1.call-update) | async-done | bytes 393232 | tf_op jit(solution)/shard_map/reduce_scatter | solution.py:180
  1009.2 210.4 %reduce-scatter.18.cloned.1.call-done = f32[32,4608]{1,0:T(8,128)} async-done(((f32[1024,4608]{1,0:T(8,128)}), f32[32,4608]{1,0:T(8,128)}) %reduce-scatter.18.cloned.1.call-update) | async-done | bytes 589840 | tf_op jit(solution)/shard_map/reduce_scatter | solution.py:184
  1222.2 210.8 %reduce-scatter.16.cloned.1.call-done = f32[32,4608]{1,0:T(8,128)} async-done(((f32[1024,4608]{1,0:T(8,128)}), f32[32,4608]{1,0:T(8,128)}) %reduce-scatter.16.cloned.1.call-update) | async-done | bytes 589840 | tf_op jit(solution)/shard_map/reduce_scatter | solution.py:183
  1435.5 210.4 %reduce-scatter.20.cloned.1.call-done = f32[144,1024]{1,0:T(8,128)} async-done(((f32[4608,1024]{1,0:T(8,128)}), f32[144,1024]{1,0:T(8,128)}) %reduce-scatter.20.cloned.1.call-update) | async-done | bytes 589840 | tf_op jit(solution)/shard_map/reduce_scatter | solution.py:185
  1645.9 2.6 multiply_subtract_fusion
  (169 shorter events, 40.2 us)
Async XLA Ops:
  7.2 129.3 %all-gather.8.cloned.1.call-start = ((), (), s32[]{:S(2)}) async-start(), calls=%async_computation.7 | async-start | bytes 6488064 | tf_op jit(solution)/shard_map/all_gather | solution.py:94
  9.1 143.2 %all-gather.10.cloned.1.call-start = ((), (), s32[]{:S(2)}) async-start(), calls=%async_computation.8 | async-start | bytes 2162688 | tf_op jit(solution)/shard_map/all_gather | solution.py:95
  10.8 214.5 %all-gather.14.cloned.1.call-start = ((), (), s32[]{:S(2)}) async-start(), calls=%async_computation.10 | async-start | bytes 9732096 | tf_op jit(solution)/shard_map/all_gather | solution.py:98
  12.6 60.3 %copy-start.35 = (f32[3,32]{1,0:T(4,128)S(1)}, f32[3,32]{1,0:T(4,128)}, u32[]{:S(2)}) copy-start(f32[3,32]{1,0:T(4,128)} %param.29) | copy-start | bytes 1156
  12.7 296.6 %all-gather.12.cloned.1.call-start = ((), (), s32[]{:S(2)}) async-start(), calls=%async_computation.9 | async-start | bytes 9732096 | tf_op jit(solution)/shard_map/all_gather | solution.py:97
  13.5 379.8 %all-gather.16.cloned.1.call-start = ((), (), s32[]{:S(2)}) async-start(), calls=%async_computation.11 | async-start | bytes 9732096 | tf_op jit(solution)/shard_map/all_gather | solution.py:99
  14.3 548.3 %reduce-scatter.22.cloned.1.call-start = ((), (), s32[]{:S(2)}) async-start(), calls=%async_computation.17 | async-start | bytes 540672
  14.5 122.1 %collective-permute-start.1 = (bf16[2,2]{1,0:T(2,128)(2,1)S(1)}, bf16[2,2]{1,0:T(2,128)(2,1)S(1)}, u32[]{:S(2)}, u32[]{:S(2)}) collective-permute-start(bf16[2,2]{1,0:T(2,128)(2,1)S(1)} %slice_convert_fusion), channel_id=1, source_target_pairs={{0,1},{1,2},{2,3},{4,5},{5,6},{6,7},{8,9},{9,10},{10,11},{12,13},{... | collective-permute-start | bytes 32 | tf_op jit(solution)/shard_map/ppermute | solution.py:21
  142.8 5.5 collective-permute-start
  437.7 5.6 collective-permute-start.2
  440.1 255.2 %reduce-scatter.24.cloned.1.call-start = ((), (), s32[]{:S(2)}) async-start(), calls=%async_computation.18 | async-start | bytes 540672
  455.1 382.0 %reduce-scatter.14.cloned.1.call-start = ((), (), s32[]{:S(2)}) async-start(), calls=%async_computation.13 | async-start | bytes 4325376 | tf_op jit(solution)/shard_map/reduce_scatter | solution.py:181
  459.6 547.2 %reduce-scatter.12.cloned.1.call-start = ((), (), s32[]{:S(2)}) async-start(), calls=%async_computation.12 | async-start | bytes 12976128 | tf_op jit(solution)/shard_map/reduce_scatter | solution.py:180
  469.9 749.7 %reduce-scatter.18.cloned.1.call-start = ((), (), s32[]{:S(2)}) async-start(), calls=%async_computation.15 | async-start | bytes 19464192 | tf_op jit(solution)/shard_map/reduce_scatter | solution.py:184
  481.7 951.2 %reduce-scatter.16.cloned.1.call-start = ((), (), s32[]{:S(2)}) async-start(), calls=%async_computation.14 | async-start | bytes 19464192 | tf_op jit(solution)/shard_map/reduce_scatter | solution.py:183
  493.4 1152.5 %reduce-scatter.20.cloned.1.call-start = ((), (), s32[]{:S(2)}) async-start(), calls=%async_computation.16 | async-start | bytes 19464192 | tf_op jit(solution)/shard_map/reduce_scatter | solution.py:185
  516.4 179.7 %copy-start.41 = (f32[2,32]{1,0:T(2,128)S(1)}, f32[2,32]{1,0:T(2,128)}, u32[]{:S(2)}) copy-start(f32[2,32]{1,0:T(2,128)} %param.33) | copy-start | bytes 772
  516.4 179.7 %copy-start.42 = (f32[2,32]{1,0:T(2,128)S(1)}, f32[2,32]{1,0:T(2,128)}, u32[]{:S(2)}) copy-start(f32[2,32]{1,0:T(2,128)} %param.40) | copy-start | bytes 772
  516.4 179.7 %copy-start.43 = (f32[2,32]{1,0:T(2,128)S(1)}, f32[2,32]{1,0:T(2,128)}, u32[]{:S(2)}) copy-start(f32[2,32]{1,0:T(2,128)} %param.47) | copy-start | bytes 772
  516.4 320.7 %copy-start.32 = (f32[32,1024]{1,0:T(8,128)S(1)}, f32[32,1024]{1,0:T(8,128)}, u32[]{:S(2)}) copy-start(f32[32,1024]{1,0:T(8,128)} %param.28) | copy-start | bytes 393220
  516.4 320.6 %copy-start.33 = (f32[32,1024]{1,0:T(8,128)S(1)}, f32[32,1024]{1,0:T(8,128)}, u32[]{:S(2)}) copy-start(f32[32,1024]{1,0:T(8,128)} %param.35) | copy-start | bytes 393220
  516.4 320.6 %copy-start.34 = (f32[32,1024]{1,0:T(8,128)S(1)}, f32[32,1024]{1,0:T(8,128)}, u32[]{:S(2)}) copy-start(f32[32,1024]{1,0:T(8,128)} %param.42) | copy-start | bytes 393220
  516.4 490.4 %copy-start.23 = (f32[32,3072]{1,0:T(8,128)S(1)}, f32[32,3072]{1,0:T(8,128)}, u32[]{:S(2)}) copy-start(f32[32,3072]{1,0:T(8,128)} %param.27) | copy-start | bytes 1179652
  518.3 701.3 %copy-start.16 = (f32[32,4608]{1,0:T(8,128)S(1)}, f32[32,4608]{1,0:T(8,128)}, u32[]{:S(2)}) copy-start(f32[32,4608]{1,0:T(8,128)} %param.31) | copy-start | bytes 1769476
  518.3 701.3 %copy-start.26 = (f32[32,4608]{1,0:T(8,128)S(1)}, f32[32,4608]{1,0:T(8,128)}, u32[]{:S(2)}) copy-start(f32[32,4608]{1,0:T(8,128)} %param.38) | copy-start | bytes 1769476
  518.3 701.3 %copy-start.27 = (f32[32,4608]{1,0:T(8,128)S(1)}, f32[32,4608]{1,0:T(8,128)}, u32[]{:S(2)}) copy-start(f32[32,4608]{1,0:T(8,128)} %param.45) | copy-start | bytes 1769476
  1009.2 423.7 %copy-start.18 = (f32[32,4608]{1,0:T(8,128)S(1)}, f32[32,4608]{1,0:T(8,128)}, u32[]{:S(2)}) copy-start(f32[32,4608]{1,0:T(8,128)} %param.30) | copy-start | bytes 1769476
  1009.2 423.7 %copy-start.28 = (f32[32,4608]{1,0:T(8,128)S(1)}, f32[32,4608]{1,0:T(8,128)}, u32[]{:S(2)}) copy-start(f32[32,4608]{1,0:T(8,128)} %param.37) | copy-start | bytes 1769476
  1009.2 423.7 %copy-start.29 = (f32[32,4608]{1,0:T(8,128)S(1)}, f32[32,4608]{1,0:T(8,128)}, u32[]{:S(2)}) copy-start(f32[32,4608]{1,0:T(8,128)} %param.44) | copy-start | bytes 1769476
  1222.1 423.7 %copy-start.20 = (f32[144,1024]{1,0:T(8,128)S(1)}, f32[144,1024]{1,0:T(8,128)}, u32[]{:S(2)}) copy-start(f32[144,1024]{1,0:T(8,128)} %param.32) | copy-start | bytes 1769476
  1222.1 423.7 %copy-start.30 = (f32[144,1024]{1,0:T(8,128)S(1)}, f32[144,1024]{1,0:T(8,128)}, u32[]{:S(2)}) copy-start(f32[144,1024]{1,0:T(8,128)} %param.39) | copy-start | bytes 1769476
  1222.2 423.7 %copy-start.31 = (f32[144,1024]{1,0:T(8,128)S(1)}, f32[144,1024]{1,0:T(8,128)}, u32[]{:S(2)}) copy-start(f32[144,1024]{1,0:T(8,128)} %param.46) | copy-start | bytes 1769476
  (29 other events, 289.6 us)
Sparse Core Ops, SparseCore 0:
  11.5 70.8 all-gather.7
  85.9 54.0 all-gather.9
  143.5 81.7 all-gather.13
  228.6 80.6 all-gather.11
  312.6 80.6 all-gather.15
  440.2 122.3 reduce-scatter.21
  565.5 129.7 reduce-scatter.23
  697.6 139.4 reduce-scatter.13
  843.1 163.6 reduce-scatter.11
  1014.2 205.3 reduce-scatter.17
  1227.1 205.7 reduce-scatter.15
  1440.3 205.5 reduce-scatter.19
where the time goes:
time: 1660 us
  waiting for transfers between devices  1330 us (80%)
  matrix products  136 us (8%)
  blocking collectives  118 us (7%)
  other arithmetic  34.1 us (2%)
    reduce_scatter x1, waiting for transfers between devices, local(): lax.psum_scatter(grad_gate, ('dp', 'seq'), scatter_dimension=0, tiled=True)  211 us
    reduce_scatter x1, waiting for transfers between devices, local(): lax.psum_scatter(grad_down, ('dp', 'seq'), scatter_dimension=0, tiled=True)  210 us
    reduce_scatter x1, waiting for transfers between devices, local(): lax.psum_scatter(grad_up, ('dp', 'seq'), scatter_dimension=0, tiled=True)  210 us
    unnamed x14, waiting for transfers between devices  176 us
    reduce_scatter x1, waiting for transfers between devices, local(): lax.psum_scatter(grad_in, ('dp', 'seq'), scatter_dimension=0, tiled=True)  168 us
    reduce_scatter x1, waiting for transfers between devices, local(): lax.psum_scatter(grad_out, ('dp', 'seq'), scatter_dimension=0, tiled=True)  140 us
    all_gather x1, waiting for transfers between devices, local(): lax.all_gather(low_down, ('dp', 'seq'), axis=0, tiled=True)  72.9 us
    all_gather x1, waiting for transfers between devices, local(): lax.all_gather(low_gate, ('dp', 'seq'), axis=0, tiled=True)  72.7 us
  transfers between devices with their start and end apart: 15, of which 12 were waited for; matrix products, arithmetic and copies ran while one was open for 8% of the time, Pallas kernels for 0%

commit v1 on v0

v1 whole, which is shorter than its diff:
```python
import jax
import jax.numpy as jnp
from jax import lax
from jax.sharding import PartitionSpec as P

STEP = 10


norm_eps = 1e-05
learn_rate = 0.02
small_rate = 1.0
beta_one = 0.9
beta_two = 0.95
adam_eps = 1e-08
weight_decay = 0.1
LANES = 128
bf16 = jnp.bfloat16
f32 = jnp.float32


def from_behind(shard, axis, by):
    peers = lax.axis_size(axis)
    pairs = [(i, i + by) for i in range(peers) if 0 <= i + by < peers]
    return lax.ppermute(shard, axis, pairs)


def to_sibling(block):
    return lax.ppermute(block, "dp", [(i, i ^ 1) for i in range(lax.axis_size("dp"))])


def along_z(block, by):
    count = lax.axis_size("dp")
    return lax.ppermute(block, "dp", [(i, (i + 2 * by) % count) for i in range(count)])


def across_seq(block, by):
    return lax.ppermute(block, "seq", [(i, i ^ by) for i in range(lax.axis_size("seq"))])


def dot(first, second):
    return jnp.dot(first, second, preferred_element_type=f32)


def left_contract(first, second):
    return lax.dot_general(first, second, (((0,), (0,)), ((), ())), preferred_element_type=f32)


def right_contract(first, second):
    return lax.dot_general(first, second, (((1,), (1,)), ((), ())), preferred_element_type=f32)


def pick(stacked, index):
    return lax.dynamic_index_in_dim(stacked, index, 0, keepdims=False)


def normed(values, gain):
    scale = lax.rsqrt(jnp.mean(values * values, -1, keepdims=True) + norm_eps)
    unit = values * scale
    return (unit, scale, (unit * gain).astype(bf16))


def norm_back(grad_out, unit, scale, gain):
    grad_gain = jnp.sum(grad_out * unit, 0)
    grad_unit = grad_out * gain
    grad_in = scale * (grad_unit - unit * jnp.mean(grad_unit * unit, -1, keepdims=True))
    return (grad_in, grad_gain)


def adamw(master, first, second, grad, rate, decay):
    first_new = beta_one * first + (1.0 - beta_one) * grad
    second_new = beta_two * second + (1.0 - beta_two) * grad * grad
    first_hat = first_new / (1.0 - beta_one**STEP)
    second_hat = second_new / (1.0 - beta_two**STEP)
    master_new = master - rate * (first_hat / (jnp.sqrt(second_hat) + adam_eps) + decay * master)
    return (master_new, first_new, second_new)


def local(
    inputs,
    cotangent,
    segments,
    w_in,
    w_out,
    conv_w,
    w_gate,
    w_up,
    w_down,
    gains,
    m_in,
    m_out,
    m_conv,
    m_gate,
    m_up,
    m_down,
    m_gains,
    v_in,
    v_out,
    v_conv,
    v_gate,
    v_up,
    v_down,
    v_gains,
):
    seqs_here, stretch, width = inputs.shape
    rows = seqs_here * stretch
    n_dp = lax.axis_size("dp")
    n_seq = lax.axis_size("seq")
    n_z = n_dp // 2
    own = w_in.shape[0]
    own_ff = w_down.shape[0]
    ff_part = n_dp * own_ff
    dp = lax.axis_index("dp")
    sq = lax.axis_index("seq")
    z = dp // 2
    core = dp % 2
    first_core = core == 0

    def halves(full):
        split = full.reshape(rows, n_z, 2, n_seq * own)
        even, odd = split[:, :, 0], split[:, :, 1]
        mine = jnp.where(first_core, even, odd).reshape(rows, width // 2)
        other = jnp.where(first_core, odd, even).reshape(rows, width // 2)
        return mine, other

    def joined(mine, other):
        shape = (rows, n_z, 1, n_seq * own)
        mine, other = mine.reshape(shape), other.reshape(shape)
        return jnp.concatenate(
            [jnp.where(first_core, mine, other), jnp.where(first_core, other, mine)], 2
        ).reshape(rows, width)

    def seq_ordered(pieces):
        stacked = jnp.stack(pieces, 0)
        return jnp.stack([pick(stacked, sq ^ j) for j in range(n_seq)], 0)

    def by_part(weight):
        low = weight.astype(bf16).reshape(own, n_dp, n_seq, own_ff)
        return low.transpose(2, 0, 1, 3).reshape(n_seq, own, ff_part)

    smalls = jnp.pad(
        jnp.concatenate([conv_w, gains], 0).astype(bf16), ((0, own - 5), (0, LANES - own))
    )
    mix = jnp.concatenate([w_in.astype(bf16), w_out.astype(bf16), smalls], 1)
    z_blocks = jnp.stack([mix] + [along_z(mix, -k) for k in range(1, n_z)], 0)
    z_twice = jnp.concatenate([z_blocks, z_blocks], 0)
    z_order = lax.dynamic_slice_in_dim(z_twice, (n_z - z) % n_z, n_z, 0)
    mix_mine = lax.all_gather(z_order, "seq", axis=1).reshape(width // 2, -1)
    mix_other = to_sibling(mix_mine)

    gate_up = jnp.concatenate([by_part(w_gate), by_part(w_up)], 2)
    gate_up = seq_ordered(
        [pick(gate_up, sq)] + [across_seq(pick(gate_up, sq ^ k), k) for k in range(1, n_seq)]
    )
    mat_gate_up = lax.all_gather(gate_up, "dp", axis=0).reshape(width, 2 * ff_part)
    mat_down = lax.all_gather(w_down.astype(bf16), "dp", axis=0, tiled=True)

    grad_top = cotangent.reshape(rows, width)
    tops = [grad_top] + [across_seq(grad_top, k) for k in range(1, n_seq)]

    cut_in, cut_out = 3 * width, 4 * width
    in_mine, in_other = mix_mine[:, :cut_in], mix_other[:, :cut_in]
    out_mine, out_other = mix_mine[:, cut_in:cut_out], mix_other[:, cut_in:cut_out]
    small_mine = mix_mine[:, cut_out:].reshape(n_z, n_seq, own, LANES)[:, :, :5, :own]
    small_other = mix_other[:, cut_out:].reshape(n_z, n_seq, own, LANES)[:, :, :5, :own]
    small_all = jnp.stack(
        [
            jnp.where(first_core, small_mine, small_other),
            jnp.where(first_core, small_other, small_mine),
        ],
        1,
    )
    small_all = small_all.transpose(3, 0, 1, 2, 4).reshape(5, width).astype(f32)
    taps, gain_vals = small_all[:3], small_all[3:]

    residual = inputs.reshape(rows, width).astype(f32)
    unit_one, scale_one, norm_one = normed(residual, gain_vals[0])
    norm_mine, norm_other = halves(norm_one)
    projected = dot(norm_mine, in_mine) + dot(norm_other, in_other)
    b_gate = projected[:, :width]
    c_gate = projected[:, width : 2 * width]
    x_part = projected[:, 2 * width :]
    conv_in = (b_gate * x_part).astype(bf16).reshape(seqs_here, stretch, width)
    prev_rows, prev_ids = from_behind(
        (conv_in[:, -2:, :], segments[:, -2:].astype(bf16)), "seq", 1
    )
    extended = jnp.concatenate([prev_rows, conv_in], 1).astype(f32)
    ext_ids = jnp.concatenate([prev_ids.astype(jnp.int32), segments], 1)
    near_one = (ext_ids[:, 1:-1] == segments).astype(f32)[..., None]
    near_two = (ext_ids[:, :-2] == segments).astype(f32)[..., None]
    tap_now = extended[:, 2:]
    tap_one = extended[:, 1:-1] * near_one
    tap_two = extended[:, :-2] * near_two
    conv_out = (taps[2] * tap_now + taps[1] * tap_one + taps[0] * tap_two).reshape(rows, width)
    mixed_in = (c_gate * conv_out).astype(bf16)
    mixed_mine, mixed_other = halves(mixed_in)
    middle = residual + dot(mixed_mine, out_mine) + dot(mixed_other, out_other)
    unit_two, scale_two, norm_two = normed(middle, gain_vals[1])

    norms = [norm_two] + [across_seq(norm_two, k) for k in range(1, n_seq)]
    hiddens, act_grads, norm_parts, out_parts = [], [], [], []
    for block, top in zip(norms, tops):
        both = dot(block, mat_gate_up)
        gate, up_part = both[:, :ff_part], both[:, ff_part:]
        sigma = jax.nn.sigmoid(gate)
        silu_vals = gate * sigma
        grad_hidden = right_contract(top, mat_down)
        hiddens.append((silu_vals * up_part).astype(bf16))
        grad_gate_act = (grad_hidden * up_part * sigma * (1.0 + gate * (1.0 - sigma))).astype(bf16)
        grad_up_act = (grad_hidden * silu_vals).astype(bf16)
        act_grads.append(jnp.concatenate([grad_gate_act, grad_up_act], 1))
        norm_parts.append(right_contract(act_grads[-1], mat_gate_up))
        out_parts.append(dot(hiddens[-1], mat_down))
    grad_norm_two = norm_parts[0]
    for k in range(1, n_seq):
        grad_norm_two = grad_norm_two + across_seq(norm_parts[k].astype(bf16), k).astype(f32)
    output = middle + out_parts[0]
    for k in range(1, n_seq):
        output = output + across_seq(out_parts[k].astype(bf16), k).astype(f32)
    output = output.astype(bf16)
    hidden_all = jnp.concatenate(hiddens, 0)
    top_all = jnp.concatenate(tops, 0)
    norm_all = jnp.concatenate(norms, 0)
    act_all = jnp.concatenate(act_grads, 0)
    grad_down = left_contract(hidden_all, top_all)
    grad_gate_up = left_contract(norm_all, act_all)

    back_two, gain_two = norm_back(grad_norm_two, unit_two, scale_two, gain_vals[1])
    grad_middle = grad_top.astype(f32) + back_two
    grad_branch = grad_middle.astype(bf16)
    grad_out_mine = left_contract(mixed_mine, grad_branch)
    grad_out_other = left_contract(mixed_other, grad_branch)
    grad_mixed = joined(
        right_contract(grad_branch, out_mine), right_contract(grad_branch, out_other)
    )
    grad_c = grad_mixed * conv_out
    grad_conv = (grad_mixed * c_gate).reshape(seqs_here, stretch, width)
    grad_taps = [
        jnp.sum(tap_two * grad_conv, (0, 1)),
        jnp.sum(tap_one * grad_conv, (0, 1)),
        jnp.sum(tap_now * grad_conv, (0, 1)),
    ]
    term_now = taps[2] * grad_conv
    term_one = taps[1] * grad_conv * near_one
    term_two = taps[0] * grad_conv * near_two
    grad_ext = (
        jnp.pad(term_now, ((0, 0), (2, 0), (0, 0)))
        + jnp.pad(term_one, ((0, 0), (1, 1), (0, 0)))
        + jnp.pad(term_two, ((0, 0), (0, 2), (0, 0)))
    )
    next_terms = from_behind(grad_ext[:, :2, :], "seq", -1)
    grad_conv_in = (
        grad_ext[:, 2:, :] + jnp.pad(next_terms, ((0, 0), (stretch - 2, 0), (0, 0)))
    ).reshape(rows, width)
    grad_proj = jnp.concatenate([grad_conv_in * x_part, grad_c, grad_conv_in * b_gate], -1).astype(
        bf16
    )
    grad_in_mine = left_contract(norm_mine, grad_proj)
    grad_in_other = left_contract(norm_other, grad_proj)
    grad_norm_one = joined(right_contract(grad_proj, in_mine), right_contract(grad_proj, in_other))
    back_one, gain_one = norm_back(grad_norm_one, unit_one, scale_one, gain_vals[0])
    input_grad = (grad_middle + back_one).reshape(seqs_here, stretch, width)

    def sum_core(mine, other):
        return mine + to_sibling(other.astype(bf16)).astype(f32)

    def sum_z(blocks):
        low = blocks.astype(bf16)
        total = pick(blocks, z)
        for k in range(1, n_z):
            total = total + along_z(pick(low, (z + k) % n_z), k).astype(f32)
        return total

    def sum_seq_z(mine):
        blocks = mine.reshape(n_z, n_seq, own, -1)
        low = blocks.astype(bf16)
        total = lax.dynamic_index_in_dim(blocks, sq, 1, keepdims=False)
        for k in range(1, n_seq):
            part = lax.dynamic_index_in_dim(low, sq ^ k, 1, keepdims=False)
            total = total + across_seq(part, k).astype(f32)
        return sum_z(total)

    small_grads = jnp.stack(grad_taps + [gain_one, gain_two], 0)
    small_grads = small_grads.reshape(5, n_z, 2, n_seq, own).transpose(2, 1, 3, 0, 4)
    small_grads = jnp.pad(
        small_grads, ((0, 0), (0, 0), (0, 0), (0, own - 5), (0, LANES - own))
    ).reshape(2, width // 2, LANES)
    small_sum = sum_seq_z(sum_core(pick(small_grads, core), pick(small_grads, 1 - core)))
    sum_out = sum_seq_z(sum_core(grad_out_mine, grad_out_other))
    sum_in = sum_seq_z(sum_core(grad_in_mine, grad_in_other))

    gu_blocks = grad_gate_up.reshape(n_z, 2, n_seq * own, 2 * ff_part)
    gu_mine = jnp.where(first_core, gu_blocks[:, 0], gu_blocks[:, 1])
    gu_other = jnp.where(first_core, gu_blocks[:, 1], gu_blocks[:, 0])
    gu_sum = sum_z(sum_core(gu_mine, gu_other)).astype(bf16).reshape(n_seq, own, 2 * ff_part)
    gu_sum = seq_ordered(
        [pick(gu_sum, sq)] + [across_seq(pick(gu_sum, sq ^ k), k) for k in range(1, n_seq)]
    ).astype(f32)

    def by_row(part):
        return (
            part.reshape(n_seq, own, n_dp, own_ff)
            .transpose(1, 2, 0, 3)
            .reshape(own, n_seq * ff_part)
        )

    sum_gate = by_row(gu_sum[:, :, :ff_part])
    sum_up = by_row(gu_sum[:, :, ff_part:])
    sum_down = lax.psum_scatter(grad_down, "dp", scatter_dimension=0, tiled=True)

    reduced = (
        sum_in,
        sum_out,
        small_sum[:3, :own],
        sum_gate,
        sum_up,
        sum_down,
        small_sum[3:5, :own],
    )
    masters = (w_in, w_out, conv_w, w_gate, w_up, w_down, gains)
    firsts = (m_in, m_out, m_conv, m_gate, m_up, m_down, m_gains)
    seconds = (v_in, v_out, v_conv, v_gate, v_up, v_down, v_gains)
    rates = (learn_rate, learn_rate, small_rate, learn_rate, learn_rate, learn_rate, small_rate)
    decays = (weight_decay, weight_decay, 0.0, weight_decay, weight_decay, weight_decay, 0.0)
    updated = [
        adamw(
            masters[index],
            firsts[index],
            seconds[index],
            reduced[index],
            rates[index],
            decays[index],
        )
        for index in range(7)
    ]
    new_w = [item[0] for item in updated]
    new_m = [item[1] for item in updated]
    new_v = [item[2] for item in updated]
    return (
        output.reshape(seqs_here, stretch, width),
        input_grad,
        *new_w,
        *new_m,
        *new_v,
    )


def solution(mesh):
    tokens = P("dp", "seq", None)
    matrix = P(("dp", "seq"), None)
    vector = P(None, ("dp", "seq"))
    weights = (matrix, matrix, vector, matrix, matrix, matrix, vector)
    return jax.shard_map(
        local,
        mesh=mesh,
        in_specs=(tokens, tokens, P("dp", "seq")) + weights * 3,
        out_specs=(tokens, tokens) + weights * 3,
        check_vma=False,
    )
```

time: 1660 us -> 613 us (0.37)
  waiting for transfers between devices: 1330 us -> 218 us
  blocking collectives: 118 us -> 0 us
  starting transfers between devices: 9.32 us -> 81.4 us
  local copies, waits for them, and re-layouts: 8.86 us -> 71.7 us
  other arithmetic: 34.1 us -> 76.5 us
    reduce_scatter x5 -> x1, waiting for transfers between devices: 940 us -> 0.01 us  [local(): lax.psum_scatter(grad_down, 'dp', scatter_dimension=0, tiled=True)]
    unnamed x14 -> x4, waiting for transfers between devices: 176 us -> 0.07 us
    all_gather x5 -> x3, waiting for transfers between devices: 214 us -> 39.9 us  [the longest x1 39.8 us: local(): mix_mine = lax.all_gather(z_order, 'seq', axis=1).reshape(width // 2, -1)]
    ppermute x0 -> x47, waiting for transfers between devices: none -> 141 us  [the longest x27 81.8 us: across_seq(): lax.ppermute(block, 'seq', [(i, i ^ by) for i in range(lax.axis_size('seq...]
    all_gather x2 -> x0, blocking collectives: 118 us -> none  [the longest x1 63.1 us: local(): lax.all_gather(low_conv, ('dp', 'seq'), axis=1, tiled=True)]
    ppermute x0 -> x47, starting transfers between devices: none -> 71.6 us  [the longest x27 38 us: across_seq(): lax.ppermute(block, 'seq', [(i, i ^ by) for i in range(lax.axis_size('seq...]
    ppermute x3, waiting for transfers between devices: 4.46 us -> 36.4 us  [from_behind(): return lax.ppermute(shard, axis, pairs)]
    select_n x0 -> x8, local copies, waits for them, and re-layouts: none -> 22.3 us  [the longest x2 6.19 us: joined(): jnp.where(first_core, other, mine)]
  transfers between devices with their start and end apart: 15 -> 54, of which waited for: 12 -> 22; matrix products, arithmetic and copies ran while one was open for 8% -> 44% of each run, Pallas kernels for 0% -> 0%
where the time goes in v1:
time: 613 us; the launch traced here: 603 us
  waiting for transfers between devices  218 us (36%)
  matrix products  139 us (23%)
  starting transfers between devices  81.4 us (13%)
  other arithmetic  76.5 us (12%)
  local copies, waits for them, and re-layouts  71.7 us (12%)
  between operations  15.7 us (3%)
    ppermute x27, waiting for transfers between devices, across_seq(): lax.ppermute(block, 'seq', [(i, i ^ by) for i in range(lax.axis_size('seq...  81.8 us
    ppermute x15, waiting for transfers between devices, along_z(): lax.ppermute(block, 'dp', [(i, (i + 2 * by) % count) for i in range(count)])  58.7 us
    dot_general x12, matrix products, dot(): return jnp.dot(first, second, preferred_element_type=f32)  48.5 us
    dot_general x12, matrix products, right_contract(): lax.dot_general(first, second, (((1,), (1,)), ((), ())), preferred_elemen...  48.3 us
    dot_general x6, matrix products, left_contract(): lax.dot_general(first, second, (((0,), (0,)), ((), ())), preferred_elemen...  42.5 us
    all_gather x1, waiting for transfers between devices, local(): mix_mine = lax.all_gather(z_order, 'seq', axis=1).reshape(width // 2, -1)  39.8 us
    ppermute x27, starting transfers between devices, across_seq(): lax.ppermute(block, 'seq', [(i, i ^ by) for i in range(lax.axis_size('seq...  38 us
    ppermute x3, waiting for transfers between devices, from_behind(): return lax.ppermute(shard, axis, pairs)  36.4 us
  transfers between devices with their start and end apart: 54, of which 22 were waited for; matrix products, arithmetic and copies ran while one was open for 44% of the time, Pallas kernels for 0%

profile of v1, /device:TPU:8, one launch (start us, length us, event | category | flops | bytes accessed | tf_op | source)
XLA Modules:
  0.0 602.5 jit_solution(17382774849430942403)
XLA Ops:
  16.9 14.7 %collective-permute-done = bf16[32,4224]{1,0:T(8,128)(2,1)S(1)} collective-permute-done((bf16[32,4224]{1,0:T(8,128)(2,1)S(1)}, bf16[32,4224]{1,0:T(8,128)(2,1)S(1)}, u32[]{:S(2)}, u32[]{:S(2)}) %collective-permute-start) | collective-permute-done | bytes 270368 | tf_op jit(solution)/shard_map/ppermute | solution.py:33
  58.0 39.8 %all-gather.8.cloned.1.call-done = bf16[4,128,4224]{2,1,0:T(8,128)(2,1)} async-done(((bf16[4,32,4224]{2,1,0:T(8,128)(2,1)}), bf16[4,128,4224]{2,1,0:T(8,128)(2,1)}) %all-gather.8.cloned.1.call-update) | async-done | bytes 4325392 | tf_op jit(solution)/shard_map/all_gather | solution.py:147
  108.9 36.3 %collective-permute-done.5 = bf16[2,2]{1,0:T(2,128)(2,1)S(1)} collective-permute-done((bf16[2,2]{1,0:T(2,128)(2,1)S(1)}, bf16[2,2]{1,0:T(2,128)(2,1)S(1)}, u32[]{:S(2)}, u32[]{:S(2)}) %collective-permute-start.5) | collective-permute-done | bytes 40 | tf_op jit(solution)/shard_map/ppermute | solution.py:24
  153.7 6.5 %fusion.45 = f32[512,3072]{1,0:T(8,128)} fusion(bf16[512,512]{0,1:T(8,128)(2,1)} %bitcast.310, bf16[512,4224]{1,0:T(8,128)(2,1)} %bitcast.294), kind=kOutput, calls=%fused_computation.51 | convolution fusion | flops 1610612736 | bytes 9961472 | tf_op jit(solution)/shard_map/dot_general | solution.py:41
  161.6 5.9 convolution_add_fusion
  171.5 4.6 collective-permute-start.4
  186.6 4.9 broadcast_select_fusion
  208.4 6.9 %fusion.159 = f32[512,2304]{1,0:T(8,128)} fusion(bf16[512,1024]{1,0:T(8,128)(2,1)S(1)} %multiply_convert_fusion.12, bf16[1024,2304]{1,0:T(8,128)(2,1)} %bitcast.336), kind=kOutput, calls=%fused_computation.314 | convolution fusion | flops 2415919104 | bytes 10485760 | tf_op jit(solution)/shard_map/dot_general | solution.py:41
  215.4 7.2 %multiply_convert_fusion.7 = (bf16[512,1152]{1,0:T(8,128)(2,1)}, bf16[512,1152]{1,0:T(8,128)(2,1)}, bf16[512,1152]{1,0:T(8,128)(2,1)S(1)}) fusion(f32[512,2304]{1,0:T(8,128)} %fusion.159, bf16[512,1024]{1,0:T(8,128)(2,1)} %bitcast.27, bf16[1152,1024]{1,0:T(8,128)(2,1)} %all-gather.6.cloned.1.call-done), kind=kOutput, calls=%fused_computation.77 | convolution fusion | flops 1216806912 | bytes 11665408 | tf_op jit(solution)/shard_map/dot_general | solution.py:49
  222.6 7.4 %collective-permute-done.13 = bf16[512,1024]{1,0:T(8,128)(2,1)} collective-permute-done((bf16[512,1024]{1,0:T(8,128)(2,1)S(1)}, bf16[512,1024]{1,0:T(8,128)(2,1)}, u32[]{:S(2)}, u32[]{:S(2)}) %collective-permute-start.13) | collective-permute-done | bytes 1048608 | tf_op jit(solution)/shard_map/ppermute | solution.py:37
  244.6 9.2 %collective-permute-done.11 = bf16[512,1024]{1,0:T(8,128)(2,1)} collective-permute-done((bf16[512,1024]{1,0:T(8,128)(2,1)S(1)}, bf16[512,1024]{1,0:T(8,128)(2,1)}, u32[]{:S(2)}, u32[]{:S(2)}) %collective-permute-start.11) | collective-permute-done | bytes 1048608 | tf_op jit(solution)/shard_map/ppermute | solution.py:37
  287.0 9.8 %fusion.16 = f32[1152,1024]{1,0:T(8,128)} fusion(bf16[512,1152]{1,0:T(8,128)(2,1)S(1)} %get-tuple-element.73, bf16[512,1152]{1,0:T(8,128)(2,1)S(1)} %get-tuple-element.72, bf16[512,1152]{1,0:T(8,128)(2,1)S(1)} %get-tuple-element.71, bf16[512,1152]{1,0:T(8,128)(2,1)S(1)} %get-tuple-element.70, bf16[512,1024]{1,0:T(8,128)(2,1)} %collective-permute-done.19, ...), kind=kOutput, calls=%fused_computation.18 | convolution fusion | flops 4867489792 | bytes 13631488 | tf_op jit(solution)/shard_map/dot_general | solution.py:45
  296.8 20.9 %fusion = f32[1024,2304]{1,0:T(8,128)} fusion(bf16[512,1152]{1,0:T(8,128)(2,1)} %copy-done.70, bf16[512,1152]{1,0:T(8,128)(2,1)} %copy-done.69, bf16[512,1152]{1,0:T(8,128)(2,1)} %copy-done.72, bf16[512,1152]{1,0:T(8,128)(2,1)} %copy-done.71, bf16[512,1152]{1,0:T(8,128)(2,1)} %copy-done.74, bf16[512,1152]{1,0:T(8,128)(2,1)} %copy-done.73, ...), kind=kOutput, calls=%fused_computation | convolution fusion | flops 9755951104 | bytes 23068672 | tf_op jit(solution)/shard_map/dot_general | solution.py:45
  317.8 4.6 convolution_convert_fusion.3
  322.4 5.8 fusion.47
  329.7 15.1 %collective-permute-done.18 = bf16[512,1024]{1,0:T(8,128)(2,1)} collective-permute-done((bf16[512,1024]{1,0:T(8,128)(2,1)}, bf16[512,1024]{1,0:T(8,128)(2,1)}, u32[]{:S(2)}, u32[]{:S(2)}) %collective-permute-start.18) | collective-permute-done | bytes 1048608 | tf_op jit(solution)/shard_map/ppermute | solution.py:37
  344.8 6.6 %multiply_reduce_fusion = (f32[1024]{0:T(1024)S(1)}, f32[512]{0:T(512)S(1)}, f32[512,1024]{1,0:T(8,128)S(1)}) fusion(f32[512,1024]{1,0:T(8,128)S(1)} %copy-done.2, f32[512]{0:T(512)S(1)} %add_rsqrt_fusion, f32[1024]{0:T(1024)S(1)} %mul.541, bf16[512,1024]{1,0:T(8,128)(2,1)} %collective-permute-done.20, bf16[512,1024]{1,0:T(8,128)(2,1)} %collective-permute-done.18, ...), kind=kOutput, calls=%fused_computation.118 | convolution fusion | flops 2426927616 | bytes 14430208 | tf_op jit(solution)/shard_map/dot_general | solution.py:49
  364.9 4.8 pad_maximum_fusion.1
  381.0 4.5 pad_add_fusion
  389.9 4.7 add_convert_fusion
  400.0 4.6 fusion.40
  414.0 4.4 pad_maximum_fusion.2
  422.3 4.0 concatenate.70
  434.8 4.4 fusion.76
  464.8 4.3 collective-permute-done.31
  472.9 29.4 %collective-permute-done.46 = bf16[128,2304]{1,0:T(8,128)(2,1)S(1)} collective-permute-done((bf16[128,2304]{1,0:T(8,128)(2,1)S(1)}, bf16[128,2304]{1,0:T(8,128)(2,1)S(1)}, u32[]{:S(2)}, u32[]{:S(2)}) %collective-permute-start.46) | collective-permute-done | bytes 589856 | tf_op jit(solution)/shard_map/ppermute | solution.py:33
  502.3 12.9 %collective-permute-start.33 = (bf16[32,1024]{1,0:T(8,128)(2,1)S(1)}, bf16[32,1024]{1,0:T(8,128)(2,1)S(1)}, u32[]{:S(2)}, u32[]{:S(2)}) collective-permute-start(bf16[32,1024]{1,0:T(8,128)(2,1)S(1)} %get-tuple-element.115), channel_id=1, source_target_pairs={{0,8},{4,12},{8,16},{12,20},{16,24},{20,28},{24,0},{28,4},{1,9},{5... | collective-permute-start | bytes 196616 | tf_op jit(solution)/shard_map/ppermute | solution.py:33
  525.8 4.4 convert_add_fusion
  542.8 13.3 %collective-permute-done.25 = bf16[4,32,3072]{2,1,0:T(8,128)(2,1)} collective-permute-done((bf16[4,32,3072]{2,1,0:T(8,128)(2,1)}, bf16[4,32,3072]{2,1,0:T(8,128)(2,1)}, u32[]{:S(2)}, u32[]{:S(2)}) %collective-permute-start.25) | collective-permute-done | bytes 786464 | tf_op jit(solution)/shard_map/ppermute | solution.py:37
  556.1 15.9 %collective-permute-done.24 = bf16[4,32,3072]{2,1,0:T(8,128)(2,1)} collective-permute-done((bf16[4,32,3072]{2,1,0:T(8,128)(2,1)}, bf16[4,32,3072]{2,1,0:T(8,128)(2,1)}, u32[]{:S(2)}, u32[]{:S(2)}) %collective-permute-start.24) | collective-permute-done | bytes 786464 | tf_op jit(solution)/shard_map/ppermute | solution.py:37
  574.7 3.9 collective-permute-start.27
  583.3 5.4 collective-permute-done.27
  (415 shorter events, 259.6 us)
Async XLA Ops:
  7.2 90.7 %all-gather.8.cloned.1.call-start = ((), (), s32[]{:S(2)}) async-start(), calls=%async_computation.3 | async-start | bytes 5406720 | tf_op jit(solution)/shard_map/all_gather | solution.py:147
  10.6 21.0 %collective-permute-start = (bf16[32,4224]{1,0:T(8,128)(2,1)S(1)}, bf16[32,4224]{1,0:T(8,128)(2,1)S(1)}, u32[]{:S(2)}, u32[]{:S(2)}) collective-permute-start(bf16[32,4224]{1,0:T(8,128)(2,1)S(1)} %pad_maximum_fusion.6), channel_id=1, source_target_pairs={{0,24},{4,28},{8,0},{12,4},{16,8},{20,12},{24,16},{28,20},{1,25},{... | collective-permute-start | bytes 811016 | tf_op jit(solution)/shard_map/ppermute | solution.py:33
  10.6 21.7 %collective-permute-start.1 = (bf16[32,4224]{1,0:T(8,128)(2,1)S(1)}, bf16[32,4224]{1,0:T(8,128)(2,1)S(1)}, u32[]{:S(2)}, u32[]{:S(2)}) collective-permute-start(bf16[32,4224]{1,0:T(8,128)(2,1)S(1)} %pad_maximum_fusion.6), channel_id=1, source_target_pairs={{0,16},{4,20},{8,24},{12,28},{16,0},{20,4},{24,8},{28,12},{1,17},{... | collective-permute-start | bytes 811016 | tf_op jit(solution)/shard_map/ppermute | solution.py:33
  13.7 22.9 %collective-permute-start.2 = (bf16[32,4224]{1,0:T(8,128)(2,1)S(1)}, bf16[32,4224]{1,0:T(8,128)(2,1)S(1)}, u32[]{:S(2)}, u32[]{:S(2)}) collective-permute-start(bf16[32,4224]{1,0:T(8,128)(2,1)S(1)} %pad_maximum_fusion.6), channel_id=1, source_target_pairs={{0,8},{4,12},{8,16},{12,20},{16,24},{20,28},{24,0},{28,4},{1,9},{5... | collective-permute-start | bytes 811016 | tf_op jit(solution)/shard_map/ppermute | solution.py:33
  42.5 165.9 %all-gather.10.cloned.1.call-start = ((), (), s32[]{:S(2)}) async-start(), calls=%async_computation.4 | async-start | bytes 5308416 | tf_op jit(solution)/shard_map/all_gather | solution.py:154
  58.0 157.4 %all-gather.6.cloned.1.call-start = ((), (), s32[]{:S(2)}) async-start(), calls=%async_computation.1 | async-start | bytes 2654208 | tf_op jit(solution)/shard_map/all_gather | solution.py:155
  97.9 48.3 %collective-permute-start.3 = (bf16[512,4224]{1,0:T(8,128)(2,1)}, bf16[512,4224]{1,0:T(8,128)(2,1)}, u32[]{:S(2)}, u32[]{:S(2)}) collective-permute-start(bf16[512,4224]{1,0:T(8,128)(2,1)} %bitcast.292), channel_id=1, source_target_pairs={{0,4},{4,0},{8,12},{12,8},{16,20},{20,16},{24,28},{28,24},{1,5},{5... | collective-permute-start | bytes 12976136 | tf_op jit(solution)/shard_map/ppermute | solution.py:28
  97.9 138.0 %collective-permute-start.19 = (bf16[512,1024]{1,0:T(8,128)(2,1)}, bf16[512,1024]{1,0:T(8,128)(2,1)}, u32[]{:S(2)}, u32[]{:S(2)}) collective-permute-start(bf16[512,1024]{1,0:T(8,128)(2,1)} %bitcast.27), channel_id=1, source_target_pairs={{0,3},{1,2},{2,1},{3,0},{4,7},{5,6},{6,5},{7,4},{8,11},{9,10},{10,... | collective-permute-start | bytes 3145736 | tf_op jit(solution)/shard_map/ppermute | solution.py:37
  99.3 158.4 %collective-permute-start.17 = (bf16[512,1024]{1,0:T(8,128)(2,1)}, bf16[512,1024]{1,0:T(8,128)(2,1)}, u32[]{:S(2)}, u32[]{:S(2)}) collective-permute-start(bf16[512,1024]{1,0:T(8,128)(2,1)} %bitcast.27), channel_id=1, source_target_pairs={{0,2},{1,3},{2,0},{3,1},{4,6},{5,7},{6,4},{7,5},{8,10},{9,11},{10,... | collective-permute-start | bytes 3145736 | tf_op jit(solution)/shard_map/ppermute | solution.py:37
  100.8 178.4 %collective-permute-start.15 = (bf16[512,1024]{1,0:T(8,128)(2,1)}, bf16[512,1024]{1,0:T(8,128)(2,1)}, u32[]{:S(2)}, u32[]{:S(2)}) collective-permute-start(bf16[512,1024]{1,0:T(8,128)(2,1)} %bitcast.27), channel_id=1, source_target_pairs={{0,1},{1,0},{2,3},{3,2},{4,5},{5,4},{6,7},{7,6},{8,9},{9,8},{10,11... | collective-permute-start | bytes 3145736 | tf_op jit(solution)/shard_map/ppermute | solution.py:37
  101.4 43.8 %collective-permute-start.5 = (bf16[2,2]{1,0:T(2,128)(2,1)S(1)}, bf16[2,2]{1,0:T(2,128)(2,1)S(1)}, u32[]{:S(2)}, u32[]{:S(2)}) collective-permute-start(bf16[2,2]{1,0:T(2,128)(2,1)S(1)} %slice_convert_fusion), channel_id=1, source_target_pairs={{0,1},{1,2},{2,3},{4,5},{5,6},{6,7},{8,9},{9,10},{10,11},{12,13},{... | collective-permute-start | bytes 32 | tf_op jit(solution)/shard_map/ppermute | solution.py:24
  105.6 487.5 %reduce-scatter.2.cloned.1.call-start = ((), (), s32[]{:S(2)}) async-start(), calls=%async_computation.2 | async-start | bytes 5308416 | tf_op jit(solution)/shard_map/reduce_scatter | solution.py:308
  204.3 25.7 %collective-permute-start.13 = (bf16[512,1024]{1,0:T(8,128)(2,1)S(1)}, bf16[512,1024]{1,0:T(8,128)(2,1)}, u32[]{:S(2)}, u32[]{:S(2)}) collective-permute-start(bf16[512,1024]{1,0:T(8,128)(2,1)S(1)} %multiply_convert_fusion.12), channel_id=1, source_target_pairs={{0,3},{1,2},{2,1},{3,0},{4,7},{5,6},{6,5},{7,4},{8,11},{9,10},{10,... | collective-permute-start | bytes 3145736 | tf_op jit(solution)/shard_map/ppermute | solution.py:37
  207.6 46.2 %collective-permute-start.11 = (bf16[512,1024]{1,0:T(8,128)(2,1)S(1)}, bf16[512,1024]{1,0:T(8,128)(2,1)}, u32[]{:S(2)}, u32[]{:S(2)}) collective-permute-start(bf16[512,1024]{1,0:T(8,128)(2,1)S(1)} %multiply_convert_fusion.12), channel_id=1, source_target_pairs={{0,2},{1,3},{2,0},{3,1},{4,6},{5,7},{6,4},{7,5},{8,10},{9,11},{10,... | collective-permute-start | bytes 3145736 | tf_op jit(solution)/shard_map/ppermute | solution.py:37
  230.0 45.0 %collective-permute-start.9 = (bf16[512,1024]{1,0:T(8,128)(2,1)S(1)}, bf16[512,1024]{1,0:T(8,128)(2,1)S(1)}, u32[]{:S(2)}, u32[]{:S(2)}) collective-permute-start(bf16[512,1024]{1,0:T(8,128)(2,1)S(1)} %multiply_convert_fusion.12), channel_id=1, source_target_pairs={{0,1},{1,0},{2,3},{3,2},{4,5},{5,4},{6,7},{7,6},{8,9},{9,8},{10,11... | collective-permute-start | bytes 3145736 | tf_op jit(solution)/shard_map/ppermute | solution.py:37
  241.9 145.8 %collective-permute-start.14 = (bf16[512,1024]{1,0:T(8,128)(2,1)}, bf16[512,1024]{1,0:T(8,128)(2,1)}, u32[]{:S(2)}, u32[]{:S(2)}) collective-permute-start(bf16[512,1024]{1,0:T(8,128)(2,1)} %convolution_convert_fusion.1), channel_id=1, source_target_pairs={{0,3},{1,2},{2,1},{3,0},{4,7},{5,6},{6,5},{7,4},{8,11},{9,10},{10,... | collective-permute-start | bytes 3145736 | tf_op jit(solution)/shard_map/ppermute | solution.py:37
  263.9 124.3 %collective-permute-start.12 = (bf16[512,1024]{1,0:T(8,128)(2,1)}, bf16[512,1024]{1,0:T(8,128)(2,1)}, u32[]{:S(2)}, u32[]{:S(2)}) collective-permute-start(bf16[512,1024]{1,0:T(8,128)(2,1)} %convolution_convert_fusion.2), channel_id=1, source_target_pairs={{0,2},{1,3},{2,0},{3,1},{4,6},{5,7},{6,4},{7,5},{8,10},{9,11},{10,... | collective-permute-start | bytes 3145736 | tf_op jit(solution)/shard_map/ppermute | solution.py:37
  270.0 58.2 %collective-permute-start.20 = (bf16[512,1024]{1,0:T(8,128)(2,1)}, bf16[512,1024]{1,0:T(8,128)(2,1)}, u32[]{:S(2)}, u32[]{:S(2)}) collective-permute-start(bf16[512,1024]{1,0:T(8,128)(2,1)} %fusion.84), channel_id=1, source_target_pairs={{0,3},{1,2},{2,1},{3,0},{4,7},{5,6},{6,5},{7,4},{8,11},{9,10},{10,... | collective-permute-start | bytes 3145736 | tf_op jit(solution)/shard_map/ppermute | solution.py:37
  275.1 69.7 %collective-permute-start.18 = (bf16[512,1024]{1,0:T(8,128)(2,1)}, bf16[512,1024]{1,0:T(8,128)(2,1)}, u32[]{:S(2)}, u32[]{:S(2)}) collective-permute-start(bf16[512,1024]{1,0:T(8,128)(2,1)} %fusion.87), channel_id=1, source_target_pairs={{0,2},{1,3},{2,0},{3,1},{4,6},{5,7},{6,4},{7,5},{8,10},{9,11},{10,... | collective-permute-start | bytes 3145736 | tf_op jit(solution)/shard_map/ppermute | solution.py:37
  286.4 58.4 %collective-permute-start.16 = (bf16[512,1024]{1,0:T(8,128)(2,1)}, bf16[512,1024]{1,0:T(8,128)(2,1)}, u32[]{:S(2)}, u32[]{:S(2)}) collective-permute-start(bf16[512,1024]{1,0:T(8,128)(2,1)} %fusion.90), channel_id=1, source_target_pairs={{0,1},{1,0},{2,3},{3,2},{4,5},{5,4},{6,7},{7,6},{8,9},{9,8},{10,11... | collective-permute-start | bytes 3145736 | tf_op jit(solution)/shard_map/ppermute | solution.py:37
  328.2 60.0 %collective-permute-start.10 = (bf16[512,1024]{1,0:T(8,128)(2,1)}, bf16[512,1024]{1,0:T(8,128)(2,1)}, u32[]{:S(2)}, u32[]{:S(2)}) collective-permute-start(bf16[512,1024]{1,0:T(8,128)(2,1)} %convolution_convert_fusion.3), channel_id=1, source_target_pairs={{0,1},{1,0},{2,3},{3,2},{4,5},{5,4},{6,7},{7,6},{8,9},{9,8},{10,11... | collective-permute-start | bytes 3145736 | tf_op jit(solution)/shard_map/ppermute | solution.py:37
  344.8 112.3 %collective-permute-start.43 = (bf16[4,128,2304]{2,1,0:T(8,128)(2,1)}, bf16[4,128,2304]{2,1,0:T(8,128)(2,1)}, u32[]{:S(2)}, u32[]{:S(2)}) collective-permute-start(bf16[4,128,2304]{2,1,0:T(8,128)(2,1)} %fusion.47), channel_id=1, source_target_pairs={{0,4},{4,0},{8,12},{12,8},{16,20},{20,16},{24,28},{28,24},{1,5},{5... | collective-permute-start | bytes 7077896 | tf_op jit(solution)/shard_map/ppermute | solution.py:28
  387.7 62.9 %collective-permute-start.29 = (bf16[512,1024]{1,0:T(8,128)(2,1)}, bf16[512,1024]{1,0:T(8,128)(2,1)}, u32[]{:S(2)}, u32[]{:S(2)}) collective-permute-start(bf16[512,1024]{1,0:T(8,128)(2,1)} %convolution_convert_fusion.4), channel_id=1, source_target_pairs={{0,4},{4,0},{8,12},{12,8},{16,20},{20,16},{24,28},{28,24},{1,5},{5... | collective-permute-start | bytes 3145736 | tf_op jit(solution)/shard_map/ppermute | solution.py:28
  449.8 75.9 %collective-permute-start.22 = (bf16[512,3072]{1,0:T(8,128)(2,1)}, bf16[512,3072]{1,0:T(8,128)(2,1)}, u32[]{:S(2)}, u32[]{:S(2)}) collective-permute-start(bf16[512,3072]{1,0:T(8,128)(2,1)} %convolution_convert_fusion), channel_id=1, source_target_pairs={{0,4},{4,0},{8,12},{12,8},{16,20},{20,16},{24,28},{28,24},{1,5},{5... | collective-permute-start | bytes 9437192 | tf_op jit(solution)/shard_map/ppermute | solution.py:28
  460.0 42.2 %collective-permute-start.46 = (bf16[128,2304]{1,0:T(8,128)(2,1)S(1)}, bf16[128,2304]{1,0:T(8,128)(2,1)S(1)}, u32[]{:S(2)}, u32[]{:S(2)}) collective-permute-start(bf16[128,2304]{1,0:T(8,128)(2,1)S(1)} %get-tuple-element.78), channel_id=1, source_target_pairs={{0,24},{4,28},{8,0},{12,4},{16,8},{20,12},{24,16},{28,20},{1,25},{... | collective-permute-start | bytes 1769480 | tf_op jit(solution)/shard_map/ppermute | solution.py:33
  463.9 38.4 %collective-permute-start.45 = (bf16[128,2304]{1,0:T(8,128)(2,1)S(1)}, bf16[128,2304]{1,0:T(8,128)(2,1)S(1)}, u32[]{:S(2)}, u32[]{:S(2)}) collective-permute-start(bf16[128,2304]{1,0:T(8,128)(2,1)S(1)} %get-tuple-element.79), channel_id=1, source_target_pairs={{0,16},{4,20},{8,24},{12,28},{16,0},{20,4},{24,8},{28,12},{1,17},{... | collective-permute-start | bytes 1769480 | tf_op jit(solution)/shard_map/ppermute | solution.py:33
  469.0 46.4 %collective-permute-start.44 = (bf16[128,2304]{1,0:T(8,128)(2,1)S(1)}, bf16[128,2304]{1,0:T(8,128)(2,1)S(1)}, u32[]{:S(2)}, u32[]{:S(2)}) collective-permute-start(bf16[128,2304]{1,0:T(8,128)(2,1)S(1)} %get-tuple-element.77), channel_id=1, source_target_pairs={{0,8},{4,12},{8,16},{12,20},{16,24},{20,28},{24,0},{28,4},{1,9},{5... | collective-permute-start | bytes 1769480 | tf_op jit(solution)/shard_map/ppermute | solution.py:33
  470.8 46.5 %collective-permute-start.35 = (bf16[32,1024]{1,0:T(8,128)(2,1)S(1)}, bf16[32,1024]{1,0:T(8,128)(2,1)S(1)}, u32[]{:S(2)}, u32[]{:S(2)}) collective-permute-start(bf16[32,1024]{1,0:T(8,128)(2,1)S(1)} %get-tuple-element.116), channel_id=1, source_target_pairs={{0,24},{4,28},{8,0},{12,4},{16,8},{20,12},{24,16},{28,20},{1,25},{... | collective-permute-start | bytes 196616 | tf_op jit(solution)/shard_map/ppermute | solution.py:33
  502.3 17.1 %collective-permute-start.33 = (bf16[32,1024]{1,0:T(8,128)(2,1)S(1)}, bf16[32,1024]{1,0:T(8,128)(2,1)S(1)}, u32[]{:S(2)}, u32[]{:S(2)}) collective-permute-start(bf16[32,1024]{1,0:T(8,128)(2,1)S(1)} %get-tuple-element.115), channel_id=1, source_target_pairs={{0,8},{4,12},{8,16},{12,20},{16,24},{20,28},{24,0},{28,4},{1,9},{5... | collective-permute-start | bytes 196616 | tf_op jit(solution)/shard_map/ppermute | solution.py:33
  534.4 21.7 %collective-permute-start.25 = (bf16[4,32,3072]{2,1,0:T(8,128)(2,1)}, bf16[4,32,3072]{2,1,0:T(8,128)(2,1)}, u32[]{:S(2)}, u32[]{:S(2)}) collective-permute-start(bf16[4,32,3072]{2,1,0:T(8,128)(2,1)} %get-tuple-element.75), channel_id=1, source_target_pairs={{0,3},{1,2},{2,1},{3,0},{4,7},{5,6},{6,5},{7,4},{8,11},{9,10},{10,... | collective-permute-start | bytes 2359304 | tf_op jit(solution)/shard_map/ppermute | solution.py:37
  536.2 35.8 %collective-permute-start.24 = (bf16[4,32,3072]{2,1,0:T(8,128)(2,1)}, bf16[4,32,3072]{2,1,0:T(8,128)(2,1)}, u32[]{:S(2)}, u32[]{:S(2)}) collective-permute-start(bf16[4,32,3072]{2,1,0:T(8,128)(2,1)} %get-tuple-element.76), channel_id=1, source_target_pairs={{0,2},{1,3},{2,0},{3,1},{4,6},{5,7},{6,4},{7,5},{8,10},{9,11},{10,... | collective-permute-start | bytes 2359304 | tf_op jit(solution)/shard_map/ppermute | solution.py:37
  537.6 34.4 %collective-permute-start.23 = (bf16[4,32,3072]{2,1,0:T(8,128)(2,1)}, bf16[4,32,3072]{2,1,0:T(8,128)(2,1)}, u32[]{:S(2)}, u32[]{:S(2)}) collective-permute-start(bf16[4,32,3072]{2,1,0:T(8,128)(2,1)} %get-tuple-element.74), channel_id=1, source_target_pairs={{0,1},{1,0},{2,3},{3,2},{4,5},{5,4},{6,7},{7,6},{8,9},{9,8},{10,11... | collective-permute-start | bytes 2359304 | tf_op jit(solution)/shard_map/ppermute | solution.py:37
  (104 other events, 1262.2 us)
Sparse Core Ops, SparseCore 0:
  42.6 55.1 all-gather.7
  100.1 50.1 all-gather.9
  152.5 31.4 all-gather.5
  297.0 51.2 reduce-scatter.1

commit v2 on v1

--- a/solution.py
+++ b/solution.py
@@ -47,6 +47,10 @@
 
 def right_contract(first, second):
     return lax.dot_general(first, second, (((1,), (1,)), ((), ())), preferred_element_type=f32)
+
+
+def tie(values):
+    return lax.optimization_barrier(values)
 
 
 def pick(stacked, index):
@@ -115,19 +119,21 @@
     core = dp % 2
     first_core = core == 0
 
+    lane = n_seq * own
+
     def halves(full):
-        split = full.reshape(rows, n_z, 2, n_seq * own)
-        even, odd = split[:, :, 0], split[:, :, 1]
-        mine = jnp.where(first_core, even, odd).reshape(rows, width // 2)
-        other = jnp.where(first_core, odd, even).reshape(rows, width // 2)
-        return mine, other
+        blocks = [full[:, i * lane : (i + 1) * lane] for i in range(2 * n_z)]
+        even = jnp.concatenate(blocks[0::2], 1)
+        odd = jnp.concatenate(blocks[1::2], 1)
+        return jnp.where(first_core, even, odd), jnp.where(first_core, odd, even)
 
     def joined(mine, other):
-        shape = (rows, n_z, 1, n_seq * own)
-        mine, other = mine.reshape(shape), other.reshape(shape)
-        return jnp.concatenate(
-            [jnp.where(first_core, mine, other), jnp.where(first_core, other, mine)], 2
-        ).reshape(rows, width)
+        even = jnp.where(first_core, mine, other)
+        odd = jnp.where(first_core, other, mine)
+        blocks = []
+        for i in range(n_z):
+            blocks += [even[:, i * lane : (i + 1) * lane], odd[:, i * lane : (i + 1) * lane]]
+        return jnp.concatenate(blocks, 1)
 
     def seq_ordered(pieces):
         stacked = jnp.stack(pieces, 0)
@@ -141,21 +147,30 @@
         jnp.concatenate([conv_w, gains], 0).astype(bf16), ((0, own - 5), (0, LANES - own))
     )
     mix = jnp.concatenate([w_in.astype(bf16), w_out.astype(bf16), smalls], 1)
-    z_blocks = jnp.stack([mix] + [along_z(mix, -k) for k in range(1, n_z)], 0)
-    z_twice = jnp.concatenate([z_blocks, z_blocks], 0)
+    gate_up = jnp.concatenate([by_part(w_gate), by_part(w_up)], 2)
+
+    z_parts = [along_z(mix, -k) for k in range(1, n_z)]
+    gu_parts = [across_seq(pick(gate_up, sq ^ k), k) for k in range(1, n_seq)]
+    grad_top = cotangent.reshape(rows, width)
+    gu_parts, top_out = tie((gu_parts, grad_top))
+    last = n_seq - 1
+    top_last = across_seq(top_out, last)
+    z_parts, gu_parts, top_last = tie((z_parts, gu_parts, top_last))
+    gate_up = seq_ordered([pick(gate_up, sq)] + gu_parts)
+    mat_gate_up = lax.all_gather(gate_up, "dp", axis=0).reshape(width, 2 * ff_part)
+
+    z_twice = jnp.stack(([mix] + z_parts) * 2, 0)
     z_order = lax.dynamic_slice_in_dim(z_twice, (n_z - z) % n_z, n_z, 0)
-    mix_mine = lax.all_gather(z_order, "seq", axis=1).reshape(width // 2, -1)
+    mix_parts = {k: across_seq(z_order, k) for k in range(n_seq - 1, 0, -1)}
+    mix_parts, top_out, low_down = tie((mix_parts, top_out, w_down.astype(bf16)))
+    mix_parts[0] = z_order
+    mix_mine = seq_ordered([mix_parts[k] for k in range(n_seq)])
+    mix_mine = mix_mine.transpose(1, 0, 2, 3).reshape(width // 2, -1)
+
     mix_other = to_sibling(mix_mine)
-
-    gate_up = jnp.concatenate([by_part(w_gate), by_part(w_up)], 2)
-    gate_up = seq_ordered(
-        [pick(gate_up, sq)] + [across_seq(pick(gate_up, sq ^ k), k) for k in range(1, n_seq)]
-    )
-    mat_gate_up = lax.all_gather(gate_up, "dp", axis=0).reshape(width, 2 * ff_part)
-    mat_down = lax.all_gather(w_down.astype(bf16), "dp", axis=0, tiled=True)
-
-    grad_top = cotangent.reshape(rows, width)
-    tops = [grad_top] + [across_seq(grad_top, k) for k in range(1, n_seq)]
+    mat_down = lax.all_gather(low_down, "dp", axis=0, tiled=True)
+    tops = {k: across_seq(top_out, k) for k in range(1, last)}
+    tops[0], tops[last] = grad_top, top_last
 
     cut_in, cut_out = 3 * width, 4 * width
     in_mine, in_other = mix_mine[:, :cut_in], mix_other[:, :cut_in]
@@ -180,9 +195,9 @@
     c_gate = projected[:, width : 2 * width]
     x_part = projected[:, 2 * width :]
     conv_in = (b_gate * x_part).astype(bf16).reshape(seqs_here, stretch, width)
-    prev_rows, prev_ids = from_behind(
-        (conv_in[:, -2:, :], segments[:, -2:].astype(bf16)), "seq", 1
-    )
+    edge_ids = jnp.pad(segments[:, -2:, None].astype(bf16), ((0, 0), (0, 0), (0, LANES - 1)))
+    edge = from_behind(jnp.concatenate([conv_in[:, -2:, :], edge_ids], 2), "seq", 1)
+    prev_rows, prev_ids = edge[:, :, :width], edge[:, :, width]
     extended = jnp.concatenate([prev_rows, conv_in], 1).astype(f32)
     ext_ids = jnp.concatenate([prev_ids.astype(jnp.int32), segments], 1)
     near_one = (ext_ids[:, 1:-1] == segments).astype(f32)[..., None]
@@ -196,33 +211,38 @@
     middle = residual + dot(mixed_mine, out_mine) + dot(mixed_other, out_other)
     unit_two, scale_two, norm_two = normed(middle, gain_vals[1])
 
-    norms = [norm_two] + [across_seq(norm_two, k) for k in range(1, n_seq)]
-    hiddens, act_grads, norm_parts, out_parts = [], [], [], []
-    for block, top in zip(norms, tops):
-        both = dot(block, mat_gate_up)
+    norms = {k: across_seq(norm_two, k) for k in range(last, 0, -1)}
+    norms[0] = norm_two
+    order = [0] + list(range(last, 0, -1))
+    hiddens, act_grads, norm_parts = {}, {}, {}
+    for k in order:
+        both = dot(norms[k], mat_gate_up)
         gate, up_part = both[:, :ff_part], both[:, ff_part:]
         sigma = jax.nn.sigmoid(gate)
         silu_vals = gate * sigma
-        grad_hidden = right_contract(top, mat_down)
-        hiddens.append((silu_vals * up_part).astype(bf16))
+        grad_hidden = right_contract(tops[k], mat_down)
+        hiddens[k] = (silu_vals * up_part).astype(bf16)
         grad_gate_act = (grad_hidden * up_part * sigma * (1.0 + gate * (1.0 - sigma))).astype(bf16)
         grad_up_act = (grad_hidden * silu_vals).astype(bf16)
-        act_grads.append(jnp.concatenate([grad_gate_act, grad_up_act], 1))
-        norm_parts.append(right_contract(act_grads[-1], mat_gate_up))
-        out_parts.append(dot(hiddens[-1], mat_down))
+        act_grads[k] = jnp.concatenate([grad_gate_act, grad_up_act], 1)
+        norm_parts[k] = right_contract(act_grads[k], mat_gate_up)
+    norm_sums = {k: across_seq(norm_parts[k].astype(bf16), k) for k in order[1:]}
+
+    def rows_of(blocks):
+        return jnp.concatenate([blocks[k] for k in order], 0)
+
+    grad_down = left_contract(rows_of(hiddens), rows_of(tops)).astype(bf16)
+    grad_gate_up = left_contract(rows_of(norms), rows_of(act_grads)).astype(bf16)
+    sum_down = lax.psum_scatter(grad_down, "dp", scatter_dimension=0, tiled=True).astype(f32)
+    gu_sum = lax.psum_scatter(grad_gate_up, "dp", scatter_dimension=0, tiled=True)
+    out_parts = {k: dot(hiddens[k], mat_down) for k in order}
+    norm_sums, out_low = tie((norm_sums, {k: out_parts[k].astype(bf16) for k in order[1:]}))
     grad_norm_two = norm_parts[0]
-    for k in range(1, n_seq):
-        grad_norm_two = grad_norm_two + across_seq(norm_parts[k].astype(bf16), k).astype(f32)
     output = middle + out_parts[0]
-    for k in range(1, n_seq):
-        output = output + across_seq(out_parts[k].astype(bf16), k).astype(f32)
+    for k in order[1:]:
+        grad_norm_two = grad_norm_two + norm_sums[k].astype(f32)
+        output = output + across_seq(out_low[k], k).astype(f32)
     output = output.astype(bf16)
-    hidden_all = jnp.concatenate(hiddens, 0)
-    top_all = jnp.concatenate(tops, 0)
-    norm_all = jnp.concatenate(norms, 0)
-    act_all = jnp.concatenate(act_grads, 0)
-    grad_down = left_contract(hidden_all, top_all)
-    grad_gate_up = left_contract(norm_all, act_all)
 
     back_two, gain_two = norm_back(grad_norm_two, unit_two, scale_two, gain_vals[1])
     grad_middle = grad_top.astype(f32) + back_two
@@ -263,35 +283,36 @@
     def sum_core(mine, other):
         return mine + to_sibling(other.astype(bf16)).astype(f32)
 
-    def sum_z(blocks):
-        low = blocks.astype(bf16)
-        total = pick(blocks, z)
-        for k in range(1, n_z):
-            total = total + along_z(pick(low, (z + k) % n_z), k).astype(f32)
-        return total
-
-    def sum_seq_z(mine):
-        blocks = mine.reshape(n_z, n_seq, own, -1)
-        low = blocks.astype(bf16)
-        total = lax.dynamic_index_in_dim(blocks, sq, 1, keepdims=False)
-        for k in range(1, n_seq):
-            part = lax.dynamic_index_in_dim(low, sq ^ k, 1, keepdims=False)
-            total = total + across_seq(part, k).astype(f32)
-        return sum_z(total)
-
     small_grads = jnp.stack(grad_taps + [gain_one, gain_two], 0)
     small_grads = small_grads.reshape(5, n_z, 2, n_seq, own).transpose(2, 1, 3, 0, 4)
     small_grads = jnp.pad(
         small_grads, ((0, 0), (0, 0), (0, 0), (0, own - 5), (0, LANES - own))
     ).reshape(2, width // 2, LANES)
-    small_sum = sum_seq_z(sum_core(pick(small_grads, core), pick(small_grads, 1 - core)))
-    sum_out = sum_seq_z(sum_core(grad_out_mine, grad_out_other))
-    sum_in = sum_seq_z(sum_core(grad_in_mine, grad_in_other))
-
-    gu_blocks = grad_gate_up.reshape(n_z, 2, n_seq * own, 2 * ff_part)
-    gu_mine = jnp.where(first_core, gu_blocks[:, 0], gu_blocks[:, 1])
-    gu_other = jnp.where(first_core, gu_blocks[:, 1], gu_blocks[:, 0])
-    gu_sum = sum_z(sum_core(gu_mine, gu_other)).astype(bf16).reshape(n_seq, own, 2 * ff_part)
+    mixed = jnp.concatenate(
+        [
+            sum_core(grad_in_mine, grad_in_other),
+            sum_core(grad_out_mine, grad_out_other),
+            sum_core(pick(small_grads, core), pick(small_grads, 1 - core)),
+        ],
+        1,
+    ).astype(bf16)
+    mixed = mixed.reshape(n_z, n_seq, own, -1)
+
+    def seq_block(index):
+        return lax.dynamic_index_in_dim(mixed, index, 1, keepdims=False)
+
+    seq_parts = [across_seq(seq_block(sq ^ k), k) for k in range(n_seq - 1, 0, -1)]
+    total = seq_block(sq).astype(f32)
+    for part in seq_parts:
+        total = total + part.astype(f32)
+    low = total.astype(bf16)
+    z_sums = [along_z(pick(low, (z + k) % n_z), k) for k in range(1, n_z)]
+    total = pick(total, z)
+    for part in z_sums:
+        total = total + part.astype(f32)
+    sum_in, sum_out, small_sum = total[:, :cut_in], total[:, cut_in:cut_out], total[:, cut_out:]
+
+    gu_sum = gu_sum.reshape(n_seq, own, 2 * ff_part)
     gu_sum = seq_ordered(
         [pick(gu_sum, sq)] + [across_seq(pick(gu_sum, sq ^ k), k) for k in range(1, n_seq)]
     ).astype(f32)
@@ -305,7 +326,6 @@
 
     sum_gate = by_row(gu_sum[:, :, :ff_part])
     sum_up = by_row(gu_sum[:, :, ff_part:])
-    sum_down = lax.psum_scatter(grad_down, "dp", scatter_dimension=0, tiled=True)
 
     reduced = (
         sum_in,

time: 613 us -> 501 us (0.82)
  starting transfers between devices: 81.4 us -> 46.8 us
  other arithmetic: 76.5 us -> 47.7 us
  local copies, waits for them, and re-layouts: 71.7 us -> 43.6 us
  waiting for transfers between devices: 218 us -> 198 us
    ppermute x27 -> x24, waiting for transfers between devices: 81.8 us -> 156 us  [across_seq(): lax.ppermute(block, 'seq', [(i, i ^ by) for i in range(lax.axis_size('seq...]
    all_gather x2 -> x1, waiting for transfers between devices: 39.9 us -> 0.01 us  [local(): mat_down = lax.all_gather(low_down, 'dp', axis=0, tiled=True)]
    ppermute x3 -> x2, waiting for transfers between devices: 36.4 us -> 0.79 us  [from_behind(): return lax.ppermute(shard, axis, pairs)]
    ppermute x15 -> x6, starting transfers between devices: 32.5 us -> 9.49 us  [along_z(): lax.ppermute(block, 'dp', [(i, (i + 2 * by) % count) for i in range(count)])]
    ppermute x15 -> x6, waiting for transfers between devices: 58.7 us -> 36.1 us  [along_z(): lax.ppermute(block, 'dp', [(i, (i + 2 * by) % count) for i in range(count)])]
    select_n x8 -> x0, local copies, waits for them, and re-layouts: 22.3 us -> none  [the longest x2 6.19 us: joined(): jnp.where(first_core, other, mine)]
    convert_element_type x10 -> x3, other arithmetic: 14 us -> 2.42 us  [the longest x1 1.82 us: local(): w_down.astype(bf16)]
    reshape x3 -> x0, local copies, waits for them, and re-layouts: 10.4 us -> none  [the longest x2 7.79 us: joined(): return jnp.concatenate([jnp.where(first_core, mine, other), jnp.where(fir...]
  transfers between devices with their start and end apart: 54 -> 40, of which waited for: 22 -> 21; matrix products, arithmetic and copies ran while one was open for 44% -> 38% of each run, Pallas kernels for 0% -> 0%
where the time goes in v2:
time: 501 us; the launch traced here: 492 us
  waiting for transfers between devices  198 us (40%)
  matrix products  139 us (28%)
  other arithmetic  47.7 us (10%)
  starting transfers between devices  46.8 us (9%)
  local copies, waits for them, and re-layouts  43.6 us (9%)
  between operations  16.4 us (3%)
    ppermute x24, waiting for transfers between devices, across_seq(): lax.ppermute(block, 'seq', [(i, i ^ by) for i in range(lax.axis_size('seq...  156 us
    dot_general x12, matrix products, right_contract(): lax.dot_general(first, second, (((1,), (1,)), ((), ())), preferred_elemen...  52.5 us
    dot_general x12, matrix products, dot(): return jnp.dot(first, second, preferred_element_type=f32)  44.8 us
    dot_general x6, matrix products, left_contract(): lax.dot_general(first, second, (((0,), (0,)), ((), ())), preferred_elemen...  41.9 us
    ppermute x6, waiting for transfers between devices, along_z(): lax.ppermute(block, 'dp', [(i, (i + 2 * by) % count) for i in range(count)])  36.1 us
    ppermute x24, starting transfers between devices, across_seq(): lax.ppermute(block, 'seq', [(i, i ^ by) for i in range(lax.axis_size('seq...  32.3 us
    unnamed x281, local copies, waits for them, and re-layouts  22.3 us
  transfers between devices with their start and end apart: 40, of which 21 were waited for; matrix products, arithmetic and copies ran while one was open for 38% of the time, Pallas kernels for 0%

profile of v2, /device:TPU:8, one launch (start us, length us, event | category | flops | bytes accessed | tf_op | source)
XLA Modules:
  0.0 492.1 jit_solution(17589081147082046066)
XLA Ops:
  31.8 13.7 %collective-permute-done = bf16[32,4224]{1,0:T(8,128)(2,1)} collective-permute-done((bf16[32,4224]{1,0:T(8,128)(2,1)}, bf16[32,4224]{1,0:T(8,128)(2,1)}, u32[]{:S(2)}, u32[]{:S(2)}) %collective-permute-start) | collective-permute-done | bytes 270368 | tf_op jit(solution)/shard_map/ppermute | solution.py:33
  60.9 22.3 %collective-permute-done.7 = bf16[4,32,4224]{2,1,0:T(8,128)(2,1)S(1)} collective-permute-done((bf16[4,32,4224]{2,1,0:T(8,128)(2,1)}, bf16[4,32,4224]{2,1,0:T(8,128)(2,1)S(1)}, u32[]{:S(2)}, u32[]{:S(2)}) %collective-permute-start.7) | collective-permute-done | bytes 1081376 | tf_op jit(solution)/shard_map/ppermute | solution.py:37
  83.2 21.0 %collective-permute-done.8 = bf16[4,32,4224]{2,1,0:T(8,128)(2,1)} collective-permute-done((bf16[4,32,4224]{2,1,0:T(8,128)(2,1)}, bf16[4,32,4224]{2,1,0:T(8,128)(2,1)}, u32[]{:S(2)}, u32[]{:S(2)}) %collective-permute-start.8) | collective-permute-done | bytes 1081376 | tf_op jit(solution)/shard_map/ppermute | solution.py:37
  112.3 5.7 %collective-permute-done.10 = bf16[512,4224]{1,0:T(8,128)(2,1)} collective-permute-done((bf16[512,4224]{1,0:T(8,128)(2,1)}, bf16[512,4224]{1,0:T(8,128)(2,1)}, u32[]{:S(2)}, u32[]{:S(2)}) %collective-permute-start.10) | collective-permute-done | bytes 4325408 | tf_op jit(solution)/shard_map/ppermute | solution.py:28
  119.7 4.0 fusion.51
  123.8 3.8 convolution_add_fusion
  155.7 20.4 %collective-permute-done.18 = bf16[512,1024]{1,0:T(8,128)(2,1)} collective-permute-done((bf16[512,1024]{1,0:T(8,128)(2,1)}, bf16[512,1024]{1,0:T(8,128)(2,1)}, u32[]{:S(2)}, u32[]{:S(2)}) %collective-permute-start.18) | collective-permute-done | bytes 1048608 | tf_op jit(solution)/shard_map/ppermute | solution.py:37
  176.0 7.5 %fusion.158 = f32[512,2304]{1,0:T(8,128)} fusion(bf16[512,1024]{1,0:T(8,128)(2,1)} %collective-permute-done.18, bf16[1024,2304]{1,0:T(8,128)(2,1)} %bitcast.238), kind=kOutput, calls=%fused_computation.325 | convolution fusion | flops 2415919104 | bytes 10485760 | tf_op jit(solution)/shard_map/dot_general | solution.py:41
  183.6 7.2 %multiply_convert_fusion.6 = (bf16[512,1152]{1,0:T(8,128)(2,1)}, bf16[512,1152]{1,0:T(8,128)(2,1)}, bf16[512,1152]{1,0:T(8,128)(2,1)S(1)}) fusion(f32[512,2304]{1,0:T(8,128)} %fusion.158, bf16[512,1024]{1,0:T(8,128)(2,1)} %collective-permute-done.6, bf16[1152,1024]{1,0:T(8,128)(2,1)} %all-gather.4.cloned.1.call-done), kind=kOutput, calls=%fused_computation.77 | convolution fusion | flops 1216806912 | bytes 11665408 | tf_op jit(solution)/shard_map/dot_general | solution.py:49
  190.8 4.3 fusion.154
  195.1 24.1 %collective-permute-done.16 = bf16[512,1024]{1,0:T(8,128)(2,1)} collective-permute-done((bf16[512,1024]{1,0:T(8,128)(2,1)}, bf16[512,1024]{1,0:T(8,128)(2,1)}, u32[]{:S(2)}, u32[]{:S(2)}) %collective-permute-start.16) | collective-permute-done | bytes 1048608 | tf_op jit(solution)/shard_map/ppermute | solution.py:37
  219.2 4.0 fusion.157
  223.2 5.0 %multiply_convert_fusion.8 = (bf16[512,1152]{1,0:T(8,128)(2,1)}, bf16[512,1152]{1,0:T(8,128)(2,1)}, bf16[512,1152]{1,0:T(8,128)(2,1)S(1)}) fusion(f32[512,2304]{1,0:T(8,128)S(1)} %fusion.157, bf16[512,1024]{1,0:T(8,128)(2,1)} %collective-permute-done.15, bf16[1152,1024]{1,0:T(8,128)(2,1)S(1)} %copy-done.104), kind=kOutput, calls=%fused_computation.81 | convolution fusion | flops 1216806912 | bytes 11665408 | tf_op jit(solution)/shard_map/dot_general | solution.py:49
  228.2 4.3 fusion.156
  232.5 3.8 multiply_convert_fusion.1
  236.3 5.5 %multiply_convert_fusion.10 = (bf16[512,1152]{1,0:T(8,128)(2,1)}, bf16[512,1152]{1,0:T(8,128)(2,1)}, bf16[512,1152]{1,0:T(8,128)(2,1)S(1)}) fusion(f32[512,2304]{1,0:T(8,128)S(1)} %fusion.156, bf16[512,1024]{1,0:T(8,128)(2,1)} %collective-permute-done.12, bf16[1152,1024]{1,0:T(8,128)(2,1)S(1)} %copy-done.104), kind=kOutput, calls=%fused_computation.85 | convolution fusion | flops 1216806912 | bytes 11665408 | tf_op jit(solution)/shard_map/dot_general | solution.py:49
  242.7 8.9 %fusion.41 = bf16[1152,1024]{1,0:T(8,128)(2,1)} fusion(bf16[512,1024]{1,0:T(8,128)(2,1)} %collective-permute-done.12, bf16[512,1024]{1,0:T(8,128)(2,1)} %collective-permute-done.15, bf16[512,1024]{1,0:T(8,128)(2,1)} %collective-permute-done.6, bf16[512,1024]{1,0:T(8,128)(2,1)S(1)} %bitcast.204, bf16[512,1152]{1,0:T(8,128)(2,1)S(1)} %get-tuple-element.112, ...), kind=kOutput, calls=%fused_computation.45 | convolution fusion | flops 4868669440 | bytes 11272192 | tf_op jit(solution)/shard_map/dot_general | solution.py:45
  251.7 6.8 %fusion.91 = bf16[512,1024]{1,0:T(8,128)(2,1)} fusion(bf16[1024,2304]{1,0:T(8,128)(2,1)} %bitcast.239, bf16[512,1152]{1,0:T(8,128)(2,1)} %get-tuple-element.104, bf16[512,1152]{1,0:T(8,128)(2,1)} %get-tuple-element.103), kind=kOutput, calls=%fused_computation.138 | convolution fusion | flops 2421161984 | bytes 8126464 | tf_op jit(solution)/shard_map/dot_general | solution.py:49
  261.2 6.1 %fusion.94 = bf16[512,1024]{1,0:T(8,128)(2,1)} fusion(bf16[1024,2304]{1,0:T(8,128)(2,1)} %bitcast.240, bf16[512,1152]{1,0:T(8,128)(2,1)S(1)} %copy-done.117, bf16[512,1152]{1,0:T(8,128)(2,1)S(1)} %copy-done.116), kind=kOutput, calls=%fused_computation.139 | convolution fusion | flops 2421161984 | bytes 8126464 | tf_op jit(solution)/shard_map/dot_general | solution.py:49
  271.8 20.5 %fusion.16 = bf16[1024,2304]{1,0:T(8,128)(2,1)} fusion(bf16[512,1152]{1,0:T(8,128)(2,1)} %get-tuple-element.108, bf16[512,1152]{1,0:T(8,128)(2,1)} %get-tuple-element.107, bf16[512,1152]{1,0:T(8,128)(2,1)} %get-tuple-element.106, bf16[512,1152]{1,0:T(8,128)(2,1)} %get-tuple-element.105, bf16[512,1152]{1,0:T(8,128)(2,1)} %get-tuple-element.104, ...), kind=kOutput, calls=%fused_computation.17 | convolution fusion | flops 9758310400 | bytes 18350080 | tf_op jit(solution)/shard_map/dot_general | solution.py:45
  292.3 4.7 convolution_convert_fusion.1
  327.5 3.8 collective-permute-start.20
  339.6 3.8 fusion.49
  366.4 4.8 add_convert_fusion
  378.0 10.3 %collective-permute-done.22 = bf16[512,1024]{1,0:T(8,128)(2,1)S(1)} collective-permute-done((bf16[512,1024]{1,0:T(8,128)(2,1)S(1)}, bf16[512,1024]{1,0:T(8,128)(2,1)S(1)}, u32[]{:S(2)}, u32[]{:S(2)}) %collective-permute-start.22) | collective-permute-done | bytes 1048608 | tf_op jit(solution)/shard_map/ppermute | solution.py:37
  388.3 4.1 fusion.86
  392.4 20.2 %collective-permute-done.27 = bf16[4,32,4224]{2,1,0:T(8,128)(2,1)S(1)} collective-permute-done((bf16[4,32,4224]{2,1,0:T(8,128)(2,1)S(1)}, bf16[4,32,4224]{2,1,0:T(8,128)(2,1)S(1)}, u32[]{:S(2)}, u32[]{:S(2)}) %collective-permute-start.27) | collective-permute-done | bytes 1081376 | tf_op jit(solution)/shard_map/ppermute | solution.py:37
  412.6 11.5 %collective-permute-done.28 = bf16[4,32,4224]{2,1,0:T(8,128)(2,1)S(1)} collective-permute-done((bf16[4,32,4224]{2,1,0:T(8,128)(2,1)S(1)}, bf16[4,32,4224]{2,1,0:T(8,128)(2,1)S(1)}, u32[]{:S(2)}, u32[]{:S(2)}) %collective-permute-start.28) | collective-permute-done | bytes 1081376 | tf_op jit(solution)/shard_map/ppermute | solution.py:37
  424.1 9.6 %collective-permute-done.29 = bf16[4,32,4224]{2,1,0:T(8,128)(2,1)S(1)} collective-permute-done((bf16[4,32,4224]{2,1,0:T(8,128)(2,1)S(1)}, bf16[4,32,4224]{2,1,0:T(8,128)(2,1)S(1)}, u32[]{:S(2)}, u32[]{:S(2)}) %collective-permute-start.29) | collective-permute-done | bytes 1081376 | tf_op jit(solution)/shard_map/ppermute | solution.py:37
  441.9 14.6 %collective-permute-done.30 = bf16[32,4224]{1,0:T(8,128)(2,1)} collective-permute-done((bf16[32,4224]{1,0:T(8,128)(2,1)}, bf16[32,4224]{1,0:T(8,128)(2,1)}, u32[]{:S(2)}, u32[]{:S(2)}) %collective-permute-start.30) | collective-permute-done | bytes 270368 | tf_op jit(solution)/shard_map/ppermute | solution.py:33
  456.4 3.9 collective-permute-done.31
  481.0 4.1 multiply_subtract_fusion.1
  (471 shorter events, 181.5 us)
Async XLA Ops:
  7.2 168.8 %all-gather.6.cloned.1.call-start = ((), (), s32[]{:S(2)}) async-start(), calls=%async_computation.5 | async-start | bytes 5308416 | tf_op jit(solution)/shard_map/all_gather | solution.py:160
  13.6 8.5 %collective-permute-start.4 = (bf16[32,2304]{1,0:T(8,128)(2,1)S(1)}, bf16[32,2304]{1,0:T(8,128)(2,1)S(1)}, u32[]{:S(2)}, u32[]{:S(2)}) collective-permute-start(bf16[32,2304]{1,0:T(8,128)(2,1)S(1)} %get-tuple-element.174), channel_id=1, source_target_pairs={{0,2},{1,3},{2,0},{3,1},{4,6},{5,7},{6,4},{7,5},{8,10},{9,11},{10,... | collective-permute-start | bytes 442376 | tf_op jit(solution)/shard_map/ppermute | solution.py:37
  22.1 27.0 %collective-permute-start.6 = (bf16[512,1024]{1,0:T(8,128)(2,1)S(1)}, bf16[512,1024]{1,0:T(8,128)(2,1)}, u32[]{:S(2)}, u32[]{:S(2)}) collective-permute-start(bf16[512,1024]{1,0:T(8,128)(2,1)S(1)} %bitcast.200), channel_id=1, source_target_pairs={{0,3},{1,2},{2,1},{3,0},{4,7},{5,6},{6,5},{7,4},{8,11},{9,10},{10,... | collective-permute-start | bytes 3145736 | tf_op jit(solution)/shard_map/ppermute | solution.py:37
  24.4 21.2 %collective-permute-start = (bf16[32,4224]{1,0:T(8,128)(2,1)}, bf16[32,4224]{1,0:T(8,128)(2,1)}, u32[]{:S(2)}, u32[]{:S(2)}) collective-permute-start(bf16[32,4224]{1,0:T(8,128)(2,1)} %pad_maximum_fusion.11), channel_id=1, source_target_pairs={{0,24},{4,28},{8,0},{12,4},{16,8},{20,12},{24,16},{28,20},{1,25},{... | collective-permute-start | bytes 811016 | tf_op jit(solution)/shard_map/ppermute | solution.py:33
  24.8 20.7 %collective-permute-start.1 = (bf16[32,4224]{1,0:T(8,128)(2,1)}, bf16[32,4224]{1,0:T(8,128)(2,1)}, u32[]{:S(2)}, u32[]{:S(2)}) collective-permute-start(bf16[32,4224]{1,0:T(8,128)(2,1)} %pad_maximum_fusion.11), channel_id=1, source_target_pairs={{0,16},{4,20},{8,24},{12,28},{16,0},{20,4},{24,8},{28,12},{1,17},{... | collective-permute-start | bytes 811016 | tf_op jit(solution)/shard_map/ppermute | solution.py:33
  27.4 21.7 %collective-permute-start.2 = (bf16[32,4224]{1,0:T(8,128)(2,1)}, bf16[32,4224]{1,0:T(8,128)(2,1)}, u32[]{:S(2)}, u32[]{:S(2)}) collective-permute-start(bf16[32,4224]{1,0:T(8,128)(2,1)} %pad_maximum_fusion.11), channel_id=1, source_target_pairs={{0,8},{4,12},{8,16},{12,20},{16,24},{20,28},{24,0},{28,4},{1,9},{5... | collective-permute-start | bytes 811016 | tf_op jit(solution)/shard_map/ppermute | solution.py:33
  56.2 27.0 %collective-permute-start.7 = (bf16[4,32,4224]{2,1,0:T(8,128)(2,1)}, bf16[4,32,4224]{2,1,0:T(8,128)(2,1)S(1)}, u32[]{:S(2)}, u32[]{:S(2)}) collective-permute-start(bf16[4,32,4224]{2,1,0:T(8,128)(2,1)} %constant_dynamic-slice_fusion.14), channel_id=1, source_target_pairs={{0,1},{1,0},{2,3},{3,2},{4,5},{5,4},{6,7},{7,6},{8,9},{9,8},{10,11... | collective-permute-start | bytes 3244040 | tf_op jit(solution)/shard_map/ppermute | solution.py:37
  57.0 47.2 %collective-permute-start.8 = (bf16[4,32,4224]{2,1,0:T(8,128)(2,1)}, bf16[4,32,4224]{2,1,0:T(8,128)(2,1)}, u32[]{:S(2)}, u32[]{:S(2)}) collective-permute-start(bf16[4,32,4224]{2,1,0:T(8,128)(2,1)} %constant_dynamic-slice_fusion.14), channel_id=1, source_target_pairs={{0,2},{1,3},{2,0},{3,1},{4,6},{5,7},{6,4},{7,5},{8,10},{9,11},{10,... | collective-permute-start | bytes 3244040 | tf_op jit(solution)/shard_map/ppermute | solution.py:37
  58.5 47.2 %collective-permute-start.9 = (bf16[4,32,4224]{2,1,0:T(8,128)(2,1)}, bf16[4,32,4224]{2,1,0:T(8,128)(2,1)}, u32[]{:S(2)}, u32[]{:S(2)}) collective-permute-start(bf16[4,32,4224]{2,1,0:T(8,128)(2,1)} %constant_dynamic-slice_fusion.14), channel_id=1, source_target_pairs={{0,3},{1,2},{2,1},{3,0},{4,7},{5,6},{6,5},{7,4},{8,11},{9,10},{10,... | collective-permute-start | bytes 3244040 | tf_op jit(solution)/shard_map/ppermute | solution.py:37
  60.8 122.8 %all-gather.4.cloned.1.call-start = ((), (), s32[]{:S(2)}) async-start(), calls=%async_computation.2 | async-start | bytes 2654208 | tf_op jit(solution)/shard_map/all_gather | solution.py:171
  134.3 304.8 %reduce-scatter.5.cloned.1.call-start = ((), (), s32[]{:S(2)}) async-start(), calls=%async_computation.4 | async-start | bytes 2654208 | tf_op jit(solution)/shard_map/reduce_scatter | solution.py:236
  148.3 27.7 %collective-permute-start.18 = (bf16[512,1024]{1,0:T(8,128)(2,1)}, bf16[512,1024]{1,0:T(8,128)(2,1)}, u32[]{:S(2)}, u32[]{:S(2)}) collective-permute-start(bf16[512,1024]{1,0:T(8,128)(2,1)} %multiply_convert_fusion.12), channel_id=1, source_target_pairs={{0,3},{1,2},{2,1},{3,0},{4,7},{5,6},{6,5},{7,4},{8,11},{9,10},{10,... | collective-permute-start | bytes 3145736 | tf_op jit(solution)/shard_map/ppermute | solution.py:37
  151.6 71.6 %collective-permute-start.15 = (bf16[512,1024]{1,0:T(8,128)(2,1)S(1)}, bf16[512,1024]{1,0:T(8,128)(2,1)}, u32[]{:S(2)}, u32[]{:S(2)}) collective-permute-start(bf16[512,1024]{1,0:T(8,128)(2,1)S(1)} %bitcast.201), channel_id=1, source_target_pairs={{0,2},{1,3},{2,0},{3,1},{4,6},{5,7},{6,4},{7,5},{8,10},{9,11},{10,... | collective-permute-start | bytes 3145736 | tf_op jit(solution)/shard_map/ppermute | solution.py:37
  152.1 84.2 %collective-permute-start.12 = (bf16[512,1024]{1,0:T(8,128)(2,1)S(1)}, bf16[512,1024]{1,0:T(8,128)(2,1)}, u32[]{:S(2)}, u32[]{:S(2)}) collective-permute-start(bf16[512,1024]{1,0:T(8,128)(2,1)S(1)} %bitcast.202), channel_id=1, source_target_pairs={{0,1},{1,0},{2,3},{3,2},{4,5},{5,4},{6,7},{7,6},{8,9},{9,8},{10,11... | collective-permute-start | bytes 3145736 | tf_op jit(solution)/shard_map/ppermute | solution.py:37
  153.2 66.0 %collective-permute-start.16 = (bf16[512,1024]{1,0:T(8,128)(2,1)}, bf16[512,1024]{1,0:T(8,128)(2,1)}, u32[]{:S(2)}, u32[]{:S(2)}) collective-permute-start(bf16[512,1024]{1,0:T(8,128)(2,1)} %multiply_convert_fusion.12), channel_id=1, source_target_pairs={{0,2},{1,3},{2,0},{3,1},{4,6},{5,7},{6,4},{7,5},{8,10},{9,11},{10,... | collective-permute-start | bytes 3145736 | tf_op jit(solution)/shard_map/ppermute | solution.py:37
  155.2 73.0 %collective-permute-start.13 = (bf16[512,1024]{1,0:T(8,128)(2,1)}, bf16[512,1024]{1,0:T(8,128)(2,1)}, u32[]{:S(2)}, u32[]{:S(2)}) collective-permute-start(bf16[512,1024]{1,0:T(8,128)(2,1)} %multiply_convert_fusion.12), channel_id=1, source_target_pairs={{0,1},{1,0},{2,3},{3,2},{4,5},{5,4},{6,7},{7,6},{8,9},{9,8},{10,11... | collective-permute-start | bytes 3145736 | tf_op jit(solution)/shard_map/ppermute | solution.py:37
  251.6 213.0 %reduce-scatter.3.cloned.1.call-start = ((), (), s32[]{:S(2)}) async-start(), calls=%async_computation.3 | async-start | bytes 5308416 | tf_op jit(solution)/shard_map/reduce_scatter | solution.py:237
  258.5 49.1 %collective-permute-start.19 = (bf16[512,1024]{1,0:T(8,128)(2,1)}, bf16[512,1024]{1,0:T(8,128)(2,1)}, u32[]{:S(2)}, u32[]{:S(2)}) collective-permute-start(bf16[512,1024]{1,0:T(8,128)(2,1)} %fusion.91), channel_id=1, source_target_pairs={{0,3},{1,2},{2,1},{3,0},{4,7},{5,6},{6,5},{7,4},{8,11},{9,10},{10,... | collective-permute-start | bytes 3145736 | tf_op jit(solution)/shard_map/ppermute | solution.py:37
  267.3 40.3 %collective-permute-start.17 = (bf16[512,1024]{1,0:T(8,128)(2,1)}, bf16[512,1024]{1,0:T(8,128)(2,1)}, u32[]{:S(2)}, u32[]{:S(2)}) collective-permute-start(bf16[512,1024]{1,0:T(8,128)(2,1)} %fusion.94), channel_id=1, source_target_pairs={{0,2},{1,3},{2,0},{3,1},{4,6},{5,7},{6,4},{7,5},{8,10},{9,11},{10,... | collective-permute-start | bytes 3145736 | tf_op jit(solution)/shard_map/ppermute | solution.py:37
  271.4 36.2 %collective-permute-start.14 = (bf16[512,1024]{1,0:T(8,128)(2,1)}, bf16[512,1024]{1,0:T(8,128)(2,1)}, u32[]{:S(2)}, u32[]{:S(2)}) collective-permute-start(bf16[512,1024]{1,0:T(8,128)(2,1)} %fusion.97), channel_id=1, source_target_pairs={{0,1},{1,0},{2,3},{3,2},{4,5},{5,4},{6,7},{7,6},{8,9},{9,8},{10,11... | collective-permute-start | bytes 3145736 | tf_op jit(solution)/shard_map/ppermute | solution.py:37
  327.2 36.9 %collective-permute-start.25 = (bf16[512,1024]{1,0:T(8,128)(2,1)}, bf16[512,1024]{1,0:T(8,128)(2,1)}, u32[]{:S(2)}, u32[]{:S(2)}) collective-permute-start(bf16[512,1024]{1,0:T(8,128)(2,1)} %convolution_convert_fusion.4), channel_id=1, source_target_pairs={{0,4},{4,0},{8,12},{12,8},{16,20},{20,16},{24,28},{28,24},{1,5},{5... | collective-permute-start | bytes 3145736 | tf_op jit(solution)/shard_map/ppermute | solution.py:28
  327.5 46.2 %collective-permute-start.20 = (bf16[512,1024]{1,0:T(8,128)(2,1)}, bf16[512,1024]{1,0:T(8,128)(2,1)}, u32[]{:S(2)}, u32[]{:S(2)}) collective-permute-start(bf16[512,1024]{1,0:T(8,128)(2,1)} %convolution_convert_fusion.1), channel_id=1, source_target_pairs={{0,3},{1,2},{2,1},{3,0},{4,7},{5,6},{6,5},{7,4},{8,11},{9,10},{10,... | collective-permute-start | bytes 3145736 | tf_op jit(solution)/shard_map/ppermute | solution.py:37
  331.3 46.7 %collective-permute-start.21 = (bf16[512,1024]{1,0:T(8,128)(2,1)}, bf16[512,1024]{1,0:T(8,128)(2,1)}, u32[]{:S(2)}, u32[]{:S(2)}) collective-permute-start(bf16[512,1024]{1,0:T(8,128)(2,1)} %convolution_convert_fusion.2), channel_id=1, source_target_pairs={{0,2},{1,3},{2,0},{3,1},{4,6},{5,7},{6,4},{7,5},{8,10},{9,11},{10,... | collective-permute-start | bytes 3145736 | tf_op jit(solution)/shard_map/ppermute | solution.py:37
  343.4 23.0 %collective-permute-start.24 = (bf16[512,3072]{1,0:T(8,128)(2,1)}, bf16[512,3072]{1,0:T(8,128)(2,1)}, u32[]{:S(2)}, u32[]{:S(2)}) collective-permute-start(bf16[512,3072]{1,0:T(8,128)(2,1)} %convolution_convert_fusion), channel_id=1, source_target_pairs={{0,4},{4,0},{8,12},{12,8},{16,20},{20,16},{24,28},{28,24},{1,5},{5... | collective-permute-start | bytes 9437192 | tf_op jit(solution)/shard_map/ppermute | solution.py:28
  362.2 26.0 %collective-permute-start.22 = (bf16[512,1024]{1,0:T(8,128)(2,1)S(1)}, bf16[512,1024]{1,0:T(8,128)(2,1)S(1)}, u32[]{:S(2)}, u32[]{:S(2)}) collective-permute-start(bf16[512,1024]{1,0:T(8,128)(2,1)S(1)} %copy-done.106), channel_id=1, source_target_pairs={{0,1},{1,0},{2,3},{3,2},{4,5},{5,4},{6,7},{7,6},{8,9},{9,8},{10,11... | collective-permute-start | bytes 3145736 | tf_op jit(solution)/shard_map/ppermute | solution.py:37
  371.9 40.8 %collective-permute-start.27 = (bf16[4,32,4224]{2,1,0:T(8,128)(2,1)S(1)}, bf16[4,32,4224]{2,1,0:T(8,128)(2,1)S(1)}, u32[]{:S(2)}, u32[]{:S(2)}) collective-permute-start(bf16[4,32,4224]{2,1,0:T(8,128)(2,1)S(1)} %get-tuple-element.113), channel_id=1, source_target_pairs={{0,3},{1,2},{2,1},{3,0},{4,7},{5,6},{6,5},{7,4},{8,11},{9,10},{10,... | collective-permute-start | bytes 3244040 | tf_op jit(solution)/shard_map/ppermute | solution.py:37
  373.4 50.7 %collective-permute-start.28 = (bf16[4,32,4224]{2,1,0:T(8,128)(2,1)S(1)}, bf16[4,32,4224]{2,1,0:T(8,128)(2,1)S(1)}, u32[]{:S(2)}, u32[]{:S(2)}) collective-permute-start(bf16[4,32,4224]{2,1,0:T(8,128)(2,1)S(1)} %get-tuple-element.115), channel_id=1, source_target_pairs={{0,2},{1,3},{2,0},{3,1},{4,6},{5,7},{6,4},{7,5},{8,10},{9,11},{10,... | collective-permute-start | bytes 3244040 | tf_op jit(solution)/shard_map/ppermute | solution.py:37
  373.7 60.0 %collective-permute-start.29 = (bf16[4,32,4224]{2,1,0:T(8,128)(2,1)S(1)}, bf16[4,32,4224]{2,1,0:T(8,128)(2,1)S(1)}, u32[]{:S(2)}, u32[]{:S(2)}) collective-permute-start(bf16[4,32,4224]{2,1,0:T(8,128)(2,1)S(1)} %get-tuple-element.114), channel_id=1, source_target_pairs={{0,1},{1,0},{2,3},{3,2},{4,5},{5,4},{6,7},{7,6},{8,9},{9,8},{10,11... | collective-permute-start | bytes 3244040 | tf_op jit(solution)/shard_map/ppermute | solution.py:37
  435.2 21.3 %collective-permute-start.30 = (bf16[32,4224]{1,0:T(8,128)(2,1)}, bf16[32,4224]{1,0:T(8,128)(2,1)}, u32[]{:S(2)}, u32[]{:S(2)}) collective-permute-start(bf16[32,4224]{1,0:T(8,128)(2,1)} %get-tuple-element.131), channel_id=1, source_target_pairs={{0,8},{4,12},{8,16},{12,20},{16,24},{20,28},{24,0},{28,4},{1,9},{5... | collective-permute-start | bytes 811016 | tf_op jit(solution)/shard_map/ppermute | solution.py:33
  437.6 22.8 %collective-permute-start.31 = (bf16[32,4224]{1,0:T(8,128)(2,1)}, bf16[32,4224]{1,0:T(8,128)(2,1)}, u32[]{:S(2)}, u32[]{:S(2)}) collective-permute-start(bf16[32,4224]{1,0:T(8,128)(2,1)} %get-tuple-element.133), channel_id=1, source_target_pairs={{0,16},{4,20},{8,24},{12,28},{16,0},{20,4},{24,8},{28,12},{1,17},{... | collective-permute-start | bytes 811016 | tf_op jit(solution)/shard_map/ppermute | solution.py:33
  437.6 23.1 %collective-permute-start.32 = (bf16[32,4224]{1,0:T(8,128)(2,1)}, bf16[32,4224]{1,0:T(8,128)(2,1)}, u32[]{:S(2)}, u32[]{:S(2)}) collective-permute-start(bf16[32,4224]{1,0:T(8,128)(2,1)} %get-tuple-element.132), channel_id=1, source_target_pairs={{0,24},{4,28},{8,0},{12,4},{16,8},{20,12},{24,16},{28,20},{1,25},{... | collective-permute-start | bytes 811016 | tf_op jit(solution)/shard_map/ppermute | solution.py:33
  467.4 8.6 %collective-permute-start.34 = (bf16[32,2304]{1,0:T(8,128)(2,1)S(1)}, bf16[32,2304]{1,0:T(8,128)(2,1)S(1)}, u32[]{:S(2)}, u32[]{:S(2)}) collective-permute-start(bf16[32,2304]{1,0:T(8,128)(2,1)S(1)} %get-tuple-element.166), channel_id=1, source_target_pairs={{0,2},{1,3},{2,0},{3,1},{4,6},{5,7},{6,4},{7,5},{8,10},{9,11},{10,... | collective-permute-start | bytes 442376 | tf_op jit(solution)/shard_map/ppermute | solution.py:37
  (132 other events, 1365.2 us)
Sparse Core Ops, SparseCore 0:
  60.9 50.5 all-gather.5
  134.5 31.4 all-gather.3
  251.7 33.6 reduce-scatter.4
  292.4 52.8 reduce-scatter.2

commit v3 on v2

--- a/solution.py
+++ b/solution.py
@@ -1,6 +1,8 @@
 import jax
 import jax.numpy as jnp
 from jax import lax
+from jax.experimental import pallas as pl
+from jax.experimental.pallas import tpu as pltpu
 from jax.sharding import PartitionSpec as P
 
 STEP = 10
@@ -55,6 +57,30 @@
 
 def pick(stacked, index):
     return lax.dynamic_index_in_dim(stacked, index, 0, keepdims=False)
+
+
+def place(blocks, slots, shape, axis):
+    def kernel(slots_ref, *refs):
+        sources, out, sems = refs[:-2], refs[-2], refs[-1]
+        copies = []
+        for k, source in enumerate(sources):
+            target = out.at[slots_ref[k]] if axis == 0 else out.at[:, slots_ref[k]]
+            copies.append(pltpu.make_async_copy(source, target, sems.at[k]))
+        for copy in copies:
+            copy.start()
+        for copy in copies:
+            copy.wait()
+
+    anywhere = pl.BlockSpec(memory_space=pl.ANY)
+    size = sum(block.size for block in blocks) * 4
+    return pl.pallas_call(
+        kernel,
+        out_shape=jax.ShapeDtypeStruct(shape, blocks[0].dtype),
+        in_specs=[pl.BlockSpec(memory_space=pltpu.SMEM)] + [anywhere] * len(blocks),
+        out_specs=anywhere,
+        scratch_shapes=[pltpu.SemaphoreType.DMA((len(blocks),))],
+        cost_estimate=pl.CostEstimate(flops=0, bytes_accessed=size, transcendentals=0),
+    )(slots.astype(jnp.int32), *blocks)
 
 
 def normed(values, gain):
@@ -127,14 +153,6 @@
         odd = jnp.concatenate(blocks[1::2], 1)
         return jnp.where(first_core, even, odd), jnp.where(first_core, odd, even)
 
-    def joined(mine, other):
-        even = jnp.where(first_core, mine, other)
-        odd = jnp.where(first_core, other, mine)
-        blocks = []
-        for i in range(n_z):
-            blocks += [even[:, i * lane : (i + 1) * lane], odd[:, i * lane : (i + 1) * lane]]
-        return jnp.concatenate(blocks, 1)
-
     def seq_ordered(pieces):
         stacked = jnp.stack(pieces, 0)
         return jnp.stack([pick(stacked, sq ^ j) for j in range(n_seq)], 0)
@@ -149,57 +167,81 @@
     mix = jnp.concatenate([w_in.astype(bf16), w_out.astype(bf16), smalls], 1)
     gate_up = jnp.concatenate([by_part(w_gate), by_part(w_up)], 2)
 
+    residual_low = inputs.reshape(rows, width)
+    edge_ids = jnp.pad(segments[:, -2:, None].astype(bf16), ((0, 0), (0, 0), (0, LANES - 1)))
+    edge = from_behind(jnp.concatenate([inputs[:, -2:, :], edge_ids], 2), "seq", 1)
     z_parts = [along_z(mix, -k) for k in range(1, n_z)]
     gu_parts = [across_seq(pick(gate_up, sq ^ k), k) for k in range(1, n_seq)]
-    grad_top = cotangent.reshape(rows, width)
-    gu_parts, top_out = tie((gu_parts, grad_top))
-    last = n_seq - 1
-    top_last = across_seq(top_out, last)
-    z_parts, gu_parts, top_last = tie((z_parts, gu_parts, top_last))
+    low_down = w_down.astype(bf16)
+    z_parts, gu_parts, edge, low_down = tie((z_parts, gu_parts, edge, low_down))
     gate_up = seq_ordered([pick(gate_up, sq)] + gu_parts)
     mat_gate_up = lax.all_gather(gate_up, "dp", axis=0).reshape(width, 2 * ff_part)
-
-    z_twice = jnp.stack(([mix] + z_parts) * 2, 0)
-    z_order = lax.dynamic_slice_in_dim(z_twice, (n_z - z) % n_z, n_z, 0)
-    mix_parts = {k: across_seq(z_order, k) for k in range(n_seq - 1, 0, -1)}
-    mix_parts, top_out, low_down = tie((mix_parts, top_out, w_down.astype(bf16)))
+    mat_down = lax.all_gather(low_down, "dp", axis=0, tiled=True)
+
+    columns = mix.shape[1]
+
+    z_slots = (z + jnp.arange(n_z)) % n_z
+    seq_slots = sq ^ jnp.arange(n_seq)
+    core_slots = core ^ jnp.arange(2)
+    last = n_seq - 1
+    order = [0] + list(range(last, 0, -1))
+    grad_top = cotangent.reshape(rows, width)
+    z_order = place([mix] + z_parts, z_slots, (n_z, own, columns), 0)
+    mix_parts = {k: across_seq(z_order, k) for k in order[1:]}
+    mix_parts, top_out = tie((mix_parts, grad_top))
     mix_parts[0] = z_order
-    mix_mine = seq_ordered([mix_parts[k] for k in range(n_seq)])
-    mix_mine = mix_mine.transpose(1, 0, 2, 3).reshape(width // 2, -1)
+    mix_mine = place(
+        [mix_parts[k] for k in range(n_seq)], seq_slots, (n_z, n_seq, own, columns), 1
+    ).reshape(width // 2, columns)
 
     mix_other = to_sibling(mix_mine)
-    mat_down = lax.all_gather(low_down, "dp", axis=0, tiled=True)
-    tops = {k: across_seq(top_out, k) for k in range(1, last)}
-    tops[0], tops[last] = grad_top, top_last
+    tops = {k: across_seq(top_out, k) for k in order[1:]}
 
     cut_in, cut_out = 3 * width, 4 * width
     in_mine, in_other = mix_mine[:, :cut_in], mix_other[:, :cut_in]
     out_mine, out_other = mix_mine[:, cut_in:cut_out], mix_other[:, cut_in:cut_out]
-    small_mine = mix_mine[:, cut_out:].reshape(n_z, n_seq, own, LANES)[:, :, :5, :own]
-    small_other = mix_other[:, cut_out:].reshape(n_z, n_seq, own, LANES)[:, :, :5, :own]
-    small_all = jnp.stack(
-        [
-            jnp.where(first_core, small_mine, small_other),
-            jnp.where(first_core, small_other, small_mine),
-        ],
-        1,
-    )
-    small_all = small_all.transpose(3, 0, 1, 2, 4).reshape(5, width).astype(f32)
-    taps, gain_vals = small_all[:3], small_all[3:]
-
-    residual = inputs.reshape(rows, width).astype(f32)
+
+    half = width // 2
+    feature = lax.broadcasted_iota(jnp.int32, (1, width), 1)
+    lane_of = lax.broadcasted_iota(jnp.int32, (LANES, width), 0)
+    spread = (lane_of == feature % own).astype(bf16)
+
+    def row_blocks(which):
+        row = lax.broadcasted_iota(jnp.int32, (half, 1), 0) // own
+        return ((row // n_seq) * 2 + which) * n_seq + row % n_seq
+
+    def small_rows(packed, which):
+        wide = jnp.where(row_blocks(which) == feature // own, dot(packed, spread), 0.0)
+        chosen = lax.broadcasted_iota(jnp.int32, (8, half), 1) % own
+        chosen = chosen == lax.broadcasted_iota(jnp.int32, (8, half), 0)
+        return dot(chosen.astype(bf16), wide.astype(bf16))
+
+    small_all = small_rows(mix_mine[:, cut_out:], core) + small_rows(
+        mix_other[:, cut_out:], 1 - core
+    )
+    taps, gain_vals = small_all[:3], small_all[3:5]
+
+    residual = residual_low.astype(f32)
     unit_one, scale_one, norm_one = normed(residual, gain_vals[0])
+    edge_rows = jnp.pad(edge[:, :, :width].reshape(2 * seqs_here, width), ((0, 12), (0, 0)))
+    edge_mine, edge_other = halves(normed(edge_rows.astype(f32), gain_vals[0])[2])
+
+    def edge_dot(start):
+        stop = start + width
+        return dot(edge_mine, in_mine[:, start:stop]) + dot(edge_other, in_other[:, start:stop])
+
+    prev_rows = (edge_dot(0) * edge_dot(2 * width)).astype(bf16)[: 2 * seqs_here]
+    prev_rows = prev_rows.reshape(seqs_here, 2, width)
+    first_block = sq == 0
+    prev_ids = jnp.where(first_block, -1, edge[:, :, width].astype(jnp.int32))
     norm_mine, norm_other = halves(norm_one)
     projected = dot(norm_mine, in_mine) + dot(norm_other, in_other)
     b_gate = projected[:, :width]
     c_gate = projected[:, width : 2 * width]
     x_part = projected[:, 2 * width :]
     conv_in = (b_gate * x_part).astype(bf16).reshape(seqs_here, stretch, width)
-    edge_ids = jnp.pad(segments[:, -2:, None].astype(bf16), ((0, 0), (0, 0), (0, LANES - 1)))
-    edge = from_behind(jnp.concatenate([conv_in[:, -2:, :], edge_ids], 2), "seq", 1)
-    prev_rows, prev_ids = edge[:, :, :width], edge[:, :, width]
     extended = jnp.concatenate([prev_rows, conv_in], 1).astype(f32)
-    ext_ids = jnp.concatenate([prev_ids.astype(jnp.int32), segments], 1)
+    ext_ids = jnp.concatenate([prev_ids, segments], 1)
     near_one = (ext_ids[:, 1:-1] == segments).astype(f32)[..., None]
     near_two = (ext_ids[:, :-2] == segments).astype(f32)[..., None]
     tap_now = extended[:, 2:]
@@ -211,11 +253,27 @@
     middle = residual + dot(mixed_mine, out_mine) + dot(mixed_other, out_other)
     unit_two, scale_two, norm_two = normed(middle, gain_vals[1])
 
-    norms = {k: across_seq(norm_two, k) for k in range(last, 0, -1)}
+    shape = (n_z, 2, half // n_z)
+    in_full = place(
+        [in_mine.reshape(n_z, -1, cut_in), in_other.reshape(n_z, -1, cut_in)],
+        core_slots,
+        shape + (cut_in,),
+        1,
+    ).reshape(width, cut_in)
+    out_full = place(
+        [out_mine.reshape(n_z, -1, width), out_other.reshape(n_z, -1, width)],
+        core_slots,
+        shape + (width,),
+        1,
+    ).reshape(width, width)
+
+    norm_two, tops = tie((norm_two, tops))
+    tops[0] = grad_top
+    norms = {k: across_seq(norm_two, k) for k in order[1:]}
     norms[0] = norm_two
-    order = [0] + list(range(last, 0, -1))
-    hiddens, act_grads, norm_parts = {}, {}, {}
-    for k in order:
+    hiddens, act_grads, norm_parts, out_parts = {}, {}, {}, {}
+
+    def hidden_block(k):
         both = dot(norms[k], mat_gate_up)
         gate, up_part = both[:, :ff_part], both[:, ff_part:]
         sigma = jax.nn.sigmoid(gate)
@@ -225,33 +283,48 @@
         grad_gate_act = (grad_hidden * up_part * sigma * (1.0 + gate * (1.0 - sigma))).astype(bf16)
         grad_up_act = (grad_hidden * silu_vals).astype(bf16)
         act_grads[k] = jnp.concatenate([grad_gate_act, grad_up_act], 1)
-        norm_parts[k] = right_contract(act_grads[k], mat_gate_up)
-    norm_sums = {k: across_seq(norm_parts[k].astype(bf16), k) for k in order[1:]}
+
+    hidden_block(0)
+    norms[last], hiddens[0], act_grads[0], in_full, out_full = tie(
+        (norms[last], hiddens[0], act_grads[0], in_full, out_full)
+    )
+    hidden_block(last)
+    norm_parts[last] = right_contract(act_grads[last], mat_gate_up).astype(bf16)
+    out_parts[0] = dot(hiddens[0], mat_down)
+    norm_parts[0] = right_contract(act_grads[0], mat_gate_up)
+    norm_sums = {last: across_seq(norm_parts[last], last)}
+    for k in order[2:]:
+        norms[k], norm_parts, out_parts, act_grads = tie(
+            (norms[k], norm_parts, out_parts, act_grads)
+        )
+        hidden_block(k)
+        if k == order[-1]:
+            act_grads, norm_sums[last] = tie((act_grads, norm_sums[last]))
+        norm_parts[k] = right_contract(act_grads[k], mat_gate_up).astype(bf16)
+        norm_sums[k] = across_seq(norm_parts[k], k)
+    norm_parts, hiddens, act_grads = tie((norm_parts, hiddens, act_grads))
 
     def rows_of(blocks):
         return jnp.concatenate([blocks[k] for k in order], 0)
 
     grad_down = left_contract(rows_of(hiddens), rows_of(tops)).astype(bf16)
+    sum_down = lax.psum_scatter(grad_down, "dp", scatter_dimension=0, tiled=True).astype(f32)
+    hiddens, grad_down = tie((hiddens, grad_down))
     grad_gate_up = left_contract(rows_of(norms), rows_of(act_grads)).astype(bf16)
-    sum_down = lax.psum_scatter(grad_down, "dp", scatter_dimension=0, tiled=True).astype(f32)
     gu_sum = lax.psum_scatter(grad_gate_up, "dp", scatter_dimension=0, tiled=True)
-    out_parts = {k: dot(hiddens[k], mat_down) for k in order}
-    norm_sums, out_low = tie((norm_sums, {k: out_parts[k].astype(bf16) for k in order[1:]}))
+    hiddens, grad_gate_up = tie((hiddens, grad_gate_up))
+    out_low = {k: dot(hiddens[k], mat_down).astype(bf16) for k in order[1:]}
+    norm_sums, out_low = tie((norm_sums, out_low))
     grad_norm_two = norm_parts[0]
-    output = middle + out_parts[0]
     for k in order[1:]:
         grad_norm_two = grad_norm_two + norm_sums[k].astype(f32)
-        output = output + across_seq(out_low[k], k).astype(f32)
-    output = output.astype(bf16)
 
     back_two, gain_two = norm_back(grad_norm_two, unit_two, scale_two, gain_vals[1])
     grad_middle = grad_top.astype(f32) + back_two
     grad_branch = grad_middle.astype(bf16)
     grad_out_mine = left_contract(mixed_mine, grad_branch)
     grad_out_other = left_contract(mixed_other, grad_branch)
-    grad_mixed = joined(
-        right_contract(grad_branch, out_mine), right_contract(grad_branch, out_other)
-    )
+    grad_mixed = right_contract(grad_branch, out_full)
     grad_c = grad_mixed * conv_out
     grad_conv = (grad_mixed * c_gate).reshape(seqs_here, stretch, width)
     grad_taps = [
@@ -268,6 +341,8 @@
         + jnp.pad(term_two, ((0, 0), (0, 2), (0, 0)))
     )
     next_terms = from_behind(grad_ext[:, :2, :], "seq", -1)
+    next_terms, out_low[last] = tie((next_terms, out_low[last]))
+    out_sums = {last: across_seq(out_low[last], last)}
     grad_conv_in = (
         grad_ext[:, 2:, :] + jnp.pad(next_terms, ((0, 0), (stretch - 2, 0), (0, 0)))
     ).reshape(rows, width)
@@ -276,7 +351,7 @@
     )
     grad_in_mine = left_contract(norm_mine, grad_proj)
     grad_in_other = left_contract(norm_other, grad_proj)
-    grad_norm_one = joined(right_contract(grad_proj, in_mine), right_contract(grad_proj, in_other))
+    grad_norm_one = right_contract(grad_proj, in_full)
     back_one, gain_one = norm_back(grad_norm_one, unit_one, scale_one, gain_vals[0])
     input_grad = (grad_middle + back_one).reshape(seqs_here, stretch, width)
 
@@ -284,38 +359,45 @@
         return mine + to_sibling(other.astype(bf16)).astype(f32)
 
     small_grads = jnp.stack(grad_taps + [gain_one, gain_two], 0)
-    small_grads = small_grads.reshape(5, n_z, 2, n_seq, own).transpose(2, 1, 3, 0, 4)
-    small_grads = jnp.pad(
-        small_grads, ((0, 0), (0, 0), (0, 0), (0, own - 5), (0, LANES - own))
-    ).reshape(2, width // 2, LANES)
+    small_grads = (small_grads + to_sibling(small_grads)).astype(bf16)
+    small_wide = jnp.tile(jnp.pad(small_grads, ((0, own - 5), (0, 0))), (half // own, 1))
+    small_wide = jnp.where(row_blocks(core) == feature // own, small_wide, 0.0).astype(bf16)
     mixed = jnp.concatenate(
         [
             sum_core(grad_in_mine, grad_in_other),
             sum_core(grad_out_mine, grad_out_other),
-            sum_core(pick(small_grads, core), pick(small_grads, 1 - core)),
+            right_contract(small_wide, spread),
         ],
         1,
     ).astype(bf16)
+    mixed, out_sums, sum_down = tie((mixed, out_sums, sum_down))
     mixed = mixed.reshape(n_z, n_seq, own, -1)
 
     def seq_block(index):
         return lax.dynamic_index_in_dim(mixed, index, 1, keepdims=False)
 
-    seq_parts = [across_seq(seq_block(sq ^ k), k) for k in range(n_seq - 1, 0, -1)]
+    seq_parts = [across_seq(seq_block(sq ^ k), k) for k in order[1:]]
+    seq_parts, gu_sum, out_low = tie((seq_parts, gu_sum, out_low))
     total = seq_block(sq).astype(f32)
     for part in seq_parts:
         total = total + part.astype(f32)
     low = total.astype(bf16)
     z_sums = [along_z(pick(low, (z + k) % n_z), k) for k in range(1, n_z)]
+    gu_sum = gu_sum.reshape(n_seq, own, 2 * ff_part)
+    gu_parts = [across_seq(pick(gu_sum, sq ^ k), k) for k in range(1, n_seq)]
+    for k in order[2:]:
+        out_sums[k] = across_seq(out_low[k], k)
+    z_sums, gu_parts = tie((z_sums, gu_parts))
     total = pick(total, z)
     for part in z_sums:
         total = total + part.astype(f32)
     sum_in, sum_out, small_sum = total[:, :cut_in], total[:, cut_in:cut_out], total[:, cut_out:]
 
-    gu_sum = gu_sum.reshape(n_seq, own, 2 * ff_part)
-    gu_sum = seq_ordered(
-        [pick(gu_sum, sq)] + [across_seq(pick(gu_sum, sq ^ k), k) for k in range(1, n_seq)]
-    ).astype(f32)
+    gu_sum = seq_ordered([pick(gu_sum, sq)] + gu_parts).astype(f32)
+    output = middle + out_parts[0]
+    for k in order[1:]:
+        output = output + out_sums[k].astype(f32)
+    output = output.astype(bf16)
 
     def by_row(part):
         return (

time: 501 us -> 846 us (1.69)
  Pallas kernels: 0 us -> 425 us
  waiting for transfers between devices: 198 us -> 132 us
    pallas_call x0 -> x4, Pallas kernels: none -> 425 us  [place(): pl.pallas_call(kernel, out_shape=jax.ShapeDtypeStruct(shape, blocks[0].dt...]
    ppermute x24, waiting for transfers between devices: 156 us -> 115 us  [across_seq(): lax.ppermute(block, 'seq', [(i, i ^ by) for i in range(lax.axis_size('seq...]
    ppermute x6, waiting for transfers between devices: 36.1 us -> 11.5 us  [along_z(): lax.ppermute(block, 'dp', [(i, (i + 2 * by) % count) for i in range(count)])]
    dot_general x12 -> x11, matrix products: 52.5 us -> 39.2 us  [right_contract(): lax.dot_general(first, second, (((1,), (1,)), ((), ())), preferred_elemen...]
    dot_general x12 -> x18, matrix products: 44.8 us -> 58 us  [dot(): return jnp.dot(first, second, preferred_element_type=f32)]
    unnamed x281 -> x241, local copies, waits for them, and re-layouts: 22.3 us -> 10.5 us
    slice x8 -> x6, local copies, waits for them, and re-layouts: 3.59 us -> 12.3 us  [the longest x2 7.63 us: local(): in_mine, in_other = (mix_mine[:, :cut_in], mix_other[:, :cut_in])]
  transfers between devices with their start and end apart: 40 -> 40, of which waited for: 21 -> 17; matrix products, arithmetic and copies ran while one was open for 38% -> 22% of each run, Pallas kernels for 0% -> 51%
where the time goes in v3:
time: 846 us; the launch traced here: 840 us
  Pallas kernels  425 us (50%)
  matrix products  135 us (16%)
  waiting for transfers between devices  132 us (16%)
  other arithmetic  48.7 us (6%)
  starting transfers between devices  45.5 us (5%)
  local copies, waits for them, and re-layouts  37.4 us (4%)
  between operations  16.1 us (2%)
    pallas_call x4, Pallas kernels, place(): pl.pallas_call(kernel, out_shape=jax.ShapeDtypeStruct(shape, blocks[0].dt...  425 us
    ppermute x24, waiting for transfers between devices, across_seq(): lax.ppermute(block, 'seq', [(i, i ^ by) for i in range(lax.axis_size('seq...  115 us
    dot_general x18, matrix products, dot(): return jnp.dot(first, second, preferred_element_type=f32)  58 us
    dot_general x11, matrix products, right_contract(): lax.dot_general(first, second, (((1,), (1,)), ((), ())), preferred_elemen...  39.2 us
    dot_general x6, matrix products, left_contract(): lax.dot_general(first, second, (((0,), (0,)), ((), ())), preferred_elemen...  37.8 us
    ppermute x24, starting transfers between devices, across_seq(): lax.ppermute(block, 'seq', [(i, i ^ by) for i in range(lax.axis_size('seq...  30.4 us
  transfers between devices with their start and end apart: 40, of which 17 were waited for; matrix products, arithmetic and copies ran while one was open for 22% of the time, Pallas kernels for 51%

profile of v3, /device:TPU:8, one launch (start us, length us, event | category | flops | bytes accessed | tf_op | source)
XLA Modules:
  0.0 840.2 jit_solution(231837353772715758)
XLA Ops:
  25.9 4.2 collective-permute-start.4
  38.2 34.6 %shard_map.407.refs_0_ = bf16[4,32,4224]{2,1,0:T(8,128)(2,1)} custom-call(s32[4]{0:T(128)} %and_select_fusion.slots_ref, bf16[32,4224]{1,0:T(8,128)(2,1)} %copy-done.24, bf16[32,4224]{1,0:T(8,128)(2,1)} %collective-permute-done.refs_1_, bf16[32,4224]{1,0:T(8,128)(2,1)} %collective-permute-done.1.refs_2_, bf16[32,4224]{1,0:T(8,128)(2,1)} %collective-permute-done.2.refs_3_), custom_call_target="tpu_custom_call" | custom-call | bytes 2162688 | tf_op jit(solution)/shard_map/pallas_call | solution.py:76
  76.9 23.0 %collective-permute-done.7.refs_1_ = bf16[4,32,4224]{2,1,0:T(8,128)(2,1)S(1)} collective-permute-done((bf16[4,32,4224]{2,1,0:T(8,128)(2,1)}, bf16[4,32,4224]{2,1,0:T(8,128)(2,1)S(1)}, u32[]{:S(2)}, u32[]{:S(2)}) %collective-permute-start.7) | collective-permute-done | bytes 1081376 | tf_op jit(solution)/shard_map/ppermute | solution.py:39
  99.9 22.6 %collective-permute-done.8.refs_2_ = bf16[4,32,4224]{2,1,0:T(8,128)(2,1)S(1)} collective-permute-done((bf16[4,32,4224]{2,1,0:T(8,128)(2,1)}, bf16[4,32,4224]{2,1,0:T(8,128)(2,1)S(1)}, u32[]{:S(2)}, u32[]{:S(2)}) %collective-permute-start.8) | collective-permute-done | bytes 1081376 | tf_op jit(solution)/shard_map/ppermute | solution.py:39
  123.4 132.8 %shard_map.408 = bf16[4,4,32,4224]{3,2,1,0:T(8,128)(2,1)} custom-call(s32[4]{0:T(128)} %iota_xor_fusion.1.slots_ref, bf16[4,32,4224]{2,1,0:T(8,128)(2,1)} %shard_map.407.refs_0_, bf16[4,32,4224]{2,1,0:T(8,128)(2,1)} %copy-done.22, bf16[4,32,4224]{2,1,0:T(8,128)(2,1)} %copy-done.23, bf16[4,32,4224]{2,1,0:T(8,128)(2,1)} %collective-permute-done.9.refs_3_), custom_call_target="tpu_custom_call" | custom-call | bytes 8650752 | tf_op jit(solution)/shard_map/pallas_call | solution.py:76
  261.7 3.8 slice.305
  274.6 6.7 fusion.93
  284.5 5.6 convolution_add_fusion
  301.4 4.5 collective-permute-done.12
  311.0 3.8 slice.306
  314.8 192.4 %shard_map.409 = bf16[4,2,128,3072]{3,2,1,0:T(8,128)(2,1)} custom-call(s32[2]{0:T(128)} %iota_xor_fusion.slots_ref, bf16[4,128,3072]{2,1,0:T(8,128)(2,1)} %bitcast.176, bf16[4,128,3072]{2,1,0:T(8,128)(2,1)} %bitcast.177), custom_call_target="tpu_custom_call" | custom-call | bytes 12582912 | tf_op jit(solution)/shard_map/pallas_call | solution.py:76
  509.4 65.3 %shard_map.410 = bf16[4,2,128,1024]{3,2,1,0:T(8,128)(2,1)} custom-call(s32[2]{0:T(128)} %iota_xor_fusion.slots_ref, bf16[4,128,1024]{2,1,0:T(8,128)(2,1)} %bitcast.184, bf16[4,128,1024]{2,1,0:T(8,128)(2,1)} %bitcast.185), custom_call_target="tpu_custom_call" | custom-call | bytes 4194304 | tf_op jit(solution)/shard_map/pallas_call | solution.py:76
  574.8 7.6 fusion.170
  582.4 5.4 multiply_convert_fusion.10
  591.0 4.0 fusion.172
  607.6 3.9 fusion.171
  611.6 4.1 fusion.174
  624.5 3.9 fusion.175
  628.4 3.6 multiply_convert_fusion.4
  635.9 8.9 %fusion.33 = bf16[1152,1024]{1,0:T(8,128)(2,1)} fusion(bf16[512,1024]{1,0:T(8,128)(2,1)} %collective-permute-done.11, bf16[512,1024]{1,0:T(8,128)(2,1)} %collective-permute-done.12, bf16[512,1024]{1,0:T(8,128)(2,1)} %collective-permute-done.13, bf16[512,1024]{1,0:T(8,128)(2,1)S(1)} %bitcast.196, bf16[512,1152]{1,0:T(8,128)(2,1)S(1)} %get-tuple-element.145, ...), kind=kOutput, calls=%fused_computation.35 | convolution fusion | flops 4868669440 | bytes 11272192 | tf_op jit(solution)/shard_map/dot_general | solution.py:47
  646.7 16.5 %fusion.8 = bf16[1024,2304]{1,0:T(8,128)(2,1)} fusion(bf16[512,2304]{1,0:T(8,128)(2,1)} %copy-done.12, bf16[512,2304]{1,0:T(8,128)(2,1)} %pad_maximum_fusion.4, bf16[512,2304]{1,0:T(8,128)(2,1)} %pad_maximum_fusion.3, bf16[512,2304]{1,0:T(8,128)(2,1)} %copy-done.11, bf16[512,1024]{1,0:T(8,128)(2,1)} %collective-permute-done.14, ...), kind=kOutput, calls=%fused_computation.9 | convolution fusion | flops 9720561664 | bytes 18350080 | tf_op jit(solution)/shard_map/dot_general | solution.py:47
  663.3 4.8 convolution_convert_fusion.1
  694.1 5.6 fusion.55
  707.3 4.8 add_convert_fusion
  716.2 11.9 %collective-permute-done.24 = bf16[512,1024]{1,0:T(8,128)(2,1)} collective-permute-done((bf16[512,1024]{1,0:T(8,128)(2,1)}, bf16[512,1024]{1,0:T(8,128)(2,1)}, u32[]{:S(2)}, u32[]{:S(2)}) %collective-permute-start.24) | collective-permute-done | bytes 1048608 | tf_op jit(solution)/shard_map/ppermute | solution.py:39
  728.1 3.7 dynamic-slice_bitcast_fusion
  738.7 21.1 %collective-permute-done.25 = bf16[4,32,4224]{2,1,0:T(8,128)(2,1)} collective-permute-done((bf16[4,32,4224]{2,1,0:T(8,128)(2,1)}, bf16[4,32,4224]{2,1,0:T(8,128)(2,1)}, u32[]{:S(2)}, u32[]{:S(2)}) %collective-permute-start.25) | collective-permute-done | bytes 1081376 | tf_op jit(solution)/shard_map/ppermute | solution.py:39
  759.8 21.8 %collective-permute-done.26 = bf16[4,32,4224]{2,1,0:T(8,128)(2,1)} collective-permute-done((bf16[4,32,4224]{2,1,0:T(8,128)(2,1)}, bf16[4,32,4224]{2,1,0:T(8,128)(2,1)}, u32[]{:S(2)}, u32[]{:S(2)}) %collective-permute-start.26) | collective-permute-done | bytes 1081376 | tf_op jit(solution)/shard_map/ppermute | solution.py:39
  784.0 4.2 fusion.163
  803.4 6.0 collective-permute-done.30
  809.4 4.2 collective-permute-done.31
  829.7 3.7 add_convert_fusion.1
  (434 shorter events, 175.2 us)
Async XLA Ops:
  7.2 567.5 %all-gather.6.cloned.1.call-start = ((), (), s32[]{:S(2)}) async-start(), calls=%async_computation.5 | async-start | bytes 5308416 | tf_op jit(solution)/shard_map/all_gather | solution.py:178
  10.6 25.5 %collective-permute-start = (bf16[32,4224]{1,0:T(8,128)(2,1)S(1)}, bf16[32,4224]{1,0:T(8,128)(2,1)}, u32[]{:S(2)}, u32[]{:S(2)}) collective-permute-start(bf16[32,4224]{1,0:T(8,128)(2,1)S(1)} %pad_maximum_fusion.13.refs_0_), channel_id=1, source_target_pairs={{0,24},{4,28},{8,0},{12,4},{16,8},{20,12},{24,16},{28,20},{1,25},{... | collective-permute-start | bytes 811016 | tf_op jit(solution)/shard_map/ppermute | solution.py:35
  10.7 25.5 %collective-permute-start.1 = (bf16[32,4224]{1,0:T(8,128)(2,1)S(1)}, bf16[32,4224]{1,0:T(8,128)(2,1)}, u32[]{:S(2)}, u32[]{:S(2)}) collective-permute-start(bf16[32,4224]{1,0:T(8,128)(2,1)S(1)} %pad_maximum_fusion.13.refs_0_), channel_id=1, source_target_pairs={{0,16},{4,20},{8,24},{12,28},{16,0},{20,4},{24,8},{28,12},{1,17},{... | collective-permute-start | bytes 811016 | tf_op jit(solution)/shard_map/ppermute | solution.py:35
  13.7 22.9 %collective-permute-start.2 = (bf16[32,4224]{1,0:T(8,128)(2,1)S(1)}, bf16[32,4224]{1,0:T(8,128)(2,1)}, u32[]{:S(2)}, u32[]{:S(2)}) collective-permute-start(bf16[32,4224]{1,0:T(8,128)(2,1)S(1)} %pad_maximum_fusion.13.refs_0_), channel_id=1, source_target_pairs={{0,8},{4,12},{8,16},{12,20},{16,24},{20,28},{24,0},{28,4},{1,9},{5... | collective-permute-start | bytes 811016 | tf_op jit(solution)/shard_map/ppermute | solution.py:35
  37.6 544.8 %all-gather.4.cloned.1.call-start = ((), (), s32[]{:S(2)}) async-start(), calls=%async_computation.2 | async-start | bytes 2654208 | tf_op jit(solution)/shard_map/all_gather | solution.py:179
  72.8 27.1 %collective-permute-start.7 = (bf16[4,32,4224]{2,1,0:T(8,128)(2,1)}, bf16[4,32,4224]{2,1,0:T(8,128)(2,1)S(1)}, u32[]{:S(2)}, u32[]{:S(2)}) collective-permute-start(bf16[4,32,4224]{2,1,0:T(8,128)(2,1)} %shard_map.407.refs_0_), channel_id=1, source_target_pairs={{0,1},{1,0},{2,3},{3,2},{4,5},{5,4},{6,7},{7,6},{8,9},{9,8},{10,11... | collective-permute-start | bytes 3244040 | tf_op jit(solution)/shard_map/ppermute | solution.py:39
  74.3 48.1 %collective-permute-start.8 = (bf16[4,32,4224]{2,1,0:T(8,128)(2,1)}, bf16[4,32,4224]{2,1,0:T(8,128)(2,1)S(1)}, u32[]{:S(2)}, u32[]{:S(2)}) collective-permute-start(bf16[4,32,4224]{2,1,0:T(8,128)(2,1)} %shard_map.407.refs_0_), channel_id=1, source_target_pairs={{0,2},{1,3},{2,0},{3,1},{4,6},{5,7},{6,4},{7,5},{8,10},{9,11},{10,... | collective-permute-start | bytes 3244040 | tf_op jit(solution)/shard_map/ppermute | solution.py:39
  75.9 46.6 %collective-permute-start.9 = (bf16[4,32,4224]{2,1,0:T(8,128)(2,1)}, bf16[4,32,4224]{2,1,0:T(8,128)(2,1)}, u32[]{:S(2)}, u32[]{:S(2)}) collective-permute-start(bf16[4,32,4224]{2,1,0:T(8,128)(2,1)} %shard_map.407.refs_0_), channel_id=1, source_target_pairs={{0,3},{1,2},{2,1},{3,0},{4,7},{5,6},{6,5},{7,4},{8,11},{9,10},{10,... | collective-permute-start | bytes 3244040 | tf_op jit(solution)/shard_map/ppermute | solution.py:39
  256.3 13.2 %collective-permute-start.10 = (bf16[512,4224]{1,0:T(8,128)(2,1)}, bf16[512,4224]{1,0:T(8,128)(2,1)}, u32[]{:S(2)}, u32[]{:S(2)}) collective-permute-start(bf16[512,4224]{1,0:T(8,128)(2,1)} %bitcast.168), channel_id=1, source_target_pairs={{0,4},{4,0},{8,12},{12,8},{16,20},{20,16},{24,28},{28,24},{1,5},{5... | collective-permute-start | bytes 12976136 | tf_op jit(solution)/shard_map/ppermute | solution.py:30
  257.3 457.1 %reduce-scatter.3.cloned.1.call-start = ((), (), s32[]{:S(2)}) async-start(), calls=%async_computation.3 | async-start | bytes 2654208 | tf_op jit(solution)/shard_map/reduce_scatter | solution.py:311
  258.2 43.2 %collective-permute-start.11 = (bf16[512,1024]{1,0:T(8,128)(2,1)}, bf16[512,1024]{1,0:T(8,128)(2,1)}, u32[]{:S(2)}, u32[]{:S(2)}) collective-permute-start(bf16[512,1024]{1,0:T(8,128)(2,1)} %bitcast.192), channel_id=1, source_target_pairs={{0,1},{1,0},{2,3},{3,2},{4,5},{5,4},{6,7},{7,6},{8,9},{9,8},{10,11... | collective-permute-start | bytes 3145736 | tf_op jit(solution)/shard_map/ppermute | solution.py:39
  258.6 47.3 %collective-permute-start.12 = (bf16[512,1024]{1,0:T(8,128)(2,1)}, bf16[512,1024]{1,0:T(8,128)(2,1)}, u32[]{:S(2)}, u32[]{:S(2)}) collective-permute-start(bf16[512,1024]{1,0:T(8,128)(2,1)} %bitcast.193), channel_id=1, source_target_pairs={{0,2},{1,3},{2,0},{3,1},{4,6},{5,7},{6,4},{7,5},{8,10},{9,11},{10,... | collective-permute-start | bytes 3145736 | tf_op jit(solution)/shard_map/ppermute | solution.py:39
  260.2 47.2 %collective-permute-start.13 = (bf16[512,1024]{1,0:T(8,128)(2,1)}, bf16[512,1024]{1,0:T(8,128)(2,1)}, u32[]{:S(2)}, u32[]{:S(2)}) collective-permute-start(bf16[512,1024]{1,0:T(8,128)(2,1)} %bitcast.194), channel_id=1, source_target_pairs={{0,3},{1,2},{2,1},{3,0},{4,7},{5,6},{6,5},{7,4},{8,11},{9,10},{10,... | collective-permute-start | bytes 3145736 | tf_op jit(solution)/shard_map/ppermute | solution.py:39
  307.5 280.5 %collective-permute-start.16 = (bf16[512,1024]{1,0:T(8,128)(2,1)}, bf16[512,1024]{1,0:T(8,128)(2,1)}, u32[]{:S(2)}, u32[]{:S(2)}) collective-permute-start(bf16[512,1024]{1,0:T(8,128)(2,1)} %multiply_convert_fusion.12), channel_id=1, source_target_pairs={{0,3},{1,2},{2,1},{3,0},{4,7},{5,6},{6,5},{7,4},{8,11},{9,10},{10,... | collective-permute-start | bytes 3145736 | tf_op jit(solution)/shard_map/ppermute | solution.py:39
  309.2 302.4 %collective-permute-start.15 = (bf16[512,1024]{1,0:T(8,128)(2,1)}, bf16[512,1024]{1,0:T(8,128)(2,1)}, u32[]{:S(2)}, u32[]{:S(2)}) collective-permute-start(bf16[512,1024]{1,0:T(8,128)(2,1)} %multiply_convert_fusion.12), channel_id=1, source_target_pairs={{0,2},{1,3},{2,0},{3,1},{4,6},{5,7},{6,4},{7,5},{8,10},{9,11},{10,... | collective-permute-start | bytes 3145736 | tf_op jit(solution)/shard_map/ppermute | solution.py:39
  309.7 314.8 %collective-permute-start.14 = (bf16[512,1024]{1,0:T(8,128)(2,1)}, bf16[512,1024]{1,0:T(8,128)(2,1)}, u32[]{:S(2)}, u32[]{:S(2)}) collective-permute-start(bf16[512,1024]{1,0:T(8,128)(2,1)} %multiply_convert_fusion.12), channel_id=1, source_target_pairs={{0,1},{1,0},{2,3},{3,2},{4,5},{5,4},{6,7},{7,6},{8,9},{9,8},{10,11... | collective-permute-start | bytes 3145736 | tf_op jit(solution)/shard_map/ppermute | solution.py:39
  602.9 29.3 %collective-permute-start.17 = (bf16[512,1024]{1,0:T(8,128)(2,1)S(1)}, bf16[512,1024]{1,0:T(8,128)(2,1)S(1)}, u32[]{:S(2)}, u32[]{:S(2)}) collective-permute-start(bf16[512,1024]{1,0:T(8,128)(2,1)S(1)} %convolution_convert_fusion.6), channel_id=1, source_target_pairs={{0,3},{1,2},{2,1},{3,0},{4,7},{5,6},{6,5},{7,4},{8,11},{9,10},{10,... | collective-permute-start | bytes 3145736 | tf_op jit(solution)/shard_map/ppermute | solution.py:39
  644.8 136.8 %reduce-scatter.5.cloned.1.call-start = ((), (), s32[]{:S(2)}) async-start(), calls=%async_computation.4 | async-start | bytes 5308416 | tf_op jit(solution)/shard_map/reduce_scatter | solution.py:314
  644.9 28.3 %collective-permute-start.19 = (bf16[512,1024]{1,0:T(8,128)(2,1)}, bf16[512,1024]{1,0:T(8,128)(2,1)}, u32[]{:S(2)}, u32[]{:S(2)}) collective-permute-start(bf16[512,1024]{1,0:T(8,128)(2,1)} %convolution_convert_fusion.5), channel_id=1, source_target_pairs={{0,2},{1,3},{2,0},{3,1},{4,6},{5,7},{6,4},{7,5},{8,10},{9,11},{10,... | collective-permute-start | bytes 3145736 | tf_op jit(solution)/shard_map/ppermute | solution.py:39
  645.5 27.7 %collective-permute-start.18 = (bf16[512,1024]{1,0:T(8,128)(2,1)}, bf16[512,1024]{1,0:T(8,128)(2,1)}, u32[]{:S(2)}, u32[]{:S(2)}) collective-permute-start(bf16[512,1024]{1,0:T(8,128)(2,1)} %convolution_convert_fusion.4), channel_id=1, source_target_pairs={{0,1},{1,0},{2,3},{3,2},{4,5},{5,4},{6,7},{7,6},{8,9},{9,8},{10,11... | collective-permute-start | bytes 3145736 | tf_op jit(solution)/shard_map/ppermute | solution.py:39
  691.6 15.6 %collective-permute-start.21 = (bf16[512,3072]{1,0:T(8,128)(2,1)}, bf16[512,3072]{1,0:T(8,128)(2,1)}, u32[]{:S(2)}, u32[]{:S(2)}) collective-permute-start(bf16[512,3072]{1,0:T(8,128)(2,1)} %convolution_convert_fusion), channel_id=1, source_target_pairs={{0,4},{4,0},{8,12},{12,8},{16,20},{20,16},{24,28},{28,24},{1,5},{5... | collective-permute-start | bytes 9437192 | tf_op jit(solution)/shard_map/ppermute | solution.py:30
  693.6 11.4 %collective-permute-start.22 = (bf16[512,1024]{1,0:T(8,128)(2,1)}, bf16[512,1024]{1,0:T(8,128)(2,1)}, u32[]{:S(2)}, u32[]{:S(2)}) collective-permute-start(bf16[512,1024]{1,0:T(8,128)(2,1)} %convolution_convert_fusion.7), channel_id=1, source_target_pairs={{0,4},{4,0},{8,12},{12,8},{16,20},{20,16},{24,28},{28,24},{1,5},{5... | collective-permute-start | bytes 3145736 | tf_op jit(solution)/shard_map/ppermute | solution.py:30
  701.3 26.8 %collective-permute-start.24 = (bf16[512,1024]{1,0:T(8,128)(2,1)}, bf16[512,1024]{1,0:T(8,128)(2,1)}, u32[]{:S(2)}, u32[]{:S(2)}) collective-permute-start(bf16[512,1024]{1,0:T(8,128)(2,1)} %convolution_convert_fusion.1), channel_id=1, source_target_pairs={{0,3},{1,2},{2,1},{3,0},{4,7},{5,6},{6,5},{7,4},{8,11},{9,10},{10,... | collective-permute-start | bytes 3145736 | tf_op jit(solution)/shard_map/ppermute | solution.py:39
  731.8 28.0 %collective-permute-start.25 = (bf16[4,32,4224]{2,1,0:T(8,128)(2,1)}, bf16[4,32,4224]{2,1,0:T(8,128)(2,1)}, u32[]{:S(2)}, u32[]{:S(2)}) collective-permute-start(bf16[4,32,4224]{2,1,0:T(8,128)(2,1)} %get-tuple-element.221), channel_id=1, source_target_pairs={{0,3},{1,2},{2,1},{3,0},{4,7},{5,6},{6,5},{7,4},{8,11},{9,10},{10,... | collective-permute-start | bytes 3244040 | tf_op jit(solution)/shard_map/ppermute | solution.py:39
  732.1 49.5 %collective-permute-start.26 = (bf16[4,32,4224]{2,1,0:T(8,128)(2,1)}, bf16[4,32,4224]{2,1,0:T(8,128)(2,1)}, u32[]{:S(2)}, u32[]{:S(2)}) collective-permute-start(bf16[4,32,4224]{2,1,0:T(8,128)(2,1)} %get-tuple-element.220), channel_id=1, source_target_pairs={{0,2},{1,3},{2,0},{3,1},{4,6},{5,7},{6,4},{7,5},{8,10},{9,11},{10,... | collective-permute-start | bytes 3244040 | tf_op jit(solution)/shard_map/ppermute | solution.py:39
  734.9 46.7 %collective-permute-start.27 = (bf16[4,32,4224]{2,1,0:T(8,128)(2,1)}, bf16[4,32,4224]{2,1,0:T(8,128)(2,1)}, u32[]{:S(2)}, u32[]{:S(2)}) collective-permute-start(bf16[4,32,4224]{2,1,0:T(8,128)(2,1)} %get-tuple-element.219), channel_id=1, source_target_pairs={{0,1},{1,0},{2,3},{3,2},{4,5},{5,4},{6,7},{7,6},{8,9},{9,8},{10,11... | collective-permute-start | bytes 3244040 | tf_op jit(solution)/shard_map/ppermute | solution.py:39
  782.8 11.0 %collective-permute-start.33 = (bf16[32,2304]{1,0:T(8,128)(2,1)S(1)}, bf16[32,2304]{1,0:T(8,128)(2,1)S(1)}, u32[]{:S(2)}, u32[]{:S(2)}) collective-permute-start(bf16[32,2304]{1,0:T(8,128)(2,1)S(1)} %get-tuple-element.253), channel_id=1, source_target_pairs={{0,1},{1,0},{2,3},{3,2},{4,5},{5,4},{6,7},{7,6},{8,9},{9,8},{10,11... | collective-permute-start | bytes 442376 | tf_op jit(solution)/shard_map/ppermute | solution.py:39
  788.2 21.2 %collective-permute-start.30 = (bf16[32,4224]{1,0:T(8,128)(2,1)S(1)}, bf16[32,4224]{1,0:T(8,128)(2,1)S(1)}, u32[]{:S(2)}, u32[]{:S(2)}) collective-permute-start(bf16[32,4224]{1,0:T(8,128)(2,1)S(1)} %get-tuple-element.229), channel_id=1, source_target_pairs={{0,8},{4,12},{8,16},{12,20},{16,24},{20,28},{24,0},{28,4},{1,9},{5... | collective-permute-start | bytes 811016 | tf_op jit(solution)/shard_map/ppermute | solution.py:35
  790.9 22.7 %collective-permute-start.31 = (bf16[32,4224]{1,0:T(8,128)(2,1)S(1)}, bf16[32,4224]{1,0:T(8,128)(2,1)S(1)}, u32[]{:S(2)}, u32[]{:S(2)}) collective-permute-start(bf16[32,4224]{1,0:T(8,128)(2,1)S(1)} %get-tuple-element.228), channel_id=1, source_target_pairs={{0,16},{4,20},{8,24},{12,28},{16,0},{20,4},{24,8},{28,12},{1,17},{... | collective-permute-start | bytes 811016 | tf_op jit(solution)/shard_map/ppermute | solution.py:35
  791.6 22.8 %collective-permute-start.32 = (bf16[32,4224]{1,0:T(8,128)(2,1)S(1)}, bf16[32,4224]{1,0:T(8,128)(2,1)S(1)}, u32[]{:S(2)}, u32[]{:S(2)}) collective-permute-start(bf16[32,4224]{1,0:T(8,128)(2,1)S(1)} %get-tuple-element.227), channel_id=1, source_target_pairs={{0,24},{4,28},{8,0},{12,4},{16,8},{20,12},{24,16},{28,20},{1,25},{... | collective-permute-start | bytes 811016 | tf_op jit(solution)/shard_map/ppermute | solution.py:35
  800.3 28.6 %collective-permute-start.28 = (bf16[512,1024]{1,0:T(8,128)(2,1)}, bf16[512,1024]{1,0:T(8,128)(2,1)}, u32[]{:S(2)}, u32[]{:S(2)}) collective-permute-start(bf16[512,1024]{1,0:T(8,128)(2,1)} %convolution_convert_fusion.2), channel_id=1, source_target_pairs={{0,2},{1,3},{2,0},{3,1},{4,6},{5,7},{6,4},{7,5},{8,10},{9,11},{10,... | collective-permute-start | bytes 3145736 | tf_op jit(solution)/shard_map/ppermute | solution.py:39
  801.9 27.0 %collective-permute-start.29 = (bf16[512,1024]{1,0:T(8,128)(2,1)}, bf16[512,1024]{1,0:T(8,128)(2,1)}, u32[]{:S(2)}, u32[]{:S(2)}) collective-permute-start(bf16[512,1024]{1,0:T(8,128)(2,1)} %convolution_convert_fusion.3), channel_id=1, source_target_pairs={{0,1},{1,0},{2,3},{3,2},{4,5},{5,4},{6,7},{7,6},{8,9},{9,8},{10,11... | collective-permute-start | bytes 3145736 | tf_op jit(solution)/shard_map/ppermute | solution.py:39
  (127 other events, 700.2 us)
Sparse Core Ops, SparseCore 0:
  37.8 51.3 all-gather.5
  257.4 31.4 all-gather.3
  645.0 32.4 reduce-scatter.2
  679.7 54.5 reduce-scatter.4

commit v4 on v3

--- a/solution.py
+++ b/solution.py
@@ -59,26 +59,24 @@
     return lax.dynamic_index_in_dim(stacked, index, 0, keepdims=False)
 
 
-def place(blocks, slots, shape, axis):
+def place(blocks, slots, chunk, first=0, columns=None):
+    outer, depth, width = blocks[0].shape
+    columns = width if columns is None else columns
+    count = len(blocks)
+
     def kernel(slots_ref, *refs):
-        sources, out, sems = refs[:-2], refs[-2], refs[-1]
-        copies = []
-        for k, source in enumerate(sources):
-            target = out.at[slots_ref[k]] if axis == 0 else out.at[:, slots_ref[k]]
-            copies.append(pltpu.make_async_copy(source, target, sems.at[k]))
-        for copy in copies:
-            copy.start()
-        for copy in copies:
-            copy.wait()
-
-    anywhere = pl.BlockSpec(memory_space=pl.ANY)
-    size = sum(block.size for block in blocks) * 4
+        for k in range(count):
+            refs[-1][:, slots_ref[k]] = refs[k][...]
+
+    size = 4 * count * outer * depth * columns
     return pl.pallas_call(
         kernel,
-        out_shape=jax.ShapeDtypeStruct(shape, blocks[0].dtype),
-        in_specs=[pl.BlockSpec(memory_space=pltpu.SMEM)] + [anywhere] * len(blocks),
-        out_specs=anywhere,
-        scratch_shapes=[pltpu.SemaphoreType.DMA((len(blocks),))],
+        grid=(columns // chunk,),
+        out_shape=jax.ShapeDtypeStruct((outer, count, depth, columns), blocks[0].dtype),
+        in_specs=[pl.BlockSpec(memory_space=pltpu.SMEM)]
+        + [pl.BlockSpec((outer, depth, chunk), lambda j: (0, 0, j + first // chunk))] * count,
+        out_specs=pl.BlockSpec((outer, count, depth, chunk), lambda j: (0, 0, 0, j)),
+        compiler_params=pltpu.CompilerParams(vmem_limit_bytes=32 * 2**20),
         cost_estimate=pl.CostEstimate(flops=0, bytes_accessed=size, transcendentals=0),
     )(slots.astype(jnp.int32), *blocks)
 
@@ -186,13 +184,12 @@
     last = n_seq - 1
     order = [0] + list(range(last, 0, -1))
     grad_top = cotangent.reshape(rows, width)
-    z_order = place([mix] + z_parts, z_slots, (n_z, own, columns), 0)
+    z_order = place([part[None] for part in [mix] + z_parts], z_slots, columns // 3)[0]
     mix_parts = {k: across_seq(z_order, k) for k in order[1:]}
     mix_parts, top_out = tie((mix_parts, grad_top))
     mix_parts[0] = z_order
-    mix_mine = place(
-        [mix_parts[k] for k in range(n_seq)], seq_slots, (n_z, n_seq, own, columns), 1
-    ).reshape(width // 2, columns)
+    mix_mine = place([mix_parts[k] for k in range(n_seq)], seq_slots, columns // 3)
+    mix_mine = mix_mine.reshape(width // 2, columns)
 
     mix_other = to_sibling(mix_mine)
     tops = {k: across_seq(top_out, k) for k in order[1:]}
@@ -253,19 +250,9 @@
     middle = residual + dot(mixed_mine, out_mine) + dot(mixed_other, out_other)
     unit_two, scale_two, norm_two = normed(middle, gain_vals[1])
 
-    shape = (n_z, 2, half // n_z)
-    in_full = place(
-        [in_mine.reshape(n_z, -1, cut_in), in_other.reshape(n_z, -1, cut_in)],
-        core_slots,
-        shape + (cut_in,),
-        1,
-    ).reshape(width, cut_in)
-    out_full = place(
-        [out_mine.reshape(n_z, -1, width), out_other.reshape(n_z, -1, width)],
-        core_slots,
-        shape + (width,),
-        1,
-    ).reshape(width, width)
+    both_halves = [mix_mine.reshape(n_z, -1, columns), mix_other.reshape(n_z, -1, columns)]
+    in_full = place(both_halves, core_slots, width, 0, cut_in).reshape(width, cut_in)
+    out_full = place(both_halves, core_slots, width, cut_in, width).reshape(width, width)
 
     norm_two, tops = tie((norm_two, tops))
     tops[0] = grad_top
@@ -362,42 +349,33 @@
     small_grads = (small_grads + to_sibling(small_grads)).astype(bf16)
     small_wide = jnp.tile(jnp.pad(small_grads, ((0, own - 5), (0, 0))), (half // own, 1))
     small_wide = jnp.where(row_blocks(core) == feature // own, small_wide, 0.0).astype(bf16)
+    in_received = to_sibling(grad_in_other.astype(bf16))
+    in_received, out_sums[last] = tie((in_received, out_sums[last]))
     mixed = jnp.concatenate(
         [
-            sum_core(grad_in_mine, grad_in_other),
+            grad_in_mine + in_received.astype(f32),
             sum_core(grad_out_mine, grad_out_other),
             right_contract(small_wide, spread),
         ],
         1,
     ).astype(bf16)
-    mixed, out_sums, sum_down = tie((mixed, out_sums, sum_down))
     mixed = mixed.reshape(n_z, n_seq, own, -1)
 
     def seq_block(index):
         return lax.dynamic_index_in_dim(mixed, index, 1, keepdims=False)
 
     seq_parts = [across_seq(seq_block(sq ^ k), k) for k in order[1:]]
-    seq_parts, gu_sum, out_low = tie((seq_parts, gu_sum, out_low))
+    gu_sum = gu_sum.reshape(n_seq, own, 2 * ff_part)
+    gu_parts = [across_seq(pick(gu_sum, sq ^ k), k) for k in range(1, n_seq)]
+    seq_parts, gu_parts, out_low, sum_down = tie((seq_parts, gu_parts, out_low, sum_down))
     total = seq_block(sq).astype(f32)
     for part in seq_parts:
         total = total + part.astype(f32)
     low = total.astype(bf16)
     z_sums = [along_z(pick(low, (z + k) % n_z), k) for k in range(1, n_z)]
-    gu_sum = gu_sum.reshape(n_seq, own, 2 * ff_part)
-    gu_parts = [across_seq(pick(gu_sum, sq ^ k), k) for k in range(1, n_seq)]
     for k in order[2:]:
         out_sums[k] = across_seq(out_low[k], k)
-    z_sums, gu_parts = tie((z_sums, gu_parts))
-    total = pick(total, z)
-    for part in z_sums:
-        total = total + part.astype(f32)
-    sum_in, sum_out, small_sum = total[:, :cut_in], total[:, cut_in:cut_out], total[:, cut_out:]
-
     gu_sum = seq_ordered([pick(gu_sum, sq)] + gu_parts).astype(f32)
-    output = middle + out_parts[0]
-    for k in order[1:]:
-        output = output + out_sums[k].astype(f32)
-    output = output.astype(bf16)
 
     def by_row(part):
         return (
@@ -406,34 +384,28 @@
             .reshape(own, n_seq * ff_part)
         )
 
-    sum_gate = by_row(gu_sum[:, :, :ff_part])
-    sum_up = by_row(gu_sum[:, :, ff_part:])
-
-    reduced = (
-        sum_in,
-        sum_out,
-        small_sum[:3, :own],
-        sum_gate,
-        sum_up,
-        sum_down,
-        small_sum[3:5, :own],
-    )
-    masters = (w_in, w_out, conv_w, w_gate, w_up, w_down, gains)
-    firsts = (m_in, m_out, m_conv, m_gate, m_up, m_down, m_gains)
-    seconds = (v_in, v_out, v_conv, v_gate, v_up, v_down, v_gains)
-    rates = (learn_rate, learn_rate, small_rate, learn_rate, learn_rate, learn_rate, small_rate)
-    decays = (weight_decay, weight_decay, 0.0, weight_decay, weight_decay, weight_decay, 0.0)
-    updated = [
-        adamw(
-            masters[index],
-            firsts[index],
-            seconds[index],
-            reduced[index],
-            rates[index],
-            decays[index],
-        )
-        for index in range(7)
-    ]
+    def matrix_step(master, first, second, grad):
+        return adamw(master, first, second, grad, learn_rate, weight_decay)
+
+    step_gate = matrix_step(w_gate, m_gate, v_gate, by_row(gu_sum[:, :, :ff_part]))
+    step_up = matrix_step(w_up, m_up, v_up, by_row(gu_sum[:, :, ff_part:]))
+    step_down = matrix_step(w_down, m_down, v_down, sum_down)
+    z_sums, step_gate, step_up, step_down = tie((z_sums, step_gate, step_up, step_down))
+    total = pick(total, z)
+    for part in z_sums:
+        total = total + part.astype(f32)
+    sum_in, sum_out, small_sum = total[:, :cut_in], total[:, cut_in:cut_out], total[:, cut_out:]
+
+    output = middle + out_parts[0]
+    for k in order[1:]:
+        output = output + out_sums[k].astype(f32)
+    output = output.astype(bf16)
+
+    step_in = matrix_step(w_in, m_in, v_in, sum_in)
+    step_out = matrix_step(w_out, m_out, v_out, sum_out)
+    step_conv = adamw(conv_w, m_conv, v_conv, small_sum[:3, :own], small_rate, 0.0)
+    step_gains = adamw(gains, m_gains, v_gains, small_sum[3:5, :own], small_rate, 0.0)
+    updated = [step_in, step_out, step_conv, step_gate, step_up, step_down, step_gains]
     new_w = [item[0] for item in updated]
     new_m = [item[1] for item in updated]
     new_v = [item[2] for item in updated]

time: 846 us -> 432 us (0.51)
  Pallas kernels: 425 us -> 9.79 us
    pallas_call x4, Pallas kernels: 425 us -> 9.79 us  [place(): pl.pallas_call(kernel, grid=(columns // chunk,), out_shape=jax.ShapeDtype...]
    slice x5 -> x1, local copies, waits for them, and re-layouts: 12.4 us -> 0.09 us  [local(): step_up = matrix_step(w_up, m_up, v_up, by_row(gu_sum[:, :, ff_part:]))]
  transfers between devices with their start and end apart: 40 -> 40, of which waited for: 17 -> 22; matrix products, arithmetic and copies ran while one was open for 22% -> 40% of each run, Pallas kernels for 51% -> 2%
where the time goes in v4:
time: 432 us; the launch traced here: 424 us
  matrix products  142 us (33%)
  waiting for transfers between devices  137 us (32%)
  other arithmetic  48.2 us (11%)
  starting transfers between devices  42.1 us (10%)
  local copies, waits for them, and re-layouts  29.2 us (7%)
  between operations  15.8 us (4%)
  Pallas kernels  9.79 us (2%)
    ppermute x24, waiting for transfers between devices, across_seq(): lax.ppermute(block, 'seq', [(i, i ^ by) for i in range(lax.axis_size('seq...  118 us
    dot_general x18, matrix products, dot(): return jnp.dot(first, second, preferred_element_type=f32)  57.7 us
    dot_general x11, matrix products, right_contract(): lax.dot_general(first, second, (((1,), (1,)), ((), ())), preferred_elemen...  44.9 us
    dot_general x6, matrix products, left_contract(): lax.dot_general(first, second, (((0,), (0,)), ((), ())), preferred_elemen...  39.5 us
    ppermute x24, starting transfers between devices, across_seq(): lax.ppermute(block, 'seq', [(i, i ^ by) for i in range(lax.axis_size('seq...  27.3 us
    ppermute x6, waiting for transfers between devices, along_z(): lax.ppermute(block, 'dp', [(i, (i + 2 * by) % count) for i in range(count)])  13.9 us
    unnamed x209, local copies, waits for them, and re-layouts  11.5 us
    pallas_call x4, Pallas kernels, place(): pl.pallas_call(kernel, grid=(columns // chunk,), out_shape=jax.ShapeDtype...  9.79 us
  transfers between devices with their start and end apart: 40, of which 22 were waited for; matrix products, arithmetic and copies ran while one was open for 40% of the time, Pallas kernels for 2%

profile of v4, /device:TPU:8, one launch (start us, length us, event | category | flops | bytes accessed | tf_op | source)
XLA Modules:
  0.0 424.3 jit_solution(9087066558879312857)
XLA Ops:
  31.5 4.2 collective-permute-start.4
  36.5 3.5 collective-permute-done.4
  48.3 23.3 %collective-permute-done.7.refs_1_ = bf16[4,32,4224]{2,1,0:T(8,128)(2,1)S(1)} collective-permute-done((bf16[4,32,4224]{2,1,0:T(8,128)(2,1)S(1)}, bf16[4,32,4224]{2,1,0:T(8,128)(2,1)S(1)}, u32[]{:S(2)}, u32[]{:S(2)}) %collective-permute-start.7) | collective-permute-done | bytes 1081376 | tf_op jit(solution)/shard_map/ppermute | solution.py:39
  71.7 18.6 %collective-permute-done.9.refs_3_ = bf16[4,32,4224]{2,1,0:T(8,128)(2,1)S(1)} collective-permute-done((bf16[4,32,4224]{2,1,0:T(8,128)(2,1)S(1)}, bf16[4,32,4224]{2,1,0:T(8,128)(2,1)S(1)}, u32[]{:S(2)}, u32[]{:S(2)}) %collective-permute-start.9) | collective-permute-done | bytes 1081376 | tf_op jit(solution)/shard_map/ppermute | solution.py:39
  106.4 6.7 %fusion.39 = f32[512,3072]{1,0:T(8,128)} fusion(bf16[512,4224]{1,0:T(8,128)(2,1)} %bitcast.13, pred[]{:T(512)S(6)} %eq.90, bf16[512,128]{1,0:T(8,128)(2,1)S(1)} %get-tuple-element.255, bf16[512,128]{1,0:T(8,128)(2,1)S(1)} %get-tuple-element.256, bf16[512,128]{1,0:T(8,128)(2,1)S(1)} %get-tuple-element.257, bf16[512,128]{1,0:T(8,128)(2,1)S(1)} %get-tuple-element.258, ...), kind=kOutput, calls=%fused_computation.38 | convolution fusion | flops 1615069184 | bytes 10485761 | tf_op jit(solution)/shard_map/dot_general | solution.py:43
  116.2 5.7 %convolution_add_fusion = f32[512,3072]{1,0:T(8,128)S(1)} fusion(f32[512,3072]{1,0:T(8,128)} %fusion.39, bf16[512,4224]{1,0:T(8,128)(2,1)} %collective-permute-done.10, pred[]{:T(512)S(6)} %eq.90, bf16[512,128]{1,0:T(8,128)(2,1)S(1)} %get-tuple-element.255, bf16[512,128]{1,0:T(8,128)(2,1)S(1)} %get-tuple-element.256, ...), kind=kOutput, calls=%fused_computation.10 | convolution fusion | flops 1616642048 | bytes 16777216 | tf_op jit(solution)/shard_map/dot_general | solution.py:43
  129.0 4.0 shard_map.409
  147.9 7.4 %fusion.180 = f32[512,2304]{1,0:T(8,128)} fusion(bf16[512,1024]{1,0:T(8,128)(2,1)} %multiply_convert_fusion.12, bf16[1024,2304]{1,0:T(8,128)(2,1)} %bitcast.218), kind=kOutput, calls=%fused_computation.349 | convolution fusion | flops 2415919104 | bytes 10485760 | tf_op jit(solution)/shard_map/dot_general | solution.py:43
  155.3 5.7 %multiply_convert_fusion.10 = (bf16[512,1152]{1,0:T(8,128)(2,1)S(1)}, bf16[512,1152]{1,0:T(8,128)(2,1)S(1)}, bf16[512,1152]{1,0:T(8,128)(2,1)S(1)}) fusion(f32[512,2304]{1,0:T(8,128)} %fusion.180, bf16[1152,1024]{1,0:T(8,128)(2,1)} %all-gather.4.cloned.1.call-done, bf16[512,1024]{1,0:T(8,128)(2,1)} %bitcast.12), kind=kOutput, calls=%fused_computation.61 | convolution fusion | flops 1216806912 | bytes 11665408 | tf_op jit(solution)/shard_map/dot_general | solution.py:51
  161.2 10.6 %collective-permute-done.16 = bf16[512,1024]{1,0:T(8,128)(2,1)} collective-permute-done((bf16[512,1024]{1,0:T(8,128)(2,1)}, bf16[512,1024]{1,0:T(8,128)(2,1)}, u32[]{:S(2)}, u32[]{:S(2)}) %collective-permute-start.16) | collective-permute-done | bytes 1048608 | tf_op jit(solution)/shard_map/ppermute | solution.py:39
  171.8 4.0 fusion.182
  175.8 4.6 %multiply_convert_fusion.8 = (bf16[512,1152]{1,0:T(8,128)(2,1)S(1)}, bf16[512,1152]{1,0:T(8,128)(2,1)S(1)}, bf16[512,1152]{1,0:T(8,128)(2,1)}) fusion(f32[512,2304]{1,0:T(8,128)S(1)} %fusion.182, bf16[512,1024]{1,0:T(8,128)(2,1)} %collective-permute-done.13, bf16[1152,1024]{1,0:T(8,128)(2,1)S(1)} %copy-done.94), kind=kOutput, calls=%fused_computation.57 | convolution fusion | flops 1216806912 | bytes 11665408 | tf_op jit(solution)/shard_map/dot_general | solution.py:51
  188.9 3.9 fusion.181
  194.2 3.9 fusion.184
  198.0 4.6 %multiply_convert_fusion.6 = (bf16[512,1152]{1,0:T(8,128)(2,1)S(1)}, bf16[512,1152]{1,0:T(8,128)(2,1)S(1)}, bf16[512,1152]{1,0:T(8,128)(2,1)}) fusion(f32[512,2304]{1,0:T(8,128)S(1)} %fusion.184, bf16[512,1024]{1,0:T(8,128)(2,1)} %collective-permute-done.12, bf16[1152,1024]{1,0:T(8,128)(2,1)S(1)} %copy-done.94), kind=kOutput, calls=%fused_computation.53 | convolution fusion | flops 1216806912 | bytes 11665408 | tf_op jit(solution)/shard_map/dot_general | solution.py:51
  204.3 3.6 convolution_convert_fusion.5
  207.9 3.9 fusion.185
  211.8 4.7 %multiply_convert_fusion.4 = (bf16[512,1152]{1,0:T(8,128)(2,1)S(1)}, bf16[512,1152]{1,0:T(8,128)(2,1)S(1)}, bf16[512,1152]{1,0:T(8,128)(2,1)}) fusion(f32[512,2304]{1,0:T(8,128)S(1)} %fusion.185, bf16[512,1024]{1,0:T(8,128)(2,1)} %collective-permute-done.11, bf16[1152,1024]{1,0:T(8,128)(2,1)S(1)} %copy-done.94), kind=kOutput, calls=%fused_computation.49 | convolution fusion | flops 1216806912 | bytes 11665408 | tf_op jit(solution)/shard_map/dot_general | solution.py:51
  217.0 3.6 convolution_convert_fusion.4
  220.7 16.4 %fusion.8 = bf16[1024,2304]{1,0:T(8,128)(2,1)} fusion(bf16[512,2304]{1,0:T(8,128)(2,1)} %copy-done.14, bf16[512,2304]{1,0:T(8,128)(2,1)} %pad_maximum_fusion.4, bf16[512,2304]{1,0:T(8,128)(2,1)} %pad_maximum_fusion.3, bf16[512,2304]{1,0:T(8,128)(2,1)} %copy-done.13, bf16[512,1024]{1,0:T(8,128)(2,1)} %collective-permute-done.14, ...), kind=kOutput, calls=%fused_computation.9 | convolution fusion | flops 9720561664 | bytes 18350080 | tf_op jit(solution)/shard_map/dot_general | solution.py:47
  239.1 10.1 %fusion.33 = bf16[1152,1024]{1,0:T(8,128)(2,1)} fusion(bf16[512,1024]{1,0:T(8,128)(2,1)} %collective-permute-done.11, bf16[512,1024]{1,0:T(8,128)(2,1)} %collective-permute-done.12, bf16[512,1024]{1,0:T(8,128)(2,1)} %collective-permute-done.13, bf16[512,1024]{1,0:T(8,128)(2,1)} %bitcast.12, bf16[512,1152]{1,0:T(8,128)(2,1)} %get-tuple-element.153, ...), kind=kOutput, calls=%fused_computation.35 | convolution fusion | flops 4868669440 | bytes 11272192 | tf_op jit(solution)/shard_map/dot_general | solution.py:47
  249.2 4.7 %convolution_convert_fusion.1 = bf16[512,1024]{1,0:T(8,128)(2,1)} fusion(bf16[512,1152]{1,0:T(8,128)(2,1)} %get-tuple-element.155, bf16[1152,1024]{1,0:T(8,128)(2,1)} %all-gather.4.cloned.1.call-done), kind=kOutput, calls=%fused_computation.114 | convolution fusion | flops 1208483840 | bytes 4587520 | tf_op jit(solution)/shard_map/dot_general | solution.py:43
  259.0 3.7 collective-permute-done.19
  278.4 3.6 convolution_convert_fusion
  287.3 8.5 %fusion.57 = (f32[512]{0:T(512)}, f32[1024]{0:T(1024)}, f32[512,1024]{1,0:T(8,128)}) fusion(bf16[2,256,1024]{2,1,0:T(8,128)(2,1)S(1)} %copy-done.12, f32[1024]{0:T(1024)S(1)} %bitcast.202, f32[512]{0:T(512)S(1)} %bitcast.211, bf16[1024,3072]{1,0:T(8,128)(2,1)} %bitcast.174, bf16[512,1024]{1,0:T(8,128)(2,1)S(1)} %copy-done.31, ...), kind=kOutput, calls=%fused_computation.89 | convolution fusion | flops 3234331136 | bytes 12595200 | tf_op jit(solution)/shard_map/dot_general | solution.py:51
  297.4 4.2 fusion.100
  304.9 8.6 %collective-permute-done.22 = bf16[512,1024]{1,0:T(8,128)(2,1)} collective-permute-done((bf16[512,1024]{1,0:T(8,128)(2,1)}, bf16[512,1024]{1,0:T(8,128)(2,1)}, u32[]{:S(2)}, u32[]{:S(2)}) %collective-permute-start.22) | collective-permute-done | bytes 1048608 | tf_op jit(solution)/shard_map/ppermute | solution.py:39
  327.4 20.8 %collective-permute-done.25 = bf16[4,32,4224]{2,1,0:T(8,128)(2,1)} collective-permute-done((bf16[4,32,4224]{2,1,0:T(8,128)(2,1)}, bf16[4,32,4224]{2,1,0:T(8,128)(2,1)}, u32[]{:S(2)}, u32[]{:S(2)}) %collective-permute-start.25) | collective-permute-done | bytes 1081376 | tf_op jit(solution)/shard_map/ppermute | solution.py:39
  348.7 3.4 fusion.60
  354.0 16.2 %collective-permute-done.26 = bf16[4,32,4224]{2,1,0:T(8,128)(2,1)} collective-permute-done((bf16[4,32,4224]{2,1,0:T(8,128)(2,1)}, bf16[4,32,4224]{2,1,0:T(8,128)(2,1)}, u32[]{:S(2)}, u32[]{:S(2)}) %collective-permute-start.26) | collective-permute-done | bytes 1081376 | tf_op jit(solution)/shard_map/ppermute | solution.py:39
  396.9 9.1 %collective-permute-done.33 = bf16[32,4224]{1,0:T(8,128)(2,1)S(1)} collective-permute-done((bf16[32,4224]{1,0:T(8,128)(2,1)S(1)}, bf16[32,4224]{1,0:T(8,128)(2,1)S(1)}, u32[]{:S(2)}, u32[]{:S(2)}) %collective-permute-start.33) | collective-permute-done | bytes 270368 | tf_op jit(solution)/shard_map/ppermute | solution.py:35
  406.0 3.6 collective-permute-done.34
  (398 shorter events, 169.1 us)
Async XLA Ops:
  7.2 140.7 %all-gather.6.cloned.1.call-start = ((), (), s32[]{:S(2)}) async-start(), calls=%async_computation.5 | async-start | bytes 5308416 | tf_op jit(solution)/shard_map/all_gather | solution.py:176
  11.3 30.5 %collective-permute-start = (bf16[32,4224]{1,0:T(8,128)(2,1)}, bf16[32,4224]{1,0:T(8,128)(2,1)S(1)}, u32[]{:S(2)}, u32[]{:S(2)}) collective-permute-start(bf16[32,4224]{1,0:T(8,128)(2,1)} %get-tuple-element.278), channel_id=1, source_target_pairs={{0,24},{4,28},{8,0},{12,4},{16,8},{20,12},{24,16},{28,20},{1,25},{... | collective-permute-start | bytes 811016 | tf_op jit(solution)/shard_map/ppermute | solution.py:35
  11.3 30.5 %collective-permute-start.1 = (bf16[32,4224]{1,0:T(8,128)(2,1)}, bf16[32,4224]{1,0:T(8,128)(2,1)S(1)}, u32[]{:S(2)}, u32[]{:S(2)}) collective-permute-start(bf16[32,4224]{1,0:T(8,128)(2,1)} %get-tuple-element.278), channel_id=1, source_target_pairs={{0,16},{4,20},{8,24},{12,28},{16,0},{20,4},{24,8},{28,12},{1,17},{... | collective-permute-start | bytes 811016 | tf_op jit(solution)/shard_map/ppermute | solution.py:35
  14.3 27.5 %collective-permute-start.2 = (bf16[32,4224]{1,0:T(8,128)(2,1)}, bf16[32,4224]{1,0:T(8,128)(2,1)S(1)}, u32[]{:S(2)}, u32[]{:S(2)}) collective-permute-start(bf16[32,4224]{1,0:T(8,128)(2,1)} %get-tuple-element.278), channel_id=1, source_target_pairs={{0,8},{4,12},{8,16},{12,20},{16,24},{20,28},{24,0},{28,4},{1,9},{5... | collective-permute-start | bytes 811016 | tf_op jit(solution)/shard_map/ppermute | solution.py:35
  43.8 111.5 %all-gather.4.cloned.1.call-start = ((), (), s32[]{:S(2)}) async-start(), calls=%async_computation.2 | async-start | bytes 2654208 | tf_op jit(solution)/shard_map/all_gather | solution.py:177
  44.8 26.9 %collective-permute-start.7 = (bf16[4,32,4224]{2,1,0:T(8,128)(2,1)S(1)}, bf16[4,32,4224]{2,1,0:T(8,128)(2,1)S(1)}, u32[]{:S(2)}, u32[]{:S(2)}) collective-permute-start(bf16[4,32,4224]{2,1,0:T(8,128)(2,1)S(1)} %bitcast.175), channel_id=1, source_target_pairs={{0,1},{1,0},{2,3},{3,2},{4,5},{5,4},{6,7},{7,6},{8,9},{9,8},{10,11... | collective-permute-start | bytes 3244040 | tf_op jit(solution)/shard_map/ppermute | solution.py:39
  44.9 26.8 %collective-permute-start.8 = (bf16[4,32,4224]{2,1,0:T(8,128)(2,1)S(1)}, bf16[4,32,4224]{2,1,0:T(8,128)(2,1)S(1)}, u32[]{:S(2)}, u32[]{:S(2)}) collective-permute-start(bf16[4,32,4224]{2,1,0:T(8,128)(2,1)S(1)} %bitcast.176), channel_id=1, source_target_pairs={{0,2},{1,3},{2,0},{3,1},{4,6},{5,7},{6,4},{7,5},{8,10},{9,11},{10,... | collective-permute-start | bytes 3244040 | tf_op jit(solution)/shard_map/ppermute | solution.py:39
  45.5 44.7 %collective-permute-start.9 = (bf16[4,32,4224]{2,1,0:T(8,128)(2,1)S(1)}, bf16[4,32,4224]{2,1,0:T(8,128)(2,1)S(1)}, u32[]{:S(2)}, u32[]{:S(2)}) collective-permute-start(bf16[4,32,4224]{2,1,0:T(8,128)(2,1)S(1)} %bitcast.177), channel_id=1, source_target_pairs={{0,3},{1,2},{2,1},{3,0},{4,7},{5,6},{6,5},{7,4},{8,11},{9,10},{10,... | collective-permute-start | bytes 3244040 | tf_op jit(solution)/shard_map/ppermute | solution.py:39
  93.9 229.8 %reduce-scatter.3.cloned.1.call-start = ((), (), s32[]{:S(2)}) async-start(), calls=%async_computation.3 | async-start | bytes 5308416 | tf_op jit(solution)/shard_map/reduce_scatter | solution.py:301
  94.8 47.2 %collective-permute-start.11 = (bf16[512,1024]{1,0:T(8,128)(2,1)}, bf16[512,1024]{1,0:T(8,128)(2,1)}, u32[]{:S(2)}, u32[]{:S(2)}) collective-permute-start(bf16[512,1024]{1,0:T(8,128)(2,1)} %bitcast.12), channel_id=1, source_target_pairs={{0,1},{1,0},{2,3},{3,2},{4,5},{5,4},{6,7},{7,6},{8,9},{9,8},{10,11... | collective-permute-start | bytes 3145736 | tf_op jit(solution)/shard_map/ppermute | solution.py:39
  96.3 48.1 %collective-permute-start.12 = (bf16[512,1024]{1,0:T(8,128)(2,1)}, bf16[512,1024]{1,0:T(8,128)(2,1)}, u32[]{:S(2)}, u32[]{:S(2)}) collective-permute-start(bf16[512,1024]{1,0:T(8,128)(2,1)} %bitcast.12), channel_id=1, source_target_pairs={{0,2},{1,3},{2,0},{3,1},{4,6},{5,7},{6,4},{7,5},{8,10},{9,11},{10,... | collective-permute-start | bytes 3145736 | tf_op jit(solution)/shard_map/ppermute | solution.py:39
  97.1 47.3 %collective-permute-start.13 = (bf16[512,1024]{1,0:T(8,128)(2,1)}, bf16[512,1024]{1,0:T(8,128)(2,1)}, u32[]{:S(2)}, u32[]{:S(2)}) collective-permute-start(bf16[512,1024]{1,0:T(8,128)(2,1)} %bitcast.12), channel_id=1, source_target_pairs={{0,3},{1,2},{2,1},{3,0},{4,7},{5,6},{6,5},{7,4},{8,11},{9,10},{10,... | collective-permute-start | bytes 3145736 | tf_op jit(solution)/shard_map/ppermute | solution.py:39
  144.4 27.4 %collective-permute-start.16 = (bf16[512,1024]{1,0:T(8,128)(2,1)}, bf16[512,1024]{1,0:T(8,128)(2,1)}, u32[]{:S(2)}, u32[]{:S(2)}) collective-permute-start(bf16[512,1024]{1,0:T(8,128)(2,1)} %multiply_convert_fusion.12), channel_id=1, source_target_pairs={{0,3},{1,2},{2,1},{3,0},{4,7},{5,6},{6,5},{7,4},{8,11},{9,10},{10,... | collective-permute-start | bytes 3145736 | tf_op jit(solution)/shard_map/ppermute | solution.py:39
  145.6 48.6 %collective-permute-start.15 = (bf16[512,1024]{1,0:T(8,128)(2,1)}, bf16[512,1024]{1,0:T(8,128)(2,1)}, u32[]{:S(2)}, u32[]{:S(2)}) collective-permute-start(bf16[512,1024]{1,0:T(8,128)(2,1)} %multiply_convert_fusion.12), channel_id=1, source_target_pairs={{0,2},{1,3},{2,0},{3,1},{4,6},{5,7},{6,4},{7,5},{8,10},{9,11},{10,... | collective-permute-start | bytes 3145736 | tf_op jit(solution)/shard_map/ppermute | solution.py:39
  146.4 61.5 %collective-permute-start.14 = (bf16[512,1024]{1,0:T(8,128)(2,1)}, bf16[512,1024]{1,0:T(8,128)(2,1)}, u32[]{:S(2)}, u32[]{:S(2)}) collective-permute-start(bf16[512,1024]{1,0:T(8,128)(2,1)} %multiply_convert_fusion.12), channel_id=1, source_target_pairs={{0,1},{1,0},{2,3},{3,2},{4,5},{5,4},{6,7},{7,6},{8,9},{9,8},{10,11... | collective-permute-start | bytes 3145736 | tf_op jit(solution)/shard_map/ppermute | solution.py:39
  184.7 32.3 %collective-permute-start.17 = (bf16[512,1024]{1,0:T(8,128)(2,1)S(1)}, bf16[512,1024]{1,0:T(8,128)(2,1)S(1)}, u32[]{:S(2)}, u32[]{:S(2)}) collective-permute-start(bf16[512,1024]{1,0:T(8,128)(2,1)S(1)} %convolution_convert_fusion.6), channel_id=1, source_target_pairs={{0,3},{1,2},{2,1},{3,0},{4,7},{5,6},{6,5},{7,4},{8,11},{9,10},{10,... | collective-permute-start | bytes 3145736 | tf_op jit(solution)/shard_map/ppermute | solution.py:39
  237.1 115.0 %reduce-scatter.5.cloned.1.call-start = ((), (), s32[]{:S(2)}) async-start(), calls=%async_computation.4 | async-start | bytes 2654208 | tf_op jit(solution)/shard_map/reduce_scatter | solution.py:298
  237.3 25.4 %collective-permute-start.19 = (bf16[512,1024]{1,0:T(8,128)(2,1)}, bf16[512,1024]{1,0:T(8,128)(2,1)}, u32[]{:S(2)}, u32[]{:S(2)}) collective-permute-start(bf16[512,1024]{1,0:T(8,128)(2,1)} %convolution_convert_fusion.5), channel_id=1, source_target_pairs={{0,2},{1,3},{2,0},{3,1},{4,6},{5,7},{6,4},{7,5},{8,10},{9,11},{10,... | collective-permute-start | bytes 3145736 | tf_op jit(solution)/shard_map/ppermute | solution.py:39
  238.2 25.0 %collective-permute-start.18 = (bf16[512,1024]{1,0:T(8,128)(2,1)}, bf16[512,1024]{1,0:T(8,128)(2,1)}, u32[]{:S(2)}, u32[]{:S(2)}) collective-permute-start(bf16[512,1024]{1,0:T(8,128)(2,1)} %convolution_convert_fusion.4), channel_id=1, source_target_pairs={{0,1},{1,0},{2,3},{3,2},{4,5},{5,4},{6,7},{7,6},{8,9},{9,8},{10,11... | collective-permute-start | bytes 3145736 | tf_op jit(solution)/shard_map/ppermute | solution.py:39
  282.0 31.6 %collective-permute-start.21 = (bf16[512,3072]{1,0:T(8,128)(2,1)}, bf16[512,3072]{1,0:T(8,128)(2,1)}, u32[]{:S(2)}, u32[]{:S(2)}) collective-permute-start(bf16[512,3072]{1,0:T(8,128)(2,1)} %convolution_convert_fusion), channel_id=1, source_target_pairs={{0,4},{4,0},{8,12},{12,8},{16,20},{20,16},{24,28},{28,24},{1,5},{5... | collective-permute-start | bytes 9437192 | tf_op jit(solution)/shard_map/ppermute | solution.py:30
  286.8 26.8 %collective-permute-start.22 = (bf16[512,1024]{1,0:T(8,128)(2,1)}, bf16[512,1024]{1,0:T(8,128)(2,1)}, u32[]{:S(2)}, u32[]{:S(2)}) collective-permute-start(bf16[512,1024]{1,0:T(8,128)(2,1)} %convolution_convert_fusion.1), channel_id=1, source_target_pairs={{0,3},{1,2},{2,1},{3,0},{4,7},{5,6},{6,5},{7,4},{8,11},{9,10},{10,... | collective-permute-start | bytes 3145736 | tf_op jit(solution)/shard_map/ppermute | solution.py:39
  320.2 28.0 %collective-permute-start.25 = (bf16[4,32,4224]{2,1,0:T(8,128)(2,1)}, bf16[4,32,4224]{2,1,0:T(8,128)(2,1)}, u32[]{:S(2)}, u32[]{:S(2)}) collective-permute-start(bf16[4,32,4224]{2,1,0:T(8,128)(2,1)} %get-tuple-element.237), channel_id=1, source_target_pairs={{0,3},{1,2},{2,1},{3,0},{4,7},{5,6},{6,5},{7,4},{8,11},{9,10},{10,... | collective-permute-start | bytes 3244040 | tf_op jit(solution)/shard_map/ppermute | solution.py:39
  320.7 49.5 %collective-permute-start.26 = (bf16[4,32,4224]{2,1,0:T(8,128)(2,1)}, bf16[4,32,4224]{2,1,0:T(8,128)(2,1)}, u32[]{:S(2)}, u32[]{:S(2)}) collective-permute-start(bf16[4,32,4224]{2,1,0:T(8,128)(2,1)} %get-tuple-element.236), channel_id=1, source_target_pairs={{0,2},{1,3},{2,0},{3,1},{4,6},{5,7},{6,4},{7,5},{8,10},{9,11},{10,... | collective-permute-start | bytes 3244040 | tf_op jit(solution)/shard_map/ppermute | solution.py:39
  323.5 47.7 %collective-permute-start.27 = (bf16[4,32,4224]{2,1,0:T(8,128)(2,1)}, bf16[4,32,4224]{2,1,0:T(8,128)(2,1)}, u32[]{:S(2)}, u32[]{:S(2)}) collective-permute-start(bf16[4,32,4224]{2,1,0:T(8,128)(2,1)} %get-tuple-element.235), channel_id=1, source_target_pairs={{0,1},{1,0},{2,3},{3,2},{4,5},{5,4},{6,7},{7,6},{8,9},{9,8},{10,11... | collective-permute-start | bytes 3244040 | tf_op jit(solution)/shard_map/ppermute | solution.py:39
  325.6 48.7 %collective-permute-start.28 = (bf16[32,2304]{1,0:T(8,128)(2,1)}, bf16[32,2304]{1,0:T(8,128)(2,1)}, u32[]{:S(2)}, u32[]{:S(2)}) collective-permute-start(bf16[32,2304]{1,0:T(8,128)(2,1)} %get-tuple-element.269), channel_id=1, source_target_pairs={{0,1},{1,0},{2,3},{3,2},{4,5},{5,4},{6,7},{7,6},{8,9},{9,8},{10,11... | collective-permute-start | bytes 442376 | tf_op jit(solution)/shard_map/ppermute | solution.py:39
  327.4 47.1 %collective-permute-start.29 = (bf16[32,2304]{1,0:T(8,128)(2,1)}, bf16[32,2304]{1,0:T(8,128)(2,1)}, u32[]{:S(2)}, u32[]{:S(2)}) collective-permute-start(bf16[32,2304]{1,0:T(8,128)(2,1)} %get-tuple-element.268), channel_id=1, source_target_pairs={{0,2},{1,3},{2,0},{3,1},{4,6},{5,7},{6,4},{7,5},{8,10},{9,11},{10,... | collective-permute-start | bytes 442376 | tf_op jit(solution)/shard_map/ppermute | solution.py:39
  348.2 28.2 %collective-permute-start.30 = (bf16[32,2304]{1,0:T(8,128)(2,1)S(1)}, bf16[32,2304]{1,0:T(8,128)(2,1)}, u32[]{:S(2)}, u32[]{:S(2)}) collective-permute-start(bf16[32,2304]{1,0:T(8,128)(2,1)S(1)} %get-tuple-element.267), channel_id=1, source_target_pairs={{0,3},{1,2},{2,1},{3,0},{4,7},{5,6},{6,5},{7,4},{8,11},{9,10},{10,... | collective-permute-start | bytes 442376 | tf_op jit(solution)/shard_map/ppermute | solution.py:39
  385.5 20.5 %collective-permute-start.33 = (bf16[32,4224]{1,0:T(8,128)(2,1)S(1)}, bf16[32,4224]{1,0:T(8,128)(2,1)S(1)}, u32[]{:S(2)}, u32[]{:S(2)}) collective-permute-start(bf16[32,4224]{1,0:T(8,128)(2,1)S(1)} %get-tuple-element.245), channel_id=1, source_target_pairs={{0,8},{4,12},{8,16},{12,20},{16,24},{20,28},{24,0},{28,4},{1,9},{5... | collective-permute-start | bytes 811016 | tf_op jit(solution)/shard_map/ppermute | solution.py:35
  387.5 22.1 %collective-permute-start.34 = (bf16[32,4224]{1,0:T(8,128)(2,1)S(1)}, bf16[32,4224]{1,0:T(8,128)(2,1)S(1)}, u32[]{:S(2)}, u32[]{:S(2)}) collective-permute-start(bf16[32,4224]{1,0:T(8,128)(2,1)S(1)} %get-tuple-element.244), channel_id=1, source_target_pairs={{0,16},{4,20},{8,24},{12,28},{16,0},{20,4},{24,8},{28,12},{1,17},{... | collective-permute-start | bytes 811016 | tf_op jit(solution)/shard_map/ppermute | solution.py:35
  388.2 22.6 %collective-permute-start.35 = (bf16[32,4224]{1,0:T(8,128)(2,1)S(1)}, bf16[32,4224]{1,0:T(8,128)(2,1)S(1)}, u32[]{:S(2)}, u32[]{:S(2)}) collective-permute-start(bf16[32,4224]{1,0:T(8,128)(2,1)S(1)} %get-tuple-element.243), channel_id=1, source_target_pairs={{0,24},{4,28},{8,0},{12,4},{16,8},{20,12},{24,16},{28,20},{1,25},{... | collective-permute-start | bytes 811016 | tf_op jit(solution)/shard_map/ppermute | solution.py:35
  389.7 24.6 %collective-permute-start.31 = (bf16[512,1024]{1,0:T(8,128)(2,1)S(1)}, bf16[512,1024]{1,0:T(8,128)(2,1)S(1)}, u32[]{:S(2)}, u32[]{:S(2)}) collective-permute-start(bf16[512,1024]{1,0:T(8,128)(2,1)S(1)} %copy-done.97), channel_id=1, source_target_pairs={{0,2},{1,3},{2,0},{3,1},{4,6},{5,7},{6,4},{7,5},{8,10},{9,11},{10,... | collective-permute-start | bytes 3145736 | tf_op jit(solution)/shard_map/ppermute | solution.py:39
  390.4 23.8 %collective-permute-start.32 = (bf16[512,1024]{1,0:T(8,128)(2,1)S(1)}, bf16[512,1024]{1,0:T(8,128)(2,1)S(1)}, u32[]{:S(2)}, u32[]{:S(2)}) collective-permute-start(bf16[512,1024]{1,0:T(8,128)(2,1)S(1)} %copy-done.96), channel_id=1, source_target_pairs={{0,1},{1,0},{2,3},{3,2},{4,5},{5,4},{6,7},{7,6},{8,9},{9,8},{10,11... | collective-permute-start | bytes 3145736 | tf_op jit(solution)/shard_map/ppermute | solution.py:39
  (111 other events, 799.0 us)
Sparse Core Ops, SparseCore 0:
  43.9 48.1 all-gather.5
  94.3 31.4 all-gather.3
  237.2 51.5 reduce-scatter.2
  291.0 34.1 reduce-scatter.4

commit v5 on v4

--- a/solution.py
+++ b/solution.py
@@ -37,6 +37,36 @@
 
 def across_seq(block, by):
     return lax.ppermute(block, "seq", [(i, i ^ by) for i in range(lax.axis_size("seq"))])
+
+
+def swap_near(block):
+    count = lax.axis_size("seq")
+    near = (1, 2) if count == 4 else range(1, count)
+    return {k: across_seq(block, k) for k in near}
+
+
+def swap_far(near):
+    if lax.axis_size("seq") != 4:
+        return {}
+    half = near[1].shape[0] // 2
+    first, second = across_seq(near[1][:half], 2), across_seq(near[2][half:], 1)
+    return {3: jnp.concatenate([first, second], 0)}
+
+
+def sum_far(block):
+    half = block.shape[0] // 2
+    return across_seq(block[:half], 1), across_seq(block[half:], 2)
+
+
+def add_far(terms, received):
+    if not received:
+        return terms
+    first, second = received
+    half = first.shape[0]
+    terms = dict(terms)
+    terms[2] = jnp.concatenate([terms[2][:half] + first.astype(f32), terms[2][half:]], 0)
+    terms[1] = jnp.concatenate([terms[1][:half], terms[1][half:] + second.astype(f32)], 0)
+    return terms
 
 
 def dot(first, second):
@@ -181,18 +211,22 @@
     z_slots = (z + jnp.arange(n_z)) % n_z
     seq_slots = sq ^ jnp.arange(n_seq)
     core_slots = core ^ jnp.arange(2)
-    last = n_seq - 1
-    order = [0] + list(range(last, 0, -1))
+    order = list(range(n_seq))
+    near = order[1:3] if n_seq == 4 else order[1:]
+    last = order[-1]
     grad_top = cotangent.reshape(rows, width)
     z_order = place([part[None] for part in [mix] + z_parts], z_slots, columns // 3)[0]
-    mix_parts = {k: across_seq(z_order, k) for k in order[1:]}
+    mix_parts = swap_near(z_order)
+    mix_parts = tie(mix_parts)
+    mix_parts.update(swap_far(mix_parts))
     mix_parts, top_out = tie((mix_parts, grad_top))
     mix_parts[0] = z_order
     mix_mine = place([mix_parts[k] for k in range(n_seq)], seq_slots, columns // 3)
     mix_mine = mix_mine.reshape(width // 2, columns)
 
     mix_other = to_sibling(mix_mine)
-    tops = {k: across_seq(top_out, k) for k in order[1:]}
+    tops = swap_near(top_out)
+    tops.update(swap_far(tops))
 
     cut_in, cut_out = 3 * width, 4 * width
     in_mine, in_other = mix_mine[:, :cut_in], mix_other[:, :cut_in]
@@ -221,18 +255,18 @@
     residual = residual_low.astype(f32)
     unit_one, scale_one, norm_one = normed(residual, gain_vals[0])
     edge_rows = jnp.pad(edge[:, :, :width].reshape(2 * seqs_here, width), ((0, 12), (0, 0)))
-    edge_mine, edge_other = halves(normed(edge_rows.astype(f32), gain_vals[0])[2])
-
-    def edge_dot(start):
-        stop = start + width
-        return dot(edge_mine, in_mine[:, start:stop]) + dot(edge_other, in_other[:, start:stop])
-
-    prev_rows = (edge_dot(0) * edge_dot(2 * width)).astype(bf16)[: 2 * seqs_here]
+    edge_norm = normed(edge_rows.astype(f32), gain_vals[0])[2]
+    norm_mine, norm_other = halves(norm_one)
+    edge_mine, edge_other = halves(edge_norm)
+    projected = dot(jnp.concatenate([norm_mine, edge_mine], 0), in_mine) + dot(
+        jnp.concatenate([norm_other, edge_other], 0), in_other
+    )
+    edge_rows = projected[rows : rows + 2 * seqs_here]
+    prev_rows = (edge_rows[:, :width] * edge_rows[:, 2 * width :]).astype(bf16)
     prev_rows = prev_rows.reshape(seqs_here, 2, width)
+    projected = projected[:rows]
     first_block = sq == 0
     prev_ids = jnp.where(first_block, -1, edge[:, :, width].astype(jnp.int32))
-    norm_mine, norm_other = halves(norm_one)
-    projected = dot(norm_mine, in_mine) + dot(norm_other, in_other)
     b_gate = projected[:, :width]
     c_gate = projected[:, width : 2 * width]
     x_part = projected[:, 2 * width :]
@@ -256,8 +290,7 @@
 
     norm_two, tops = tie((norm_two, tops))
     tops[0] = grad_top
-    norms = {k: across_seq(norm_two, k) for k in order[1:]}
-    norms[0] = norm_two
+    norms = swap_near(norm_two)
     hiddens, act_grads, norm_parts, out_parts = {}, {}, {}, {}
 
     def hidden_block(k):
@@ -271,37 +304,39 @@
         grad_up_act = (grad_hidden * silu_vals).astype(bf16)
         act_grads[k] = jnp.concatenate([grad_gate_act, grad_up_act], 1)
 
+    norms[0] = norm_two
     hidden_block(0)
-    norms[last], hiddens[0], act_grads[0], in_full, out_full = tie(
-        (norms[last], hiddens[0], act_grads[0], in_full, out_full)
-    )
-    hidden_block(last)
-    norm_parts[last] = right_contract(act_grads[last], mat_gate_up).astype(bf16)
+    norm_parts[0] = right_contract(act_grads[0], mat_gate_up)
     out_parts[0] = dot(hiddens[0], mat_down)
-    norm_parts[0] = right_contract(act_grads[0], mat_gate_up)
-    norm_sums = {last: across_seq(norm_parts[last], last)}
-    for k in order[2:]:
-        norms[k], norm_parts, out_parts, act_grads = tie(
-            (norms[k], norm_parts, out_parts, act_grads)
-        )
+    norms, hiddens, act_grads, norm_parts, out_parts, in_full, out_full = tie(
+        (norms, hiddens, act_grads, norm_parts, out_parts, in_full, out_full)
+    )
+    norms.update(swap_far(norms))
+    norm_sums = {}
+    for k in order[1:]:
         hidden_block(k)
-        if k == order[-1]:
-            act_grads, norm_sums[last] = tie((act_grads, norm_sums[last]))
         norm_parts[k] = right_contract(act_grads[k], mat_gate_up).astype(bf16)
         norm_sums[k] = across_seq(norm_parts[k], k)
-    norm_parts, hiddens, act_grads = tie((norm_parts, hiddens, act_grads))
+        if k != last:
+            norms[k + 1], act_grads, norm_parts = tie((norms[k + 1], act_grads, norm_parts))
+    early = {k: norm_sums[k] for k in order[1:-2]}
+    norm_parts, hiddens, act_grads, early = tie((norm_parts, hiddens, act_grads, early))
+    norm_sums.update(early)
 
     def rows_of(blocks):
         return jnp.concatenate([blocks[k] for k in order], 0)
 
     grad_down = left_contract(rows_of(hiddens), rows_of(tops)).astype(bf16)
     sum_down = lax.psum_scatter(grad_down, "dp", scatter_dimension=0, tiled=True).astype(f32)
-    hiddens, grad_down = tie((hiddens, grad_down))
+    hiddens, act_grads, grad_down, norm_sums[order[-2]] = tie(
+        (hiddens, act_grads, grad_down, norm_sums[order[-2]])
+    )
     grad_gate_up = left_contract(rows_of(norms), rows_of(act_grads)).astype(bf16)
     gu_sum = lax.psum_scatter(grad_gate_up, "dp", scatter_dimension=0, tiled=True)
-    hiddens, grad_gate_up = tie((hiddens, grad_gate_up))
-    out_low = {k: dot(hiddens[k], mat_down).astype(bf16) for k in order[1:]}
-    norm_sums, out_low = tie((norm_sums, out_low))
+    out_far = dot(hiddens[last], mat_down).astype(bf16)
+    norm_sums[last], grad_gate_up, out_far, hiddens = tie(
+        (norm_sums[last], grad_gate_up, out_far, hiddens)
+    )
     grad_norm_two = norm_parts[0]
     for k in order[1:]:
         grad_norm_two = grad_norm_two + norm_sums[k].astype(f32)
@@ -328,8 +363,8 @@
         + jnp.pad(term_two, ((0, 0), (0, 2), (0, 0)))
     )
     next_terms = from_behind(grad_ext[:, :2, :], "seq", -1)
-    next_terms, out_low[last] = tie((next_terms, out_low[last]))
-    out_sums = {last: across_seq(out_low[last], last)}
+    next_terms, out_far = tie((next_terms, out_far))
+    out_relay = sum_far(out_far) if n_seq == 4 else ()
     grad_conv_in = (
         grad_ext[:, 2:, :] + jnp.pad(next_terms, ((0, 0), (stretch - 2, 0), (0, 0)))
     ).reshape(rows, width)
@@ -350,7 +385,6 @@
     small_wide = jnp.tile(jnp.pad(small_grads, ((0, own - 5), (0, 0))), (half // own, 1))
     small_wide = jnp.where(row_blocks(core) == feature // own, small_wide, 0.0).astype(bf16)
     in_received = to_sibling(grad_in_other.astype(bf16))
-    in_received, out_sums[last] = tie((in_received, out_sums[last]))
     mixed = jnp.concatenate(
         [
             grad_in_mine + in_received.astype(f32),
@@ -359,22 +393,30 @@
         ],
         1,
     ).astype(bf16)
+    mixed, out_relay, hiddens = tie((mixed, out_relay, hiddens))
     mixed = mixed.reshape(n_z, n_seq, own, -1)
 
     def seq_block(index):
         return lax.dynamic_index_in_dim(mixed, index, 1, keepdims=False)
 
-    seq_parts = [across_seq(seq_block(sq ^ k), k) for k in order[1:]]
     gu_sum = gu_sum.reshape(n_seq, own, 2 * ff_part)
     gu_parts = [across_seq(pick(gu_sum, sq ^ k), k) for k in range(1, n_seq)]
+    seq_terms = {k: seq_block(sq ^ k) for k in near}
+    if n_seq == 4:
+        seq_relay = tie(sum_far(seq_block(sq ^ last)))
+        seq_terms = {k: term.astype(f32) for k, term in seq_terms.items()}
+        seq_terms = {k: term.astype(bf16) for k, term in add_far(seq_terms, seq_relay).items()}
+    seq_parts = [across_seq(seq_terms[k], k) for k in near]
+    out_low = add_far({k: dot(hiddens[k], mat_down) for k in near}, out_relay)
+    out_low = {k: term.astype(bf16) for k, term in out_low.items()}
     seq_parts, gu_parts, out_low, sum_down = tie((seq_parts, gu_parts, out_low, sum_down))
     total = seq_block(sq).astype(f32)
     for part in seq_parts:
         total = total + part.astype(f32)
     low = total.astype(bf16)
+    low, gu_parts = tie((low, gu_parts))
     z_sums = [along_z(pick(low, (z + k) % n_z), k) for k in range(1, n_z)]
-    for k in order[2:]:
-        out_sums[k] = across_seq(out_low[k], k)
+    out_sums = {k: across_seq(out_low[k], k) for k in near}
     gu_sum = seq_ordered([pick(gu_sum, sq)] + gu_parts).astype(f32)
 
     def by_row(part):
@@ -397,7 +439,7 @@
     sum_in, sum_out, small_sum = total[:, :cut_in], total[:, cut_in:cut_out], total[:, cut_out:]
 
     output = middle + out_parts[0]
-    for k in order[1:]:
+    for k in near:
         output = output + out_sums[k].astype(f32)
     output = output.astype(bf16)
 

time: 432 us -> 448 us (1.037)
  matrix products: 142 us -> 124 us
  waiting for transfers between devices: 137 us -> 151 us
  other arithmetic: 48.2 us -> 57.6 us
  local copies, waits for them, and re-layouts: 29.2 us -> 37.8 us
    ppermute x24 -> x29, waiting for transfers between devices: 118 us -> 137 us  [across_seq(): lax.ppermute(block, 'seq', [(i, i ^ by) for i in range(lax.axis_size('seq...]
    dot_general x18 -> x14, matrix products: 57.7 us -> 43.7 us  [dot(): return jnp.dot(first, second, preferred_element_type=f32)]
    slice x0 -> x10, local copies, waits for them, and re-layouts: none -> 7.34 us  [the longest x3 2.19 us: swap_far(): near[2][half:]]
    concatenate x0 -> x7, other arithmetic: none -> 5.6 us  [the longest x2 2.22 us: add_far(): jnp.concatenate([terms[1][:half], terms[1][half:] + second.astype(f32)], 0)]
    ppermute x6, waiting for transfers between devices: 13.9 us -> 9.34 us  [along_z(): lax.ppermute(block, 'dp', [(i, (i + 2 * by) % count) for i in range(count)])]
    ppermute x24 -> x29, starting transfers between devices: 27.3 us -> 29.1 us  [across_seq(): lax.ppermute(block, 'seq', [(i, i ^ by) for i in range(lax.axis_size('seq...]
    unnamed x209 -> x211, local copies, waits for them, and re-layouts: 11.5 us -> 11.9 us
  transfers between devices with their start and end apart: 40 -> 45, of which waited for: 22 -> 24; matrix products, arithmetic and copies ran while one was open for 40% -> 36% of each run, Pallas kernels for 2% -> 2%
where the time goes in v5:
time: 448 us; the launch traced here: 439 us
  waiting for transfers between devices  151 us (34%)
  matrix products  124 us (28%)
  other arithmetic  57.6 us (13%)
  starting transfers between devices  43.8 us (10%)
  local copies, waits for them, and re-layouts  37.8 us (8%)
  between operations  15.8 us (4%)
  Pallas kernels  9.71 us (2%)
    ppermute x29, waiting for transfers between devices, across_seq(): lax.ppermute(block, 'seq', [(i, i ^ by) for i in range(lax.axis_size('seq...  137 us
    dot_general x14, matrix products, dot(): return jnp.dot(first, second, preferred_element_type=f32)  43.7 us
    dot_general x11, matrix products, right_contract(): lax.dot_general(first, second, (((1,), (1,)), ((), ())), preferred_elemen...  42.3 us
    dot_general x6, matrix products, left_contract(): lax.dot_general(first, second, (((0,), (0,)), ((), ())), preferred_elemen...  37.7 us
    ppermute x29, starting transfers between devices, across_seq(): lax.ppermute(block, 'seq', [(i, i ^ by) for i in range(lax.axis_size('seq...  29.1 us
    unnamed x211, local copies, waits for them, and re-layouts  11.9 us
    pallas_call x4, Pallas kernels, place(): pl.pallas_call(kernel, grid=(columns // chunk,), out_shape=jax.ShapeDtype...  9.71 us
    ppermute x6, starting transfers between devices, along_z(): lax.ppermute(block, 'dp', [(i, (i + 2 * by) % count) for i in range(count)])  9.51 us
  transfers between devices with their start and end apart: 45, of which 24 were waited for; matrix products, arithmetic and copies ran while one was open for 36% of the time, Pallas kernels for 2%

profile of v5, /device:TPU:8, one launch (start us, length us, event | category | flops | bytes accessed | tf_op | source)
XLA Modules:
  0.0 439.4 jit_solution(7204006704668617099)
XLA Ops:
  31.5 4.2 collective-permute-start.4
  36.5 3.5 collective-permute-done.4
  45.5 23.2 %collective-permute-done.7.refs_1_ = bf16[4,32,4224]{2,1,0:T(8,128)(2,1)S(1)} collective-permute-done((bf16[4,32,4224]{2,1,0:T(8,128)(2,1)S(1)}, bf16[4,32,4224]{2,1,0:T(8,128)(2,1)S(1)}, u32[]{:S(2)}, u32[]{:S(2)}) %collective-permute-start.7) | collective-permute-done | bytes 1081376 | tf_op jit(solution)/shard_map/ppermute | solution.py:39
  70.2 8.3 %collective-permute-done.10 = bf16[2,32,4224]{2,1,0:T(8,128)(2,1)S(1)} collective-permute-done((bf16[2,32,4224]{2,1,0:T(8,128)(2,1)S(1)}, bf16[2,32,4224]{2,1,0:T(8,128)(2,1)S(1)}, u32[]{:S(2)}, u32[]{:S(2)}) %collective-permute-start.10) | collective-permute-done | bytes 540704 | tf_op jit(solution)/shard_map/ppermute | solution.py:39
  85.4 23.0 %collective-permute-done.12 = bf16[512,1024]{1,0:T(8,128)(2,1)} collective-permute-done((bf16[512,1024]{1,0:T(8,128)(2,1)S(1)}, bf16[512,1024]{1,0:T(8,128)(2,1)}, u32[]{:S(2)}, u32[]{:S(2)}) %collective-permute-start.12) | collective-permute-done | bytes 1048608 | tf_op jit(solution)/shard_map/ppermute | solution.py:39
  114.0 9.2 %collective-permute-done.14 = bf16[256,1024]{1,0:T(8,128)(2,1)S(1)} collective-permute-done((bf16[256,1024]{1,0:T(8,128)(2,1)S(1)}, bf16[256,1024]{1,0:T(8,128)(2,1)S(1)}, u32[]{:S(2)}, u32[]{:S(2)}) %collective-permute-start.14) | collective-permute-done | bytes 524320 | tf_op jit(solution)/shard_map/ppermute | solution.py:39
  128.0 4.1 fusion.39
  132.2 3.9 convolution_add_fusion
  154.3 4.0 shard_map.409
  162.6 7.4 %fusion.175 = f32[512,2304]{1,0:T(8,128)} fusion(bf16[512,1024]{1,0:T(8,128)(2,1)} %multiply_convert_fusion.12, bf16[1024,2304]{1,0:T(8,128)(2,1)} %bitcast.247), kind=kOutput, calls=%fused_computation.348 | convolution fusion | flops 2415919104 | bytes 10485760 | tf_op jit(solution)/shard_map/dot_general | solution.py:73
  169.9 5.8 %multiply_convert_fusion.10 = (bf16[512,1152]{1,0:T(8,128)(2,1)S(1)}, bf16[512,1152]{1,0:T(8,128)(2,1)S(1)}, bf16[512,1152]{1,0:T(8,128)(2,1)S(1)}) fusion(f32[512,2304]{1,0:T(8,128)} %fusion.175, bf16[1152,1024]{1,0:T(8,128)(2,1)} %all-gather.4.cloned.1.call-done, bf16[512,1024]{1,0:T(8,128)(2,1)} %bitcast.217), kind=kOutput, calls=%fused_computation.63 | convolution fusion | flops 1216806912 | bytes 11665408 | tf_op jit(solution)/shard_map/dot_general | solution.py:81
  180.5 4.0 fusion.159
  184.4 3.8 fusion.177
  188.3 3.5 multiply_convert_fusion.8
  199.8 3.8 fusion.178
  205.1 3.5 multiply_convert_fusion.6
  208.7 3.6 convolution_convert_fusion.3
  218.2 14.7 %collective-permute-done.19 = bf16[256,1024]{1,0:T(8,128)(2,1)S(1)} collective-permute-done((bf16[256,1024]{1,0:T(8,128)(2,1)S(1)}, bf16[256,1024]{1,0:T(8,128)(2,1)S(1)}, u32[]{:S(2)}, u32[]{:S(2)}) %collective-permute-start.19) | collective-permute-done | bytes 524320 | tf_op jit(solution)/shard_map/ppermute | solution.py:39
  235.6 3.3 multiply_convert_fusion.4
  240.6 4.1 convolution_convert_fusion.2
  244.7 8.2 %fusion.33 = bf16[1152,1024]{1,0:T(8,128)(2,1)} fusion(bf16[512,1024]{1,0:T(8,128)(2,1)S(1)} %copy-done.29, bf16[512,1024]{1,0:T(8,128)(2,1)} %collective-permute-done.13, bf16[512,1024]{1,0:T(8,128)(2,1)} %collective-permute-done.12, bf16[512,1024]{1,0:T(8,128)(2,1)S(1)} %bitcast.220, bf16[512,1152]{1,0:T(8,128)(2,1)S(1)} %copy-done.99, ...), kind=kOutput, calls=%fused_computation.35 | convolution fusion | flops 4868669440 | bytes 11272192 | tf_op jit(solution)/shard_map/dot_general | solution.py:77
  252.9 16.5 %fusion.8 = bf16[1024,2304]{1,0:T(8,128)(2,1)} fusion(bf16[512,2304]{1,0:T(8,128)(2,1)} %pad_maximum_fusion.5, bf16[512,2304]{1,0:T(8,128)(2,1)} %pad_maximum_fusion.4, bf16[512,2304]{1,0:T(8,128)(2,1)} %pad_maximum_fusion.3, bf16[512,2304]{1,0:T(8,128)(2,1)} %pad_maximum_fusion.2, bf16[512,1024]{1,0:T(8,128)(2,1)} %copy-done.30, ...), kind=kOutput, calls=%fused_computation.9 | convolution fusion | flops 9720561664 | bytes 18350080 | tf_op jit(solution)/shard_map/dot_general | solution.py:77
  270.7 4.7 %convolution_convert_fusion.1 = bf16[512,1024]{1,0:T(8,128)(2,1)} fusion(bf16[512,1152]{1,0:T(8,128)(2,1)} %get-tuple-element.163, bf16[1152,1024]{1,0:T(8,128)(2,1)} %all-gather.4.cloned.1.call-done), kind=kOutput, calls=%fused_computation.114 | convolution fusion | flops 1208483840 | bytes 4587520 | tf_op jit(solution)/shard_map/dot_general | solution.py:73
  275.4 17.7 %collective-permute-done.22 = bf16[512,1024]{1,0:T(8,128)(2,1)S(1)} collective-permute-done((bf16[512,1024]{1,0:T(8,128)(2,1)}, bf16[512,1024]{1,0:T(8,128)(2,1)S(1)}, u32[]{:S(2)}, u32[]{:S(2)}) %collective-permute-start.22) | collective-permute-done | bytes 1048608 | tf_op jit(solution)/shard_map/ppermute | solution.py:39
  293.1 3.2 multiply_reduce_fusion
  308.2 3.5 convolution_convert_fusion
  316.5 8.5 %fusion.57 = (f32[512]{0:T(512)}, f32[1024]{0:T(1024)}, f32[512,1024]{1,0:T(8,128)}) fusion(bf16[2,256,1024]{2,1,0:T(8,128)(2,1)S(1)} %copy-done.12, f32[1024]{0:T(1024)S(1)} %bitcast.231, f32[512]{0:T(512)S(1)} %bitcast.240, bf16[1024,3072]{1,0:T(8,128)(2,1)} %bitcast.196, bf16[512,1024]{1,0:T(8,128)(2,1)S(1)} %copy-done.38, ...), kind=kOutput, calls=%fused_computation.91 | convolution fusion | flops 3234331136 | bytes 12595200 | tf_op jit(solution)/shard_map/dot_general | solution.py:81
  336.6 4.2 add_convert_fusion
  348.1 9.3 %collective-permute-done.29 = bf16[2,32,4224]{2,1,0:T(8,128)(2,1)S(1)} collective-permute-done((bf16[2,32,4224]{2,1,0:T(8,128)(2,1)S(1)}, bf16[2,32,4224]{2,1,0:T(8,128)(2,1)S(1)}, u32[]{:S(2)}, u32[]{:S(2)}) %collective-permute-start.29) | collective-permute-done | bytes 540704 | tf_op jit(solution)/shard_map/ppermute | solution.py:39
  373.3 11.6 %collective-permute-done.32 = bf16[4,32,4224]{2,1,0:T(8,128)(2,1)S(1)} collective-permute-done((bf16[4,32,4224]{2,1,0:T(8,128)(2,1)}, bf16[4,32,4224]{2,1,0:T(8,128)(2,1)S(1)}, u32[]{:S(2)}, u32[]{:S(2)}) %collective-permute-start.32) | collective-permute-done | bytes 1081376 | tf_op jit(solution)/shard_map/ppermute | solution.py:39
  391.9 3.3 fusion.167
  417.0 5.9 %collective-permute-done.38 = bf16[32,4224]{1,0:T(8,128)(2,1)S(1)} collective-permute-done((bf16[32,4224]{1,0:T(8,128)(2,1)S(1)}, bf16[32,4224]{1,0:T(8,128)(2,1)S(1)}, u32[]{:S(2)}, u32[]{:S(2)}) %collective-permute-start.38) | collective-permute-done | bytes 270368 | tf_op jit(solution)/shard_map/ppermute | solution.py:35
  (427 shorter events, 185.9 us)
Async XLA Ops:
  7.2 155.4 %all-gather.6.cloned.1.call-start = ((), (), s32[]{:S(2)}) async-start(), calls=%async_computation.5 | async-start | bytes 5308416 | tf_op jit(solution)/shard_map/all_gather | solution.py:206
  11.3 30.5 %collective-permute-start = (bf16[32,4224]{1,0:T(8,128)(2,1)}, bf16[32,4224]{1,0:T(8,128)(2,1)S(1)}, u32[]{:S(2)}, u32[]{:S(2)}) collective-permute-start(bf16[32,4224]{1,0:T(8,128)(2,1)} %get-tuple-element.301), channel_id=1, source_target_pairs={{0,24},{4,28},{8,0},{12,4},{16,8},{20,12},{24,16},{28,20},{1,25},{... | collective-permute-start | bytes 811016 | tf_op jit(solution)/shard_map/ppermute | solution.py:35
  11.3 30.5 %collective-permute-start.1 = (bf16[32,4224]{1,0:T(8,128)(2,1)}, bf16[32,4224]{1,0:T(8,128)(2,1)S(1)}, u32[]{:S(2)}, u32[]{:S(2)}) collective-permute-start(bf16[32,4224]{1,0:T(8,128)(2,1)} %get-tuple-element.301), channel_id=1, source_target_pairs={{0,16},{4,20},{8,24},{12,28},{16,0},{20,4},{24,8},{28,12},{1,17},{... | collective-permute-start | bytes 811016 | tf_op jit(solution)/shard_map/ppermute | solution.py:35
  14.3 27.5 %collective-permute-start.2 = (bf16[32,4224]{1,0:T(8,128)(2,1)}, bf16[32,4224]{1,0:T(8,128)(2,1)S(1)}, u32[]{:S(2)}, u32[]{:S(2)}) collective-permute-start(bf16[32,4224]{1,0:T(8,128)(2,1)} %get-tuple-element.301), channel_id=1, source_target_pairs={{0,8},{4,12},{8,16},{12,20},{16,24},{20,28},{24,0},{28,4},{1,9},{5... | collective-permute-start | bytes 811016 | tf_op jit(solution)/shard_map/ppermute | solution.py:35
  43.8 126.1 %all-gather.4.cloned.1.call-start = ((), (), s32[]{:S(2)}) async-start(), calls=%async_computation.2 | async-start | bytes 2654208 | tf_op jit(solution)/shard_map/all_gather | solution.py:207
  44.8 23.9 %collective-permute-start.7 = (bf16[4,32,4224]{2,1,0:T(8,128)(2,1)S(1)}, bf16[4,32,4224]{2,1,0:T(8,128)(2,1)S(1)}, u32[]{:S(2)}, u32[]{:S(2)}) collective-permute-start(bf16[4,32,4224]{2,1,0:T(8,128)(2,1)S(1)} %bitcast.197), channel_id=1, source_target_pairs={{0,1},{1,0},{2,3},{3,2},{4,5},{5,4},{6,7},{7,6},{8,9},{9,8},{10,11... | collective-permute-start | bytes 3244040 | tf_op jit(solution)/shard_map/ppermute | solution.py:39
  44.9 23.8 %collective-permute-start.8 = (bf16[4,32,4224]{2,1,0:T(8,128)(2,1)S(1)}, bf16[4,32,4224]{2,1,0:T(8,128)(2,1)S(1)}, u32[]{:S(2)}, u32[]{:S(2)}) collective-permute-start(bf16[4,32,4224]{2,1,0:T(8,128)(2,1)S(1)} %bitcast.198), channel_id=1, source_target_pairs={{0,2},{1,3},{2,0},{3,1},{4,6},{5,7},{6,4},{7,5},{8,10},{9,11},{10,... | collective-permute-start | bytes 3244040 | tf_op jit(solution)/shard_map/ppermute | solution.py:39
  82.8 42.7 %collective-permute-start.11 = (bf16[512,4224]{1,0:T(8,128)(2,1)}, bf16[512,4224]{1,0:T(8,128)(2,1)}, u32[]{:S(2)}, u32[]{:S(2)}) collective-permute-start(bf16[512,4224]{1,0:T(8,128)(2,1)} %bitcast.13), channel_id=1, source_target_pairs={{0,4},{4,0},{8,12},{12,8},{16,20},{20,16},{24,28},{28,24},{1,5},{5... | collective-permute-start | bytes 12976136 | tf_op jit(solution)/shard_map/ppermute | solution.py:30
  82.8 25.7 %collective-permute-start.12 = (bf16[512,1024]{1,0:T(8,128)(2,1)S(1)}, bf16[512,1024]{1,0:T(8,128)(2,1)}, u32[]{:S(2)}, u32[]{:S(2)}) collective-permute-start(bf16[512,1024]{1,0:T(8,128)(2,1)S(1)} %bitcast.218), channel_id=1, source_target_pairs={{0,1},{1,0},{2,3},{3,2},{4,5},{5,4},{6,7},{7,6},{8,9},{9,8},{10,11... | collective-permute-start | bytes 3145736 | tf_op jit(solution)/shard_map/ppermute | solution.py:39
  83.6 26.4 %collective-permute-start.13 = (bf16[512,1024]{1,0:T(8,128)(2,1)S(1)}, bf16[512,1024]{1,0:T(8,128)(2,1)}, u32[]{:S(2)}, u32[]{:S(2)}) collective-permute-start(bf16[512,1024]{1,0:T(8,128)(2,1)S(1)} %bitcast.219), channel_id=1, source_target_pairs={{0,2},{1,3},{2,0},{3,1},{4,6},{5,7},{6,4},{7,5},{8,10},{9,11},{10,... | collective-permute-start | bytes 3145736 | tf_op jit(solution)/shard_map/ppermute | solution.py:39
  84.7 277.9 %reduce-scatter.3.cloned.1.call-start = ((), (), s32[]{:S(2)}) async-start(), calls=%async_computation.3 | async-start | bytes 5308416 | tf_op jit(solution)/shard_map/reduce_scatter | solution.py:335
  151.8 32.6 %collective-permute-start.16 = (bf16[512,1024]{1,0:T(8,128)(2,1)}, bf16[512,1024]{1,0:T(8,128)(2,1)}, u32[]{:S(2)}, u32[]{:S(2)}) collective-permute-start(bf16[512,1024]{1,0:T(8,128)(2,1)} %multiply_convert_fusion.12), channel_id=1, source_target_pairs={{0,1},{1,0},{2,3},{3,2},{4,5},{5,4},{6,7},{7,6},{8,9},{9,8},{10,11... | collective-permute-start | bytes 3145736 | tf_op jit(solution)/shard_map/ppermute | solution.py:39
  152.9 31.6 %collective-permute-start.17 = (bf16[512,1024]{1,0:T(8,128)(2,1)}, bf16[512,1024]{1,0:T(8,128)(2,1)}, u32[]{:S(2)}, u32[]{:S(2)}) collective-permute-start(bf16[512,1024]{1,0:T(8,128)(2,1)} %multiply_convert_fusion.12), channel_id=1, source_target_pairs={{0,2},{1,3},{2,0},{3,1},{4,6},{5,7},{6,4},{7,5},{8,10},{9,11},{10,... | collective-permute-start | bytes 3145736 | tf_op jit(solution)/shard_map/ppermute | solution.py:39
  198.5 46.2 %collective-permute-start.20 = (bf16[512,1024]{1,0:T(8,128)(2,1)S(1)}, bf16[512,1024]{1,0:T(8,128)(2,1)}, u32[]{:S(2)}, u32[]{:S(2)}) collective-permute-start(bf16[512,1024]{1,0:T(8,128)(2,1)S(1)} %convolution_convert_fusion.4), channel_id=1, source_target_pairs={{0,1},{1,0},{2,3},{3,2},{4,5},{5,4},{6,7},{7,6},{8,9},{9,8},{10,11... | collective-permute-start | bytes 3145736 | tf_op jit(solution)/shard_map/ppermute | solution.py:39
  203.6 14.6 %collective-permute-start.18 = (bf16[256,1024]{1,0:T(8,128)(2,1)S(1)}, bf16[256,1024]{1,0:T(8,128)(2,1)S(1)}, u32[]{:S(2)}, u32[]{:S(2)}) collective-permute-start(bf16[256,1024]{1,0:T(8,128)(2,1)S(1)} %slice.356), channel_id=1, source_target_pairs={{0,2},{1,3},{2,0},{3,1},{4,6},{5,7},{6,4},{7,5},{8,10},{9,11},{10,... | collective-permute-start | bytes 1572872 | tf_op jit(solution)/shard_map/ppermute | solution.py:39
  204.1 28.8 %collective-permute-start.19 = (bf16[256,1024]{1,0:T(8,128)(2,1)S(1)}, bf16[256,1024]{1,0:T(8,128)(2,1)S(1)}, u32[]{:S(2)}, u32[]{:S(2)}) collective-permute-start(bf16[256,1024]{1,0:T(8,128)(2,1)S(1)} %slice.357), channel_id=1, source_target_pairs={{0,1},{1,0},{2,3},{3,2},{4,5},{5,4},{6,7},{7,6},{8,9},{9,8},{10,11... | collective-permute-start | bytes 1572872 | tf_op jit(solution)/shard_map/ppermute | solution.py:39
  212.4 40.5 %collective-permute-start.21 = (bf16[512,1024]{1,0:T(8,128)(2,1)}, bf16[512,1024]{1,0:T(8,128)(2,1)}, u32[]{:S(2)}, u32[]{:S(2)}) collective-permute-start(bf16[512,1024]{1,0:T(8,128)(2,1)} %convolution_convert_fusion.3), channel_id=1, source_target_pairs={{0,2},{1,3},{2,0},{3,1},{4,6},{5,7},{6,4},{7,5},{8,10},{9,11},{10,... | collective-permute-start | bytes 3145736 | tf_op jit(solution)/shard_map/ppermute | solution.py:39
  269.4 102.1 %reduce-scatter.5.cloned.1.call-start = ((), (), s32[]{:S(2)}) async-start(), calls=%async_computation.4 | async-start | bytes 2654208 | tf_op jit(solution)/shard_map/reduce_scatter | solution.py:330
  269.6 23.5 %collective-permute-start.22 = (bf16[512,1024]{1,0:T(8,128)(2,1)}, bf16[512,1024]{1,0:T(8,128)(2,1)S(1)}, u32[]{:S(2)}, u32[]{:S(2)}) collective-permute-start(bf16[512,1024]{1,0:T(8,128)(2,1)} %convolution_convert_fusion.2), channel_id=1, source_target_pairs={{0,3},{1,2},{2,1},{3,0},{4,7},{5,6},{6,5},{7,4},{8,11},{9,10},{10,... | collective-permute-start | bytes 3145736 | tf_op jit(solution)/shard_map/ppermute | solution.py:39
  311.7 24.8 %collective-permute-start.24 = (bf16[512,3072]{1,0:T(8,128)(2,1)}, bf16[512,3072]{1,0:T(8,128)(2,1)}, u32[]{:S(2)}, u32[]{:S(2)}) collective-permute-start(bf16[512,3072]{1,0:T(8,128)(2,1)} %convolution_convert_fusion), channel_id=1, source_target_pairs={{0,4},{4,0},{8,12},{12,8},{16,20},{20,16},{24,28},{28,24},{1,5},{5... | collective-permute-start | bytes 9437192 | tf_op jit(solution)/shard_map/ppermute | solution.py:30
  316.4 17.5 %collective-permute-start.25 = (bf16[512,1024]{1,0:T(8,128)(2,1)}, bf16[512,1024]{1,0:T(8,128)(2,1)}, u32[]{:S(2)}, u32[]{:S(2)}) collective-permute-start(bf16[512,1024]{1,0:T(8,128)(2,1)} %convolution_convert_fusion.5), channel_id=1, source_target_pairs={{0,4},{4,0},{8,12},{12,8},{16,20},{20,16},{24,28},{28,24},{1,5},{5... | collective-permute-start | bytes 3145736 | tf_op jit(solution)/shard_map/ppermute | solution.py:30
  328.3 14.3 %collective-permute-start.27 = (bf16[256,1024]{1,0:T(8,128)(2,1)S(1)}, bf16[256,1024]{1,0:T(8,128)(2,1)S(1)}, u32[]{:S(2)}, u32[]{:S(2)}) collective-permute-start(bf16[256,1024]{1,0:T(8,128)(2,1)S(1)} %get-tuple-element.266), channel_id=1, source_target_pairs={{0,1},{1,0},{2,3},{3,2},{4,5},{5,4},{6,7},{7,6},{8,9},{9,8},{10,11... | collective-permute-start | bytes 1572872 | tf_op jit(solution)/shard_map/ppermute | solution.py:39
  359.2 25.6 %collective-permute-start.32 = (bf16[4,32,4224]{2,1,0:T(8,128)(2,1)}, bf16[4,32,4224]{2,1,0:T(8,128)(2,1)S(1)}, u32[]{:S(2)}, u32[]{:S(2)}) collective-permute-start(bf16[4,32,4224]{2,1,0:T(8,128)(2,1)} %pad_maximum_fusion.8), channel_id=1, source_target_pairs={{0,2},{1,3},{2,0},{3,1},{4,6},{5,7},{6,4},{7,5},{8,10},{9,11},{10,... | collective-permute-start | bytes 3244040 | tf_op jit(solution)/shard_map/ppermute | solution.py:39
  360.6 27.1 %collective-permute-start.31 = (bf16[4,32,4224]{2,1,0:T(8,128)(2,1)}, bf16[4,32,4224]{2,1,0:T(8,128)(2,1)}, u32[]{:S(2)}, u32[]{:S(2)}) collective-permute-start(bf16[4,32,4224]{2,1,0:T(8,128)(2,1)} %pad_maximum_fusion.7), channel_id=1, source_target_pairs={{0,1},{1,0},{2,3},{3,2},{4,5},{5,4},{6,7},{7,6},{8,9},{9,8},{10,11... | collective-permute-start | bytes 3244040 | tf_op jit(solution)/shard_map/ppermute | solution.py:39
  364.5 24.9 %collective-permute-start.33 = (bf16[32,2304]{1,0:T(8,128)(2,1)}, bf16[32,2304]{1,0:T(8,128)(2,1)S(1)}, u32[]{:S(2)}, u32[]{:S(2)}) collective-permute-start(bf16[32,2304]{1,0:T(8,128)(2,1)} %get-tuple-element.292), channel_id=1, source_target_pairs={{0,1},{1,0},{2,3},{3,2},{4,5},{5,4},{6,7},{7,6},{8,9},{9,8},{10,11... | collective-permute-start | bytes 442376 | tf_op jit(solution)/shard_map/ppermute | solution.py:39
  364.8 24.6 %collective-permute-start.34 = (bf16[32,2304]{1,0:T(8,128)(2,1)S(1)}, bf16[32,2304]{1,0:T(8,128)(2,1)S(1)}, u32[]{:S(2)}, u32[]{:S(2)}) collective-permute-start(bf16[32,2304]{1,0:T(8,128)(2,1)S(1)} %get-tuple-element.291), channel_id=1, source_target_pairs={{0,2},{1,3},{2,0},{3,1},{4,6},{5,7},{6,4},{7,5},{8,10},{9,11},{10,... | collective-permute-start | bytes 442376 | tf_op jit(solution)/shard_map/ppermute | solution.py:39
  366.5 25.4 %collective-permute-start.35 = (bf16[32,2304]{1,0:T(8,128)(2,1)S(1)}, bf16[32,2304]{1,0:T(8,128)(2,1)}, u32[]{:S(2)}, u32[]{:S(2)}) collective-permute-start(bf16[32,2304]{1,0:T(8,128)(2,1)S(1)} %get-tuple-element.290), channel_id=1, source_target_pairs={{0,3},{1,2},{2,1},{3,0},{4,7},{5,6},{6,5},{7,4},{8,11},{9,10},{10,... | collective-permute-start | bytes 442376 | tf_op jit(solution)/shard_map/ppermute | solution.py:39
  403.9 18.9 %collective-permute-start.38 = (bf16[32,4224]{1,0:T(8,128)(2,1)S(1)}, bf16[32,4224]{1,0:T(8,128)(2,1)S(1)}, u32[]{:S(2)}, u32[]{:S(2)}) collective-permute-start(bf16[32,4224]{1,0:T(8,128)(2,1)S(1)} %get-tuple-element.264), channel_id=1, source_target_pairs={{0,8},{4,12},{8,16},{12,20},{16,24},{20,28},{24,0},{28,4},{1,9},{5... | collective-permute-start | bytes 811016 | tf_op jit(solution)/shard_map/ppermute | solution.py:35
  406.2 19.7 %collective-permute-start.39 = (bf16[32,4224]{1,0:T(8,128)(2,1)S(1)}, bf16[32,4224]{1,0:T(8,128)(2,1)S(1)}, u32[]{:S(2)}, u32[]{:S(2)}) collective-permute-start(bf16[32,4224]{1,0:T(8,128)(2,1)S(1)} %get-tuple-element.263), channel_id=1, source_target_pairs={{0,16},{4,20},{8,24},{12,28},{16,0},{20,4},{24,8},{28,12},{1,17},{... | collective-permute-start | bytes 811016 | tf_op jit(solution)/shard_map/ppermute | solution.py:35
  406.2 20.1 %collective-permute-start.40 = (bf16[32,4224]{1,0:T(8,128)(2,1)S(1)}, bf16[32,4224]{1,0:T(8,128)(2,1)S(1)}, u32[]{:S(2)}, u32[]{:S(2)}) collective-permute-start(bf16[32,4224]{1,0:T(8,128)(2,1)S(1)} %get-tuple-element.262), channel_id=1, source_target_pairs={{0,24},{4,28},{8,0},{12,4},{16,8},{20,12},{24,16},{28,20},{1,25},{... | collective-permute-start | bytes 811016 | tf_op jit(solution)/shard_map/ppermute | solution.py:35
  407.9 22.9 %collective-permute-start.36 = (bf16[512,1024]{1,0:T(8,128)(2,1)}, bf16[512,1024]{1,0:T(8,128)(2,1)S(1)}, u32[]{:S(2)}, u32[]{:S(2)}) collective-permute-start(bf16[512,1024]{1,0:T(8,128)(2,1)} %pad_maximum_fusion.11), channel_id=1, source_target_pairs={{0,1},{1,0},{2,3},{3,2},{4,5},{5,4},{6,7},{7,6},{8,9},{9,8},{10,11... | collective-permute-start | bytes 3145736 | tf_op jit(solution)/shard_map/ppermute | solution.py:39
  409.2 21.6 %collective-permute-start.37 = (bf16[512,1024]{1,0:T(8,128)(2,1)}, bf16[512,1024]{1,0:T(8,128)(2,1)S(1)}, u32[]{:S(2)}, u32[]{:S(2)}) collective-permute-start(bf16[512,1024]{1,0:T(8,128)(2,1)} %pad_maximum_fusion.12), channel_id=1, source_target_pairs={{0,2},{1,3},{2,0},{3,1},{4,6},{5,7},{6,4},{7,5},{8,10},{9,11},{10,... | collective-permute-start | bytes 3145736 | tf_op jit(solution)/shard_map/ppermute | solution.py:39
  (117 other events, 1047.2 us)
Sparse Core Ops, SparseCore 0:
  43.9 48.1 all-gather.5
  94.3 31.4 all-gather.3
  269.5 52.5 reduce-scatter.2
  324.2 34.2 reduce-scatter.4

commit v6 on v5

--- a/solution.py
+++ b/solution.py
@@ -226,7 +226,6 @@
 
     mix_other = to_sibling(mix_mine)
     tops = swap_near(top_out)
-    tops.update(swap_far(tops))
 
     cut_in, cut_out = 3 * width, 4 * width
     in_mine, in_other = mix_mine[:, :cut_in], mix_other[:, :cut_in]
@@ -280,6 +279,8 @@
     tap_two = extended[:, :-2] * near_two
     conv_out = (taps[2] * tap_now + taps[1] * tap_one + taps[0] * tap_two).reshape(rows, width)
     mixed_in = (c_gate * conv_out).astype(bf16)
+    mixed_in, tops = tie((mixed_in, tops))
+    tops.update(swap_far(tops))
     mixed_mine, mixed_other = halves(mixed_in)
     middle = residual + dot(mixed_mine, out_mine) + dot(mixed_other, out_other)
     unit_two, scale_two, norm_two = normed(middle, gain_vals[1])
@@ -313,30 +314,37 @@
     )
     norms.update(swap_far(norms))
     norm_sums = {}
-    for k in order[1:]:
+    for k in order[1:-1]:
         hidden_block(k)
         norm_parts[k] = right_contract(act_grads[k], mat_gate_up).astype(bf16)
         norm_sums[k] = across_seq(norm_parts[k], k)
-        if k != last:
-            norms[k + 1], act_grads, norm_parts = tie((norms[k + 1], act_grads, norm_parts))
+        norms, act_grads, norm_parts = tie((norms, act_grads, norm_parts))
+    hidden_block(last)
+    last_parts = [
+        right_contract(act_grads[last][start : start + rows // 2], mat_gate_up).astype(bf16)
+        for start in (0, rows // 2)
+    ]
+    last_sums = [across_seq(part, last) for part in last_parts]
     early = {k: norm_sums[k] for k in order[1:-2]}
-    norm_parts, hiddens, act_grads, early = tie((norm_parts, hiddens, act_grads, early))
+    out_far = dot(hiddens[last], mat_down).astype(bf16)
+    last_parts, hiddens, act_grads, early, out_far = tie(
+        (last_parts, hiddens, act_grads, early, out_far)
+    )
     norm_sums.update(early)
 
     def rows_of(blocks):
         return jnp.concatenate([blocks[k] for k in order], 0)
 
     grad_down = left_contract(rows_of(hiddens), rows_of(tops)).astype(bf16)
-    sum_down = lax.psum_scatter(grad_down, "dp", scatter_dimension=0, tiled=True).astype(f32)
-    hiddens, act_grads, grad_down, norm_sums[order[-2]] = tie(
-        (hiddens, act_grads, grad_down, norm_sums[order[-2]])
+    hiddens, act_grads, grad_down, norm_sums[order[-2]], last_sums[0] = tie(
+        (hiddens, act_grads, grad_down, norm_sums[order[-2]], last_sums[0])
     )
     grad_gate_up = left_contract(rows_of(norms), rows_of(act_grads)).astype(bf16)
     gu_sum = lax.psum_scatter(grad_gate_up, "dp", scatter_dimension=0, tiled=True)
-    out_far = dot(hiddens[last], mat_down).astype(bf16)
-    norm_sums[last], grad_gate_up, out_far, hiddens = tie(
-        (norm_sums[last], grad_gate_up, out_far, hiddens)
-    )
+    grad_down, grad_gate_up = tie((grad_down, grad_gate_up))
+    sum_down = lax.psum_scatter(grad_down, "dp", scatter_dimension=0, tiled=True)
+    last_sums, grad_gate_up, hiddens = tie((last_sums, grad_gate_up, hiddens))
+    norm_sums[last] = jnp.concatenate(last_sums, 0)
     grad_norm_two = norm_parts[0]
     for k in order[1:]:
         grad_norm_two = grad_norm_two + norm_sums[k].astype(f32)
@@ -393,30 +401,23 @@
         ],
         1,
     ).astype(bf16)
-    mixed, out_relay, hiddens = tie((mixed, out_relay, hiddens))
+    gu_sum = gu_sum.reshape(n_seq, own, 2 * ff_part)
+    gu_parts = [across_seq(pick(gu_sum, sq ^ k), k) for k in range(1, n_seq)]
+    mixed, out_relay = tie((mixed, out_relay))
     mixed = mixed.reshape(n_z, n_seq, own, -1)
 
     def seq_block(index):
         return lax.dynamic_index_in_dim(mixed, index, 1, keepdims=False)
 
-    gu_sum = gu_sum.reshape(n_seq, own, 2 * ff_part)
-    gu_parts = [across_seq(pick(gu_sum, sq ^ k), k) for k in range(1, n_seq)]
     seq_terms = {k: seq_block(sq ^ k) for k in near}
     if n_seq == 4:
-        seq_relay = tie(sum_far(seq_block(sq ^ last)))
+        seq_relay = sum_far(seq_block(sq ^ last))
+        seq_relay, gu_parts, hiddens = tie((seq_relay, gu_parts, hiddens))
         seq_terms = {k: term.astype(f32) for k, term in seq_terms.items()}
         seq_terms = {k: term.astype(bf16) for k, term in add_far(seq_terms, seq_relay).items()}
     seq_parts = [across_seq(seq_terms[k], k) for k in near]
     out_low = add_far({k: dot(hiddens[k], mat_down) for k in near}, out_relay)
     out_low = {k: term.astype(bf16) for k, term in out_low.items()}
-    seq_parts, gu_parts, out_low, sum_down = tie((seq_parts, gu_parts, out_low, sum_down))
-    total = seq_block(sq).astype(f32)
-    for part in seq_parts:
-        total = total + part.astype(f32)
-    low = total.astype(bf16)
-    low, gu_parts = tie((low, gu_parts))
-    z_sums = [along_z(pick(low, (z + k) % n_z), k) for k in range(1, n_z)]
-    out_sums = {k: across_seq(out_low[k], k) for k in near}
     gu_sum = seq_ordered([pick(gu_sum, sq)] + gu_parts).astype(f32)
 
     def by_row(part):
@@ -431,8 +432,14 @@
 
     step_gate = matrix_step(w_gate, m_gate, v_gate, by_row(gu_sum[:, :, :ff_part]))
     step_up = matrix_step(w_up, m_up, v_up, by_row(gu_sum[:, :, ff_part:]))
-    step_down = matrix_step(w_down, m_down, v_down, sum_down)
-    z_sums, step_gate, step_up, step_down = tie((z_sums, step_gate, step_up, step_down))
+    seq_parts, out_low, step_gate, step_up = tie((seq_parts, out_low, step_gate, step_up))
+    total = seq_block(sq).astype(f32)
+    for part in seq_parts:
+        total = total + part.astype(f32)
+    low = total.astype(bf16)
+    low, sum_down = tie((low, sum_down))
+    z_sums = [along_z(pick(low, (z + k) % n_z), k) for k in range(1, n_z)]
+    out_sums = {k: across_seq(out_low[k], k) for k in near}
     total = pick(total, z)
     for part in z_sums:
         total = total + part.astype(f32)
@@ -443,6 +450,7 @@
         output = output + out_sums[k].astype(f32)
     output = output.astype(bf16)
 
+    step_down = matrix_step(w_down, m_down, v_down, sum_down.astype(f32))
     step_in = matrix_step(w_in, m_in, v_in, sum_in)
     step_out = matrix_step(w_out, m_out, v_out, sum_out)
     step_conv = adamw(conv_w, m_conv, v_conv, small_sum[:3, :own], small_rate, 0.0)

time: 448 us -> 416 us (0.929)
  the two profiles are of different devices: /device:TPU:8 before, /device:TPU:0 now
where the time goes in v6:
time: 416 us; the launch traced here: 409 us
  matrix products  128 us (31%)
  waiting for transfers between devices  116 us (28%)
  other arithmetic  55.1 us (13%)
  starting transfers between devices  52.1 us (13%)
  local copies, waits for them, and re-layouts  31.7 us (8%)
  between operations  15.7 us (4%)
  Pallas kernels  9.71 us (2%)
    ppermute x30, waiting for transfers between devices, across_seq(): lax.ppermute(block, 'seq', [(i, i ^ by) for i in range(lax.axis_size('seq...  103 us
    dot_general x12, matrix products, right_contract(): lax.dot_general(first, second, (((1,), (1,)), ((), ())), preferred_elemen...  45.9 us
    dot_general x14, matrix products, dot(): return jnp.dot(first, second, preferred_element_type=f32)  44.3 us
    dot_general x6, matrix products, left_contract(): lax.dot_general(first, second, (((0,), (0,)), ((), ())), preferred_elemen...  38.1 us
    ppermute x30, starting transfers between devices, across_seq(): lax.ppermute(block, 'seq', [(i, i ^ by) for i in range(lax.axis_size('seq...  34.8 us
    ppermute x6, starting transfers between devices, along_z(): lax.ppermute(block, 'dp', [(i, (i + 2 * by) % count) for i in range(count)])  12.8 us
    pallas_call x4, Pallas kernels, place(): pl.pallas_call(kernel, grid=(columns // chunk,), out_shape=jax.ShapeDtype...  9.71 us
    unnamed x193, local copies, waits for them, and re-layouts  9.29 us
  transfers between devices with their start and end apart: 46, of which 28 were waited for; matrix products, arithmetic and copies ran while one was open for 43% of the time, Pallas kernels for 2%

profile of v6, /device:TPU:0, one launch (start us, length us, event | category | flops | bytes accessed | tf_op | source)
XLA Modules:
  0.0 409.1 jit_solution(16340230659210536086)
XLA Ops:
  11.3 5.0 %collective-permute-start = (bf16[32,4224]{1,0:T(8,128)(2,1)}, bf16[32,4224]{1,0:T(8,128)(2,1)S(1)}, u32[]{:S(2)}, u32[]{:S(2)}) collective-permute-start(bf16[32,4224]{1,0:T(8,128)(2,1)} %get-tuple-element.305), channel_id=1, source_target_pairs={{0,24},{4,28},{8,0},{12,4},{16,8},{20,12},{24,16},{28,20},{1,25},{... | collective-permute-start | bytes 811016 | tf_op jit(solution)/shard_map/ppermute | solution.py:35
  32.1 4.2 %collective-permute-start.4 = (bf16[32,2304]{1,0:T(8,128)(2,1)S(1)}, bf16[32,2304]{1,0:T(8,128)(2,1)S(1)}, u32[]{:S(2)}, u32[]{:S(2)}) collective-permute-start(bf16[32,2304]{1,0:T(8,128)(2,1)S(1)} %get-tuple-element.303), channel_id=1, source_target_pairs={{0,2},{1,3},{2,0},{3,1},{4,6},{5,7},{6,4},{7,5},{8,10},{9,11},{10,... | collective-permute-start | bytes 442376 | tf_op jit(solution)/shard_map/ppermute | solution.py:39
  37.0 3.6 collective-permute-done.4
  46.1 21.7 %collective-permute-done.7.refs_1_ = bf16[4,32,4224]{2,1,0:T(8,128)(2,1)S(1)} collective-permute-done((bf16[4,32,4224]{2,1,0:T(8,128)(2,1)S(1)}, bf16[4,32,4224]{2,1,0:T(8,128)(2,1)S(1)}, u32[]{:S(2)}, u32[]{:S(2)}) %collective-permute-start.7) | collective-permute-done | bytes 1081376 | tf_op jit(solution)/shard_map/ppermute | solution.py:39
  70.8 8.6 %collective-permute-done.10 = bf16[2,32,4224]{2,1,0:T(8,128)(2,1)S(1)} collective-permute-done((bf16[2,32,4224]{2,1,0:T(8,128)(2,1)S(1)}, bf16[2,32,4224]{2,1,0:T(8,128)(2,1)S(1)}, u32[]{:S(2)}, u32[]{:S(2)}) %collective-permute-start.10) | collective-permute-done | bytes 540704 | tf_op jit(solution)/shard_map/ppermute | solution.py:39
  91.6 4.0 shard_map.409
  102.6 4.4 %fusion.39 = f32[528,3072]{1,0:T(8,128)S(1)} fusion(bf16[512,4224]{1,0:T(8,128)(2,1)} %bitcast.13, bf16[16,512]{1,0:T(8,128)(2,1)S(1)} %get-tuple-element.313, bf16[512,512]{1,0:T(8,128)(2,1)S(1)} %get-tuple-element.280), kind=kOutput, calls=%fused_computation.38 | convolution fusion | flops 1662025728 | bytes 10174464 | tf_op jit(solution)/shard_map/dot_general | solution.py:73
  107.0 3.9 convolution_add_fusion
  131.8 3.8 collective-permute-done.14
  141.0 7.4 %fusion.183 = f32[512,2304]{1,0:T(8,128)} fusion(bf16[512,1024]{1,0:T(8,128)(2,1)} %multiply_convert_fusion.12, bf16[1024,2304]{1,0:T(8,128)(2,1)} %bitcast.247), kind=kOutput, calls=%fused_computation.358 | convolution fusion | flops 2415919104 | bytes 10485760 | tf_op jit(solution)/shard_map/dot_general | solution.py:73
  148.4 6.0 %multiply_convert_fusion.10 = (bf16[512,1152]{1,0:T(8,128)(2,1)S(1)}, bf16[512,1152]{1,0:T(8,128)(2,1)S(1)}, bf16[512,1152]{1,0:T(8,128)(2,1)S(1)}) fusion(f32[512,2304]{1,0:T(8,128)} %fusion.183, bf16[1152,1024]{1,0:T(8,128)(2,1)} %all-gather.4.cloned.1.call-done, bf16[512,1024]{1,0:T(8,128)(2,1)} %bitcast.12), kind=kOutput, calls=%fused_computation.67 | convolution fusion | flops 1216806912 | bytes 11665408 | tf_op jit(solution)/shard_map/dot_general | solution.py:81
  159.2 4.0 fusion.166
  164.7 3.8 fusion.185
  171.8 3.5 multiply_convert_fusion.8
  181.4 4.7 %collective-permute-done.19 = bf16[256,1024]{1,0:T(8,128)(2,1)S(1)} collective-permute-done((bf16[256,1024]{1,0:T(8,128)(2,1)S(1)}, bf16[256,1024]{1,0:T(8,128)(2,1)S(1)}, u32[]{:S(2)}, u32[]{:S(2)}) %collective-permute-start.19) | collective-permute-done | bytes 524320 | tf_op jit(solution)/shard_map/ppermute | solution.py:39
  186.2 4.2 %fusion.186 = f32[512,2304]{1,0:T(8,128)S(1)} fusion(bf16[512,1024]{1,0:T(8,128)(2,1)} %collective-permute-done.17, bf16[1024,2304]{1,0:T(8,128)(2,1)S(1)} %bitcast.253), kind=kOutput, calls=%fused_computation.361 | convolution fusion | flops 2415919104 | bytes 10485760 | tf_op jit(solution)/shard_map/dot_general | solution.py:73
  190.4 4.0 multiply_convert_fusion.6
  194.4 3.7 convolution_convert_fusion.2
  215.2 8.8 %fusion.33 = bf16[1152,1024]{1,0:T(8,128)(2,1)} fusion(bf16[512,1024]{1,0:T(8,128)(2,1)S(1)} %copy-done.25, bf16[512,1024]{1,0:T(8,128)(2,1)} %collective-permute-done.13, bf16[512,1024]{1,0:T(8,128)(2,1)} %collective-permute-done.12, bf16[512,1024]{1,0:T(8,128)(2,1)} %bitcast.12, bf16[512,1152]{1,0:T(8,128)(2,1)S(1)} %copy-done.88, ...), kind=kOutput, calls=%fused_computation.35 | convolution fusion | flops 4868669440 | bytes 11272192 | tf_op jit(solution)/shard_map/dot_general | solution.py:77
  223.9 6.0 %collective-permute-done.21 = bf16[512,1024]{1,0:T(8,128)(2,1)} collective-permute-done((bf16[512,1024]{1,0:T(8,128)(2,1)}, bf16[512,1024]{1,0:T(8,128)(2,1)}, u32[]{:S(2)}, u32[]{:S(2)}) %collective-permute-start.21) | collective-permute-done | bytes 1048608 | tf_op jit(solution)/shard_map/ppermute | solution.py:39
  230.0 16.4 %fusion.8 = bf16[1024,2304]{1,0:T(8,128)(2,1)} fusion(bf16[512,2304]{1,0:T(8,128)(2,1)} %pad_maximum_fusion.2, bf16[512,2304]{1,0:T(8,128)(2,1)} %pad_maximum_fusion.5, bf16[512,2304]{1,0:T(8,128)(2,1)} %pad_maximum_fusion.4, bf16[512,2304]{1,0:T(8,128)(2,1)} %pad_maximum_fusion.3, bf16[512,1024]{1,0:T(8,128)(2,1)} %copy-done.26, ...), kind=kOutput, calls=%fused_computation.9 | convolution fusion | flops 9720561664 | bytes 18350080 | tf_op jit(solution)/shard_map/dot_general | solution.py:77
  247.6 9.2 %collective-permute-done.23 = bf16[256,1024]{1,0:T(8,128)(2,1)S(1)} collective-permute-done((bf16[256,1024]{1,0:T(8,128)(2,1)}, bf16[256,1024]{1,0:T(8,128)(2,1)S(1)}, u32[]{:S(2)}, u32[]{:S(2)}) %collective-permute-start.23) | collective-permute-done | bytes 524320 | tf_op jit(solution)/shard_map/ppermute | solution.py:39
  256.8 4.6 %multiply_reduce_fusion = (f32[1024]{0:T(1024)}, f32[512]{0:T(512)S(1)}, f32[512,1024]{1,0:T(8,128)S(1)}) fusion(f32[512,1024]{1,0:T(8,128)} %copy-done.4, f32[512]{0:T(512)} %copy-done.58, f32[1024]{0:T(1024)S(1)} %bitcast.227, bf16[256,1024]{1,0:T(8,128)(2,1)S(1)} %collective-permute-done.23, bf16[256,1024]{1,0:T(8,128)(2,1)} %collective-permute-done.22, ...), kind=kLoop, calls=%fused_computation.102 | loop fusion | flops 7862784 | bytes 9449472 | tf_op jit(solution)/shard_map/reduce_sum | solution.py:121
  263.5 4.8 %multiply_reduce_fusion.1 = (f32[1024]{0:T(1024)}, f32[1024]{0:T(1024)}, f32[1024]{0:T(1024)}, f32[512,1024]{1,0:T(8,128)S(1)}, f32[512,1024]{1,0:T(8,128)S(1)}) fusion(f32[2,258,1024]{2,1,0:T(8,128)S(1)} %copy-done.2, f32[2,256]{1,0:T(2,128)S(1)} %copy-done.63, f32[2,256]{1,0:T(2,128)S(1)} %copy-done.61, f32[528,3072]{1,0:T(8,128)} %copy-done.3, ...), kind=kOutput, calls=%fused_computation.103 | convolution fusion | flops 1078981632 | bytes 16793600 | tf_op jit(solution)/shard_map/dot_general | solution.py:81
  276.0 3.5 convolution_convert_fusion
  283.0 9.4 %fusion.57 = (f32[512]{0:T(512)}, f32[1024]{0:T(1024)}, f32[512,1024]{1,0:T(8,128)}) fusion(bf16[2,256,1024]{2,1,0:T(8,128)(2,1)S(1)} %copy-done.12, f32[1024]{0:T(1024)S(1)} %bitcast.231, f32[512]{0:T(512)S(1)} %bitcast.240, bf16[1024,3072]{1,0:T(8,128)(2,1)} %bitcast.197, bf16[512,1024]{1,0:T(8,128)(2,1)} %copy-done.29, bf16[512,1024]{1,0:T(8,128)(2,1)} %copy-done.23, ...), kind=kOutput, calls=%fused_computation.95 | convolution fusion | flops 3234331136 | bytes 12595200 | tf_op jit(solution)/shard_map/dot_general | solution.py:81
  302.9 4.4 %add_convert_fusion = bf16[512,3072]{1,0:T(8,128)(2,1)S(1)} fusion(bf16[512,3072]{1,0:T(8,128)(2,1)} %collective-permute-done.25, bf16[512,512]{1,0:T(8,128)(2,1)S(1)} %copy-done.36, bf16[512,1024]{1,0:T(8,128)(2,1)S(1)} %copy-done.30, bf16[512,1024]{1,0:T(8,128)(2,1)S(1)} %copy-done.24, bf16[512,1024]{1,0:T(8,128)(2,1)S(1)} %copy-done.28), kind=kOutput, calls=%fused_computation.8 | convolution fusion | flops 1624768512 | bytes 9961472 | tf_op jit(solution)/shard_map/dot_general | solution.py:77
  322.5 5.3 %collective-permute-done.30 = bf16[2,32,4224]{2,1,0:T(8,128)(2,1)} collective-permute-done((bf16[2,32,4224]{2,1,0:T(8,128)(2,1)}, bf16[2,32,4224]{2,1,0:T(8,128)(2,1)}, u32[]{:S(2)}, u32[]{:S(2)}) %collective-permute-start.30) | collective-permute-done | bytes 540704 | tf_op jit(solution)/shard_map/ppermute | solution.py:39
  337.8 3.7 fusion.189
  354.4 15.1 %collective-permute-done.36 = bf16[4,32,4224]{2,1,0:T(8,128)(2,1)S(1)} collective-permute-done((bf16[4,32,4224]{2,1,0:T(8,128)(2,1)S(1)}, bf16[4,32,4224]{2,1,0:T(8,128)(2,1)S(1)}, u32[]{:S(2)}, u32[]{:S(2)}) %collective-permute-start.36) | collective-permute-done | bytes 1081376 | tf_op jit(solution)/shard_map/ppermute | solution.py:39
  383.0 7.4 %collective-permute-done.40 = bf16[32,4224]{1,0:T(8,128)(2,1)S(1)} collective-permute-done((bf16[32,4224]{1,0:T(8,128)(2,1)S(1)}, bf16[32,4224]{1,0:T(8,128)(2,1)S(1)}, u32[]{:S(2)}, u32[]{:S(2)}) %collective-permute-start.40) | collective-permute-done | bytes 270368 | tf_op jit(solution)/shard_map/ppermute | solution.py:35
  393.8 5.4 %collective-permute-done.37 = bf16[512,1024]{1,0:T(8,128)(2,1)S(1)} collective-permute-done((bf16[512,1024]{1,0:T(8,128)(2,1)}, bf16[512,1024]{1,0:T(8,128)(2,1)S(1)}, u32[]{:S(2)}, u32[]{:S(2)}) %collective-permute-start.37) | collective-permute-done | bytes 1048608 | tf_op jit(solution)/shard_map/ppermute | solution.py:39
  (412 shorter events, 189.0 us)
Async XLA Ops:
  7.2 133.8 %all-gather.6.cloned.1.call-start = ((), (), s32[]{:S(2)}) async-start(), calls=%async_computation.5 | async-start | bytes 5308416 | tf_op jit(solution)/shard_map/all_gather | solution.py:206
  11.3 31.1 %collective-permute-start = (bf16[32,4224]{1,0:T(8,128)(2,1)}, bf16[32,4224]{1,0:T(8,128)(2,1)S(1)}, u32[]{:S(2)}, u32[]{:S(2)}) collective-permute-start(bf16[32,4224]{1,0:T(8,128)(2,1)} %get-tuple-element.305), channel_id=1, source_target_pairs={{0,24},{4,28},{8,0},{12,4},{16,8},{20,12},{24,16},{28,20},{1,25},{... | collective-permute-start | bytes 811016 | tf_op jit(solution)/shard_map/ppermute | solution.py:35
  16.4 26.0 %collective-permute-start.1 = (bf16[32,4224]{1,0:T(8,128)(2,1)}, bf16[32,4224]{1,0:T(8,128)(2,1)S(1)}, u32[]{:S(2)}, u32[]{:S(2)}) collective-permute-start(bf16[32,4224]{1,0:T(8,128)(2,1)} %get-tuple-element.305), channel_id=1, source_target_pairs={{0,16},{4,20},{8,24},{12,28},{16,0},{20,4},{24,8},{28,12},{1,17},{... | collective-permute-start | bytes 811016 | tf_op jit(solution)/shard_map/ppermute | solution.py:35
  16.4 26.0 %collective-permute-start.2 = (bf16[32,4224]{1,0:T(8,128)(2,1)}, bf16[32,4224]{1,0:T(8,128)(2,1)S(1)}, u32[]{:S(2)}, u32[]{:S(2)}) collective-permute-start(bf16[32,4224]{1,0:T(8,128)(2,1)} %get-tuple-element.305), channel_id=1, source_target_pairs={{0,8},{4,12},{8,16},{12,20},{16,24},{20,28},{24,0},{28,4},{1,9},{5... | collective-permute-start | bytes 811016 | tf_op jit(solution)/shard_map/ppermute | solution.py:35
  44.4 104.0 %all-gather.4.cloned.1.call-start = ((), (), s32[]{:S(2)}) async-start(), calls=%async_computation.2 | async-start | bytes 2654208 | tf_op jit(solution)/shard_map/all_gather | solution.py:207
  45.3 22.5 %collective-permute-start.7 = (bf16[4,32,4224]{2,1,0:T(8,128)(2,1)S(1)}, bf16[4,32,4224]{2,1,0:T(8,128)(2,1)S(1)}, u32[]{:S(2)}, u32[]{:S(2)}) collective-permute-start(bf16[4,32,4224]{2,1,0:T(8,128)(2,1)S(1)} %bitcast.198), channel_id=1, source_target_pairs={{0,1},{1,0},{2,3},{3,2},{4,5},{5,4},{6,7},{7,6},{8,9},{9,8},{10,11... | collective-permute-start | bytes 3244040 | tf_op jit(solution)/shard_map/ppermute | solution.py:39
  45.4 23.1 %collective-permute-start.8 = (bf16[4,32,4224]{2,1,0:T(8,128)(2,1)S(1)}, bf16[4,32,4224]{2,1,0:T(8,128)(2,1)S(1)}, u32[]{:S(2)}, u32[]{:S(2)}) collective-permute-start(bf16[4,32,4224]{2,1,0:T(8,128)(2,1)S(1)} %bitcast.199), channel_id=1, source_target_pairs={{0,2},{1,3},{2,0},{3,1},{4,6},{5,7},{6,4},{7,5},{8,10},{9,11},{10,... | collective-permute-start | bytes 3244040 | tf_op jit(solution)/shard_map/ppermute | solution.py:39
  84.4 229.9 %reduce-scatter.3.cloned.1.call-start = ((), (), s32[]{:S(2)}) async-start(), calls=%async_computation.3 | async-start | bytes 5308416 | tf_op jit(solution)/shard_map/reduce_scatter | solution.py:343
  84.8 35.7 %collective-permute-start.12 = (bf16[512,1024]{1,0:T(8,128)(2,1)}, bf16[512,1024]{1,0:T(8,128)(2,1)}, u32[]{:S(2)}, u32[]{:S(2)}) collective-permute-start(bf16[512,1024]{1,0:T(8,128)(2,1)} %bitcast.12), channel_id=1, source_target_pairs={{0,1},{1,0},{2,3},{3,2},{4,5},{5,4},{6,7},{7,6},{8,9},{9,8},{10,11... | collective-permute-start | bytes 3145736 | tf_op jit(solution)/shard_map/ppermute | solution.py:39
  86.2 34.3 %collective-permute-start.13 = (bf16[512,1024]{1,0:T(8,128)(2,1)}, bf16[512,1024]{1,0:T(8,128)(2,1)}, u32[]{:S(2)}, u32[]{:S(2)}) collective-permute-start(bf16[512,1024]{1,0:T(8,128)(2,1)} %bitcast.12), channel_id=1, source_target_pairs={{0,2},{1,3},{2,0},{3,1},{4,6},{5,7},{6,4},{7,5},{8,10},{9,11},{10,... | collective-permute-start | bytes 3145736 | tf_op jit(solution)/shard_map/ppermute | solution.py:39
  139.3 24.3 %collective-permute-start.16 = (bf16[512,1024]{1,0:T(8,128)(2,1)}, bf16[512,1024]{1,0:T(8,128)(2,1)}, u32[]{:S(2)}, u32[]{:S(2)}) collective-permute-start(bf16[512,1024]{1,0:T(8,128)(2,1)} %multiply_convert_fusion.12), channel_id=1, source_target_pairs={{0,1},{1,0},{2,3},{3,2},{4,5},{5,4},{6,7},{7,6},{8,9},{9,8},{10,11... | collective-permute-start | bytes 3145736 | tf_op jit(solution)/shard_map/ppermute | solution.py:39
  140.6 24.1 %collective-permute-start.17 = (bf16[512,1024]{1,0:T(8,128)(2,1)}, bf16[512,1024]{1,0:T(8,128)(2,1)}, u32[]{:S(2)}, u32[]{:S(2)}) collective-permute-start(bf16[512,1024]{1,0:T(8,128)(2,1)} %multiply_convert_fusion.12), channel_id=1, source_target_pairs={{0,2},{1,3},{2,0},{3,1},{4,6},{5,7},{6,4},{7,5},{8,10},{9,11},{10,... | collective-permute-start | bytes 3145736 | tf_op jit(solution)/shard_map/ppermute | solution.py:39
  171.2 14.9 %collective-permute-start.19 = (bf16[256,1024]{1,0:T(8,128)(2,1)S(1)}, bf16[256,1024]{1,0:T(8,128)(2,1)S(1)}, u32[]{:S(2)}, u32[]{:S(2)}) collective-permute-start(bf16[256,1024]{1,0:T(8,128)(2,1)S(1)} %slice.363), channel_id=1, source_target_pairs={{0,1},{1,0},{2,3},{3,2},{4,5},{5,4},{6,7},{7,6},{8,9},{9,8},{10,11... | collective-permute-start | bytes 1572872 | tf_op jit(solution)/shard_map/ppermute | solution.py:39
  178.0 37.1 %collective-permute-start.20 = (bf16[512,1024]{1,0:T(8,128)(2,1)S(1)}, bf16[512,1024]{1,0:T(8,128)(2,1)}, u32[]{:S(2)}, u32[]{:S(2)}) collective-permute-start(bf16[512,1024]{1,0:T(8,128)(2,1)S(1)} %convolution_convert_fusion.3), channel_id=1, source_target_pairs={{0,1},{1,0},{2,3},{3,2},{4,5},{5,4},{6,7},{7,6},{8,9},{9,8},{10,11... | collective-permute-start | bytes 3145736 | tf_op jit(solution)/shard_map/ppermute | solution.py:39
  199.6 30.3 %collective-permute-start.21 = (bf16[512,1024]{1,0:T(8,128)(2,1)}, bf16[512,1024]{1,0:T(8,128)(2,1)}, u32[]{:S(2)}, u32[]{:S(2)}) collective-permute-start(bf16[512,1024]{1,0:T(8,128)(2,1)} %convolution_convert_fusion.2), channel_id=1, source_target_pairs={{0,2},{1,3},{2,0},{3,1},{4,6},{5,7},{6,4},{7,5},{8,10},{9,11},{10,... | collective-permute-start | bytes 3145736 | tf_op jit(solution)/shard_map/ppermute | solution.py:39
  208.4 15.5 %collective-permute-start.22 = (bf16[256,1024]{1,0:T(8,128)(2,1)}, bf16[256,1024]{1,0:T(8,128)(2,1)}, u32[]{:S(2)}, u32[]{:S(2)}) collective-permute-start(bf16[256,1024]{1,0:T(8,128)(2,1)} %convolution_convert_fusion.6), channel_id=1, source_target_pairs={{0,3},{1,2},{2,1},{3,0},{4,7},{5,6},{6,5},{7,4},{8,11},{9,10},{10,... | collective-permute-start | bytes 1572872 | tf_op jit(solution)/shard_map/ppermute | solution.py:39
  246.4 124.7 %reduce-scatter.5.cloned.1.call-start = ((), (), s32[]{:S(2)}) async-start(), calls=%async_computation.4 | async-start | bytes 2654208 | tf_op jit(solution)/shard_map/reduce_scatter | solution.py:345
  279.5 23.4 %collective-permute-start.25 = (bf16[512,3072]{1,0:T(8,128)(2,1)}, bf16[512,3072]{1,0:T(8,128)(2,1)}, u32[]{:S(2)}, u32[]{:S(2)}) collective-permute-start(bf16[512,3072]{1,0:T(8,128)(2,1)} %convolution_convert_fusion), channel_id=1, source_target_pairs={{0,4},{4,0},{8,12},{12,8},{16,20},{20,16},{24,28},{28,24},{1,5},{5... | collective-permute-start | bytes 9437192 | tf_op jit(solution)/shard_map/ppermute | solution.py:30
  282.5 18.1 %collective-permute-start.26 = (bf16[512,1024]{1,0:T(8,128)(2,1)}, bf16[512,1024]{1,0:T(8,128)(2,1)}, u32[]{:S(2)}, u32[]{:S(2)}) collective-permute-start(bf16[512,1024]{1,0:T(8,128)(2,1)} %convolution_convert_fusion.4), channel_id=1, source_target_pairs={{0,4},{4,0},{8,12},{12,8},{16,20},{20,16},{24,28},{28,24},{1,5},{5... | collective-permute-start | bytes 3145736 | tf_op jit(solution)/shard_map/ppermute | solution.py:30
  295.2 14.4 %collective-permute-start.28 = (bf16[256,1024]{1,0:T(8,128)(2,1)S(1)}, bf16[256,1024]{1,0:T(8,128)(2,1)S(1)}, u32[]{:S(2)}, u32[]{:S(2)}) collective-permute-start(bf16[256,1024]{1,0:T(8,128)(2,1)S(1)} %get-tuple-element.270), channel_id=1, source_target_pairs={{0,1},{1,0},{2,3},{3,2},{4,5},{5,4},{6,7},{7,6},{8,9},{9,8},{10,11... | collective-permute-start | bytes 1572872 | tf_op jit(solution)/shard_map/ppermute | solution.py:39
  296.8 14.0 %collective-permute-start.29 = (bf16[256,1024]{1,0:T(8,128)(2,1)S(1)}, bf16[256,1024]{1,0:T(8,128)(2,1)S(1)}, u32[]{:S(2)}, u32[]{:S(2)}) collective-permute-start(bf16[256,1024]{1,0:T(8,128)(2,1)S(1)} %get-tuple-element.269), channel_id=1, source_target_pairs={{0,2},{1,3},{2,0},{3,1},{4,6},{5,7},{6,4},{7,5},{8,10},{9,11},{10,... | collective-permute-start | bytes 1572872 | tf_op jit(solution)/shard_map/ppermute | solution.py:39
  312.3 15.5 %collective-permute-start.30 = (bf16[2,32,4224]{2,1,0:T(8,128)(2,1)}, bf16[2,32,4224]{2,1,0:T(8,128)(2,1)}, u32[]{:S(2)}, u32[]{:S(2)}) collective-permute-start(bf16[2,32,4224]{2,1,0:T(8,128)(2,1)} %get-tuple-element.258), channel_id=1, source_target_pairs={{0,1},{1,0},{2,3},{3,2},{4,5},{5,4},{6,7},{7,6},{8,9},{9,8},{10,11... | collective-permute-start | bytes 1622024 | tf_op jit(solution)/shard_map/ppermute | solution.py:39
  312.8 15.7 %collective-permute-start.31 = (bf16[2,32,4224]{2,1,0:T(8,128)(2,1)}, bf16[2,32,4224]{2,1,0:T(8,128)(2,1)}, u32[]{:S(2)}, u32[]{:S(2)}) collective-permute-start(bf16[2,32,4224]{2,1,0:T(8,128)(2,1)} %get-tuple-element.260), channel_id=1, source_target_pairs={{0,2},{1,3},{2,0},{3,1},{4,6},{5,7},{6,4},{7,5},{8,10},{9,11},{10,... | collective-permute-start | bytes 1622024 | tf_op jit(solution)/shard_map/ppermute | solution.py:39
  315.5 15.3 %collective-permute-start.32 = (bf16[32,2304]{1,0:T(8,128)(2,1)S(1)}, bf16[32,2304]{1,0:T(8,128)(2,1)S(1)}, u32[]{:S(2)}, u32[]{:S(2)}) collective-permute-start(bf16[32,2304]{1,0:T(8,128)(2,1)S(1)} %get-tuple-element.296), channel_id=1, source_target_pairs={{0,1},{1,0},{2,3},{3,2},{4,5},{5,4},{6,7},{7,6},{8,9},{9,8},{10,11... | collective-permute-start | bytes 442376 | tf_op jit(solution)/shard_map/ppermute | solution.py:39
  316.5 16.4 %collective-permute-start.33 = (bf16[32,2304]{1,0:T(8,128)(2,1)S(1)}, bf16[32,2304]{1,0:T(8,128)(2,1)S(1)}, u32[]{:S(2)}, u32[]{:S(2)}) collective-permute-start(bf16[32,2304]{1,0:T(8,128)(2,1)S(1)} %get-tuple-element.295), channel_id=1, source_target_pairs={{0,2},{1,3},{2,0},{3,1},{4,6},{5,7},{6,4},{7,5},{8,10},{9,11},{10,... | collective-permute-start | bytes 442376 | tf_op jit(solution)/shard_map/ppermute | solution.py:39
  317.6 15.3 %collective-permute-start.34 = (bf16[32,2304]{1,0:T(8,128)(2,1)S(1)}, bf16[32,2304]{1,0:T(8,128)(2,1)S(1)}, u32[]{:S(2)}, u32[]{:S(2)}) collective-permute-start(bf16[32,2304]{1,0:T(8,128)(2,1)S(1)} %get-tuple-element.294), channel_id=1, source_target_pairs={{0,3},{1,2},{2,1},{3,0},{4,7},{5,6},{6,5},{7,4},{8,11},{9,10},{10,... | collective-permute-start | bytes 442376 | tf_op jit(solution)/shard_map/ppermute | solution.py:39
  345.4 24.1 %collective-permute-start.36 = (bf16[4,32,4224]{2,1,0:T(8,128)(2,1)S(1)}, bf16[4,32,4224]{2,1,0:T(8,128)(2,1)S(1)}, u32[]{:S(2)}, u32[]{:S(2)}) collective-permute-start(bf16[4,32,4224]{2,1,0:T(8,128)(2,1)S(1)} %pad_maximum_fusion.8), channel_id=1, source_target_pairs={{0,2},{1,3},{2,0},{3,1},{4,6},{5,7},{6,4},{7,5},{8,10},{9,11},{10,... | collective-permute-start | bytes 3244040 | tf_op jit(solution)/shard_map/ppermute | solution.py:39
  346.9 23.8 %collective-permute-start.35 = (bf16[4,32,4224]{2,1,0:T(8,128)(2,1)S(1)}, bf16[4,32,4224]{2,1,0:T(8,128)(2,1)S(1)}, u32[]{:S(2)}, u32[]{:S(2)}) collective-permute-start(bf16[4,32,4224]{2,1,0:T(8,128)(2,1)S(1)} %pad_maximum_fusion.7), channel_id=1, source_target_pairs={{0,1},{1,0},{2,3},{3,2},{4,5},{5,4},{6,7},{7,6},{8,9},{9,8},{10,11... | collective-permute-start | bytes 3244040 | tf_op jit(solution)/shard_map/ppermute | solution.py:39
  372.5 17.9 %collective-permute-start.40 = (bf16[32,4224]{1,0:T(8,128)(2,1)S(1)}, bf16[32,4224]{1,0:T(8,128)(2,1)S(1)}, u32[]{:S(2)}, u32[]{:S(2)}) collective-permute-start(bf16[32,4224]{1,0:T(8,128)(2,1)S(1)} %get-tuple-element.268), channel_id=1, source_target_pairs={{0,16},{4,20},{8,24},{12,28},{16,0},{20,4},{24,8},{28,12},{1,17},{... | collective-permute-start | bytes 811016 | tf_op jit(solution)/shard_map/ppermute | solution.py:35
  375.1 15.3 %collective-permute-start.41 = (bf16[32,4224]{1,0:T(8,128)(2,1)S(1)}, bf16[32,4224]{1,0:T(8,128)(2,1)S(1)}, u32[]{:S(2)}, u32[]{:S(2)}) collective-permute-start(bf16[32,4224]{1,0:T(8,128)(2,1)S(1)} %get-tuple-element.267), channel_id=1, source_target_pairs={{0,24},{4,28},{8,0},{12,4},{16,8},{20,12},{24,16},{28,20},{1,25},{... | collective-permute-start | bytes 811016 | tf_op jit(solution)/shard_map/ppermute | solution.py:35
  378.0 21.2 %collective-permute-start.37 = (bf16[512,1024]{1,0:T(8,128)(2,1)}, bf16[512,1024]{1,0:T(8,128)(2,1)S(1)}, u32[]{:S(2)}, u32[]{:S(2)}) collective-permute-start(bf16[512,1024]{1,0:T(8,128)(2,1)} %pad_maximum_fusion.11), channel_id=1, source_target_pairs={{0,1},{1,0},{2,3},{3,2},{4,5},{5,4},{6,7},{7,6},{8,9},{9,8},{10,11... | collective-permute-start | bytes 3145736 | tf_op jit(solution)/shard_map/ppermute | solution.py:39
  379.4 21.3 %collective-permute-start.38 = (bf16[512,1024]{1,0:T(8,128)(2,1)}, bf16[512,1024]{1,0:T(8,128)(2,1)S(1)}, u32[]{:S(2)}, u32[]{:S(2)}) collective-permute-start(bf16[512,1024]{1,0:T(8,128)(2,1)} %pad_maximum_fusion.12), channel_id=1, source_target_pairs={{0,2},{1,3},{2,0},{3,1},{4,6},{5,7},{6,4},{7,5},{8,10},{9,11},{10,... | collective-permute-start | bytes 3145736 | tf_op jit(solution)/shard_map/ppermute | solution.py:39
  (109 other events, 820.8 us)
Sparse Core Ops, SparseCore 0:
  44.5 50.6 all-gather.5
  97.4 30.4 all-gather.3
  246.5 55.0 reduce-scatter.2
  303.8 34.5 reduce-scatter.4

commit v7 on v6

--- a/solution.py
+++ b/solution.py
@@ -285,10 +285,6 @@
     middle = residual + dot(mixed_mine, out_mine) + dot(mixed_other, out_other)
     unit_two, scale_two, norm_two = normed(middle, gain_vals[1])
 
-    both_halves = [mix_mine.reshape(n_z, -1, columns), mix_other.reshape(n_z, -1, columns)]
-    in_full = place(both_halves, core_slots, width, 0, cut_in).reshape(width, cut_in)
-    out_full = place(both_halves, core_slots, width, cut_in, width).reshape(width, width)
-
     norm_two, tops = tie((norm_two, tops))
     tops[0] = grad_top
     norms = swap_near(norm_two)
@@ -309,16 +305,27 @@
     hidden_block(0)
     norm_parts[0] = right_contract(act_grads[0], mat_gate_up)
     out_parts[0] = dot(hiddens[0], mat_down)
-    norms, hiddens, act_grads, norm_parts, out_parts, in_full, out_full = tie(
-        (norms, hiddens, act_grads, norm_parts, out_parts, in_full, out_full)
+    norms, hiddens, act_grads, norm_parts, out_parts = tie(
+        (norms, hiddens, act_grads, norm_parts, out_parts)
     )
     norms.update(swap_far(norms))
     norm_sums = {}
     for k in order[1:-1]:
         hidden_block(k)
         norm_parts[k] = right_contract(act_grads[k], mat_gate_up).astype(bf16)
+        if k == 1:
+            norm_parts, mix_mine, mix_other = tie((norm_parts, mix_mine, mix_other))
+            both_halves = [
+                mix_mine.reshape(n_z, -1, columns),
+                mix_other.reshape(n_z, -1, columns),
+            ]
+            in_full = place(both_halves, core_slots, width, 0, cut_in).reshape(width, cut_in)
+            out_full = place(both_halves, core_slots, width, cut_in, width).reshape(width, width)
+            out_parts[1] = dot(hiddens[1], mat_down)
+        norms, act_grads, norm_parts, out_parts, in_full, out_full = tie(
+            (norms, act_grads, norm_parts, out_parts, in_full, out_full)
+        )
         norm_sums[k] = across_seq(norm_parts[k], k)
-        norms, act_grads, norm_parts = tie((norms, act_grads, norm_parts))
     hidden_block(last)
     last_parts = [
         right_contract(act_grads[last][start : start + rows // 2], mat_gate_up).astype(bf16)
@@ -336,14 +343,14 @@
         return jnp.concatenate([blocks[k] for k in order], 0)
 
     grad_down = left_contract(rows_of(hiddens), rows_of(tops)).astype(bf16)
-    hiddens, act_grads, grad_down, norm_sums[order[-2]], last_sums[0] = tie(
-        (hiddens, act_grads, grad_down, norm_sums[order[-2]], last_sums[0])
+    out_parts.update({k: dot(hiddens[k], mat_down) for k in near[1:]})
+    out_parts, act_grads, grad_down, norm_sums[order[-2]], last_sums[0] = tie(
+        (out_parts, act_grads, grad_down, norm_sums[order[-2]], last_sums[0])
     )
     grad_gate_up = left_contract(rows_of(norms), rows_of(act_grads)).astype(bf16)
+    last_sums, grad_gate_up, grad_down = tie((last_sums, grad_gate_up, grad_down))
     gu_sum = lax.psum_scatter(grad_gate_up, "dp", scatter_dimension=0, tiled=True)
-    grad_down, grad_gate_up = tie((grad_down, grad_gate_up))
     sum_down = lax.psum_scatter(grad_down, "dp", scatter_dimension=0, tiled=True)
-    last_sums, grad_gate_up, hiddens = tie((last_sums, grad_gate_up, hiddens))
     norm_sums[last] = jnp.concatenate(last_sums, 0)
     grad_norm_two = norm_parts[0]
     for k in order[1:]:
@@ -389,7 +396,8 @@
         return mine + to_sibling(other.astype(bf16)).astype(f32)
 
     small_grads = jnp.stack(grad_taps + [gain_one, gain_two], 0)
-    small_grads = (small_grads + to_sibling(small_grads)).astype(bf16)
+    small_received, out_relay = tie((to_sibling(small_grads), out_relay))
+    small_grads = (small_grads + small_received).astype(bf16)
     small_wide = jnp.tile(jnp.pad(small_grads, ((0, own - 5), (0, 0))), (half // own, 1))
     small_wide = jnp.where(row_blocks(core) == feature // own, small_wide, 0.0).astype(bf16)
     in_received = to_sibling(grad_in_other.astype(bf16))
@@ -403,7 +411,6 @@
     ).astype(bf16)
     gu_sum = gu_sum.reshape(n_seq, own, 2 * ff_part)
     gu_parts = [across_seq(pick(gu_sum, sq ^ k), k) for k in range(1, n_seq)]
-    mixed, out_relay = tie((mixed, out_relay))
     mixed = mixed.reshape(n_z, n_seq, own, -1)
 
     def seq_block(index):
@@ -412,13 +419,13 @@
     seq_terms = {k: seq_block(sq ^ k) for k in near}
     if n_seq == 4:
         seq_relay = sum_far(seq_block(sq ^ last))
-        seq_relay, gu_parts, hiddens = tie((seq_relay, gu_parts, hiddens))
+        seq_relay, gu_parts = tie((seq_relay, gu_parts))
         seq_terms = {k: term.astype(f32) for k, term in seq_terms.items()}
         seq_terms = {k: term.astype(bf16) for k, term in add_far(seq_terms, seq_relay).items()}
     seq_parts = [across_seq(seq_terms[k], k) for k in near]
-    out_low = add_far({k: dot(hiddens[k], mat_down) for k in near}, out_relay)
+    out_low = add_far({k: out_parts[k] for k in near}, out_relay)
     out_low = {k: term.astype(bf16) for k, term in out_low.items()}
-    gu_sum = seq_ordered([pick(gu_sum, sq)] + gu_parts).astype(f32)
+    gu_sum = seq_ordered([pick(gu_sum, sq)] + gu_parts)
 
     def by_row(part):
         return (
@@ -430,9 +437,8 @@
     def matrix_step(master, first, second, grad):
         return adamw(master, first, second, grad, learn_rate, weight_decay)
 
-    step_gate = matrix_step(w_gate, m_gate, v_gate, by_row(gu_sum[:, :, :ff_part]))
-    step_up = matrix_step(w_up, m_up, v_up, by_row(gu_sum[:, :, ff_part:]))
-    seq_parts, out_low, step_gate, step_up = tie((seq_parts, out_low, step_gate, step_up))
+    gate_rows, up_rows = by_row(gu_sum[:, :, :ff_part]), by_row(gu_sum[:, :, ff_part:])
+    seq_parts, out_low, gate_rows, up_rows = tie((seq_parts, out_low, gate_rows, up_rows))
     total = seq_block(sq).astype(f32)
     for part in seq_parts:
         total = total + part.astype(f32)
@@ -440,6 +446,9 @@
     low, sum_down = tie((low, sum_down))
     z_sums = [along_z(pick(low, (z + k) % n_z), k) for k in range(1, n_z)]
     out_sums = {k: across_seq(out_low[k], k) for k in near}
+    step_gate = matrix_step(w_gate, m_gate, v_gate, gate_rows.astype(f32))
+    step_up = matrix_step(w_up, m_up, v_up, up_rows.astype(f32))
+    z_sums, step_gate, step_up = tie((z_sums, step_gate, step_up))
     total = pick(total, z)
     for part in z_sums:
         total = total + part.astype(f32)

time: 416 us -> 429 us (1.031)
  waiting for transfers between devices: 116 us -> 125 us
  matrix products: 128 us -> 122 us
  local copies, waits for them, and re-layouts: 31.7 us -> 36 us
    ppermute x30, waiting for transfers between devices: 103 us -> 117 us  [across_seq(): lax.ppermute(block, 'seq', [(i, i ^ by) for i in range(lax.axis_size('seq...]
    dot_general x12, matrix products: 45.9 us -> 39.4 us  [right_contract(): lax.dot_general(first, second, (((1,), (1,)), ((), ())), preferred_elemen...]
    unnamed x193 -> x191, local copies, waits for them, and re-layouts: 9.29 us -> 12.6 us
  transfers between devices with their start and end apart: 46 -> 46, of which waited for: 28 -> 26; matrix products, arithmetic and copies ran while one was open for 43% -> 42% of each run, Pallas kernels for 2% -> 2%
where the time goes in v7:
time: 429 us; the launch traced here: 423 us
  waiting for transfers between devices  125 us (29%)
  matrix products  122 us (28%)
  other arithmetic  58.5 us (14%)
  starting transfers between devices  56.3 us (13%)
  local copies, waits for them, and re-layouts  36 us (8%)
  between operations  16 us (4%)
  Pallas kernels  9.81 us (2%)
    ppermute x30, waiting for transfers between devices, across_seq(): lax.ppermute(block, 'seq', [(i, i ^ by) for i in range(lax.axis_size('seq...  117 us
    dot_general x14, matrix products, dot(): return jnp.dot(first, second, preferred_element_type=f32)  45.8 us
    dot_general x12, matrix products, right_contract(): lax.dot_general(first, second, (((1,), (1,)), ((), ())), preferred_elemen...  39.4 us
    ppermute x30, starting transfers between devices, across_seq(): lax.ppermute(block, 'seq', [(i, i ^ by) for i in range(lax.axis_size('seq...  38.6 us
    dot_general x6, matrix products, left_contract(): lax.dot_general(first, second, (((0,), (0,)), ((), ())), preferred_elemen...  36.5 us
    unnamed x191, local copies, waits for them, and re-layouts  12.6 us
    ppermute x6, starting transfers between devices, along_z(): lax.ppermute(block, 'dp', [(i, (i + 2 * by) % count) for i in range(count)])  12.2 us
    pallas_call x4, Pallas kernels, place(): pl.pallas_call(kernel, grid=(columns // chunk,), out_shape=jax.ShapeDtype...  9.81 us
  transfers between devices with their start and end apart: 46, of which 26 were waited for; matrix products, arithmetic and copies ran while one was open for 42% of the time, Pallas kernels for 2%

profile of v7, /device:TPU:0, one launch (start us, length us, event | category | flops | bytes accessed | tf_op | source)
XLA Modules:
  0.0 423.2 jit_solution(3173015634472229562)
XLA Ops:
  11.3 5.0 %collective-permute-start = (bf16[32,4224]{1,0:T(8,128)(2,1)}, bf16[32,4224]{1,0:T(8,128)(2,1)S(1)}, u32[]{:S(2)}, u32[]{:S(2)}) collective-permute-start(bf16[32,4224]{1,0:T(8,128)(2,1)} %get-tuple-element.335), channel_id=1, source_target_pairs={{0,24},{4,28},{8,0},{12,4},{16,8},{20,12},{24,16},{28,20},{1,25},{... | collective-permute-start | bytes 811016 | tf_op jit(solution)/shard_map/ppermute | solution.py:35
  32.1 4.2 collective-permute-start.4
  37.0 3.6 collective-permute-done.4
  46.1 21.7 %collective-permute-done.7.refs_1_ = bf16[4,32,4224]{2,1,0:T(8,128)(2,1)S(1)} collective-permute-done((bf16[4,32,4224]{2,1,0:T(8,128)(2,1)S(1)}, bf16[4,32,4224]{2,1,0:T(8,128)(2,1)S(1)}, u32[]{:S(2)}, u32[]{:S(2)}) %collective-permute-start.7) | collective-permute-done | bytes 1081376 | tf_op jit(solution)/shard_map/ppermute | solution.py:39
  70.8 8.6 %collective-permute-done.10 = bf16[2,32,4224]{2,1,0:T(8,128)(2,1)S(1)} collective-permute-done((bf16[2,32,4224]{2,1,0:T(8,128)(2,1)S(1)}, bf16[2,32,4224]{2,1,0:T(8,128)(2,1)S(1)}, u32[]{:S(2)}, u32[]{:S(2)}) %collective-permute-start.10) | collective-permute-done | bytes 540704 | tf_op jit(solution)/shard_map/ppermute | solution.py:39
  94.2 4.1 fusion.39
  98.4 3.9 convolution_add_fusion
  121.2 5.1 %collective-permute-done.14 = bf16[256,1024]{1,0:T(8,128)(2,1)S(1)} collective-permute-done((bf16[256,1024]{1,0:T(8,128)(2,1)S(1)}, bf16[256,1024]{1,0:T(8,128)(2,1)S(1)}, u32[]{:S(2)}, u32[]{:S(2)}) %collective-permute-start.14) | collective-permute-done | bytes 524320 | tf_op jit(solution)/shard_map/ppermute | solution.py:39
  131.8 6.7 %fusion.194 = f32[512,2304]{1,0:T(8,128)} fusion(bf16[512,1024]{1,0:T(8,128)(2,1)S(1)} %multiply_convert_fusion.12, bf16[1024,2304]{1,0:T(8,128)(2,1)} %bitcast.252), kind=kOutput, calls=%fused_computation.376 | convolution fusion | flops 2415919104 | bytes 10485760 | tf_op jit(solution)/shard_map/dot_general | solution.py:73
  138.5 5.5 %multiply_convert_fusion.10 = (bf16[512,1152]{1,0:T(8,128)(2,1)S(1)}, bf16[512,1152]{1,0:T(8,128)(2,1)S(1)}, bf16[512,1152]{1,0:T(8,128)(2,1)S(1)}) fusion(f32[512,2304]{1,0:T(8,128)} %fusion.194, bf16[1152,1024]{1,0:T(8,128)(2,1)} %all-gather.4.cloned.1.call-done, bf16[512,1024]{1,0:T(8,128)(2,1)S(1)} %bitcast.223), kind=kOutput, calls=%fused_computation.65 | convolution fusion | flops 1216806912 | bytes 11665408 | tf_op jit(solution)/shard_map/dot_general | solution.py:81
  148.5 4.0 fusion.175
  155.4 3.8 fusion.196
  172.4 4.0 shard_map.409
  180.8 4.2 fusion.198
  185.0 4.5 %multiply_convert_fusion.5 = (bf16[512,1152]{1,0:T(8,128)(2,1)S(1)}, bf16[512,1152]{1,0:T(8,128)(2,1)S(1)}, bf16[512,1152]{1,0:T(8,128)(2,1)}) fusion(f32[512,2304]{1,0:T(8,128)S(1)} %fusion.198, bf16[512,1024]{1,0:T(8,128)(2,1)} %collective-permute-done.13, bf16[1152,1024]{1,0:T(8,128)(2,1)S(1)} %copy-done.86), kind=kOutput, calls=%fused_computation.56 | convolution fusion | flops 1216806912 | bytes 11665408 | tf_op jit(solution)/shard_map/dot_general | solution.py:81
  189.5 3.6 convolution_convert_fusion.2
  214.3 6.6 %collective-permute-done.20 = bf16[512,1024]{1,0:T(8,128)(2,1)S(1)} collective-permute-done((bf16[512,1024]{1,0:T(8,128)(2,1)S(1)}, bf16[512,1024]{1,0:T(8,128)(2,1)S(1)}, u32[]{:S(2)}, u32[]{:S(2)}) %collective-permute-start.20) | collective-permute-done | bytes 1048608 | tf_op jit(solution)/shard_map/ppermute | solution.py:39
  220.9 7.9 %fusion.33 = bf16[1152,1024]{1,0:T(8,128)(2,1)} fusion(bf16[512,1024]{1,0:T(8,128)(2,1)S(1)} %copy-done.30, bf16[512,1024]{1,0:T(8,128)(2,1)} %collective-permute-done.13, bf16[512,1024]{1,0:T(8,128)(2,1)S(1)} %copy-done.50, bf16[512,1024]{1,0:T(8,128)(2,1)S(1)} %bitcast.224, bf16[512,1152]{1,0:T(8,128)(2,1)S(1)} %copy-done.89, ...), kind=kOutput, calls=%fused_computation.35 | convolution fusion | flops 4868669440 | bytes 11272192 | tf_op jit(solution)/shard_map/dot_general | solution.py:77
  228.8 4.9 %fusion.200 = f32[512,1024]{1,0:T(8,128)} fusion(bf16[512,1152]{1,0:T(8,128)(2,1)} %get-tuple-element.181, bf16[1152,1024]{1,0:T(8,128)(2,1)} %all-gather.4.cloned.1.call-done), kind=kOutput, calls=%fused_computation.382 | convolution fusion | flops 1207959552 | bytes 5636096 | tf_op jit(solution)/shard_map/dot_general | solution.py:73
  233.7 18.4 %collective-permute-done.21 = bf16[512,1024]{1,0:T(8,128)(2,1)} collective-permute-done((bf16[512,1024]{1,0:T(8,128)(2,1)}, bf16[512,1024]{1,0:T(8,128)(2,1)}, u32[]{:S(2)}, u32[]{:S(2)}) %collective-permute-start.21) | collective-permute-done | bytes 1048608 | tf_op jit(solution)/shard_map/ppermute | solution.py:39
  252.1 16.8 %fusion.8 = bf16[1024,2304]{1,0:T(8,128)(2,1)} fusion(bf16[512,2304]{1,0:T(8,128)(2,1)} %pad_maximum_fusion.2, bf16[512,2304]{1,0:T(8,128)(2,1)} %pad_maximum_fusion.5, bf16[512,2304]{1,0:T(8,128)(2,1)} %pad_maximum_fusion.4, bf16[512,2304]{1,0:T(8,128)(2,1)} %pad_maximum_fusion.3, bf16[512,1024]{1,0:T(8,128)(2,1)} %copy-done.31, ...), kind=kOutput, calls=%fused_computation.9 | convolution fusion | flops 9720561664 | bytes 18350080 | tf_op jit(solution)/shard_map/dot_general | solution.py:77
  269.0 4.0 multiply_reduce_fusion
  274.6 4.2 multiply_reduce_fusion.1
  293.5 3.6 convolution_convert_fusion
  297.6 5.0 %fusion.56 = (f32[512]{0:T(512)S(1)}, f32[1024]{0:T(1024)S(1)}, f32[512,1024]{1,0:T(8,128)}) fusion(bf16[2,256,1024]{2,1,0:T(8,128)(2,1)S(1)} %copy-done.13, f32[1024]{0:T(1024)S(1)} %bitcast.236, f32[512]{0:T(512)S(1)} %bitcast.245, bf16[1024,3072]{1,0:T(8,128)(2,1)S(1)} %bitcast.204, bf16[512,1024]{1,0:T(8,128)(2,1)S(1)} %get-tuple-element.272, ...), kind=kOutput, calls=%fused_computation.92 | convolution fusion | flops 3234331136 | bytes 12595200 | tf_op jit(solution)/shard_map/dot_general | solution.py:81
  308.0 3.6 fusion.59
  311.6 7.8 %collective-permute-done.28 = bf16[256,1024]{1,0:T(8,128)(2,1)S(1)} collective-permute-done((bf16[256,1024]{1,0:T(8,128)(2,1)S(1)}, bf16[256,1024]{1,0:T(8,128)(2,1)S(1)}, u32[]{:S(2)}, u32[]{:S(2)}) %collective-permute-start.28) | collective-permute-done | bytes 524320 | tf_op jit(solution)/shard_map/ppermute | solution.py:39
  325.0 4.2 %add_convert_fusion = bf16[512,3072]{1,0:T(8,128)(2,1)S(1)} fusion(bf16[512,3072]{1,0:T(8,128)(2,1)} %collective-permute-done.25, bf16[512,512]{1,0:T(8,128)(2,1)S(1)} %copy-done.44, bf16[512,1024]{1,0:T(8,128)(2,1)S(1)} %copy-done.38, bf16[512,1024]{1,0:T(8,128)(2,1)S(1)} %copy-done.28, bf16[512,1024]{1,0:T(8,128)(2,1)S(1)} %copy-done.36), kind=kOutput, calls=%fused_computation.8 | convolution fusion | flops 1624768512 | bytes 9961472 | tf_op jit(solution)/shard_map/dot_general | solution.py:77
  342.6 5.8 %collective-permute-done.30 = bf16[2,32,4224]{2,1,0:T(8,128)(2,1)} collective-permute-done((bf16[2,32,4224]{2,1,0:T(8,128)(2,1)}, bf16[2,32,4224]{2,1,0:T(8,128)(2,1)}, u32[]{:S(2)}, u32[]{:S(2)}) %collective-permute-start.30) | collective-permute-done | bytes 540704 | tf_op jit(solution)/shard_map/ppermute | solution.py:39
  364.8 16.9 %collective-permute-done.36 = bf16[4,32,4224]{2,1,0:T(8,128)(2,1)S(1)} collective-permute-done((bf16[4,32,4224]{2,1,0:T(8,128)(2,1)}, bf16[4,32,4224]{2,1,0:T(8,128)(2,1)S(1)}, u32[]{:S(2)}, u32[]{:S(2)}) %collective-permute-start.36) | collective-permute-done | bytes 1081376 | tf_op jit(solution)/shard_map/ppermute | solution.py:39
  400.7 4.3 %collective-permute-done.40 = bf16[32,4224]{1,0:T(8,128)(2,1)S(1)} collective-permute-done((bf16[32,4224]{1,0:T(8,128)(2,1)S(1)}, bf16[32,4224]{1,0:T(8,128)(2,1)S(1)}, u32[]{:S(2)}, u32[]{:S(2)}) %collective-permute-start.40) | collective-permute-done | bytes 270368 | tf_op jit(solution)/shard_map/ppermute | solution.py:35
  408.4 5.1 %collective-permute-done.37 = bf16[512,1024]{1,0:T(8,128)(2,1)S(1)} collective-permute-done((bf16[512,1024]{1,0:T(8,128)(2,1)}, bf16[512,1024]{1,0:T(8,128)(2,1)S(1)}, u32[]{:S(2)}, u32[]{:S(2)}) %collective-permute-start.37) | collective-permute-done | bytes 1048608 | tf_op jit(solution)/shard_map/ppermute | solution.py:39
  (409 shorter events, 195.8 us)
Async XLA Ops:
  7.2 124.6 %all-gather.6.cloned.1.call-start = ((), (), s32[]{:S(2)}) async-start(), calls=%async_computation.5 | async-start | bytes 5308416 | tf_op jit(solution)/shard_map/all_gather | solution.py:206
  11.3 31.1 %collective-permute-start = (bf16[32,4224]{1,0:T(8,128)(2,1)}, bf16[32,4224]{1,0:T(8,128)(2,1)S(1)}, u32[]{:S(2)}, u32[]{:S(2)}) collective-permute-start(bf16[32,4224]{1,0:T(8,128)(2,1)} %get-tuple-element.335), channel_id=1, source_target_pairs={{0,24},{4,28},{8,0},{12,4},{16,8},{20,12},{24,16},{28,20},{1,25},{... | collective-permute-start | bytes 811016 | tf_op jit(solution)/shard_map/ppermute | solution.py:35
  16.4 26.0 %collective-permute-start.1 = (bf16[32,4224]{1,0:T(8,128)(2,1)}, bf16[32,4224]{1,0:T(8,128)(2,1)S(1)}, u32[]{:S(2)}, u32[]{:S(2)}) collective-permute-start(bf16[32,4224]{1,0:T(8,128)(2,1)} %get-tuple-element.335), channel_id=1, source_target_pairs={{0,16},{4,20},{8,24},{12,28},{16,0},{20,4},{24,8},{28,12},{1,17},{... | collective-permute-start | bytes 811016 | tf_op jit(solution)/shard_map/ppermute | solution.py:35
  16.4 26.0 %collective-permute-start.2 = (bf16[32,4224]{1,0:T(8,128)(2,1)}, bf16[32,4224]{1,0:T(8,128)(2,1)S(1)}, u32[]{:S(2)}, u32[]{:S(2)}) collective-permute-start(bf16[32,4224]{1,0:T(8,128)(2,1)} %get-tuple-element.335), channel_id=1, source_target_pairs={{0,8},{4,12},{8,16},{12,20},{16,24},{20,28},{24,0},{28,4},{1,9},{5... | collective-permute-start | bytes 811016 | tf_op jit(solution)/shard_map/ppermute | solution.py:35
  44.4 94.2 %all-gather.4.cloned.1.call-start = ((), (), s32[]{:S(2)}) async-start(), calls=%async_computation.2 | async-start | bytes 2654208 | tf_op jit(solution)/shard_map/all_gather | solution.py:207
  45.3 22.5 %collective-permute-start.7 = (bf16[4,32,4224]{2,1,0:T(8,128)(2,1)S(1)}, bf16[4,32,4224]{2,1,0:T(8,128)(2,1)S(1)}, u32[]{:S(2)}, u32[]{:S(2)}) collective-permute-start(bf16[4,32,4224]{2,1,0:T(8,128)(2,1)S(1)} %bitcast.205), channel_id=1, source_target_pairs={{0,1},{1,0},{2,3},{3,2},{4,5},{5,4},{6,7},{7,6},{8,9},{9,8},{10,11... | collective-permute-start | bytes 3244040 | tf_op jit(solution)/shard_map/ppermute | solution.py:39
  45.4 23.1 %collective-permute-start.8 = (bf16[4,32,4224]{2,1,0:T(8,128)(2,1)S(1)}, bf16[4,32,4224]{2,1,0:T(8,128)(2,1)S(1)}, u32[]{:S(2)}, u32[]{:S(2)}) collective-permute-start(bf16[4,32,4224]{2,1,0:T(8,128)(2,1)S(1)} %bitcast.206), channel_id=1, source_target_pairs={{0,2},{1,3},{2,0},{3,1},{4,6},{5,7},{6,4},{7,5},{8,10},{9,11},{10,... | collective-permute-start | bytes 3244040 | tf_op jit(solution)/shard_map/ppermute | solution.py:39
  84.4 251.3 %reduce-scatter.3.cloned.1.call-start = ((), (), s32[]{:S(2)}) async-start(), calls=%async_computation.3 | async-start | bytes 5308416 | tf_op jit(solution)/shard_map/reduce_scatter | solution.py:352
  85.3 26.6 %collective-permute-start.12 = (bf16[512,1024]{1,0:T(8,128)(2,1)S(1)}, bf16[512,1024]{1,0:T(8,128)(2,1)S(1)}, u32[]{:S(2)}, u32[]{:S(2)}) collective-permute-start(bf16[512,1024]{1,0:T(8,128)(2,1)S(1)} %bitcast.221), channel_id=1, source_target_pairs={{0,1},{1,0},{2,3},{3,2},{4,5},{5,4},{6,7},{7,6},{8,9},{9,8},{10,11... | collective-permute-start | bytes 3145736 | tf_op jit(solution)/shard_map/ppermute | solution.py:39
  86.7 25.4 %collective-permute-start.13 = (bf16[512,1024]{1,0:T(8,128)(2,1)S(1)}, bf16[512,1024]{1,0:T(8,128)(2,1)}, u32[]{:S(2)}, u32[]{:S(2)}) collective-permute-start(bf16[512,1024]{1,0:T(8,128)(2,1)S(1)} %bitcast.222), channel_id=1, source_target_pairs={{0,2},{1,3},{2,0},{3,1},{4,6},{5,7},{6,4},{7,5},{8,10},{9,11},{10,... | collective-permute-start | bytes 3145736 | tf_op jit(solution)/shard_map/ppermute | solution.py:39
  129.9 24.3 %collective-permute-start.16 = (bf16[512,1024]{1,0:T(8,128)(2,1)S(1)}, bf16[512,1024]{1,0:T(8,128)(2,1)}, u32[]{:S(2)}, u32[]{:S(2)}) collective-permute-start(bf16[512,1024]{1,0:T(8,128)(2,1)S(1)} %multiply_convert_fusion.12), channel_id=1, source_target_pairs={{0,1},{1,0},{2,3},{3,2},{4,5},{5,4},{6,7},{7,6},{8,9},{9,8},{10,11... | collective-permute-start | bytes 3145736 | tf_op jit(solution)/shard_map/ppermute | solution.py:39
  131.3 24.1 %collective-permute-start.17 = (bf16[512,1024]{1,0:T(8,128)(2,1)S(1)}, bf16[512,1024]{1,0:T(8,128)(2,1)}, u32[]{:S(2)}, u32[]{:S(2)}) collective-permute-start(bf16[512,1024]{1,0:T(8,128)(2,1)S(1)} %multiply_convert_fusion.12), channel_id=1, source_target_pairs={{0,2},{1,3},{2,0},{3,1},{4,6},{5,7},{6,4},{7,5},{8,10},{9,11},{10,... | collective-permute-start | bytes 3145736 | tf_op jit(solution)/shard_map/ppermute | solution.py:39
  160.3 20.3 %collective-permute-start.18 = (bf16[256,1024]{1,0:T(8,128)(2,1)S(1)}, bf16[256,1024]{1,0:T(8,128)(2,1)S(1)}, u32[]{:S(2)}, u32[]{:S(2)}) collective-permute-start(bf16[256,1024]{1,0:T(8,128)(2,1)S(1)} %slice.362), channel_id=1, source_target_pairs={{0,2},{1,3},{2,0},{3,1},{4,6},{5,7},{6,4},{7,5},{8,10},{9,11},{10,... | collective-permute-start | bytes 1572872 | tf_op jit(solution)/shard_map/ppermute | solution.py:39
  162.3 18.4 %collective-permute-start.19 = (bf16[256,1024]{1,0:T(8,128)(2,1)S(1)}, bf16[256,1024]{1,0:T(8,128)(2,1)S(1)}, u32[]{:S(2)}, u32[]{:S(2)}) collective-permute-start(bf16[256,1024]{1,0:T(8,128)(2,1)S(1)} %slice.363), channel_id=1, source_target_pairs={{0,1},{1,0},{2,3},{3,2},{4,5},{5,4},{6,7},{7,6},{8,9},{9,8},{10,11... | collective-permute-start | bytes 1572872 | tf_op jit(solution)/shard_map/ppermute | solution.py:39
  194.8 26.1 %collective-permute-start.20 = (bf16[512,1024]{1,0:T(8,128)(2,1)S(1)}, bf16[512,1024]{1,0:T(8,128)(2,1)S(1)}, u32[]{:S(2)}, u32[]{:S(2)}) collective-permute-start(bf16[512,1024]{1,0:T(8,128)(2,1)S(1)} %convolution_convert_fusion.3), channel_id=1, source_target_pairs={{0,1},{1,0},{2,3},{3,2},{4,5},{5,4},{6,7},{7,6},{8,9},{9,8},{10,11... | collective-permute-start | bytes 3145736 | tf_op jit(solution)/shard_map/ppermute | solution.py:39
  206.0 27.7 %collective-permute-start.22 = (bf16[256,1024]{1,0:T(8,128)(2,1)}, bf16[256,1024]{1,0:T(8,128)(2,1)}, u32[]{:S(2)}, u32[]{:S(2)}) collective-permute-start(bf16[256,1024]{1,0:T(8,128)(2,1)} %convolution_convert_fusion.6), channel_id=1, source_target_pairs={{0,3},{1,2},{2,1},{3,0},{4,7},{5,6},{6,5},{7,4},{8,11},{9,10},{10,... | collective-permute-start | bytes 1572872 | tf_op jit(solution)/shard_map/ppermute | solution.py:39
  207.2 44.8 %collective-permute-start.21 = (bf16[512,1024]{1,0:T(8,128)(2,1)}, bf16[512,1024]{1,0:T(8,128)(2,1)}, u32[]{:S(2)}, u32[]{:S(2)}) collective-permute-start(bf16[512,1024]{1,0:T(8,128)(2,1)} %convolution_convert_fusion.2), channel_id=1, source_target_pairs={{0,2},{1,3},{2,0},{3,1},{4,6},{5,7},{6,4},{7,5},{8,10},{9,11},{10,... | collective-permute-start | bytes 3145736 | tf_op jit(solution)/shard_map/ppermute | solution.py:39
  208.0 60.8 %collective-permute-start.23 = (bf16[256,1024]{1,0:T(8,128)(2,1)}, bf16[256,1024]{1,0:T(8,128)(2,1)}, u32[]{:S(2)}, u32[]{:S(2)}) collective-permute-start(bf16[256,1024]{1,0:T(8,128)(2,1)} %convolution_convert_fusion.5), channel_id=1, source_target_pairs={{0,3},{1,2},{2,1},{3,0},{4,7},{5,6},{6,5},{7,4},{8,11},{9,10},{10,... | collective-permute-start | bytes 1572872 | tf_op jit(solution)/shard_map/ppermute | solution.py:39
  268.9 116.4 %reduce-scatter.5.cloned.1.call-start = ((), (), s32[]{:S(2)}) async-start(), calls=%async_computation.4 | async-start | bytes 2654208 | tf_op jit(solution)/shard_map/reduce_scatter | solution.py:353
  285.5 36.3 %collective-permute-start.26 = (bf16[512,1024]{1,0:T(8,128)(2,1)}, bf16[512,1024]{1,0:T(8,128)(2,1)}, u32[]{:S(2)}, u32[]{:S(2)}) collective-permute-start(bf16[512,1024]{1,0:T(8,128)(2,1)} %convolution_convert_fusion.4), channel_id=1, source_target_pairs={{0,4},{4,0},{8,12},{12,8},{16,20},{20,16},{24,28},{28,24},{1,5},{5... | collective-permute-start | bytes 3145736 | tf_op jit(solution)/shard_map/ppermute | solution.py:30
  297.1 27.9 %collective-permute-start.25 = (bf16[512,3072]{1,0:T(8,128)(2,1)}, bf16[512,3072]{1,0:T(8,128)(2,1)}, u32[]{:S(2)}, u32[]{:S(2)}) collective-permute-start(bf16[512,3072]{1,0:T(8,128)(2,1)} %convolution_convert_fusion), channel_id=1, source_target_pairs={{0,4},{4,0},{8,12},{12,8},{16,20},{20,16},{24,28},{28,24},{1,5},{5... | collective-permute-start | bytes 9437192 | tf_op jit(solution)/shard_map/ppermute | solution.py:30
  332.8 15.5 %collective-permute-start.30 = (bf16[2,32,4224]{2,1,0:T(8,128)(2,1)}, bf16[2,32,4224]{2,1,0:T(8,128)(2,1)}, u32[]{:S(2)}, u32[]{:S(2)}) collective-permute-start(bf16[2,32,4224]{2,1,0:T(8,128)(2,1)} %get-tuple-element.288), channel_id=1, source_target_pairs={{0,1},{1,0},{2,3},{3,2},{4,5},{5,4},{6,7},{7,6},{8,9},{9,8},{10,11... | collective-permute-start | bytes 1622024 | tf_op jit(solution)/shard_map/ppermute | solution.py:39
  334.0 15.7 %collective-permute-start.31 = (bf16[2,32,4224]{2,1,0:T(8,128)(2,1)}, bf16[2,32,4224]{2,1,0:T(8,128)(2,1)}, u32[]{:S(2)}, u32[]{:S(2)}) collective-permute-start(bf16[2,32,4224]{2,1,0:T(8,128)(2,1)} %get-tuple-element.290), channel_id=1, source_target_pairs={{0,2},{1,3},{2,0},{3,1},{4,6},{5,7},{6,4},{7,5},{8,10},{9,11},{10,... | collective-permute-start | bytes 1622024 | tf_op jit(solution)/shard_map/ppermute | solution.py:39
  337.3 16.8 %collective-permute-start.33 = (bf16[32,2304]{1,0:T(8,128)(2,1)S(1)}, bf16[32,2304]{1,0:T(8,128)(2,1)S(1)}, u32[]{:S(2)}, u32[]{:S(2)}) collective-permute-start(bf16[32,2304]{1,0:T(8,128)(2,1)S(1)} %get-tuple-element.325), channel_id=1, source_target_pairs={{0,2},{1,3},{2,0},{3,1},{4,6},{5,7},{6,4},{7,5},{8,10},{9,11},{10,... | collective-permute-start | bytes 442376 | tf_op jit(solution)/shard_map/ppermute | solution.py:39
  338.1 16.1 %collective-permute-start.34 = (bf16[32,2304]{1,0:T(8,128)(2,1)S(1)}, bf16[32,2304]{1,0:T(8,128)(2,1)S(1)}, u32[]{:S(2)}, u32[]{:S(2)}) collective-permute-start(bf16[32,2304]{1,0:T(8,128)(2,1)S(1)} %get-tuple-element.324), channel_id=1, source_target_pairs={{0,3},{1,2},{2,1},{3,0},{4,7},{5,6},{6,5},{7,4},{8,11},{9,10},{10,... | collective-permute-start | bytes 442376 | tf_op jit(solution)/shard_map/ppermute | solution.py:39
  357.1 24.6 %collective-permute-start.36 = (bf16[4,32,4224]{2,1,0:T(8,128)(2,1)}, bf16[4,32,4224]{2,1,0:T(8,128)(2,1)S(1)}, u32[]{:S(2)}, u32[]{:S(2)}) collective-permute-start(bf16[4,32,4224]{2,1,0:T(8,128)(2,1)} %pad_maximum_fusion.8), channel_id=1, source_target_pairs={{0,2},{1,3},{2,0},{3,1},{4,6},{5,7},{6,4},{7,5},{8,10},{9,11},{10,... | collective-permute-start | bytes 3244040 | tf_op jit(solution)/shard_map/ppermute | solution.py:39
  359.7 23.3 %collective-permute-start.35 = (bf16[4,32,4224]{2,1,0:T(8,128)(2,1)}, bf16[4,32,4224]{2,1,0:T(8,128)(2,1)}, u32[]{:S(2)}, u32[]{:S(2)}) collective-permute-start(bf16[4,32,4224]{2,1,0:T(8,128)(2,1)} %pad_maximum_fusion.7), channel_id=1, source_target_pairs={{0,1},{1,0},{2,3},{3,2},{4,5},{5,4},{6,7},{7,6},{8,9},{9,8},{10,11... | collective-permute-start | bytes 3244040 | tf_op jit(solution)/shard_map/ppermute | solution.py:39
  385.4 15.4 %collective-permute-start.39 = (bf16[32,4224]{1,0:T(8,128)(2,1)S(1)}, bf16[32,4224]{1,0:T(8,128)(2,1)S(1)}, u32[]{:S(2)}, u32[]{:S(2)}) collective-permute-start(bf16[32,4224]{1,0:T(8,128)(2,1)S(1)} %get-tuple-element.296), channel_id=1, source_target_pairs={{0,8},{4,12},{8,16},{12,20},{16,24},{20,28},{24,0},{28,4},{1,9},{5... | collective-permute-start | bytes 811016 | tf_op jit(solution)/shard_map/ppermute | solution.py:35
  385.7 19.3 %collective-permute-start.40 = (bf16[32,4224]{1,0:T(8,128)(2,1)S(1)}, bf16[32,4224]{1,0:T(8,128)(2,1)S(1)}, u32[]{:S(2)}, u32[]{:S(2)}) collective-permute-start(bf16[32,4224]{1,0:T(8,128)(2,1)S(1)} %get-tuple-element.295), channel_id=1, source_target_pairs={{0,16},{4,20},{8,24},{12,28},{16,0},{20,4},{24,8},{28,12},{1,17},{... | collective-permute-start | bytes 811016 | tf_op jit(solution)/shard_map/ppermute | solution.py:35
  388.7 16.4 %collective-permute-start.41 = (bf16[32,4224]{1,0:T(8,128)(2,1)S(1)}, bf16[32,4224]{1,0:T(8,128)(2,1)S(1)}, u32[]{:S(2)}, u32[]{:S(2)}) collective-permute-start(bf16[32,4224]{1,0:T(8,128)(2,1)S(1)} %get-tuple-element.294), channel_id=1, source_target_pairs={{0,24},{4,28},{8,0},{12,4},{16,8},{20,12},{24,16},{28,20},{1,25},{... | collective-permute-start | bytes 811016 | tf_op jit(solution)/shard_map/ppermute | solution.py:35
  391.5 22.0 %collective-permute-start.37 = (bf16[512,1024]{1,0:T(8,128)(2,1)}, bf16[512,1024]{1,0:T(8,128)(2,1)S(1)}, u32[]{:S(2)}, u32[]{:S(2)}) collective-permute-start(bf16[512,1024]{1,0:T(8,128)(2,1)} %pad_maximum_fusion.11), channel_id=1, source_target_pairs={{0,1},{1,0},{2,3},{3,2},{4,5},{5,4},{6,7},{7,6},{8,9},{9,8},{10,11... | collective-permute-start | bytes 3145736 | tf_op jit(solution)/shard_map/ppermute | solution.py:39
  393.2 21.3 %collective-permute-start.38 = (bf16[512,1024]{1,0:T(8,128)(2,1)}, bf16[512,1024]{1,0:T(8,128)(2,1)S(1)}, u32[]{:S(2)}, u32[]{:S(2)}) collective-permute-start(bf16[512,1024]{1,0:T(8,128)(2,1)} %pad_maximum_fusion.12), channel_id=1, source_target_pairs={{0,2},{1,3},{2,0},{3,1},{4,6},{5,7},{6,4},{7,5},{8,10},{9,11},{10,... | collective-permute-start | bytes 3145736 | tf_op jit(solution)/shard_map/ppermute | solution.py:39
  (108 other events, 708.9 us)
Sparse Core Ops, SparseCore 0:
  44.5 50.6 all-gather.5
  97.4 30.4 all-gather.3
  269.0 54.7 reduce-scatter.2
  326.0 34.6 reduce-scatter.4

commit v8 on v7

--- a/solution.py
+++ b/solution.py
@@ -313,19 +313,8 @@
     for k in order[1:-1]:
         hidden_block(k)
         norm_parts[k] = right_contract(act_grads[k], mat_gate_up).astype(bf16)
-        if k == 1:
-            norm_parts, mix_mine, mix_other = tie((norm_parts, mix_mine, mix_other))
-            both_halves = [
-                mix_mine.reshape(n_z, -1, columns),
-                mix_other.reshape(n_z, -1, columns),
-            ]
-            in_full = place(both_halves, core_slots, width, 0, cut_in).reshape(width, cut_in)
-            out_full = place(both_halves, core_slots, width, cut_in, width).reshape(width, width)
-            out_parts[1] = dot(hiddens[1], mat_down)
-        norms, act_grads, norm_parts, out_parts, in_full, out_full = tie(
-            (norms, act_grads, norm_parts, out_parts, in_full, out_full)
-        )
         norm_sums[k] = across_seq(norm_parts[k], k)
+        norms, act_grads, norm_parts = tie((norms, act_grads, norm_parts))
     hidden_block(last)
     last_parts = [
         right_contract(act_grads[last][start : start + rows // 2], mat_gate_up).astype(bf16)
@@ -334,8 +323,8 @@
     last_sums = [across_seq(part, last) for part in last_parts]
     early = {k: norm_sums[k] for k in order[1:-2]}
     out_far = dot(hiddens[last], mat_down).astype(bf16)
-    last_parts, hiddens, act_grads, early, out_far = tie(
-        (last_parts, hiddens, act_grads, early, out_far)
+    last_parts, hiddens, act_grads, early, out_far, mix_mine, mix_other = tie(
+        (last_parts, hiddens, act_grads, early, out_far, mix_mine, mix_other)
     )
     norm_sums.update(early)
 
@@ -343,9 +332,20 @@
         return jnp.concatenate([blocks[k] for k in order], 0)
 
     grad_down = left_contract(rows_of(hiddens), rows_of(tops)).astype(bf16)
-    out_parts.update({k: dot(hiddens[k], mat_down) for k in near[1:]})
-    out_parts, act_grads, grad_down, norm_sums[order[-2]], last_sums[0] = tie(
-        (out_parts, act_grads, grad_down, norm_sums[order[-2]], last_sums[0])
+    out_parts.update({k: dot(hiddens[k], mat_down) for k in near})
+    halves_of = [part.reshape(n_z, -1, columns) for part in (mix_mine, mix_other)]
+    in_full = place(halves_of, core_slots, width, 0, cut_in).reshape(width, cut_in)
+    out_full = place(halves_of, core_slots, width, cut_in, width).reshape(width, width)
+    out_parts, act_grads, grad_down, norm_sums[order[-2]], last_sums[0], in_full, out_full = tie(
+        (
+            out_parts,
+            act_grads,
+            grad_down,
+            norm_sums[order[-2]],
+            last_sums[0],
+            in_full,
+            out_full,
+        )
     )
     grad_gate_up = left_contract(rows_of(norms), rows_of(act_grads)).astype(bf16)
     last_sums, grad_gate_up, grad_down = tie((last_sums, grad_gate_up, grad_down))
@@ -396,8 +396,7 @@
         return mine + to_sibling(other.astype(bf16)).astype(f32)
 
     small_grads = jnp.stack(grad_taps + [gain_one, gain_two], 0)
-    small_received, out_relay = tie((to_sibling(small_grads), out_relay))
-    small_grads = (small_grads + small_received).astype(bf16)
+    small_grads = (small_grads + to_sibling(small_grads)).astype(bf16)
     small_wide = jnp.tile(jnp.pad(small_grads, ((0, own - 5), (0, 0))), (half // own, 1))
     small_wide = jnp.where(row_blocks(core) == feature // own, small_wide, 0.0).astype(bf16)
     in_received = to_sibling(grad_in_other.astype(bf16))
@@ -411,6 +410,7 @@
     ).astype(bf16)
     gu_sum = gu_sum.reshape(n_seq, own, 2 * ff_part)
     gu_parts = [across_seq(pick(gu_sum, sq ^ k), k) for k in range(1, n_seq)]
+    mixed, out_relay = tie((mixed, out_relay))
     mixed = mixed.reshape(n_z, n_seq, own, -1)
 
     def seq_block(index):

time: 429 us -> 411 us (0.958)
  the two profiles are of different devices: /device:TPU:0 before, /device:TPU:8 now
where the time goes in v8:
time: 411 us; the launch traced here: 405 us
  matrix products  127 us (31%)
  waiting for transfers between devices  114 us (28%)
  other arithmetic  55 us (13%)
  starting transfers between devices  46.9 us (11%)
  local copies, waits for them, and re-layouts  35.9 us (9%)
  between operations  16.1 us (4%)
  Pallas kernels  9.74 us (2%)
    ppermute x30, waiting for transfers between devices, across_seq(): lax.ppermute(block, 'seq', [(i, i ^ by) for i in range(lax.axis_size('seq...  93.9 us
    dot_general x14, matrix products, dot(): return jnp.dot(first, second, preferred_element_type=f32)  46.4 us
    dot_general x12, matrix products, right_contract(): lax.dot_general(first, second, (((1,), (1,)), ((), ())), preferred_elemen...  44.2 us
    dot_general x6, matrix products, left_contract(): lax.dot_general(first, second, (((0,), (0,)), ((), ())), preferred_elemen...  36.4 us
    ppermute x30, starting transfers between devices, across_seq(): lax.ppermute(block, 'seq', [(i, i ^ by) for i in range(lax.axis_size('seq...  31.4 us
    ppermute x6, waiting for transfers between devices, along_z(): lax.ppermute(block, 'dp', [(i, (i + 2 * by) % count) for i in range(count)])  12.5 us
    ppermute x6, starting transfers between devices, along_z(): lax.ppermute(block, 'dp', [(i, (i + 2 * by) % count) for i in range(count)])  10.2 us
    unnamed x203, local copies, waits for them, and re-layouts  10.1 us
  transfers between devices with their start and end apart: 46, of which 25 were waited for; matrix products, arithmetic and copies ran while one was open for 48% of the time, Pallas kernels for 2%

profile of v8, /device:TPU:8, one launch (start us, length us, event | category | flops | bytes accessed | tf_op | source)
XLA Modules:
  0.0 404.5 jit_solution(61591228321037588)
XLA Ops:
  31.5 4.2 %collective-permute-start.4 = (bf16[32,2304]{1,0:T(8,128)(2,1)S(1)}, bf16[32,2304]{1,0:T(8,128)(2,1)S(1)}, u32[]{:S(2)}, u32[]{:S(2)}) collective-permute-start(bf16[32,2304]{1,0:T(8,128)(2,1)S(1)} %get-tuple-element.313), channel_id=1, source_target_pairs={{0,2},{1,3},{2,0},{3,1},{4,6},{5,7},{6,4},{7,5},{8,10},{9,11},{10,... | collective-permute-start | bytes 442376 | tf_op jit(solution)/shard_map/ppermute | solution.py:39
  36.4 3.5 collective-permute-done.4
  45.5 23.2 %collective-permute-done.7.refs_1_ = bf16[4,32,4224]{2,1,0:T(8,128)(2,1)S(1)} collective-permute-done((bf16[4,32,4224]{2,1,0:T(8,128)(2,1)S(1)}, bf16[4,32,4224]{2,1,0:T(8,128)(2,1)S(1)}, u32[]{:S(2)}, u32[]{:S(2)}) %collective-permute-start.7) | collective-permute-done | bytes 1081376 | tf_op jit(solution)/shard_map/ppermute | solution.py:39
  70.1 8.3 %collective-permute-done.10 = bf16[2,32,4224]{2,1,0:T(8,128)(2,1)S(1)} collective-permute-done((bf16[2,32,4224]{2,1,0:T(8,128)(2,1)S(1)}, bf16[2,32,4224]{2,1,0:T(8,128)(2,1)S(1)}, u32[]{:S(2)}, u32[]{:S(2)}) %collective-permute-start.10) | collective-permute-done | bytes 540704 | tf_op jit(solution)/shard_map/ppermute | solution.py:39
  79.6 3.2 shard_map.408
  87.2 3.3 collective-permute-done.11
  93.1 4.2 %fusion.39 = f32[528,3072]{1,0:T(8,128)S(1)} fusion(bf16[512,4224]{1,0:T(8,128)(2,1)} %bitcast.13, bf16[16,512]{1,0:T(8,128)(2,1)S(1)} %get-tuple-element.323, bf16[512,512]{1,0:T(8,128)(2,1)S(1)} %get-tuple-element.288), kind=kOutput, calls=%fused_computation.38 | convolution fusion | flops 1662025728 | bytes 10174464 | tf_op jit(solution)/shard_map/dot_general | solution.py:73
  97.3 3.9 convolution_add_fusion
  119.8 6.1 %collective-permute-done.15 = bf16[256,1024]{1,0:T(8,128)(2,1)S(1)} collective-permute-done((bf16[256,1024]{1,0:T(8,128)(2,1)S(1)}, bf16[256,1024]{1,0:T(8,128)(2,1)S(1)}, u32[]{:S(2)}, u32[]{:S(2)}) %collective-permute-start.15) | collective-permute-done | bytes 524320 | tf_op jit(solution)/shard_map/ppermute | solution.py:39
  129.5 6.8 %fusion.185 = f32[512,2304]{1,0:T(8,128)} fusion(bf16[512,1024]{1,0:T(8,128)(2,1)S(1)} %multiply_convert_fusion.12, bf16[1024,2304]{1,0:T(8,128)(2,1)} %bitcast.249), kind=kOutput, calls=%fused_computation.358 | convolution fusion | flops 2415919104 | bytes 10485760 | tf_op jit(solution)/shard_map/dot_general | solution.py:73
  136.3 5.5 %multiply_convert_fusion.10 = (bf16[512,1152]{1,0:T(8,128)(2,1)S(1)}, bf16[512,1152]{1,0:T(8,128)(2,1)S(1)}, bf16[512,1152]{1,0:T(8,128)(2,1)S(1)}) fusion(f32[512,2304]{1,0:T(8,128)} %fusion.185, bf16[1152,1024]{1,0:T(8,128)(2,1)} %all-gather.4.cloned.1.call-done, bf16[512,1024]{1,0:T(8,128)(2,1)S(1)} %bitcast.220), kind=kOutput, calls=%fused_computation.67 | convolution fusion | flops 1216806912 | bytes 11665408 | tf_op jit(solution)/shard_map/dot_general | solution.py:81
  146.4 4.0 fusion.166
  153.9 3.9 fusion.187
  160.6 3.5 multiply_convert_fusion.8
  169.5 4.3 %collective-permute-done.19 = bf16[256,1024]{1,0:T(8,128)(2,1)S(1)} collective-permute-done((bf16[256,1024]{1,0:T(8,128)(2,1)S(1)}, bf16[256,1024]{1,0:T(8,128)(2,1)S(1)}, u32[]{:S(2)}, u32[]{:S(2)}) %collective-permute-start.19) | collective-permute-done | bytes 524320 | tf_op jit(solution)/shard_map/ppermute | solution.py:39
  173.9 4.5 %fusion.188 = f32[512,2304]{1,0:T(8,128)S(1)} fusion(bf16[512,1024]{1,0:T(8,128)(2,1)} %collective-permute-done.17, bf16[1024,2304]{1,0:T(8,128)(2,1)S(1)} %bitcast.255), kind=kOutput, calls=%fused_computation.361 | convolution fusion | flops 2415919104 | bytes 10485760 | tf_op jit(solution)/shard_map/dot_general | solution.py:73
  178.3 3.5 multiply_convert_fusion.6
  183.6 3.6 convolution_convert_fusion.2
  204.7 8.2 %fusion.33 = bf16[1152,1024]{1,0:T(8,128)(2,1)} fusion(bf16[512,1024]{1,0:T(8,128)(2,1)S(1)} %pad_maximum_fusion.9, bf16[512,1024]{1,0:T(8,128)(2,1)} %collective-permute-done.13, bf16[512,1024]{1,0:T(8,128)(2,1)} %collective-permute-done.12, bf16[512,1024]{1,0:T(8,128)(2,1)S(1)} %bitcast.221, bf16[512,1152]{1,0:T(8,128)(2,1)S(1)} %get-tuple-element.167, ...), kind=kOutput, calls=%fused_computation.35 | convolution fusion | flops 4868669440 | bytes 11272192 | tf_op jit(solution)/shard_map/dot_general | solution.py:77
  212.9 4.9 %fusion.190 = f32[512,1024]{1,0:T(8,128)} fusion(bf16[512,1152]{1,0:T(8,128)(2,1)} %copy-done.93, bf16[1152,1024]{1,0:T(8,128)(2,1)} %all-gather.4.cloned.1.call-done), kind=kOutput, calls=%fused_computation.363 | convolution fusion | flops 1207959552 | bytes 5636096 | tf_op jit(solution)/shard_map/dot_general | solution.py:73
  217.8 3.8 shard_map.409
  229.8 8.5 %collective-permute-done.21 = bf16[512,1024]{1,0:T(8,128)(2,1)} collective-permute-done((bf16[512,1024]{1,0:T(8,128)(2,1)}, bf16[512,1024]{1,0:T(8,128)(2,1)}, u32[]{:S(2)}, u32[]{:S(2)}) %collective-permute-start.21) | collective-permute-done | bytes 1048608 | tf_op jit(solution)/shard_map/ppermute | solution.py:39
  238.3 16.6 %fusion.8 = bf16[1024,2304]{1,0:T(8,128)(2,1)} fusion(bf16[512,2304]{1,0:T(8,128)(2,1)} %pad_maximum_fusion.2, bf16[512,2304]{1,0:T(8,128)(2,1)} %pad_maximum_fusion.5, bf16[512,2304]{1,0:T(8,128)(2,1)} %pad_maximum_fusion.4, bf16[512,2304]{1,0:T(8,128)(2,1)} %pad_maximum_fusion.3, bf16[512,1024]{1,0:T(8,128)(2,1)} %copy-done.32, ...), kind=kOutput, calls=%fused_computation.9 | convolution fusion | flops 9720561664 | bytes 18350080 | tf_op jit(solution)/shard_map/dot_general | solution.py:77
  254.9 4.0 multiply_reduce_fusion
  260.6 4.8 %multiply_reduce_fusion.1 = (f32[1024]{0:T(1024)S(1)}, f32[1024]{0:T(1024)}, f32[1024]{0:T(1024)}, f32[512,1024]{1,0:T(8,128)S(1)}, f32[512,1024]{1,0:T(8,128)S(1)}) fusion(f32[2,258,1024]{2,1,0:T(8,128)S(1)} %copy-done.2, f32[2,256]{1,0:T(2,128)S(1)} %get-tuple-element.333, f32[2,256]{1,0:T(2,128)S(1)} %get-tuple-element.332, f32[528,3072]{1,0:T(8,128)} %copy-done.3, ...), kind=kOutput, calls=%fused_computation.103 | convolution fusion | flops 1078981632 | bytes 16793600 | tf_op jit(solution)/shard_map/dot_general | solution.py:81
  273.1 3.5 convolution_convert_fusion
  283.2 9.4 %fusion.57 = (f32[512]{0:T(512)}, f32[1024]{0:T(1024)}, f32[512,1024]{1,0:T(8,128)}) fusion(bf16[2,256,1024]{2,1,0:T(8,128)(2,1)S(1)} %copy-done.13, f32[1024]{0:T(1024)S(1)} %bitcast.233, f32[512]{0:T(512)S(1)} %bitcast.242, bf16[1024,3072]{1,0:T(8,128)(2,1)} %bitcast.197, bf16[512,1024]{1,0:T(8,128)(2,1)} %copy-done.38, bf16[512,1024]{1,0:T(8,128)(2,1)} %copy-done.29, ...), kind=kOutput, calls=%fused_computation.95 | convolution fusion | flops 3234331136 | bytes 12595200 | tf_op jit(solution)/shard_map/dot_general | solution.py:81
  304.2 4.2 %add_convert_fusion = bf16[512,3072]{1,0:T(8,128)(2,1)S(1)} fusion(bf16[512,3072]{1,0:T(8,128)(2,1)} %collective-permute-done.25, bf16[512,512]{1,0:T(8,128)(2,1)S(1)} %copy-done.45, bf16[512,1024]{1,0:T(8,128)(2,1)S(1)} %copy-done.39, bf16[512,1024]{1,0:T(8,128)(2,1)S(1)} %copy-done.30, bf16[512,1024]{1,0:T(8,128)(2,1)S(1)} %copy-done.37), kind=kOutput, calls=%fused_computation.8 | convolution fusion | flops 1624768512 | bytes 9961472 | tf_op jit(solution)/shard_map/dot_general | solution.py:77
  322.3 6.1 %collective-permute-done.30 = bf16[2,32,4224]{2,1,0:T(8,128)(2,1)} collective-permute-done((bf16[2,32,4224]{2,1,0:T(8,128)(2,1)}, bf16[2,32,4224]{2,1,0:T(8,128)(2,1)}, u32[]{:S(2)}, u32[]{:S(2)}) %collective-permute-start.30) | collective-permute-done | bytes 540704 | tf_op jit(solution)/shard_map/ppermute | solution.py:39
  344.0 16.8 %collective-permute-done.35 = bf16[4,32,4224]{2,1,0:T(8,128)(2,1)S(1)} collective-permute-done((bf16[4,32,4224]{2,1,0:T(8,128)(2,1)}, bf16[4,32,4224]{2,1,0:T(8,128)(2,1)S(1)}, u32[]{:S(2)}, u32[]{:S(2)}) %collective-permute-start.35) | collective-permute-done | bytes 1081376 | tf_op jit(solution)/shard_map/ppermute | solution.py:39
  378.5 8.1 %collective-permute-done.39 = bf16[32,4224]{1,0:T(8,128)(2,1)S(1)} collective-permute-done((bf16[32,4224]{1,0:T(8,128)(2,1)S(1)}, bf16[32,4224]{1,0:T(8,128)(2,1)S(1)}, u32[]{:S(2)}, u32[]{:S(2)}) %collective-permute-start.39) | collective-permute-done | bytes 270368 | tf_op jit(solution)/shard_map/ppermute | solution.py:35
  386.6 3.2 collective-permute-done.40
  (421 shorter events, 187.0 us)
Async XLA Ops:
  7.2 122.3 %all-gather.6.cloned.1.call-start = ((), (), s32[]{:S(2)}) async-start(), calls=%async_computation.5 | async-start | bytes 5308416 | tf_op jit(solution)/shard_map/all_gather | solution.py:206
  11.3 30.5 %collective-permute-start = (bf16[32,4224]{1,0:T(8,128)(2,1)}, bf16[32,4224]{1,0:T(8,128)(2,1)S(1)}, u32[]{:S(2)}, u32[]{:S(2)}) collective-permute-start(bf16[32,4224]{1,0:T(8,128)(2,1)} %get-tuple-element.315), channel_id=1, source_target_pairs={{0,24},{4,28},{8,0},{12,4},{16,8},{20,12},{24,16},{28,20},{1,25},{... | collective-permute-start | bytes 811016 | tf_op jit(solution)/shard_map/ppermute | solution.py:35
  11.3 30.5 %collective-permute-start.1 = (bf16[32,4224]{1,0:T(8,128)(2,1)}, bf16[32,4224]{1,0:T(8,128)(2,1)S(1)}, u32[]{:S(2)}, u32[]{:S(2)}) collective-permute-start(bf16[32,4224]{1,0:T(8,128)(2,1)} %get-tuple-element.315), channel_id=1, source_target_pairs={{0,16},{4,20},{8,24},{12,28},{16,0},{20,4},{24,8},{28,12},{1,17},{... | collective-permute-start | bytes 811016 | tf_op jit(solution)/shard_map/ppermute | solution.py:35
  14.3 27.5 %collective-permute-start.2 = (bf16[32,4224]{1,0:T(8,128)(2,1)}, bf16[32,4224]{1,0:T(8,128)(2,1)S(1)}, u32[]{:S(2)}, u32[]{:S(2)}) collective-permute-start(bf16[32,4224]{1,0:T(8,128)(2,1)} %get-tuple-element.315), channel_id=1, source_target_pairs={{0,8},{4,12},{8,16},{12,20},{16,24},{20,28},{24,0},{28,4},{1,9},{5... | collective-permute-start | bytes 811016 | tf_op jit(solution)/shard_map/ppermute | solution.py:35
  43.8 92.5 %all-gather.4.cloned.1.call-start = ((), (), s32[]{:S(2)}) async-start(), calls=%async_computation.2 | async-start | bytes 2654208 | tf_op jit(solution)/shard_map/all_gather | solution.py:207
  44.8 23.9 %collective-permute-start.7 = (bf16[4,32,4224]{2,1,0:T(8,128)(2,1)S(1)}, bf16[4,32,4224]{2,1,0:T(8,128)(2,1)S(1)}, u32[]{:S(2)}, u32[]{:S(2)}) collective-permute-start(bf16[4,32,4224]{2,1,0:T(8,128)(2,1)S(1)} %bitcast.198), channel_id=1, source_target_pairs={{0,1},{1,0},{2,3},{3,2},{4,5},{5,4},{6,7},{7,6},{8,9},{9,8},{10,11... | collective-permute-start | bytes 3244040 | tf_op jit(solution)/shard_map/ppermute | solution.py:39
  44.8 23.8 %collective-permute-start.8 = (bf16[4,32,4224]{2,1,0:T(8,128)(2,1)S(1)}, bf16[4,32,4224]{2,1,0:T(8,128)(2,1)S(1)}, u32[]{:S(2)}, u32[]{:S(2)}) collective-permute-start(bf16[4,32,4224]{2,1,0:T(8,128)(2,1)S(1)} %bitcast.199), channel_id=1, source_target_pairs={{0,2},{1,3},{2,0},{3,1},{4,6},{5,7},{6,4},{7,5},{8,10},{9,11},{10,... | collective-permute-start | bytes 3244040 | tf_op jit(solution)/shard_map/ppermute | solution.py:39
  83.3 232.2 %reduce-scatter.3.cloned.1.call-start = ((), (), s32[]{:S(2)}) async-start(), calls=%async_computation.3 | async-start | bytes 5308416 | tf_op jit(solution)/shard_map/reduce_scatter | solution.py:352
  84.2 26.6 %collective-permute-start.12 = (bf16[512,1024]{1,0:T(8,128)(2,1)S(1)}, bf16[512,1024]{1,0:T(8,128)(2,1)}, u32[]{:S(2)}, u32[]{:S(2)}) collective-permute-start(bf16[512,1024]{1,0:T(8,128)(2,1)S(1)} %bitcast.218), channel_id=1, source_target_pairs={{0,1},{1,0},{2,3},{3,2},{4,5},{5,4},{6,7},{7,6},{8,9},{9,8},{10,11... | collective-permute-start | bytes 3145736 | tf_op jit(solution)/shard_map/ppermute | solution.py:39
  85.0 25.8 %collective-permute-start.13 = (bf16[512,1024]{1,0:T(8,128)(2,1)S(1)}, bf16[512,1024]{1,0:T(8,128)(2,1)}, u32[]{:S(2)}, u32[]{:S(2)}) collective-permute-start(bf16[512,1024]{1,0:T(8,128)(2,1)S(1)} %bitcast.219), channel_id=1, source_target_pairs={{0,2},{1,3},{2,0},{3,1},{4,6},{5,7},{6,4},{7,5},{8,10},{9,11},{10,... | collective-permute-start | bytes 3145736 | tf_op jit(solution)/shard_map/ppermute | solution.py:39
  127.7 24.2 %collective-permute-start.16 = (bf16[512,1024]{1,0:T(8,128)(2,1)S(1)}, bf16[512,1024]{1,0:T(8,128)(2,1)}, u32[]{:S(2)}, u32[]{:S(2)}) collective-permute-start(bf16[512,1024]{1,0:T(8,128)(2,1)S(1)} %multiply_convert_fusion.12), channel_id=1, source_target_pairs={{0,1},{1,0},{2,3},{3,2},{4,5},{5,4},{6,7},{7,6},{8,9},{9,8},{10,11... | collective-permute-start | bytes 3145736 | tf_op jit(solution)/shard_map/ppermute | solution.py:39
  129.0 23.9 %collective-permute-start.17 = (bf16[512,1024]{1,0:T(8,128)(2,1)S(1)}, bf16[512,1024]{1,0:T(8,128)(2,1)}, u32[]{:S(2)}, u32[]{:S(2)}) collective-permute-start(bf16[512,1024]{1,0:T(8,128)(2,1)S(1)} %multiply_convert_fusion.12), channel_id=1, source_target_pairs={{0,2},{1,3},{2,0},{3,1},{4,6},{5,7},{6,4},{7,5},{8,10},{9,11},{10,... | collective-permute-start | bytes 3145736 | tf_op jit(solution)/shard_map/ppermute | solution.py:39
  158.8 14.9 %collective-permute-start.19 = (bf16[256,1024]{1,0:T(8,128)(2,1)S(1)}, bf16[256,1024]{1,0:T(8,128)(2,1)S(1)}, u32[]{:S(2)}, u32[]{:S(2)}) collective-permute-start(bf16[256,1024]{1,0:T(8,128)(2,1)S(1)} %slice.363), channel_id=1, source_target_pairs={{0,1},{1,0},{2,3},{3,2},{4,5},{5,4},{6,7},{7,6},{8,9},{9,8},{10,11... | collective-permute-start | bytes 1572872 | tf_op jit(solution)/shard_map/ppermute | solution.py:39
  166.8 37.9 %collective-permute-start.20 = (bf16[512,1024]{1,0:T(8,128)(2,1)S(1)}, bf16[512,1024]{1,0:T(8,128)(2,1)S(1)}, u32[]{:S(2)}, u32[]{:S(2)}) collective-permute-start(bf16[512,1024]{1,0:T(8,128)(2,1)S(1)} %convolution_convert_fusion.3), channel_id=1, source_target_pairs={{0,1},{1,0},{2,3},{3,2},{4,5},{5,4},{6,7},{7,6},{8,9},{9,8},{10,11... | collective-permute-start | bytes 3145736 | tf_op jit(solution)/shard_map/ppermute | solution.py:39
  196.6 41.7 %collective-permute-start.21 = (bf16[512,1024]{1,0:T(8,128)(2,1)}, bf16[512,1024]{1,0:T(8,128)(2,1)}, u32[]{:S(2)}, u32[]{:S(2)}) collective-permute-start(bf16[512,1024]{1,0:T(8,128)(2,1)} %convolution_convert_fusion.2), channel_id=1, source_target_pairs={{0,2},{1,3},{2,0},{3,1},{4,6},{5,7},{6,4},{7,5},{8,10},{9,11},{10,... | collective-permute-start | bytes 3145736 | tf_op jit(solution)/shard_map/ppermute | solution.py:39
  197.2 32.6 %collective-permute-start.22 = (bf16[256,1024]{1,0:T(8,128)(2,1)}, bf16[256,1024]{1,0:T(8,128)(2,1)}, u32[]{:S(2)}, u32[]{:S(2)}) collective-permute-start(bf16[256,1024]{1,0:T(8,128)(2,1)} %convolution_convert_fusion.6), channel_id=1, source_target_pairs={{0,3},{1,2},{2,1},{3,0},{4,7},{5,6},{6,5},{7,4},{8,11},{9,10},{10,... | collective-permute-start | bytes 1572872 | tf_op jit(solution)/shard_map/ppermute | solution.py:39
  198.9 55.9 %collective-permute-start.23 = (bf16[256,1024]{1,0:T(8,128)(2,1)}, bf16[256,1024]{1,0:T(8,128)(2,1)}, u32[]{:S(2)}, u32[]{:S(2)}) collective-permute-start(bf16[256,1024]{1,0:T(8,128)(2,1)} %convolution_convert_fusion.5), channel_id=1, source_target_pairs={{0,3},{1,2},{2,1},{3,0},{4,7},{5,6},{6,5},{7,4},{8,11},{9,10},{10,... | collective-permute-start | bytes 1572872 | tf_op jit(solution)/shard_map/ppermute | solution.py:39
  254.9 112.1 %reduce-scatter.5.cloned.1.call-start = ((), (), s32[]{:S(2)}) async-start(), calls=%async_computation.4 | async-start | bytes 2654208 | tf_op jit(solution)/shard_map/reduce_scatter | solution.py:353
  276.6 27.5 %collective-permute-start.25 = (bf16[512,3072]{1,0:T(8,128)(2,1)}, bf16[512,3072]{1,0:T(8,128)(2,1)}, u32[]{:S(2)}, u32[]{:S(2)}) collective-permute-start(bf16[512,3072]{1,0:T(8,128)(2,1)} %convolution_convert_fusion), channel_id=1, source_target_pairs={{0,4},{4,0},{8,12},{12,8},{16,20},{20,16},{24,28},{28,24},{1,5},{5... | collective-permute-start | bytes 9437192 | tf_op jit(solution)/shard_map/ppermute | solution.py:30
  278.5 23.1 %collective-permute-start.26 = (bf16[512,1024]{1,0:T(8,128)(2,1)}, bf16[512,1024]{1,0:T(8,128)(2,1)}, u32[]{:S(2)}, u32[]{:S(2)}) collective-permute-start(bf16[512,1024]{1,0:T(8,128)(2,1)} %convolution_convert_fusion.4), channel_id=1, source_target_pairs={{0,4},{4,0},{8,12},{12,8},{16,20},{20,16},{24,28},{28,24},{1,5},{5... | collective-permute-start | bytes 3145736 | tf_op jit(solution)/shard_map/ppermute | solution.py:30
  312.9 15.5 %collective-permute-start.30 = (bf16[2,32,4224]{2,1,0:T(8,128)(2,1)}, bf16[2,32,4224]{2,1,0:T(8,128)(2,1)}, u32[]{:S(2)}, u32[]{:S(2)}) collective-permute-start(bf16[2,32,4224]{2,1,0:T(8,128)(2,1)} %get-tuple-element.268), channel_id=1, source_target_pairs={{0,1},{1,0},{2,3},{3,2},{4,5},{5,4},{6,7},{7,6},{8,9},{9,8},{10,11... | collective-permute-start | bytes 1622024 | tf_op jit(solution)/shard_map/ppermute | solution.py:39
  313.3 15.6 %collective-permute-start.31 = (bf16[2,32,4224]{2,1,0:T(8,128)(2,1)}, bf16[2,32,4224]{2,1,0:T(8,128)(2,1)}, u32[]{:S(2)}, u32[]{:S(2)}) collective-permute-start(bf16[2,32,4224]{2,1,0:T(8,128)(2,1)} %get-tuple-element.270), channel_id=1, source_target_pairs={{0,2},{1,3},{2,0},{3,1},{4,6},{5,7},{6,4},{7,5},{8,10},{9,11},{10,... | collective-permute-start | bytes 1622024 | tf_op jit(solution)/shard_map/ppermute | solution.py:39
  316.6 14.8 %collective-permute-start.32 = (bf16[32,2304]{1,0:T(8,128)(2,1)S(1)}, bf16[32,2304]{1,0:T(8,128)(2,1)S(1)}, u32[]{:S(2)}, u32[]{:S(2)}) collective-permute-start(bf16[32,2304]{1,0:T(8,128)(2,1)S(1)} %get-tuple-element.306), channel_id=1, source_target_pairs={{0,1},{1,0},{2,3},{3,2},{4,5},{5,4},{6,7},{7,6},{8,9},{9,8},{10,11... | collective-permute-start | bytes 442376 | tf_op jit(solution)/shard_map/ppermute | solution.py:39
  317.0 16.4 %collective-permute-start.33 = (bf16[32,2304]{1,0:T(8,128)(2,1)S(1)}, bf16[32,2304]{1,0:T(8,128)(2,1)S(1)}, u32[]{:S(2)}, u32[]{:S(2)}) collective-permute-start(bf16[32,2304]{1,0:T(8,128)(2,1)S(1)} %get-tuple-element.305), channel_id=1, source_target_pairs={{0,2},{1,3},{2,0},{3,1},{4,6},{5,7},{6,4},{7,5},{8,10},{9,11},{10,... | collective-permute-start | bytes 442376 | tf_op jit(solution)/shard_map/ppermute | solution.py:39
  318.6 14.9 %collective-permute-start.34 = (bf16[32,2304]{1,0:T(8,128)(2,1)S(1)}, bf16[32,2304]{1,0:T(8,128)(2,1)S(1)}, u32[]{:S(2)}, u32[]{:S(2)}) collective-permute-start(bf16[32,2304]{1,0:T(8,128)(2,1)S(1)} %get-tuple-element.304), channel_id=1, source_target_pairs={{0,3},{1,2},{2,1},{3,0},{4,7},{5,6},{6,5},{7,4},{8,11},{9,10},{10,... | collective-permute-start | bytes 442376 | tf_op jit(solution)/shard_map/ppermute | solution.py:39
  336.4 24.4 %collective-permute-start.35 = (bf16[4,32,4224]{2,1,0:T(8,128)(2,1)}, bf16[4,32,4224]{2,1,0:T(8,128)(2,1)S(1)}, u32[]{:S(2)}, u32[]{:S(2)}) collective-permute-start(bf16[4,32,4224]{2,1,0:T(8,128)(2,1)} %pad_maximum_fusion.7), channel_id=1, source_target_pairs={{0,1},{1,0},{2,3},{3,2},{4,5},{5,4},{6,7},{7,6},{8,9},{9,8},{10,11... | collective-permute-start | bytes 3244040 | tf_op jit(solution)/shard_map/ppermute | solution.py:39
  338.8 24.0 %collective-permute-start.36 = (bf16[4,32,4224]{2,1,0:T(8,128)(2,1)}, bf16[4,32,4224]{2,1,0:T(8,128)(2,1)}, u32[]{:S(2)}, u32[]{:S(2)}) collective-permute-start(bf16[4,32,4224]{2,1,0:T(8,128)(2,1)} %pad_maximum_fusion.8), channel_id=1, source_target_pairs={{0,2},{1,3},{2,0},{3,1},{4,6},{5,7},{6,4},{7,5},{8,10},{9,11},{10,... | collective-permute-start | bytes 3244040 | tf_op jit(solution)/shard_map/ppermute | solution.py:39
  362.8 31.5 %collective-permute-start.38 = (bf16[512,1024]{1,0:T(8,128)(2,1)}, bf16[512,1024]{1,0:T(8,128)(2,1)}, u32[]{:S(2)}, u32[]{:S(2)}) collective-permute-start(bf16[512,1024]{1,0:T(8,128)(2,1)} %pad_maximum_fusion.12), channel_id=1, source_target_pairs={{0,2},{1,3},{2,0},{3,1},{4,6},{5,7},{6,4},{7,5},{8,10},{9,11},{10,... | collective-permute-start | bytes 3145736 | tf_op jit(solution)/shard_map/ppermute | solution.py:39
  363.8 30.5 %collective-permute-start.37 = (bf16[512,1024]{1,0:T(8,128)(2,1)}, bf16[512,1024]{1,0:T(8,128)(2,1)}, u32[]{:S(2)}, u32[]{:S(2)}) collective-permute-start(bf16[512,1024]{1,0:T(8,128)(2,1)} %pad_maximum_fusion.11), channel_id=1, source_target_pairs={{0,1},{1,0},{2,3},{3,2},{4,5},{5,4},{6,7},{7,6},{8,9},{9,8},{10,11... | collective-permute-start | bytes 3145736 | tf_op jit(solution)/shard_map/ppermute | solution.py:39
  367.1 19.4 %collective-permute-start.39 = (bf16[32,4224]{1,0:T(8,128)(2,1)S(1)}, bf16[32,4224]{1,0:T(8,128)(2,1)S(1)}, u32[]{:S(2)}, u32[]{:S(2)}) collective-permute-start(bf16[32,4224]{1,0:T(8,128)(2,1)S(1)} %get-tuple-element.276), channel_id=1, source_target_pairs={{0,8},{4,12},{8,16},{12,20},{16,24},{20,28},{24,0},{28,4},{1,9},{5... | collective-permute-start | bytes 811016 | tf_op jit(solution)/shard_map/ppermute | solution.py:35
  370.2 19.5 %collective-permute-start.40 = (bf16[32,4224]{1,0:T(8,128)(2,1)S(1)}, bf16[32,4224]{1,0:T(8,128)(2,1)S(1)}, u32[]{:S(2)}, u32[]{:S(2)}) collective-permute-start(bf16[32,4224]{1,0:T(8,128)(2,1)S(1)} %get-tuple-element.275), channel_id=1, source_target_pairs={{0,16},{4,20},{8,24},{12,28},{16,0},{20,4},{24,8},{28,12},{1,17},{... | collective-permute-start | bytes 811016 | tf_op jit(solution)/shard_map/ppermute | solution.py:35
  371.1 19.8 %collective-permute-start.41 = (bf16[32,4224]{1,0:T(8,128)(2,1)S(1)}, bf16[32,4224]{1,0:T(8,128)(2,1)S(1)}, u32[]{:S(2)}, u32[]{:S(2)}) collective-permute-start(bf16[32,4224]{1,0:T(8,128)(2,1)S(1)} %get-tuple-element.274), channel_id=1, source_target_pairs={{0,24},{4,28},{8,0},{12,4},{16,8},{20,12},{24,16},{28,20},{1,25},{... | collective-permute-start | bytes 811016 | tf_op jit(solution)/shard_map/ppermute | solution.py:35
  (114 other events, 742.2 us)
Sparse Core Ops, SparseCore 0:
  43.9 48.1 all-gather.5
  94.4 31.3 all-gather.3
  255.0 52.9 reduce-scatter.2
  310.2 34.3 reduce-scatter.4

commit v9 on v8

--- a/solution.py
+++ b/solution.py
@@ -53,9 +53,8 @@
     return {3: jnp.concatenate([first, second], 0)}
 
 
-def sum_far(block):
-    half = block.shape[0] // 2
-    return across_seq(block[:half], 1), across_seq(block[half:], 2)
+def sum_far(halves):
+    return across_seq(halves[0], 1), across_seq(halves[1], 2)
 
 
 def add_far(terms, received):
@@ -322,7 +321,10 @@
     ]
     last_sums = [across_seq(part, last) for part in last_parts]
     early = {k: norm_sums[k] for k in order[1:-2]}
-    out_far = dot(hiddens[last], mat_down).astype(bf16)
+    out_far = [
+        dot(hiddens[last][start : start + rows // 2], mat_down).astype(bf16)
+        for start in (0, rows // 2)
+    ]
     last_parts, hiddens, act_grads, early, out_far, mix_mine, mix_other = tie(
         (last_parts, hiddens, act_grads, early, out_far, mix_mine, mix_other)
     )
@@ -336,19 +338,13 @@
     halves_of = [part.reshape(n_z, -1, columns) for part in (mix_mine, mix_other)]
     in_full = place(halves_of, core_slots, width, 0, cut_in).reshape(width, cut_in)
     out_full = place(halves_of, core_slots, width, cut_in, width).reshape(width, width)
-    out_parts, act_grads, grad_down, norm_sums[order[-2]], last_sums[0], in_full, out_full = tie(
-        (
-            out_parts,
-            act_grads,
-            grad_down,
-            norm_sums[order[-2]],
-            last_sums[0],
-            in_full,
-            out_full,
-        )
+    out_parts, act_grads, grad_down, last_sums[0], in_full, out_full = tie(
+        (out_parts, act_grads, grad_down, last_sums[0], in_full, out_full)
     )
     grad_gate_up = left_contract(rows_of(norms), rows_of(act_grads)).astype(bf16)
-    last_sums, grad_gate_up, grad_down = tie((last_sums, grad_gate_up, grad_down))
+    last_sums, norm_sums, grad_gate_up, grad_down = tie(
+        (last_sums, norm_sums, grad_gate_up, grad_down)
+    )
     gu_sum = lax.psum_scatter(grad_gate_up, "dp", scatter_dimension=0, tiled=True)
     sum_down = lax.psum_scatter(grad_down, "dp", scatter_dimension=0, tiled=True)
     norm_sums[last] = jnp.concatenate(last_sums, 0)
@@ -418,7 +414,8 @@
 
     seq_terms = {k: seq_block(sq ^ k) for k in near}
     if n_seq == 4:
-        seq_relay = sum_far(seq_block(sq ^ last))
+        far_block = seq_block(sq ^ last)
+        seq_relay = sum_far((far_block[: n_z // 2], far_block[n_z // 2 :]))
         seq_relay, gu_parts = tie((seq_relay, gu_parts))
         seq_terms = {k: term.astype(f32) for k, term in seq_terms.items()}
         seq_terms = {k: term.astype(bf16) for k, term in add_far(seq_terms, seq_relay).items()}

time: 411 us -> 404 us (0.983)
  waiting for transfers between devices: 114 us -> 103 us
    ppermute x30, waiting for transfers between devices: 93.9 us -> 83.1 us  [across_seq(): lax.ppermute(block, 'seq', [(i, i ^ by) for i in range(lax.axis_size('seq...]
    dot_general x14 -> x15, matrix products: 46.4 us -> 47.5 us  [dot(): return jnp.dot(first, second, preferred_element_type=f32)]
    unnamed x203 -> x191, local copies, waits for them, and re-layouts: 10.1 us -> 10.1 us
  transfers between devices with their start and end apart: 46 -> 46, of which waited for: 25 -> 24; matrix products, arithmetic and copies ran while one was open for 48% -> 49% of each run, Pallas kernels for 2% -> 2%
where the time goes in v9:
time: 404 us; the launch traced here: 397 us
  matrix products  129 us (32%)
  waiting for transfers between devices  103 us (25%)
  other arithmetic  56.2 us (14%)
  starting transfers between devices  49 us (12%)
  local copies, waits for them, and re-layouts  34.6 us (9%)
  between operations  15.8 us (4%)
  Pallas kernels  9.83 us (2%)
    ppermute x30, waiting for transfers between devices, across_seq(): lax.ppermute(block, 'seq', [(i, i ^ by) for i in range(lax.axis_size('seq...  83.1 us
    dot_general x15, matrix products, dot(): return jnp.dot(first, second, preferred_element_type=f32)  47.5 us
    dot_general x12, matrix products, right_contract(): lax.dot_general(first, second, (((1,), (1,)), ((), ())), preferred_elemen...  44.2 us
    dot_general x6, matrix products, left_contract(): lax.dot_general(first, second, (((0,), (0,)), ((), ())), preferred_elemen...  37.7 us
    ppermute x30, starting transfers between devices, across_seq(): lax.ppermute(block, 'seq', [(i, i ^ by) for i in range(lax.axis_size('seq...  32.4 us
    ppermute x6, waiting for transfers between devices, along_z(): lax.ppermute(block, 'dp', [(i, (i + 2 * by) % count) for i in range(count)])  12.1 us
    ppermute x6, starting transfers between devices, along_z(): lax.ppermute(block, 'dp', [(i, (i + 2 * by) % count) for i in range(count)])  11.4 us
    unnamed x191, local copies, waits for them, and re-layouts  10.1 us
  transfers between devices with their start and end apart: 46, of which 24 were waited for; matrix products, arithmetic and copies ran while one was open for 49% of the time, Pallas kernels for 2%

profile of v9, /device:TPU:8, one launch (start us, length us, event | category | flops | bytes accessed | tf_op | source)
XLA Modules:
  0.0 397.5 jit_solution(13875780191225957277)
XLA Ops:
  31.5 4.2 %collective-permute-start.4 = (bf16[32,2304]{1,0:T(8,128)(2,1)S(1)}, bf16[32,2304]{1,0:T(8,128)(2,1)S(1)}, u32[]{:S(2)}, u32[]{:S(2)}) collective-permute-start(bf16[32,2304]{1,0:T(8,128)(2,1)S(1)} %get-tuple-element.317), channel_id=1, source_target_pairs={{0,2},{1,3},{2,0},{3,1},{4,6},{5,7},{6,4},{7,5},{8,10},{9,11},{10,... | collective-permute-start | bytes 442376 | tf_op jit(solution)/shard_map/ppermute | solution.py:39
  36.4 3.5 collective-permute-done.4
  45.5 23.2 %collective-permute-done.7.refs_1_ = bf16[4,32,4224]{2,1,0:T(8,128)(2,1)S(1)} collective-permute-done((bf16[4,32,4224]{2,1,0:T(8,128)(2,1)S(1)}, bf16[4,32,4224]{2,1,0:T(8,128)(2,1)S(1)}, u32[]{:S(2)}, u32[]{:S(2)}) %collective-permute-start.7) | collective-permute-done | bytes 1081376 | tf_op jit(solution)/shard_map/ppermute | solution.py:39
  70.1 8.3 %collective-permute-done.10 = bf16[2,32,4224]{2,1,0:T(8,128)(2,1)S(1)} collective-permute-done((bf16[2,32,4224]{2,1,0:T(8,128)(2,1)S(1)}, bf16[2,32,4224]{2,1,0:T(8,128)(2,1)S(1)}, u32[]{:S(2)}, u32[]{:S(2)}) %collective-permute-start.10) | collective-permute-done | bytes 540704 | tf_op jit(solution)/shard_map/ppermute | solution.py:39
  87.3 3.4 collective-permute-done.11
  93.2 4.2 %fusion.39 = f32[528,3072]{1,0:T(8,128)S(1)} fusion(bf16[512,4224]{1,0:T(8,128)(2,1)} %bitcast.13, bf16[16,512]{1,0:T(8,128)(2,1)S(1)} %get-tuple-element.327, bf16[512,512]{1,0:T(8,128)(2,1)S(1)} %get-tuple-element.292), kind=kOutput, calls=%fused_computation.38 | convolution fusion | flops 1662025728 | bytes 10174464 | tf_op jit(solution)/shard_map/dot_general | solution.py:72
  97.4 3.9 convolution_add_fusion
  120.0 6.1 %collective-permute-done.15 = bf16[256,1024]{1,0:T(8,128)(2,1)S(1)} collective-permute-done((bf16[256,1024]{1,0:T(8,128)(2,1)S(1)}, bf16[256,1024]{1,0:T(8,128)(2,1)S(1)}, u32[]{:S(2)}, u32[]{:S(2)}) %collective-permute-start.15) | collective-permute-done | bytes 524320 | tf_op jit(solution)/shard_map/ppermute | solution.py:39
  129.6 6.7 %fusion.186 = f32[512,2304]{1,0:T(8,128)} fusion(bf16[512,1024]{1,0:T(8,128)(2,1)S(1)} %multiply_convert_fusion.12, bf16[1024,2304]{1,0:T(8,128)(2,1)} %bitcast.249), kind=kOutput, calls=%fused_computation.360 | convolution fusion | flops 2415919104 | bytes 10485760 | tf_op jit(solution)/shard_map/dot_general | solution.py:72
  136.4 5.5 %multiply_convert_fusion.10 = (bf16[512,1152]{1,0:T(8,128)(2,1)S(1)}, bf16[512,1152]{1,0:T(8,128)(2,1)S(1)}, bf16[512,1152]{1,0:T(8,128)(2,1)S(1)}) fusion(f32[512,2304]{1,0:T(8,128)} %fusion.186, bf16[1152,1024]{1,0:T(8,128)(2,1)} %all-gather.4.cloned.1.call-done, bf16[512,1024]{1,0:T(8,128)(2,1)S(1)} %bitcast.220), kind=kOutput, calls=%fused_computation.67 | convolution fusion | flops 1216806912 | bytes 11665408 | tf_op jit(solution)/shard_map/dot_general | solution.py:80
  146.5 4.0 fusion.168
  154.1 3.9 fusion.188
  160.8 3.5 multiply_convert_fusion.8
  169.5 4.5 %collective-permute-done.19 = bf16[256,1024]{1,0:T(8,128)(2,1)S(1)} collective-permute-done((bf16[256,1024]{1,0:T(8,128)(2,1)S(1)}, bf16[256,1024]{1,0:T(8,128)(2,1)S(1)}, u32[]{:S(2)}, u32[]{:S(2)}) %collective-permute-start.19) | collective-permute-done | bytes 524320 | tf_op jit(solution)/shard_map/ppermute | solution.py:39
  174.1 4.5 %fusion.189 = f32[512,2304]{1,0:T(8,128)S(1)} fusion(bf16[512,1024]{1,0:T(8,128)(2,1)} %collective-permute-done.17, bf16[1024,2304]{1,0:T(8,128)(2,1)S(1)} %bitcast.255), kind=kOutput, calls=%fused_computation.363 | convolution fusion | flops 2415919104 | bytes 10485760 | tf_op jit(solution)/shard_map/dot_general | solution.py:72
  178.6 3.5 multiply_convert_fusion.6
  183.8 3.6 convolution_convert_fusion.1
  205.7 8.2 %fusion.33 = bf16[1152,1024]{1,0:T(8,128)(2,1)} fusion(bf16[512,1024]{1,0:T(8,128)(2,1)S(1)} %pad_maximum_fusion.9, bf16[512,1024]{1,0:T(8,128)(2,1)} %collective-permute-done.13, bf16[512,1024]{1,0:T(8,128)(2,1)} %collective-permute-done.12, bf16[512,1024]{1,0:T(8,128)(2,1)S(1)} %bitcast.221, bf16[512,1152]{1,0:T(8,128)(2,1)S(1)} %get-tuple-element.170, ...), kind=kOutput, calls=%fused_computation.35 | convolution fusion | flops 4868669440 | bytes 11272192 | tf_op jit(solution)/shard_map/dot_general | solution.py:76
  213.9 4.9 %fusion.191 = f32[512,1024]{1,0:T(8,128)} fusion(bf16[512,1152]{1,0:T(8,128)(2,1)} %copy-done.87, bf16[1152,1024]{1,0:T(8,128)(2,1)} %all-gather.4.cloned.1.call-done), kind=kOutput, calls=%fused_computation.365 | convolution fusion | flops 1207959552 | bytes 5636096 | tf_op jit(solution)/shard_map/dot_general | solution.py:72
  218.7 3.8 shard_map.409
  230.7 16.7 %fusion.8 = bf16[1024,2304]{1,0:T(8,128)(2,1)} fusion(bf16[512,2304]{1,0:T(8,128)(2,1)} %pad_maximum_fusion.2, bf16[512,2304]{1,0:T(8,128)(2,1)} %pad_maximum_fusion.5, bf16[512,2304]{1,0:T(8,128)(2,1)} %pad_maximum_fusion.4, bf16[512,2304]{1,0:T(8,128)(2,1)} %pad_maximum_fusion.3, bf16[512,1024]{1,0:T(8,128)(2,1)} %copy-done.31, ...), kind=kOutput, calls=%fused_computation.9 | convolution fusion | flops 9720561664 | bytes 18350080 | tf_op jit(solution)/shard_map/dot_general | solution.py:76
  247.4 4.0 %multiply_reduce_fusion = (f32[1024]{0:T(1024)S(1)}, f32[512]{0:T(512)S(1)}, f32[512,1024]{1,0:T(8,128)S(1)}) fusion(f32[512,1024]{1,0:T(8,128)} %copy-done.4, f32[512]{0:T(512)S(1)} %add_rsqrt_fusion, f32[1024]{0:T(1024)S(1)} %bitcast.229, bf16[256,1024]{1,0:T(8,128)(2,1)} %collective-permute-done.22, bf16[256,1024]{1,0:T(8,128)(2,1)} %collective-permute-done.21, ...), kind=kLoop, calls=%fused_computation.102 | loop fusion | flops 7862784 | bytes 9449472 | tf_op jit(solution)/shard_map/reduce_sum | solution.py:120
  253.1 4.8 %multiply_reduce_fusion.1 = (f32[1024]{0:T(1024)S(1)}, f32[1024]{0:T(1024)}, f32[1024]{0:T(1024)}, f32[512,1024]{1,0:T(8,128)S(1)}, f32[512,1024]{1,0:T(8,128)S(1)}) fusion(f32[2,258,1024]{2,1,0:T(8,128)S(1)} %copy-done.2, f32[2,256]{1,0:T(2,128)S(1)} %get-tuple-element.337, f32[2,256]{1,0:T(2,128)S(1)} %get-tuple-element.336, f32[528,3072]{1,0:T(8,128)} %copy-done.3, ...), kind=kOutput, calls=%fused_computation.103 | convolution fusion | flops 1078981632 | bytes 16793600 | tf_op jit(solution)/shard_map/dot_general | solution.py:80
  265.6 3.4 convolution_convert_fusion
  276.8 9.4 %fusion.57 = (f32[512]{0:T(512)}, f32[1024]{0:T(1024)}, f32[512,1024]{1,0:T(8,128)}) fusion(bf16[2,256,1024]{2,1,0:T(8,128)(2,1)S(1)} %copy-done.13, f32[1024]{0:T(1024)S(1)} %bitcast.233, f32[512]{0:T(512)S(1)} %bitcast.242, bf16[1024,3072]{1,0:T(8,128)(2,1)} %bitcast.197, bf16[512,1024]{1,0:T(8,128)(2,1)} %copy-done.37, bf16[512,1024]{1,0:T(8,128)(2,1)} %copy-done.28, ...), kind=kOutput, calls=%fused_computation.95 | convolution fusion | flops 3234331136 | bytes 12595200 | tf_op jit(solution)/shard_map/dot_general | solution.py:80
  291.5 3.5 fusion.60
  298.4 4.2 %add_convert_fusion = bf16[512,3072]{1,0:T(8,128)(2,1)S(1)} fusion(bf16[512,3072]{1,0:T(8,128)(2,1)} %collective-permute-done.25, bf16[512,512]{1,0:T(8,128)(2,1)S(1)} %copy-done.44, bf16[512,1024]{1,0:T(8,128)(2,1)S(1)} %copy-done.38, bf16[512,1024]{1,0:T(8,128)(2,1)S(1)} %copy-done.29, bf16[512,1024]{1,0:T(8,128)(2,1)S(1)} %copy-done.36), kind=kOutput, calls=%fused_computation.8 | convolution fusion | flops 1624768512 | bytes 9961472 | tf_op jit(solution)/shard_map/dot_general | solution.py:76
  314.3 6.1 %collective-permute-done.30 = bf16[2,32,4224]{2,1,0:T(8,128)(2,1)} collective-permute-done((bf16[2,32,4224]{2,1,0:T(8,128)(2,1)}, bf16[2,32,4224]{2,1,0:T(8,128)(2,1)}, u32[]{:S(2)}, u32[]{:S(2)}) %collective-permute-start.30) | collective-permute-done | bytes 540704 | tf_op jit(solution)/shard_map/ppermute | solution.py:39
  336.5 16.2 %collective-permute-done.35 = bf16[4,32,4224]{2,1,0:T(8,128)(2,1)S(1)} collective-permute-done((bf16[4,32,4224]{2,1,0:T(8,128)(2,1)}, bf16[4,32,4224]{2,1,0:T(8,128)(2,1)S(1)}, u32[]{:S(2)}, u32[]{:S(2)}) %collective-permute-start.35) | collective-permute-done | bytes 1081376 | tf_op jit(solution)/shard_map/ppermute | solution.py:39
  359.4 4.4 %collective-permute-start.39 = (bf16[32,4224]{1,0:T(8,128)(2,1)S(1)}, bf16[32,4224]{1,0:T(8,128)(2,1)S(1)}, u32[]{:S(2)}, u32[]{:S(2)}) collective-permute-start(bf16[32,4224]{1,0:T(8,128)(2,1)S(1)} %get-tuple-element.282), channel_id=1, source_target_pairs={{0,8},{4,12},{8,16},{12,20},{16,24},{20,28},{24,0},{28,4},{1,9},{5... | collective-permute-start | bytes 811016 | tf_op jit(solution)/shard_map/ppermute | solution.py:35
  371.9 8.3 %collective-permute-done.39 = bf16[32,4224]{1,0:T(8,128)(2,1)S(1)} collective-permute-done((bf16[32,4224]{1,0:T(8,128)(2,1)S(1)}, bf16[32,4224]{1,0:T(8,128)(2,1)S(1)}, u32[]{:S(2)}, u32[]{:S(2)}) %collective-permute-start.39) | collective-permute-done | bytes 270368 | tf_op jit(solution)/shard_map/ppermute | solution.py:35
  380.3 3.4 collective-permute-done.40
  (409 shorter events, 183.9 us)
Async XLA Ops:
  7.2 122.4 %all-gather.6.cloned.1.call-start = ((), (), s32[]{:S(2)}) async-start(), calls=%async_computation.5 | async-start | bytes 5308416 | tf_op jit(solution)/shard_map/all_gather | solution.py:205
  11.3 30.5 %collective-permute-start = (bf16[32,4224]{1,0:T(8,128)(2,1)}, bf16[32,4224]{1,0:T(8,128)(2,1)S(1)}, u32[]{:S(2)}, u32[]{:S(2)}) collective-permute-start(bf16[32,4224]{1,0:T(8,128)(2,1)} %get-tuple-element.319), channel_id=1, source_target_pairs={{0,24},{4,28},{8,0},{12,4},{16,8},{20,12},{24,16},{28,20},{1,25},{... | collective-permute-start | bytes 811016 | tf_op jit(solution)/shard_map/ppermute | solution.py:35
  11.3 30.5 %collective-permute-start.1 = (bf16[32,4224]{1,0:T(8,128)(2,1)}, bf16[32,4224]{1,0:T(8,128)(2,1)S(1)}, u32[]{:S(2)}, u32[]{:S(2)}) collective-permute-start(bf16[32,4224]{1,0:T(8,128)(2,1)} %get-tuple-element.319), channel_id=1, source_target_pairs={{0,16},{4,20},{8,24},{12,28},{16,0},{20,4},{24,8},{28,12},{1,17},{... | collective-permute-start | bytes 811016 | tf_op jit(solution)/shard_map/ppermute | solution.py:35
  14.3 27.5 %collective-permute-start.2 = (bf16[32,4224]{1,0:T(8,128)(2,1)}, bf16[32,4224]{1,0:T(8,128)(2,1)S(1)}, u32[]{:S(2)}, u32[]{:S(2)}) collective-permute-start(bf16[32,4224]{1,0:T(8,128)(2,1)} %get-tuple-element.319), channel_id=1, source_target_pairs={{0,8},{4,12},{8,16},{12,20},{16,24},{20,28},{24,0},{28,4},{1,9},{5... | collective-permute-start | bytes 811016 | tf_op jit(solution)/shard_map/ppermute | solution.py:35
  43.8 92.6 %all-gather.4.cloned.1.call-start = ((), (), s32[]{:S(2)}) async-start(), calls=%async_computation.2 | async-start | bytes 2654208 | tf_op jit(solution)/shard_map/all_gather | solution.py:206
  44.8 23.9 %collective-permute-start.7 = (bf16[4,32,4224]{2,1,0:T(8,128)(2,1)S(1)}, bf16[4,32,4224]{2,1,0:T(8,128)(2,1)S(1)}, u32[]{:S(2)}, u32[]{:S(2)}) collective-permute-start(bf16[4,32,4224]{2,1,0:T(8,128)(2,1)S(1)} %bitcast.198), channel_id=1, source_target_pairs={{0,1},{1,0},{2,3},{3,2},{4,5},{5,4},{6,7},{7,6},{8,9},{9,8},{10,11... | collective-permute-start | bytes 3244040 | tf_op jit(solution)/shard_map/ppermute | solution.py:39
  44.8 23.8 %collective-permute-start.8 = (bf16[4,32,4224]{2,1,0:T(8,128)(2,1)S(1)}, bf16[4,32,4224]{2,1,0:T(8,128)(2,1)S(1)}, u32[]{:S(2)}, u32[]{:S(2)}) collective-permute-start(bf16[4,32,4224]{2,1,0:T(8,128)(2,1)S(1)} %bitcast.199), channel_id=1, source_target_pairs={{0,2},{1,3},{2,0},{3,1},{4,6},{5,7},{6,4},{7,5},{8,10},{9,11},{10,... | collective-permute-start | bytes 3244040 | tf_op jit(solution)/shard_map/ppermute | solution.py:39
  83.4 224.1 %reduce-scatter.3.cloned.1.call-start = ((), (), s32[]{:S(2)}) async-start(), calls=%async_computation.3 | async-start | bytes 5308416 | tf_op jit(solution)/shard_map/reduce_scatter | solution.py:348
  84.2 26.7 %collective-permute-start.12 = (bf16[512,1024]{1,0:T(8,128)(2,1)S(1)}, bf16[512,1024]{1,0:T(8,128)(2,1)}, u32[]{:S(2)}, u32[]{:S(2)}) collective-permute-start(bf16[512,1024]{1,0:T(8,128)(2,1)S(1)} %bitcast.218), channel_id=1, source_target_pairs={{0,1},{1,0},{2,3},{3,2},{4,5},{5,4},{6,7},{7,6},{8,9},{9,8},{10,11... | collective-permute-start | bytes 3145736 | tf_op jit(solution)/shard_map/ppermute | solution.py:39
  85.1 25.9 %collective-permute-start.13 = (bf16[512,1024]{1,0:T(8,128)(2,1)S(1)}, bf16[512,1024]{1,0:T(8,128)(2,1)}, u32[]{:S(2)}, u32[]{:S(2)}) collective-permute-start(bf16[512,1024]{1,0:T(8,128)(2,1)S(1)} %bitcast.219), channel_id=1, source_target_pairs={{0,2},{1,3},{2,0},{3,1},{4,6},{5,7},{6,4},{7,5},{8,10},{9,11},{10,... | collective-permute-start | bytes 3145736 | tf_op jit(solution)/shard_map/ppermute | solution.py:39
  127.8 24.1 %collective-permute-start.16 = (bf16[512,1024]{1,0:T(8,128)(2,1)S(1)}, bf16[512,1024]{1,0:T(8,128)(2,1)}, u32[]{:S(2)}, u32[]{:S(2)}) collective-permute-start(bf16[512,1024]{1,0:T(8,128)(2,1)S(1)} %multiply_convert_fusion.12), channel_id=1, source_target_pairs={{0,1},{1,0},{2,3},{3,2},{4,5},{5,4},{6,7},{7,6},{8,9},{9,8},{10,11... | collective-permute-start | bytes 3145736 | tf_op jit(solution)/shard_map/ppermute | solution.py:39
  129.2 23.9 %collective-permute-start.17 = (bf16[512,1024]{1,0:T(8,128)(2,1)S(1)}, bf16[512,1024]{1,0:T(8,128)(2,1)}, u32[]{:S(2)}, u32[]{:S(2)}) collective-permute-start(bf16[512,1024]{1,0:T(8,128)(2,1)S(1)} %multiply_convert_fusion.12), channel_id=1, source_target_pairs={{0,2},{1,3},{2,0},{3,1},{4,6},{5,7},{6,4},{7,5},{8,10},{9,11},{10,... | collective-permute-start | bytes 3145736 | tf_op jit(solution)/shard_map/ppermute | solution.py:39
  159.1 14.9 %collective-permute-start.19 = (bf16[256,1024]{1,0:T(8,128)(2,1)S(1)}, bf16[256,1024]{1,0:T(8,128)(2,1)S(1)}, u32[]{:S(2)}, u32[]{:S(2)}) collective-permute-start(bf16[256,1024]{1,0:T(8,128)(2,1)S(1)} %slice.363), channel_id=1, source_target_pairs={{0,1},{1,0},{2,3},{3,2},{4,5},{5,4},{6,7},{7,6},{8,9},{9,8},{10,11... | collective-permute-start | bytes 1572872 | tf_op jit(solution)/shard_map/ppermute | solution.py:39
  167.0 38.7 %collective-permute-start.20 = (bf16[512,1024]{1,0:T(8,128)(2,1)S(1)}, bf16[512,1024]{1,0:T(8,128)(2,1)S(1)}, u32[]{:S(2)}, u32[]{:S(2)}) collective-permute-start(bf16[512,1024]{1,0:T(8,128)(2,1)S(1)} %convolution_convert_fusion.2), channel_id=1, source_target_pairs={{0,1},{1,0},{2,3},{3,2},{4,5},{5,4},{6,7},{7,6},{8,9},{9,8},{10,11... | collective-permute-start | bytes 3145736 | tf_op jit(solution)/shard_map/ppermute | solution.py:39
  196.8 50.5 %collective-permute-start.23 = (bf16[512,1024]{1,0:T(8,128)(2,1)}, bf16[512,1024]{1,0:T(8,128)(2,1)}, u32[]{:S(2)}, u32[]{:S(2)}) collective-permute-start(bf16[512,1024]{1,0:T(8,128)(2,1)} %convolution_convert_fusion.1), channel_id=1, source_target_pairs={{0,2},{1,3},{2,0},{3,1},{4,6},{5,7},{6,4},{7,5},{8,10},{9,11},{10,... | collective-permute-start | bytes 3145736 | tf_op jit(solution)/shard_map/ppermute | solution.py:39
  197.3 33.3 %collective-permute-start.21 = (bf16[256,1024]{1,0:T(8,128)(2,1)}, bf16[256,1024]{1,0:T(8,128)(2,1)}, u32[]{:S(2)}, u32[]{:S(2)}) collective-permute-start(bf16[256,1024]{1,0:T(8,128)(2,1)} %convolution_convert_fusion.7), channel_id=1, source_target_pairs={{0,3},{1,2},{2,1},{3,0},{4,7},{5,6},{6,5},{7,4},{8,11},{9,10},{10,... | collective-permute-start | bytes 1572872 | tf_op jit(solution)/shard_map/ppermute | solution.py:39
  198.9 48.4 %collective-permute-start.22 = (bf16[256,1024]{1,0:T(8,128)(2,1)}, bf16[256,1024]{1,0:T(8,128)(2,1)}, u32[]{:S(2)}, u32[]{:S(2)}) collective-permute-start(bf16[256,1024]{1,0:T(8,128)(2,1)} %convolution_convert_fusion.6), channel_id=1, source_target_pairs={{0,3},{1,2},{2,1},{3,0},{4,7},{5,6},{6,5},{7,4},{8,11},{9,10},{10,... | collective-permute-start | bytes 1572872 | tf_op jit(solution)/shard_map/ppermute | solution.py:39
  247.4 111.9 %reduce-scatter.5.cloned.1.call-start = ((), (), s32[]{:S(2)}) async-start(), calls=%async_computation.4 | async-start | bytes 2654208 | tf_op jit(solution)/shard_map/reduce_scatter | solution.py:349
  269.0 29.3 %collective-permute-start.25 = (bf16[512,3072]{1,0:T(8,128)(2,1)}, bf16[512,3072]{1,0:T(8,128)(2,1)}, u32[]{:S(2)}, u32[]{:S(2)}) collective-permute-start(bf16[512,3072]{1,0:T(8,128)(2,1)} %convolution_convert_fusion), channel_id=1, source_target_pairs={{0,4},{4,0},{8,12},{12,8},{16,20},{20,16},{24,28},{28,24},{1,5},{5... | collective-permute-start | bytes 9437192 | tf_op jit(solution)/shard_map/ppermute | solution.py:30
  276.3 19.5 %collective-permute-start.26 = (bf16[512,1024]{1,0:T(8,128)(2,1)}, bf16[512,1024]{1,0:T(8,128)(2,1)}, u32[]{:S(2)}, u32[]{:S(2)}) collective-permute-start(bf16[512,1024]{1,0:T(8,128)(2,1)} %convolution_convert_fusion.3), channel_id=1, source_target_pairs={{0,4},{4,0},{8,12},{12,8},{16,20},{20,16},{24,28},{28,24},{1,5},{5... | collective-permute-start | bytes 3145736 | tf_op jit(solution)/shard_map/ppermute | solution.py:30
  287.6 15.4 %collective-permute-start.28 = (bf16[256,1024]{1,0:T(8,128)(2,1)}, bf16[256,1024]{1,0:T(8,128)(2,1)S(1)}, u32[]{:S(2)}, u32[]{:S(2)}) collective-permute-start(bf16[256,1024]{1,0:T(8,128)(2,1)} %convolution_convert_fusion.5), channel_id=1, source_target_pairs={{0,1},{1,0},{2,3},{3,2},{4,5},{5,4},{6,7},{7,6},{8,9},{9,8},{10,11... | collective-permute-start | bytes 1572872 | tf_op jit(solution)/shard_map/ppermute | solution.py:39
  304.9 15.5 %collective-permute-start.30 = (bf16[2,32,4224]{2,1,0:T(8,128)(2,1)}, bf16[2,32,4224]{2,1,0:T(8,128)(2,1)}, u32[]{:S(2)}, u32[]{:S(2)}) collective-permute-start(bf16[2,32,4224]{2,1,0:T(8,128)(2,1)} %get-tuple-element.274), channel_id=1, source_target_pairs={{0,1},{1,0},{2,3},{3,2},{4,5},{5,4},{6,7},{7,6},{8,9},{9,8},{10,11... | collective-permute-start | bytes 1622024 | tf_op jit(solution)/shard_map/ppermute | solution.py:39
  305.3 15.5 %collective-permute-start.31 = (bf16[2,32,4224]{2,1,0:T(8,128)(2,1)}, bf16[2,32,4224]{2,1,0:T(8,128)(2,1)}, u32[]{:S(2)}, u32[]{:S(2)}) collective-permute-start(bf16[2,32,4224]{2,1,0:T(8,128)(2,1)} %get-tuple-element.276), channel_id=1, source_target_pairs={{0,2},{1,3},{2,0},{3,1},{4,6},{5,7},{6,4},{7,5},{8,10},{9,11},{10,... | collective-permute-start | bytes 1622024 | tf_op jit(solution)/shard_map/ppermute | solution.py:39
  308.6 14.7 %collective-permute-start.32 = (bf16[32,2304]{1,0:T(8,128)(2,1)S(1)}, bf16[32,2304]{1,0:T(8,128)(2,1)S(1)}, u32[]{:S(2)}, u32[]{:S(2)}) collective-permute-start(bf16[32,2304]{1,0:T(8,128)(2,1)S(1)} %get-tuple-element.310), channel_id=1, source_target_pairs={{0,1},{1,0},{2,3},{3,2},{4,5},{5,4},{6,7},{7,6},{8,9},{9,8},{10,11... | collective-permute-start | bytes 442376 | tf_op jit(solution)/shard_map/ppermute | solution.py:39
  310.5 15.1 %collective-permute-start.34 = (bf16[32,2304]{1,0:T(8,128)(2,1)S(1)}, bf16[32,2304]{1,0:T(8,128)(2,1)S(1)}, u32[]{:S(2)}, u32[]{:S(2)}) collective-permute-start(bf16[32,2304]{1,0:T(8,128)(2,1)S(1)} %get-tuple-element.308), channel_id=1, source_target_pairs={{0,3},{1,2},{2,1},{3,0},{4,7},{5,6},{6,5},{7,4},{8,11},{9,10},{10,... | collective-permute-start | bytes 442376 | tf_op jit(solution)/shard_map/ppermute | solution.py:39
  328.6 24.1 %collective-permute-start.35 = (bf16[4,32,4224]{2,1,0:T(8,128)(2,1)}, bf16[4,32,4224]{2,1,0:T(8,128)(2,1)S(1)}, u32[]{:S(2)}, u32[]{:S(2)}) collective-permute-start(bf16[4,32,4224]{2,1,0:T(8,128)(2,1)} %pad_maximum_fusion.7), channel_id=1, source_target_pairs={{0,1},{1,0},{2,3},{3,2},{4,5},{5,4},{6,7},{7,6},{8,9},{9,8},{10,11... | collective-permute-start | bytes 3244040 | tf_op jit(solution)/shard_map/ppermute | solution.py:39
  330.7 24.0 %collective-permute-start.36 = (bf16[4,32,4224]{2,1,0:T(8,128)(2,1)}, bf16[4,32,4224]{2,1,0:T(8,128)(2,1)}, u32[]{:S(2)}, u32[]{:S(2)}) collective-permute-start(bf16[4,32,4224]{2,1,0:T(8,128)(2,1)} %pad_maximum_fusion.8), channel_id=1, source_target_pairs={{0,2},{1,3},{2,0},{3,1},{4,6},{5,7},{6,4},{7,5},{8,10},{9,11},{10,... | collective-permute-start | bytes 3244040 | tf_op jit(solution)/shard_map/ppermute | solution.py:39
  354.7 32.7 %collective-permute-start.38 = (bf16[512,1024]{1,0:T(8,128)(2,1)}, bf16[512,1024]{1,0:T(8,128)(2,1)}, u32[]{:S(2)}, u32[]{:S(2)}) collective-permute-start(bf16[512,1024]{1,0:T(8,128)(2,1)} %pad_maximum_fusion.12), channel_id=1, source_target_pairs={{0,2},{1,3},{2,0},{3,1},{4,6},{5,7},{6,4},{7,5},{8,10},{9,11},{10,... | collective-permute-start | bytes 3145736 | tf_op jit(solution)/shard_map/ppermute | solution.py:39
  356.0 31.4 %collective-permute-start.37 = (bf16[512,1024]{1,0:T(8,128)(2,1)}, bf16[512,1024]{1,0:T(8,128)(2,1)}, u32[]{:S(2)}, u32[]{:S(2)}) collective-permute-start(bf16[512,1024]{1,0:T(8,128)(2,1)} %pad_maximum_fusion.11), channel_id=1, source_target_pairs={{0,1},{1,0},{2,3},{3,2},{4,5},{5,4},{6,7},{7,6},{8,9},{9,8},{10,11... | collective-permute-start | bytes 3145736 | tf_op jit(solution)/shard_map/ppermute | solution.py:39
  359.4 20.9 %collective-permute-start.39 = (bf16[32,4224]{1,0:T(8,128)(2,1)S(1)}, bf16[32,4224]{1,0:T(8,128)(2,1)S(1)}, u32[]{:S(2)}, u32[]{:S(2)}) collective-permute-start(bf16[32,4224]{1,0:T(8,128)(2,1)S(1)} %get-tuple-element.282), channel_id=1, source_target_pairs={{0,8},{4,12},{8,16},{12,20},{16,24},{20,28},{24,0},{28,4},{1,9},{5... | collective-permute-start | bytes 811016 | tf_op jit(solution)/shard_map/ppermute | solution.py:35
  363.7 20.0 %collective-permute-start.40 = (bf16[32,4224]{1,0:T(8,128)(2,1)S(1)}, bf16[32,4224]{1,0:T(8,128)(2,1)S(1)}, u32[]{:S(2)}, u32[]{:S(2)}) collective-permute-start(bf16[32,4224]{1,0:T(8,128)(2,1)S(1)} %get-tuple-element.281), channel_id=1, source_target_pairs={{0,16},{4,20},{8,24},{12,28},{16,0},{20,4},{24,8},{28,12},{1,17},{... | collective-permute-start | bytes 811016 | tf_op jit(solution)/shard_map/ppermute | solution.py:35
  364.1 20.0 %collective-permute-start.41 = (bf16[32,4224]{1,0:T(8,128)(2,1)S(1)}, bf16[32,4224]{1,0:T(8,128)(2,1)S(1)}, u32[]{:S(2)}, u32[]{:S(2)}) collective-permute-start(bf16[32,4224]{1,0:T(8,128)(2,1)S(1)} %get-tuple-element.280), channel_id=1, source_target_pairs={{0,24},{4,28},{8,0},{12,4},{16,8},{20,12},{24,16},{28,20},{1,25},{... | collective-permute-start | bytes 811016 | tf_op jit(solution)/shard_map/ppermute | solution.py:35
  (108 other events, 736.5 us)
Sparse Core Ops, SparseCore 0:
  43.9 48.1 all-gather.5
  94.3 31.4 all-gather.3
  247.5 53.2 reduce-scatter.2
  303.0 34.0 reduce-scatter.4

commit v10 on v9

--- a/solution.py
+++ b/solution.py
@@ -416,7 +416,7 @@
     if n_seq == 4:
         far_block = seq_block(sq ^ last)
         seq_relay = sum_far((far_block[: n_z // 2], far_block[n_z // 2 :]))
-        seq_relay, gu_parts = tie((seq_relay, gu_parts))
+        seq_relay = tie(seq_relay)
         seq_terms = {k: term.astype(f32) for k, term in seq_terms.items()}
         seq_terms = {k: term.astype(bf16) for k, term in add_far(seq_terms, seq_relay).items()}
     seq_parts = [across_seq(seq_terms[k], k) for k in near]

time: 404 us -> 405 us (level)
  transfers between devices with their start and end apart: 46 -> 46, of which waited for: 24 -> 21; matrix products, arithmetic and copies ran while one was open for 49% -> 48% of each run, Pallas kernels for 2% -> 2%
where the time goes in v10:
time: 405 us; the launch traced here: 399 us
  matrix products  130 us (32%)
  waiting for transfers between devices  106 us (26%)
  other arithmetic  54.6 us (13%)
  starting transfers between devices  49.6 us (12%)
  local copies, waits for them, and re-layouts  33.8 us (8%)
  between operations  15.8 us (4%)
  Pallas kernels  9.83 us (2%)
    ppermute x30, waiting for transfers between devices, across_seq(): lax.ppermute(block, 'seq', [(i, i ^ by) for i in range(lax.axis_size('seq...  85.1 us
    dot_general x15, matrix products, dot(): return jnp.dot(first, second, preferred_element_type=f32)  47.5 us
    dot_general x12, matrix products, right_contract(): lax.dot_general(first, second, (((1,), (1,)), ((), ())), preferred_elemen...  44.2 us
    dot_general x6, matrix products, left_contract(): lax.dot_general(first, second, (((0,), (0,)), ((), ())), preferred_elemen...  37.8 us
    ppermute x30, starting transfers between devices, across_seq(): lax.ppermute(block, 'seq', [(i, i ^ by) for i in range(lax.axis_size('seq...  32.8 us
    ppermute x6, waiting for transfers between devices, along_z(): lax.ppermute(block, 'dp', [(i, (i + 2 * by) % count) for i in range(count)])  12.9 us
    ppermute x6, starting transfers between devices, along_z(): lax.ppermute(block, 'dp', [(i, (i + 2 * by) % count) for i in range(count)])  11.5 us
    unnamed x191, local copies, waits for them, and re-layouts  10.3 us
  transfers between devices with their start and end apart: 46, of which 21 were waited for; matrix products, arithmetic and copies ran while one was open for 48% of the time, Pallas kernels for 2%

profile of v10, /device:TPU:8, one launch (start us, length us, event | category | flops | bytes accessed | tf_op | source)
XLA Modules:
  0.0 398.6 jit_solution(13824688661562166701)
XLA Ops:
  31.5 4.2 %collective-permute-start.4 = (bf16[32,2304]{1,0:T(8,128)(2,1)S(1)}, bf16[32,2304]{1,0:T(8,128)(2,1)S(1)}, u32[]{:S(2)}, u32[]{:S(2)}) collective-permute-start(bf16[32,2304]{1,0:T(8,128)(2,1)S(1)} %get-tuple-element.311), channel_id=1, source_target_pairs={{0,2},{1,3},{2,0},{3,1},{4,6},{5,7},{6,4},{7,5},{8,10},{9,11},{10,... | collective-permute-start | bytes 442376 | tf_op jit(solution)/shard_map/ppermute | solution.py:39
  36.4 3.5 collective-permute-done.4
  45.5 23.2 %collective-permute-done.7.refs_1_ = bf16[4,32,4224]{2,1,0:T(8,128)(2,1)S(1)} collective-permute-done((bf16[4,32,4224]{2,1,0:T(8,128)(2,1)S(1)}, bf16[4,32,4224]{2,1,0:T(8,128)(2,1)S(1)}, u32[]{:S(2)}, u32[]{:S(2)}) %collective-permute-start.7) | collective-permute-done | bytes 1081376 | tf_op jit(solution)/shard_map/ppermute | solution.py:39
  70.1 8.3 %collective-permute-done.10 = bf16[2,32,4224]{2,1,0:T(8,128)(2,1)S(1)} collective-permute-done((bf16[2,32,4224]{2,1,0:T(8,128)(2,1)S(1)}, bf16[2,32,4224]{2,1,0:T(8,128)(2,1)S(1)}, u32[]{:S(2)}, u32[]{:S(2)}) %collective-permute-start.10) | collective-permute-done | bytes 540704 | tf_op jit(solution)/shard_map/ppermute | solution.py:39
  87.3 3.4 collective-permute-done.11
  93.2 4.2 %fusion.39 = f32[528,3072]{1,0:T(8,128)S(1)} fusion(bf16[512,4224]{1,0:T(8,128)(2,1)} %bitcast.13, bf16[16,512]{1,0:T(8,128)(2,1)S(1)} %get-tuple-element.321, bf16[512,512]{1,0:T(8,128)(2,1)S(1)} %get-tuple-element.286), kind=kOutput, calls=%fused_computation.38 | convolution fusion | flops 1662025728 | bytes 10174464 | tf_op jit(solution)/shard_map/dot_general | solution.py:72
  97.4 3.9 convolution_add_fusion
  120.0 6.2 %collective-permute-done.15 = bf16[256,1024]{1,0:T(8,128)(2,1)S(1)} collective-permute-done((bf16[256,1024]{1,0:T(8,128)(2,1)S(1)}, bf16[256,1024]{1,0:T(8,128)(2,1)S(1)}, u32[]{:S(2)}, u32[]{:S(2)}) %collective-permute-start.15) | collective-permute-done | bytes 524320 | tf_op jit(solution)/shard_map/ppermute | solution.py:39
  129.6 6.7 %fusion.186 = f32[512,2304]{1,0:T(8,128)} fusion(bf16[512,1024]{1,0:T(8,128)(2,1)S(1)} %multiply_convert_fusion.12, bf16[1024,2304]{1,0:T(8,128)(2,1)} %bitcast.249), kind=kOutput, calls=%fused_computation.360 | convolution fusion | flops 2415919104 | bytes 10485760 | tf_op jit(solution)/shard_map/dot_general | solution.py:72
  136.4 5.5 %multiply_convert_fusion.10 = (bf16[512,1152]{1,0:T(8,128)(2,1)S(1)}, bf16[512,1152]{1,0:T(8,128)(2,1)S(1)}, bf16[512,1152]{1,0:T(8,128)(2,1)S(1)}) fusion(f32[512,2304]{1,0:T(8,128)} %fusion.186, bf16[1152,1024]{1,0:T(8,128)(2,1)} %all-gather.4.cloned.1.call-done, bf16[512,1024]{1,0:T(8,128)(2,1)S(1)} %bitcast.220), kind=kOutput, calls=%fused_computation.67 | convolution fusion | flops 1216806912 | bytes 11665408 | tf_op jit(solution)/shard_map/dot_general | solution.py:80
  146.5 4.0 fusion.168
  154.2 3.9 fusion.188
  160.8 3.5 multiply_convert_fusion.8
  169.5 4.5 %collective-permute-done.19 = bf16[256,1024]{1,0:T(8,128)(2,1)S(1)} collective-permute-done((bf16[256,1024]{1,0:T(8,128)(2,1)S(1)}, bf16[256,1024]{1,0:T(8,128)(2,1)S(1)}, u32[]{:S(2)}, u32[]{:S(2)}) %collective-permute-start.19) | collective-permute-done | bytes 524320 | tf_op jit(solution)/shard_map/ppermute | solution.py:39
  174.1 4.5 %fusion.189 = f32[512,2304]{1,0:T(8,128)S(1)} fusion(bf16[512,1024]{1,0:T(8,128)(2,1)} %collective-permute-done.17, bf16[1024,2304]{1,0:T(8,128)(2,1)S(1)} %bitcast.255), kind=kOutput, calls=%fused_computation.363 | convolution fusion | flops 2415919104 | bytes 10485760 | tf_op jit(solution)/shard_map/dot_general | solution.py:72
  178.6 3.5 multiply_convert_fusion.6
  183.8 3.6 convolution_convert_fusion.1
  205.7 8.2 %fusion.33 = bf16[1152,1024]{1,0:T(8,128)(2,1)} fusion(bf16[512,1024]{1,0:T(8,128)(2,1)S(1)} %pad_maximum_fusion.9, bf16[512,1024]{1,0:T(8,128)(2,1)} %collective-permute-done.13, bf16[512,1024]{1,0:T(8,128)(2,1)} %collective-permute-done.12, bf16[512,1024]{1,0:T(8,128)(2,1)S(1)} %bitcast.221, bf16[512,1152]{1,0:T(8,128)(2,1)S(1)} %get-tuple-element.167, ...), kind=kOutput, calls=%fused_computation.35 | convolution fusion | flops 4868669440 | bytes 11272192 | tf_op jit(solution)/shard_map/dot_general | solution.py:76
  213.9 4.9 %fusion.191 = f32[512,1024]{1,0:T(8,128)} fusion(bf16[512,1152]{1,0:T(8,128)(2,1)} %copy-done.87, bf16[1152,1024]{1,0:T(8,128)(2,1)} %all-gather.4.cloned.1.call-done), kind=kOutput, calls=%fused_computation.365 | convolution fusion | flops 1207959552 | bytes 5636096 | tf_op jit(solution)/shard_map/dot_general | solution.py:72
  218.8 3.8 shard_map.409
  230.7 16.7 %fusion.8 = bf16[1024,2304]{1,0:T(8,128)(2,1)} fusion(bf16[512,2304]{1,0:T(8,128)(2,1)} %pad_maximum_fusion.2, bf16[512,2304]{1,0:T(8,128)(2,1)} %pad_maximum_fusion.5, bf16[512,2304]{1,0:T(8,128)(2,1)} %pad_maximum_fusion.4, bf16[512,2304]{1,0:T(8,128)(2,1)} %pad_maximum_fusion.3, bf16[512,1024]{1,0:T(8,128)(2,1)} %copy-done.31, ...), kind=kOutput, calls=%fused_computation.9 | convolution fusion | flops 9720561664 | bytes 18350080 | tf_op jit(solution)/shard_map/dot_general | solution.py:76
  247.5 4.0 %multiply_reduce_fusion = (f32[1024]{0:T(1024)S(1)}, f32[512]{0:T(512)S(1)}, f32[512,1024]{1,0:T(8,128)S(1)}) fusion(f32[512,1024]{1,0:T(8,128)} %copy-done.4, f32[512]{0:T(512)S(1)} %add_rsqrt_fusion, f32[1024]{0:T(1024)S(1)} %bitcast.229, bf16[256,1024]{1,0:T(8,128)(2,1)} %collective-permute-done.22, bf16[256,1024]{1,0:T(8,128)(2,1)} %collective-permute-done.21, ...), kind=kLoop, calls=%fused_computation.102 | loop fusion | flops 7862784 | bytes 9449472 | tf_op jit(solution)/shard_map/reduce_sum | solution.py:120
  253.2 4.8 %multiply_reduce_fusion.1 = (f32[1024]{0:T(1024)S(1)}, f32[1024]{0:T(1024)}, f32[1024]{0:T(1024)}, f32[512,1024]{1,0:T(8,128)S(1)}, f32[512,1024]{1,0:T(8,128)S(1)}) fusion(f32[2,258,1024]{2,1,0:T(8,128)S(1)} %copy-done.2, f32[2,256]{1,0:T(2,128)S(1)} %get-tuple-element.331, f32[2,256]{1,0:T(2,128)S(1)} %get-tuple-element.330, f32[528,3072]{1,0:T(8,128)} %copy-done.3, ...), kind=kOutput, calls=%fused_computation.103 | convolution fusion | flops 1078981632 | bytes 16793600 | tf_op jit(solution)/shard_map/dot_general | solution.py:80
  265.6 3.5 convolution_convert_fusion
  276.9 9.4 %fusion.57 = (f32[512]{0:T(512)}, f32[1024]{0:T(1024)}, f32[512,1024]{1,0:T(8,128)}) fusion(bf16[2,256,1024]{2,1,0:T(8,128)(2,1)S(1)} %copy-done.13, f32[1024]{0:T(1024)S(1)} %bitcast.233, f32[512]{0:T(512)S(1)} %bitcast.242, bf16[1024,3072]{1,0:T(8,128)(2,1)} %bitcast.197, bf16[512,1024]{1,0:T(8,128)(2,1)} %copy-done.37, bf16[512,1024]{1,0:T(8,128)(2,1)} %copy-done.28, ...), kind=kOutput, calls=%fused_computation.95 | convolution fusion | flops 3234331136 | bytes 12595200 | tf_op jit(solution)/shard_map/dot_general | solution.py:80
  291.7 3.5 fusion.60
  298.6 4.2 %add_convert_fusion = bf16[512,3072]{1,0:T(8,128)(2,1)S(1)} fusion(bf16[512,3072]{1,0:T(8,128)(2,1)} %collective-permute-done.25, bf16[512,512]{1,0:T(8,128)(2,1)S(1)} %copy-done.44, bf16[512,1024]{1,0:T(8,128)(2,1)S(1)} %copy-done.38, bf16[512,1024]{1,0:T(8,128)(2,1)S(1)} %copy-done.29, bf16[512,1024]{1,0:T(8,128)(2,1)S(1)} %copy-done.36), kind=kOutput, calls=%fused_computation.8 | convolution fusion | flops 1624768512 | bytes 9961472 | tf_op jit(solution)/shard_map/dot_general | solution.py:76
  308.9 8.6 %collective-permute-done.30 = bf16[2,32,4224]{2,1,0:T(8,128)(2,1)S(1)} collective-permute-done((bf16[2,32,4224]{2,1,0:T(8,128)(2,1)S(1)}, bf16[2,32,4224]{2,1,0:T(8,128)(2,1)S(1)}, u32[]{:S(2)}, u32[]{:S(2)}) %collective-permute-start.30) | collective-permute-done | bytes 540704 | tf_op jit(solution)/shard_map/ppermute | solution.py:39
  327.9 21.5 %collective-permute-done.36 = bf16[32,2304]{1,0:T(8,128)(2,1)S(1)} collective-permute-done((bf16[32,2304]{1,0:T(8,128)(2,1)S(1)}, bf16[32,2304]{1,0:T(8,128)(2,1)S(1)}, u32[]{:S(2)}, u32[]{:S(2)}) %collective-permute-start.36) | collective-permute-done | bytes 147488 | tf_op jit(solution)/shard_map/ppermute | solution.py:39
  359.6 4.5 %collective-permute-start.39 = (bf16[32,4224]{1,0:T(8,128)(2,1)S(1)}, bf16[32,4224]{1,0:T(8,128)(2,1)S(1)}, u32[]{:S(2)}, u32[]{:S(2)}) collective-permute-start(bf16[32,4224]{1,0:T(8,128)(2,1)S(1)} %get-tuple-element.276), channel_id=1, source_target_pairs={{0,8},{4,12},{8,16},{12,20},{16,24},{20,28},{24,0},{28,4},{1,9},{5... | collective-permute-start | bytes 811016 | tf_op jit(solution)/shard_map/ppermute | solution.py:35
  372.3 8.9 %collective-permute-done.39 = bf16[32,4224]{1,0:T(8,128)(2,1)S(1)} collective-permute-done((bf16[32,4224]{1,0:T(8,128)(2,1)S(1)}, bf16[32,4224]{1,0:T(8,128)(2,1)S(1)}, u32[]{:S(2)}, u32[]{:S(2)}) %collective-permute-start.39) | collective-permute-done | bytes 270368 | tf_op jit(solution)/shard_map/ppermute | solution.py:35
  381.2 3.4 collective-permute-done.40
  (409 shorter events, 176.5 us)
Async XLA Ops:
  7.2 122.4 %all-gather.6.cloned.1.call-start = ((), (), s32[]{:S(2)}) async-start(), calls=%async_computation.5 | async-start | bytes 5308416 | tf_op jit(solution)/shard_map/all_gather | solution.py:205
  11.3 30.5 %collective-permute-start = (bf16[32,4224]{1,0:T(8,128)(2,1)}, bf16[32,4224]{1,0:T(8,128)(2,1)S(1)}, u32[]{:S(2)}, u32[]{:S(2)}) collective-permute-start(bf16[32,4224]{1,0:T(8,128)(2,1)} %get-tuple-element.313), channel_id=1, source_target_pairs={{0,24},{4,28},{8,0},{12,4},{16,8},{20,12},{24,16},{28,20},{1,25},{... | collective-permute-start | bytes 811016 | tf_op jit(solution)/shard_map/ppermute | solution.py:35
  11.3 30.5 %collective-permute-start.1 = (bf16[32,4224]{1,0:T(8,128)(2,1)}, bf16[32,4224]{1,0:T(8,128)(2,1)S(1)}, u32[]{:S(2)}, u32[]{:S(2)}) collective-permute-start(bf16[32,4224]{1,0:T(8,128)(2,1)} %get-tuple-element.313), channel_id=1, source_target_pairs={{0,16},{4,20},{8,24},{12,28},{16,0},{20,4},{24,8},{28,12},{1,17},{... | collective-permute-start | bytes 811016 | tf_op jit(solution)/shard_map/ppermute | solution.py:35
  14.3 27.5 %collective-permute-start.2 = (bf16[32,4224]{1,0:T(8,128)(2,1)}, bf16[32,4224]{1,0:T(8,128)(2,1)S(1)}, u32[]{:S(2)}, u32[]{:S(2)}) collective-permute-start(bf16[32,4224]{1,0:T(8,128)(2,1)} %get-tuple-element.313), channel_id=1, source_target_pairs={{0,8},{4,12},{8,16},{12,20},{16,24},{20,28},{24,0},{28,4},{1,9},{5... | collective-permute-start | bytes 811016 | tf_op jit(solution)/shard_map/ppermute | solution.py:35
  43.8 92.6 %all-gather.4.cloned.1.call-start = ((), (), s32[]{:S(2)}) async-start(), calls=%async_computation.2 | async-start | bytes 2654208 | tf_op jit(solution)/shard_map/all_gather | solution.py:206
  44.8 23.9 %collective-permute-start.7 = (bf16[4,32,4224]{2,1,0:T(8,128)(2,1)S(1)}, bf16[4,32,4224]{2,1,0:T(8,128)(2,1)S(1)}, u32[]{:S(2)}, u32[]{:S(2)}) collective-permute-start(bf16[4,32,4224]{2,1,0:T(8,128)(2,1)S(1)} %bitcast.198), channel_id=1, source_target_pairs={{0,1},{1,0},{2,3},{3,2},{4,5},{5,4},{6,7},{7,6},{8,9},{9,8},{10,11... | collective-permute-start | bytes 3244040 | tf_op jit(solution)/shard_map/ppermute | solution.py:39
  44.8 23.8 %collective-permute-start.8 = (bf16[4,32,4224]{2,1,0:T(8,128)(2,1)S(1)}, bf16[4,32,4224]{2,1,0:T(8,128)(2,1)S(1)}, u32[]{:S(2)}, u32[]{:S(2)}) collective-permute-start(bf16[4,32,4224]{2,1,0:T(8,128)(2,1)S(1)} %bitcast.199), channel_id=1, source_target_pairs={{0,2},{1,3},{2,0},{3,1},{4,6},{5,7},{6,4},{7,5},{8,10},{9,11},{10,... | collective-permute-start | bytes 3244040 | tf_op jit(solution)/shard_map/ppermute | solution.py:39
  83.4 237.3 %reduce-scatter.3.cloned.1.call-start = ((), (), s32[]{:S(2)}) async-start(), calls=%async_computation.3 | async-start | bytes 5308416 | tf_op jit(solution)/shard_map/reduce_scatter | solution.py:348
  84.2 26.7 %collective-permute-start.12 = (bf16[512,1024]{1,0:T(8,128)(2,1)S(1)}, bf16[512,1024]{1,0:T(8,128)(2,1)}, u32[]{:S(2)}, u32[]{:S(2)}) collective-permute-start(bf16[512,1024]{1,0:T(8,128)(2,1)S(1)} %bitcast.218), channel_id=1, source_target_pairs={{0,1},{1,0},{2,3},{3,2},{4,5},{5,4},{6,7},{7,6},{8,9},{9,8},{10,11... | collective-permute-start | bytes 3145736 | tf_op jit(solution)/shard_map/ppermute | solution.py:39
  85.1 25.9 %collective-permute-start.13 = (bf16[512,1024]{1,0:T(8,128)(2,1)S(1)}, bf16[512,1024]{1,0:T(8,128)(2,1)}, u32[]{:S(2)}, u32[]{:S(2)}) collective-permute-start(bf16[512,1024]{1,0:T(8,128)(2,1)S(1)} %bitcast.219), channel_id=1, source_target_pairs={{0,2},{1,3},{2,0},{3,1},{4,6},{5,7},{6,4},{7,5},{8,10},{9,11},{10,... | collective-permute-start | bytes 3145736 | tf_op jit(solution)/shard_map/ppermute | solution.py:39
  127.8 24.2 %collective-permute-start.16 = (bf16[512,1024]{1,0:T(8,128)(2,1)S(1)}, bf16[512,1024]{1,0:T(8,128)(2,1)}, u32[]{:S(2)}, u32[]{:S(2)}) collective-permute-start(bf16[512,1024]{1,0:T(8,128)(2,1)S(1)} %multiply_convert_fusion.12), channel_id=1, source_target_pairs={{0,1},{1,0},{2,3},{3,2},{4,5},{5,4},{6,7},{7,6},{8,9},{9,8},{10,11... | collective-permute-start | bytes 3145736 | tf_op jit(solution)/shard_map/ppermute | solution.py:39
  129.2 23.9 %collective-permute-start.17 = (bf16[512,1024]{1,0:T(8,128)(2,1)S(1)}, bf16[512,1024]{1,0:T(8,128)(2,1)}, u32[]{:S(2)}, u32[]{:S(2)}) collective-permute-start(bf16[512,1024]{1,0:T(8,128)(2,1)S(1)} %multiply_convert_fusion.12), channel_id=1, source_target_pairs={{0,2},{1,3},{2,0},{3,1},{4,6},{5,7},{6,4},{7,5},{8,10},{9,11},{10,... | collective-permute-start | bytes 3145736 | tf_op jit(solution)/shard_map/ppermute | solution.py:39
  159.1 14.9 %collective-permute-start.19 = (bf16[256,1024]{1,0:T(8,128)(2,1)S(1)}, bf16[256,1024]{1,0:T(8,128)(2,1)S(1)}, u32[]{:S(2)}, u32[]{:S(2)}) collective-permute-start(bf16[256,1024]{1,0:T(8,128)(2,1)S(1)} %slice.363), channel_id=1, source_target_pairs={{0,1},{1,0},{2,3},{3,2},{4,5},{5,4},{6,7},{7,6},{8,9},{9,8},{10,11... | collective-permute-start | bytes 1572872 | tf_op jit(solution)/shard_map/ppermute | solution.py:39
  159.8 14.2 %collective-permute-start.18 = (bf16[256,1024]{1,0:T(8,128)(2,1)S(1)}, bf16[256,1024]{1,0:T(8,128)(2,1)S(1)}, u32[]{:S(2)}, u32[]{:S(2)}) collective-permute-start(bf16[256,1024]{1,0:T(8,128)(2,1)S(1)} %slice.362), channel_id=1, source_target_pairs={{0,2},{1,3},{2,0},{3,1},{4,6},{5,7},{6,4},{7,5},{8,10},{9,11},{10,... | collective-permute-start | bytes 1572872 | tf_op jit(solution)/shard_map/ppermute | solution.py:39
  167.0 38.7 %collective-permute-start.20 = (bf16[512,1024]{1,0:T(8,128)(2,1)S(1)}, bf16[512,1024]{1,0:T(8,128)(2,1)S(1)}, u32[]{:S(2)}, u32[]{:S(2)}) collective-permute-start(bf16[512,1024]{1,0:T(8,128)(2,1)S(1)} %convolution_convert_fusion.2), channel_id=1, source_target_pairs={{0,1},{1,0},{2,3},{3,2},{4,5},{5,4},{6,7},{7,6},{8,9},{9,8},{10,11... | collective-permute-start | bytes 3145736 | tf_op jit(solution)/shard_map/ppermute | solution.py:39
  196.8 50.5 %collective-permute-start.23 = (bf16[512,1024]{1,0:T(8,128)(2,1)}, bf16[512,1024]{1,0:T(8,128)(2,1)}, u32[]{:S(2)}, u32[]{:S(2)}) collective-permute-start(bf16[512,1024]{1,0:T(8,128)(2,1)} %convolution_convert_fusion.1), channel_id=1, source_target_pairs={{0,2},{1,3},{2,0},{3,1},{4,6},{5,7},{6,4},{7,5},{8,10},{9,11},{10,... | collective-permute-start | bytes 3145736 | tf_op jit(solution)/shard_map/ppermute | solution.py:39
  197.3 33.4 %collective-permute-start.21 = (bf16[256,1024]{1,0:T(8,128)(2,1)}, bf16[256,1024]{1,0:T(8,128)(2,1)}, u32[]{:S(2)}, u32[]{:S(2)}) collective-permute-start(bf16[256,1024]{1,0:T(8,128)(2,1)} %convolution_convert_fusion.7), channel_id=1, source_target_pairs={{0,3},{1,2},{2,1},{3,0},{4,7},{5,6},{6,5},{7,4},{8,11},{9,10},{10,... | collective-permute-start | bytes 1572872 | tf_op jit(solution)/shard_map/ppermute | solution.py:39
  199.0 48.4 %collective-permute-start.22 = (bf16[256,1024]{1,0:T(8,128)(2,1)}, bf16[256,1024]{1,0:T(8,128)(2,1)}, u32[]{:S(2)}, u32[]{:S(2)}) collective-permute-start(bf16[256,1024]{1,0:T(8,128)(2,1)} %convolution_convert_fusion.6), channel_id=1, source_target_pairs={{0,3},{1,2},{2,1},{3,0},{4,7},{5,6},{6,5},{7,4},{8,11},{9,10},{10,... | collective-permute-start | bytes 1572872 | tf_op jit(solution)/shard_map/ppermute | solution.py:39
  247.4 112.1 %reduce-scatter.5.cloned.1.call-start = ((), (), s32[]{:S(2)}) async-start(), calls=%async_computation.4 | async-start | bytes 2654208 | tf_op jit(solution)/shard_map/reduce_scatter | solution.py:349
  269.1 29.4 %collective-permute-start.25 = (bf16[512,3072]{1,0:T(8,128)(2,1)}, bf16[512,3072]{1,0:T(8,128)(2,1)}, u32[]{:S(2)}, u32[]{:S(2)}) collective-permute-start(bf16[512,3072]{1,0:T(8,128)(2,1)} %convolution_convert_fusion), channel_id=1, source_target_pairs={{0,4},{4,0},{8,12},{12,8},{16,20},{20,16},{24,28},{28,24},{1,5},{5... | collective-permute-start | bytes 9437192 | tf_op jit(solution)/shard_map/ppermute | solution.py:30
  276.5 19.5 %collective-permute-start.26 = (bf16[512,1024]{1,0:T(8,128)(2,1)}, bf16[512,1024]{1,0:T(8,128)(2,1)}, u32[]{:S(2)}, u32[]{:S(2)}) collective-permute-start(bf16[512,1024]{1,0:T(8,128)(2,1)} %convolution_convert_fusion.3), channel_id=1, source_target_pairs={{0,4},{4,0},{8,12},{12,8},{16,20},{20,16},{24,28},{28,24},{1,5},{5... | collective-permute-start | bytes 3145736 | tf_op jit(solution)/shard_map/ppermute | solution.py:30
  287.8 15.5 %collective-permute-start.28 = (bf16[256,1024]{1,0:T(8,128)(2,1)}, bf16[256,1024]{1,0:T(8,128)(2,1)S(1)}, u32[]{:S(2)}, u32[]{:S(2)}) collective-permute-start(bf16[256,1024]{1,0:T(8,128)(2,1)} %convolution_convert_fusion.5), channel_id=1, source_target_pairs={{0,1},{1,0},{2,3},{3,2},{4,5},{5,4},{6,7},{7,6},{8,9},{9,8},{10,11... | collective-permute-start | bytes 1572872 | tf_op jit(solution)/shard_map/ppermute | solution.py:39
  319.5 35.3 %collective-permute-start.32 = (bf16[4,32,4224]{2,1,0:T(8,128)(2,1)}, bf16[4,32,4224]{2,1,0:T(8,128)(2,1)S(1)}, u32[]{:S(2)}, u32[]{:S(2)}) collective-permute-start(bf16[4,32,4224]{2,1,0:T(8,128)(2,1)} %pad_maximum_fusion.7), channel_id=1, source_target_pairs={{0,1},{1,0},{2,3},{3,2},{4,5},{5,4},{6,7},{7,6},{8,9},{9,8},{10,11... | collective-permute-start | bytes 3244040 | tf_op jit(solution)/shard_map/ppermute | solution.py:39
  321.8 27.5 %collective-permute-start.36 = (bf16[32,2304]{1,0:T(8,128)(2,1)S(1)}, bf16[32,2304]{1,0:T(8,128)(2,1)S(1)}, u32[]{:S(2)}, u32[]{:S(2)}) collective-permute-start(bf16[32,2304]{1,0:T(8,128)(2,1)S(1)} %get-tuple-element.302), channel_id=1, source_target_pairs={{0,3},{1,2},{2,1},{3,0},{4,7},{5,6},{6,5},{7,4},{8,11},{9,10},{10,... | collective-permute-start | bytes 442376 | tf_op jit(solution)/shard_map/ppermute | solution.py:39
  323.6 25.8 %collective-permute-start.35 = (bf16[32,2304]{1,0:T(8,128)(2,1)S(1)}, bf16[32,2304]{1,0:T(8,128)(2,1)S(1)}, u32[]{:S(2)}, u32[]{:S(2)}) collective-permute-start(bf16[32,2304]{1,0:T(8,128)(2,1)S(1)} %get-tuple-element.303), channel_id=1, source_target_pairs={{0,2},{1,3},{2,0},{3,1},{4,6},{5,7},{6,4},{7,5},{8,10},{9,11},{10,... | collective-permute-start | bytes 442376 | tf_op jit(solution)/shard_map/ppermute | solution.py:39
  324.2 26.1 %collective-permute-start.34 = (bf16[32,2304]{1,0:T(8,128)(2,1)S(1)}, bf16[32,2304]{1,0:T(8,128)(2,1)S(1)}, u32[]{:S(2)}, u32[]{:S(2)}) collective-permute-start(bf16[32,2304]{1,0:T(8,128)(2,1)S(1)} %get-tuple-element.304), channel_id=1, source_target_pairs={{0,1},{1,0},{2,3},{3,2},{4,5},{5,4},{6,7},{7,6},{8,9},{9,8},{10,11... | collective-permute-start | bytes 442376 | tf_op jit(solution)/shard_map/ppermute | solution.py:39
  326.5 28.3 %collective-permute-start.33 = (bf16[4,32,4224]{2,1,0:T(8,128)(2,1)}, bf16[4,32,4224]{2,1,0:T(8,128)(2,1)}, u32[]{:S(2)}, u32[]{:S(2)}) collective-permute-start(bf16[4,32,4224]{2,1,0:T(8,128)(2,1)} %pad_maximum_fusion.8), channel_id=1, source_target_pairs={{0,2},{1,3},{2,0},{3,1},{4,6},{5,7},{6,4},{7,5},{8,10},{9,11},{10,... | collective-permute-start | bytes 3244040 | tf_op jit(solution)/shard_map/ppermute | solution.py:39
  354.8 33.8 %collective-permute-start.38 = (bf16[512,1024]{1,0:T(8,128)(2,1)}, bf16[512,1024]{1,0:T(8,128)(2,1)}, u32[]{:S(2)}, u32[]{:S(2)}) collective-permute-start(bf16[512,1024]{1,0:T(8,128)(2,1)} %pad_maximum_fusion.12), channel_id=1, source_target_pairs={{0,2},{1,3},{2,0},{3,1},{4,6},{5,7},{6,4},{7,5},{8,10},{9,11},{10,... | collective-permute-start | bytes 3145736 | tf_op jit(solution)/shard_map/ppermute | solution.py:39
  356.0 32.6 %collective-permute-start.37 = (bf16[512,1024]{1,0:T(8,128)(2,1)}, bf16[512,1024]{1,0:T(8,128)(2,1)}, u32[]{:S(2)}, u32[]{:S(2)}) collective-permute-start(bf16[512,1024]{1,0:T(8,128)(2,1)} %pad_maximum_fusion.11), channel_id=1, source_target_pairs={{0,1},{1,0},{2,3},{3,2},{4,5},{5,4},{6,7},{7,6},{8,9},{9,8},{10,11... | collective-permute-start | bytes 3145736 | tf_op jit(solution)/shard_map/ppermute | solution.py:39
  359.6 21.6 %collective-permute-start.39 = (bf16[32,4224]{1,0:T(8,128)(2,1)S(1)}, bf16[32,4224]{1,0:T(8,128)(2,1)S(1)}, u32[]{:S(2)}, u32[]{:S(2)}) collective-permute-start(bf16[32,4224]{1,0:T(8,128)(2,1)S(1)} %get-tuple-element.276), channel_id=1, source_target_pairs={{0,8},{4,12},{8,16},{12,20},{16,24},{20,28},{24,0},{28,4},{1,9},{5... | collective-permute-start | bytes 811016 | tf_op jit(solution)/shard_map/ppermute | solution.py:35
  364.1 20.5 %collective-permute-start.40 = (bf16[32,4224]{1,0:T(8,128)(2,1)S(1)}, bf16[32,4224]{1,0:T(8,128)(2,1)S(1)}, u32[]{:S(2)}, u32[]{:S(2)}) collective-permute-start(bf16[32,4224]{1,0:T(8,128)(2,1)S(1)} %get-tuple-element.275), channel_id=1, source_target_pairs={{0,16},{4,20},{8,24},{12,28},{16,0},{20,4},{24,8},{28,12},{1,17},{... | collective-permute-start | bytes 811016 | tf_op jit(solution)/shard_map/ppermute | solution.py:35
  364.2 21.0 %collective-permute-start.41 = (bf16[32,4224]{1,0:T(8,128)(2,1)S(1)}, bf16[32,4224]{1,0:T(8,128)(2,1)S(1)}, u32[]{:S(2)}, u32[]{:S(2)}) collective-permute-start(bf16[32,4224]{1,0:T(8,128)(2,1)S(1)} %get-tuple-element.274), channel_id=1, source_target_pairs={{0,24},{4,28},{8,0},{12,4},{16,8},{20,12},{24,16},{28,20},{1,25},{... | collective-permute-start | bytes 811016 | tf_op jit(solution)/shard_map/ppermute | solution.py:35
  (108 other events, 744.2 us)
Sparse Core Ops, SparseCore 0:
  43.9 48.1 all-gather.5
  94.3 31.4 all-gather.3
  247.5 53.2 reduce-scatter.2
  303.0 34.1 reduce-scatter.4
